TPU v7x, 32 devices: a whole 2x2x4 slice. The times are simulated.
32 devices in a mesh: dp: 8 (over y, x, core), mp: 4 (over z).
Axes of the slice: x: 2, y: 2, z: 4, core: 2. Of those that a mesh axis runs over, the one named last changes fastest.
Arguments:
- tokens: bfloat16 [16, 1024, 768], P('dp', 'mp'), may hold values from -6 to 6
- segments: int32 [16, 1024], P('dp'), may hold values from 0 to 4, as said below
- qkv_weight: bfloat16 [2, 3, 768, 768], P(None, None, None, 'mp'), may hold values from -0.21875 to 0.21875
- out_weight: bfloat16 [2, 768, 768], P(None, 'mp'), may hold values from -1.75 to 1.75
- up_weight: bfloat16 [2, 768, 3072], P(None, None, 'mp'), may hold values from -0.21875 to 0.21875
- down_projection_weight: bfloat16 [2, 3072, 768], P(None, 'mp'), may hold values from -0.109375 to 0.109375
- norm_gain: float32 [2, 2, 768], replicated, may hold values from 0.5 to 1.5
- norm_bias: float32 [2, 2, 768], replicated, may hold values from -2 to 2
- pos_bias: float32 [2, 1024, 256], replicated, may hold values from -4 to 4
- cotangent: float32 [16, 1024, 768], P('dp', 'mp'), may hold values from -6 to 6
Outputs:
- output: bfloat16 [16, 1024, 768], P('dp', 'mp')
- grad_tokens: float32 [16, 1024, 768], P('dp', 'mp')
- grad_qkv_weight: float32 [2, 3, 768, 768], P(None, None, None, 'mp')
- grad_out_weight: float32 [2, 768, 768], P(None, 'mp')
- grad_up_weight: float32 [2, 768, 3072], P(None, None, 'mp')
- grad_down_weight: float32 [2, 3072, 768], P(None, 'mp')
- grad_norm_gain: float32 [2, 2, 768], replicated
- grad_norm_bias: float32 [2, 2, 768], replicated
- grad_pos_bias: float32 [2, 1024, 256], replicated
Inputs may be any that keep to these rules, and one draw needn't show every extreme that they name: `segments`: in each sequence the document numbers start at 0, never fall and rise by at most one from one position to the next; among the 2 sequences of each index of dp, one has exactly three documents, the first and last each within 128 positions of the sequence's ends, and every other sequence ends with document number max(4, 1).
All inputs are finite; a program needn't handle non-finite values.
Results may differ from a plain program's by a relative error of at most 0.02.
Values may be sent and summed in bfloat16 or wider, within the bound.
No kernel may reach another device: no remote copies, remote signals or barrier semaphores. Data moves between devices by JAX's collectives and lax.ppermute only.
A program may use at most 192 MiB of HBM per device.

v0:
```python
import jax
import jax.numpy as jnp
from jax import lax
from jax.sharding import PartitionSpec as P


def layer_norm(values, gain_vec, shift_vec):
    center = values - jnp.mean(values, axis=-1, keepdims=True)
    inv_std = lax.rsqrt(jnp.mean(center * center, axis=-1, keepdims=True) + 1e-05)
    normal = center * inv_std
    return (normal * gain_vec + shift_vec, normal, inv_std)


def norm_back(output_gradient, normal, inv_std, gain_vec):
    grad_normal = output_gradient * gain_vec
    mean_one = jnp.mean(grad_normal, axis=-1, keepdims=True)
    mean_two = jnp.mean(grad_normal * normal, axis=-1, keepdims=True)
    return inv_std * (grad_normal - mean_one - normal * mean_two)


def spread_band(band_rows):
    q_rows, window = band_rows.shape
    flipped = band_rows[:, ::-1]
    padded = jnp.concatenate([flipped, jnp.zeros((q_rows, q_rows + 1), band_rows.dtype)], axis=1)
    flat = jnp.concatenate([jnp.zeros((1,), band_rows.dtype), padded.reshape(-1)])
    return flat[: q_rows * (q_rows + window)].reshape(q_rows, q_rows + window)


def fold_band(matrix):
    q_rows, columns = matrix.shape
    window = columns - q_rows
    flat = jnp.concatenate([matrix.reshape(-1)[1:], jnp.zeros((q_rows + 1,), matrix.dtype)])
    return flat.reshape(q_rows, columns + 1)[:, :window][:, ::-1]


def pad_front(values, window, fill_value):
    return jnp.concatenate(
        [jnp.full((window,) + values.shape[1:], fill_value, values.dtype), values], axis=0
    )


def block_weights(band_exp, seg_rows, padded_seg, offset, q_block, window):
    spread = spread_band(band_exp[offset : offset + q_block])
    query_seg = jnp.transpose(seg_rows[offset : offset + q_block])
    key_seg = jnp.transpose(padded_seg[offset : offset + q_block + window])
    same_doc = query_seg[:, :, None] == key_seg[:, None, :]
    return jnp.where(same_doc, spread[None, :, :], jnp.zeros_like(spread)[None, :, :])


def mixing_sums(keyvals, seg_rows, band_exp, window):
    length = keyvals.shape[0]
    q_block = min(512, length)
    padded_kv = pad_front(keyvals, window, 0)
    padded_seg = pad_front(seg_rows, window, -1)
    results = []
    for offset in range(0, length, q_block):
        weights = block_weights(band_exp, seg_rows, padded_seg, offset, q_block, window).astype(
            jnp.bfloat16
        )
        results.append(
            jnp.einsum(
                "sqk,ksc->qsc",
                weights,
                padded_kv[offset : offset + q_block + window],
                preferred_element_type=jnp.float32,
            )
        )
    return jnp.concatenate(results, axis=0)


def mixing_back(grad_sums, keyvals, seg_rows, band_exp, window):
    length = keyvals.shape[0]
    q_block = min(512, length)
    padded_kv = pad_front(keyvals, window, 0)
    padded_seg = pad_front(seg_rows, window, -1)
    grad_pad = jnp.zeros(padded_kv.shape, jnp.float32)
    band_parts = []
    for offset in range(0, length, q_block):
        masked = block_weights(band_exp, seg_rows, padded_seg, offset, q_block, window)
        weights = masked.astype(jnp.bfloat16)
        rows_grad = grad_sums[offset : offset + q_block]
        key_part = padded_kv[offset : offset + q_block + window]
        grad_pad = grad_pad.at[offset : offset + q_block + window].add(
            jnp.einsum("sqk,qsc->ksc", weights, rows_grad, preferred_element_type=jnp.float32)
        )
        grad_weights = jnp.einsum(
            "qsc,ksc->sqk", rows_grad, key_part, preferred_element_type=jnp.float32
        )
        band_parts.append(fold_band(jnp.sum(grad_weights * masked, axis=0)))
    return (grad_pad[window:], jnp.concatenate(band_parts, axis=0))


def project_rows(normed_low, weight):
    gathered = lax.all_gather(normed_low, "mp", axis=0, tiled=True)
    projected_rows = jnp.einsum("lsd,dc->lsc", gathered, weight, preferred_element_type=jnp.float32)
    return (gathered, projected_rows)


def weight_grad(kept_rows, grad_low):
    result = jnp.einsum("lsd,lsc->dc", kept_rows, grad_low, preferred_element_type=jnp.float32)
    return result


def branch_sum(lhs_low, weight):
    return lax.psum_scatter(
        jnp.einsum("lsc,cd->lsd", lhs_low, weight, preferred_element_type=jnp.float32),
        "mp",
        scatter_dimension=0,
        tiled=True,
    )


def back_rows(grad_low, weight):
    return lax.psum_scatter(
        jnp.einsum("lsc,dc->lsd", grad_low, weight, preferred_element_type=jnp.float32).astype(
            jnp.bfloat16
        ),
        "mp",
        scatter_dimension=0,
        tiled=True,
    ).astype(jnp.float32)


def gather_grad(grad_stream):
    return lax.all_gather(grad_stream.astype(jnp.bfloat16), "mp", axis=0, tiled=True)


def gelu_tanh(values):
    return jax.nn.gelu(values, approximate=True)


def shards(
    tokens,
    segments,
    qkv_weight,
    out_weight,
    up_weight,
    down_projection_weight,
    norm_gain,
    norm_bias,
    pos_bias,
    cotangent,
):
    seq_dev, shard_len, width = tokens.shape
    layers = qkv_weight.shape[0]
    window = pos_bias.shape[2]
    channels = qkv_weight.shape[-1]
    stream = jnp.transpose(tokens, (1, 0, 2)).astype(jnp.float32)
    seg_rows = jnp.transpose(segments)
    records = []
    for present_rows in range(layers):
        gains = norm_gain[present_rows]
        shifts = norm_bias[present_rows]
        normed, normal_a, inv_a = layer_norm(stream, gains[0], shifts[0])
        normed_low = normed.astype(jnp.bfloat16)
        w_cat = jnp.transpose(qkv_weight[present_rows], (1, 0, 2)).reshape(width, 3 * channels)
        kept_a, projected_rows = project_rows(normed_low, w_cat)
        queries = projected_rows[:, :, :channels]
        value_rows = projected_rows[:, :, 2 * channels :]
        key_exp = jnp.exp(projected_rows[:, :, channels : 2 * channels])
        keyvals = jnp.concatenate(
            [(key_exp * value_rows).astype(jnp.bfloat16), key_exp.astype(jnp.bfloat16)], axis=-1
        )
        band_exp = jnp.exp(pos_bias[present_rows])
        sums = mixing_sums(keyvals, seg_rows, band_exp, window)
        mixed_low = (
            jax.nn.sigmoid(queries) * sums[:, :, :channels] / sums[:, :, channels:]
        ).astype(jnp.bfloat16)
        stream = stream + branch_sum(mixed_low, out_weight[present_rows])
        normed_two, normal_b, inv_b = layer_norm(stream, gains[1], shifts[1])
        normed_low_b = normed_two.astype(jnp.bfloat16)
        kept_b, pre_act = project_rows(normed_low_b, up_weight[present_rows])
        activation_reduced = gelu_tanh(pre_act).astype(jnp.bfloat16)
        stream = stream + branch_sum(activation_reduced, down_projection_weight[present_rows])
        records.append(
            (
                normal_a,
                inv_a,
                kept_a,
                w_cat,
                projected_rows,
                key_exp,
                keyvals,
                band_exp,
                sums,
                mixed_low,
                normal_b,
                inv_b,
                kept_b,
                pre_act,
                activation_reduced,
            )
        )
    output = jnp.transpose(stream, (1, 0, 2)).astype(jnp.bfloat16)
    grad_stream = jnp.transpose(cotangent, (1, 0, 2))
    layer_grads = [None] * layers
    small_parts = [None] * layers
    for present_rows in reversed(range(layers)):
        (
            normal_a,
            inv_a,
            kept_a,
            w_cat,
            projected_rows,
            key_exp,
            keyvals,
            band_exp,
            sums,
            mixed_low,
            normal_b,
            inv_b,
            kept_b,
            pre_act,
            activation_reduced,
        ) = records[present_rows]
        gains = norm_gain[present_rows]
        gradient_complete = gather_grad(grad_stream)
        grad_down = jnp.einsum(
            "vwr,vwc->rc", activation_reduced, gradient_complete, preferred_element_type=jnp.float32
        )
        grad_act = jnp.einsum(
            "rme,ye->rmy",
            gradient_complete,
            down_projection_weight[present_rows],
            preferred_element_type=jnp.float32,
        )
        _, gelu_pull = jax.vjp(gelu_tanh, pre_act)
        grad_pre = gelu_pull(grad_act)[0].astype(jnp.bfloat16)
        grad_up = weight_grad(kept_b, grad_pre)
        grad_normed_b = back_rows(grad_pre, up_weight[present_rows])
        grad_stream = grad_stream + norm_back(grad_normed_b, normal_b, inv_b, gains[1])
        gain_b = jnp.sum(grad_normed_b * normal_b, axis=(0, 1))
        shift_b = jnp.sum(grad_normed_b, axis=(0, 1))
        gradient_complete = gather_grad(grad_stream)
        output_gradient = jnp.einsum(
            "lsc,lsd->cd", mixed_low, gradient_complete, preferred_element_type=jnp.float32
        )
        grad_mixed = jnp.einsum(
            "lsd,cd->lsc",
            gradient_complete,
            out_weight[present_rows],
            preferred_element_type=jnp.float32,
        )
        numerator = sums[:, :, :channels]
        denominator = sums[:, :, channels:]
        sig_query = jax.nn.sigmoid(projected_rows[:, :, :channels])
        grad_query = grad_mixed * (numerator / denominator) * sig_query * (1.0 - sig_query)
        scaled = grad_mixed * sig_query
        grad_num = (scaled / denominator).astype(jnp.bfloat16)
        grad_den = (-scaled * numerator / (denominator * denominator)).astype(jnp.bfloat16)
        grad_kv, band_grad = mixing_back(
            jnp.concatenate([grad_num, grad_den], axis=-1), keyvals, seg_rows, band_exp, window
        )
        grad_carried = grad_kv[:, :, :channels]
        grad_wsum = grad_kv[:, :, channels:]
        grad_value = grad_carried * key_exp
        grad_key = (grad_carried * projected_rows[:, :, 2 * channels :] + grad_wsum) * key_exp
        grad_qkv_low = jnp.concatenate([grad_query, grad_key, grad_value], axis=-1).astype(
            jnp.bfloat16
        )
        grad_cat = weight_grad(kept_a, grad_qkv_low)
        grad_qkv = jnp.transpose(grad_cat.reshape(width, 3, channels), (1, 0, 2))
        grad_normed_a = back_rows(grad_qkv_low, w_cat)
        grad_stream = grad_stream + norm_back(grad_normed_a, normal_a, inv_a, gains[0])
        gain_a = jnp.sum(grad_normed_a * normal_a, axis=(0, 1))
        shift_a = jnp.sum(grad_normed_a, axis=(0, 1))
        grads_here = (grad_qkv, output_gradient, grad_up, grad_down)
        layer_grads[present_rows] = grads_here
        small_parts[present_rows] = (
            jnp.stack([gain_a, gain_b]),
            jnp.stack([shift_a, shift_b]),
            band_grad,
        )
    stacked = tuple(
        (jnp.stack([layer_grads[member][entry] for member in range(layers)]) for entry in range(4))
    )
    stacked = lax.psum((stacked[0], stacked[1], stacked[2], stacked[3]), "dp")
    small_stack = tuple(
        (jnp.stack([small_parts[member][entry] for member in range(layers)]) for entry in range(3))
    )
    gain_sum, shift_sum, band_sum = lax.psum(
        (small_stack[0], small_stack[1], small_stack[2]), ("dp", "mp")
    )
    grad_tokens = jnp.transpose(grad_stream, (1, 0, 2))
    return (
        output,
        grad_tokens,
        stacked[0],
        stacked[1],
        stacked[2],
        stacked[3],
        gain_sum,
        shift_sum,
        band_sum,
    )


def solution(mesh):
    placed = (
        P("dp", "mp", None),
        P("dp", None),
        P(None, None, None, "mp"),
        P(None, "mp", None),
        P(None, None, "mp"),
        P(None, "mp", None),
        P(),
        P(),
        P(),
        P("dp", "mp", None),
    )
    return jax.shard_map(
        shards,
        mesh=mesh,
        in_specs=placed,
        out_specs=(
            P("dp", "mp", None),
            P("dp", "mp", None),
            P(None, None, None, "mp"),
            P(None, "mp", None),
            P(None, None, "mp"),
            P(None, "mp", None),
            P(),
            P(),
            P(),
        ),
        check_vma=False,
    )
```

profile of v0, /device:TPU:9, one launch (start us, length us, event | category | flops | bytes accessed | tf_op | source)
XLA Modules:
  0.0 1725.8 jit_solution(9369889578015069523)
XLA Ops:
  15.9 3.8 rev.28
  21.8 3.9 reshape.298
  31.8 3.8 reshape.297
  37.0 3.8 reshape.300
  40.8 4.4 pad_maximum_fusion.3
  50.3 23.7 %all-gather.9.cloned.1.call-done = bf16[1024,2,768]{2,0,1:T(8,128)(2,1)} async-done(((bf16[256,2,768]{2,0,1:T(8,128)(2,1)}), bf16[1024,2,768]{2,0,1:T(8,128)(2,1)}) %all-gather.9.cloned.1.call-update) | async-done | bytes 3145744 | tf_op jit(solution)/shard_map/all_gather | solution.py:94
  73.9 3.9 fusion.212
  85.0 3.7 fusion.170
  89.3 111.5 %reduce-scatter.9.cloned.1.call-done = f32[256,2,768]{2,0,1:T(8,128)} async-done(((f32[1024,2,768]{2,0,1:T(8,128)}), f32[256,2,768]{2,0,1:T(8,128)}) %reduce-scatter.9.cloned.1.call-update) | async-done | bytes 1572880 | tf_op jit(solution)/shard_map/reduce_scatter | solution.py:105
  204.0 61.6 %all-gather.11.cloned.1.call-done = bf16[1024,2,768]{2,0,1:T(8,128)(2,1)} async-done(((bf16[256,2,768]{2,0,1:T(8,128)(2,1)}), bf16[1024,2,768]{2,0,1:T(8,128)(2,1)}) %all-gather.11.cloned.1.call-update) | async-done | bytes 3145744 | tf_op jit(solution)/shard_map/all_gather | solution.py:94
  265.7 5.0 fusion.146
  273.3 5.7 fusion.143
  286.5 104.6 %reduce-scatter.11.cloned.1.call-done = f32[256,2,768]{2,0,1:T(8,128)} async-done(((f32[1024,2,768]{2,0,1:T(8,128)}), f32[256,2,768]{2,0,1:T(8,128)}) %reduce-scatter.11.cloned.1.call-update) | async-done | bytes 1572880 | tf_op jit(solution)/shard_map/reduce_scatter | solution.py:105
  402.8 53.2 %all-gather.13.cloned.1.call-done = bf16[1024,2,768]{2,0,1:T(8,128)(2,1)} async-done(((bf16[256,2,768]{2,0,1:T(8,128)(2,1)}), bf16[1024,2,768]{2,0,1:T(8,128)(2,1)}) %all-gather.13.cloned.1.call-update) | async-done | bytes 3145744 | tf_op jit(solution)/shard_map/all_gather | solution.py:94
  456.0 4.1 fusion.213
  468.9 3.7 fusion.166
  472.7 112.0 %reduce-scatter.13.cloned.1.call-done = f32[256,2,768]{2,0,1:T(8,128)} async-done(((f32[1024,2,768]{2,0,1:T(8,128)}), f32[256,2,768]{2,0,1:T(8,128)}) %reduce-scatter.13.cloned.1.call-update) | async-done | bytes 1572880 | tf_op jit(solution)/shard_map/reduce_scatter | solution.py:105
  591.5 59.0 %all-gather.15.cloned.1.call-done = bf16[1024,2,768]{2,0,1:T(8,128)(2,1)} async-done(((bf16[256,2,768]{2,0,1:T(8,128)(2,1)}), bf16[1024,2,768]{2,0,1:T(8,128)(2,1)}) %all-gather.15.cloned.1.call-update) | async-done | bytes 3145744 | tf_op jit(solution)/shard_map/all_gather | solution.py:94
  650.5 7.5 fusion.140
  658.0 56.8 %all-gather.17.cloned.1.call-done = bf16[1024,2,768]{2,0,1:T(8,128)(2,1)} async-done(((bf16[256,2,768]{2,0,1:T(8,128)(2,1)}), bf16[1024,2,768]{2,0,1:T(8,128)(2,1)}) %all-gather.17.cloned.1.call-update) | async-done | bytes 3145744 | tf_op jit(solution)/shard_map/all_gather | solution.py:125
  714.8 8.5 fusion.13
  725.0 4.0 convolution_convert_fusion.3
  729.1 61.0 %reduce-scatter.17.cloned.1.call-done = bf16[256,2,768]{2,0,1:T(8,128)(2,1)} async-done(((bf16[1024,2,768]{2,0,1:T(8,128)(2,1)}), bf16[256,2,768]{2,0,1:T(8,128)(2,1)}) %reduce-scatter.17.cloned.1.call-update) | async-done | bytes 786448 | tf_op jit(solution)/shard_map/reduce_scatter | solution.py:114
  796.6 61.2 %all-gather.19.cloned.1.call-done = bf16[1024,2,768]{2,0,1:T(8,128)(2,1)} async-done(((bf16[256,2,768]{2,0,1:T(8,128)(2,1)}), bf16[1024,2,768]{2,0,1:T(8,128)(2,1)}) %all-gather.19.cloned.1.call-update) | async-done | bytes 3145744 | tf_op jit(solution)/shard_map/all_gather | solution.py:125
  857.9 5.7 multiply_convert_fusion.5
  869.2 4.0 convolution_convert_fusion.1
  873.3 9.6 fusion.137
  883.0 51.4 %reduce-scatter.19.cloned.1.call-done = bf16[256,2,768]{2,0,1:T(8,128)(2,1)} async-done(((bf16[1024,2,768]{2,0,1:T(8,128)(2,1)}), bf16[256,2,768]{2,0,1:T(8,128)(2,1)}) %reduce-scatter.19.cloned.1.call-update) | async-done | bytes 786448 | tf_op jit(solution)/shard_map/reduce_scatter | solution.py:114
  936.3 111.5 %reduce-scatter.15.cloned.1.call-done = f32[256,2,768]{2,0,1:T(8,128)} async-done(((f32[1024,2,768]{2,0,1:T(8,128)}), f32[256,2,768]{2,0,1:T(8,128)}) %reduce-scatter.15.cloned.1.call-update) | async-done | bytes 1572880 | tf_op jit(solution)/shard_map/reduce_scatter | solution.py:105
  1047.8 4.5 fusion.206
  1052.6 61.5 %all-gather.21.cloned.1.call-done = bf16[1024,2,768]{2,0,1:T(8,128)(2,1)} async-done(((bf16[256,2,768]{2,0,1:T(8,128)(2,1)}), bf16[1024,2,768]{2,0,1:T(8,128)(2,1)}) %all-gather.21.cloned.1.call-update) | async-done | bytes 3145744 | tf_op jit(solution)/shard_map/all_gather | solution.py:125
  1114.1 8.5 fusion.6
  1124.2 4.0 convolution_convert_fusion.2
  1128.3 61.0 %reduce-scatter.21.cloned.1.call-done = bf16[256,2,768]{2,0,1:T(8,128)(2,1)} async-done(((bf16[1024,2,768]{2,0,1:T(8,128)(2,1)}), bf16[256,2,768]{2,0,1:T(8,128)(2,1)}) %reduce-scatter.21.cloned.1.call-update) | async-done | bytes 786448 | tf_op jit(solution)/shard_map/reduce_scatter | solution.py:114
  1192.8 61.6 %all-gather.23.cloned.1.call-done = bf16[1024,2,768]{2,0,1:T(8,128)(2,1)} async-done(((bf16[256,2,768]{2,0,1:T(8,128)(2,1)}), bf16[1024,2,768]{2,0,1:T(8,128)(2,1)}) %all-gather.23.cloned.1.call-update) | async-done | bytes 3145744 | tf_op jit(solution)/shard_map/all_gather | solution.py:125
  1254.5 5.7 multiply_convert_fusion.3
  1265.8 4.1 convolution_convert_fusion
  1270.2 7.1 convolution_bitcast_fusion.2
  1277.3 7.9 convolution_bitcast_fusion
  1299.7 4.2 reshape.309
  1305.8 5.0 rev.34
  1320.4 3.6 convolution_bitcast_fusion.4
  1355.4 4.2 reshape.305
  1361.5 5.0 rev.32
  1389.4 41.4 %all-reduce.13 = (f32[2,2,768]{2,1,0:T(2,128)}, f32[2,2,768]{2,1,0:T(2,128)}) all-reduce(f32[2,2,768]{2,1,0:T(2,128)S(1)} %pad_maximum_fusion.25, f32[2,2,768]{2,1,0:T(2,128)S(1)} %pad_maximum_fusion.26), channel_id=1, replica_groups=mesh['dp'=8,'mp'=4] {'dp','mp'}, use_global_device_ids=true, to_apply=%region_32.33 | all-reduce | flops 6144 | bytes 49152 | tf_op jit(solution)/shard_map/psum | solution.py:281
  1434.2 74.7 %all-reduce.18.cloned.1.call-done = f32[2,1024,256]{2,1,0:T(8,128)} async-done(((f32[2,1024,256]{2,1,0:T(8,128)}), f32[2,1024,256]{2,1,0:T(8,128)}) %all-reduce.18.cloned.1.call-update) | async-done | bytes 2097168 | tf_op jit(solution)/shard_map/psum | solution.py:281
  1508.9 196.5 %all-reduce.20.cloned.1.call-done = (f32[2,3,768,192]{2,3,1,0:T(8,128)}, f32[2,192,768]{2,1,0:T(8,128)}, f32[2,768,768]{2,1,0:T(8,128)}, f32[2,768,768]{2,1,0:T(8,128)}) async-done(((f32[2,3,768,192]{2,3,1,0:T(8,128)}, f32[2,192,768]{2,1,0:T(8,128)}, f32[2,768,768]{2,1,0:T(8,128)}, f32[2,768,768]{2,1,0:T(8,128)}), (f32[2,3,768,192]{2,3,1,0:T(8,128)}, f32[2,192,768]{2,1,0:T(8,128)}, ...) | async-done | bytes 14155792 | tf_op jit(solution)/shard_map/psum | solution.py:277
  1705.4 4.3 copy.62
  (391 shorter events, 192.2 us)
Async XLA Ops:
  7.2 66.7 %all-gather.9.cloned.1.call-start = ((), (), s32[]{:S(2)}) async-start(), calls=%async_computation.8 | async-start | bytes 3932160 | tf_op jit(solution)/shard_map/all_gather | solution.py:94
  11.6 189.2 %reduce-scatter.9.cloned.1.call-start = ((), (), s32[]{:S(2)}) async-start(), calls=%async_computation.9 | async-start | bytes 7864320 | tf_op jit(solution)/shard_map/reduce_scatter | solution.py:105
  30.3 48.1 %copy-start.14 = (f32[512,768]{1,0:T(8,128)}, f32[512,768]{1,0:T(8,128)S(1)}, u32[]{:S(2)}) copy-start(f32[512,768]{1,0:T(8,128)S(1)} %broadcast_in_dim.107) | copy-start | bytes 4718596
  50.3 27.6 %copy-start.54 = (bf16[1,3,768,192]{2,3,1,0:T(8,128)(2,1)}, bf16[1,3,768,192]{2,3,1,0:T(8,128)(2,1)S(1)}, u32[]{:S(2)}) copy-start(bf16[1,3,768,192]{2,3,1,0:T(8,128)(2,1)S(1)} %get-tuple-element.116) | copy-start | bytes 2654212
  77.9 5.3 copy-start.5
  88.7 176.9 %all-gather.11.cloned.1.call-start = ((), (), s32[]{:S(2)}) async-start(), calls=%async_computation.10 | async-start | bytes 3932160 | tf_op jit(solution)/shard_map/all_gather | solution.py:94
  204.0 187.2 %reduce-scatter.11.cloned.1.call-start = ((), (), s32[]{:S(2)}) async-start(), calls=%async_computation.11 | async-start | bytes 7864320 | tf_op jit(solution)/shard_map/reduce_scatter | solution.py:105
  265.7 7.7 copy-start.91
  279.1 176.9 %all-gather.13.cloned.1.call-start = ((), (), s32[]{:S(2)}) async-start(), calls=%async_computation.12 | async-start | bytes 3932160 | tf_op jit(solution)/shard_map/all_gather | solution.py:94
  394.3 190.4 %reduce-scatter.13.cloned.1.call-start = ((), (), s32[]{:S(2)}) async-start(), calls=%async_computation.13 | async-start | bytes 7864320 | tf_op jit(solution)/shard_map/reduce_scatter | solution.py:105
  460.2 5.9 copy-start.6
  472.6 177.8 %all-gather.15.cloned.1.call-start = ((), (), s32[]{:S(2)}) async-start(), calls=%async_computation.14 | async-start | bytes 3932160 | tf_op jit(solution)/shard_map/all_gather | solution.py:94
  588.8 126.0 %all-gather.17.cloned.1.call-start = ((), (), s32[]{:S(2)}) async-start(), calls=%async_computation.16 | async-start | bytes 3932160 | tf_op jit(solution)/shard_map/all_gather | solution.py:125
  591.2 198.9 %reduce-scatter.17.cloned.1.call-start = ((), (), s32[]{:S(2)}) async-start(), calls=%async_computation.17 | async-start | bytes 3932160 | tf_op jit(solution)/shard_map/reduce_scatter | solution.py:114
  714.8 10.2 copy-start.92
  729.0 128.8 %all-gather.19.cloned.1.call-start = ((), (), s32[]{:S(2)}) async-start(), calls=%async_computation.18 | async-start | bytes 3932160 | tf_op jit(solution)/shard_map/all_gather | solution.py:125
  796.2 138.2 %reduce-scatter.19.cloned.1.call-start = ((), (), s32[]{:S(2)}) async-start(), calls=%async_computation.19 | async-start | bytes 3932160 | tf_op jit(solution)/shard_map/reduce_scatter | solution.py:114
  857.8 5.7 copy-start.49
  863.5 4.5 copy-start.98
  873.3 174.5 %reduce-scatter.15.cloned.1.call-start = ((), (), s32[]{:S(2)}) async-start(), calls=%async_computation.15 | async-start | bytes 7864320 | tf_op jit(solution)/shard_map/reduce_scatter | solution.py:105
  882.9 231.1 %all-gather.21.cloned.1.call-start = ((), (), s32[]{:S(2)}) async-start(), calls=%async_computation.20 | async-start | bytes 3932160 | tf_op jit(solution)/shard_map/all_gather | solution.py:125
  1052.4 137.0 %reduce-scatter.21.cloned.1.call-start = ((), (), s32[]{:S(2)}) async-start(), calls=%async_computation.21 | async-start | bytes 3932160 | tf_op jit(solution)/shard_map/reduce_scatter | solution.py:114
  1114.0 10.2 copy-start.93
  1128.2 63.1 %copy-start.4 = (f32[256,2,768]{2,0,1:T(8,128)S(1)}, f32[256,2,768]{2,0,1:T(8,128)}, u32[]{:S(2)}) copy-start(f32[256,2,768]{2,0,1:T(8,128)} %get-tuple-element.88) | copy-start | bytes 4718596
  1128.3 126.2 %all-gather.23.cloned.1.call-start = ((), (), s32[]{:S(2)}) async-start(), calls=%async_computation.22 | async-start | bytes 3932160 | tf_op jit(solution)/shard_map/all_gather | solution.py:125
  1192.8 194.2 %reduce-scatter.23.cloned.1.call-start = ((), (), s32[]{:S(2)}) async-start(), calls=%async_computation.23 | async-start | bytes 3932160 | tf_op jit(solution)/shard_map/reduce_scatter | solution.py:114
  1254.5 5.7 copy-start.44
  1260.2 4.5 copy-start.100
  1269.9 238.9 %all-reduce.18.cloned.1.call-start = ((), (), s32[]{:S(2)}) async-start(), calls=%async_computation.24 | async-start | bytes 4194304 | tf_op jit(solution)/shard_map/psum | solution.py:281
  1270.2 7.1 copy-start.89
  1277.3 7.9 copy-start.50
  1277.3 7.9 copy-start.52
  1277.3 7.9 copy-start.58
  1277.3 7.9 copy-start.60
  1313.6 4.5 copy-start.37
  1314.7 5.6 copy-start.10
  1318.1 5.9 copy-start.88
  1324.0 8.6 slice-start.6
  1327.3 5.4 slice-start.7
  1336.8 4.0 copy-start.64
  1370.4 4.3 copy-start.23
  1376.1 3.9 copy-start.32
  1376.1 329.2 %all-reduce.20.cloned.1.call-start = ((), (), s32[]{:S(2)}) async-start(), calls=%async_computation.25 | async-start | bytes 28311552 | tf_op jit(solution)/shard_map/psum | solution.py:277
  1377.2 4.0 copy-start.86
  1386.2 44.6 %copy-start.13 = (bf16[256,2,768]{2,0,1:T(8,128)(2,1)S(1)}, bf16[256,2,768]{2,0,1:T(8,128)(2,1)}, u32[]{:S(2)}) copy-start(bf16[256,2,768]{2,0,1:T(8,128)(2,1)} %reduce-scatter.21.cloned.1.call-done) | copy-start | bytes 2359300
  1705.4 4.4 copy-start.53
  1705.4 5.4 copy-start.22
  1709.7 4.2 slice-start.4
  (80 other events, 166.7 us)
Sparse Core Ops, SparseCore 0:
  11.7 62.2 all-gather.8
  88.9 111.8 reduce-scatter.8
  204.1 61.5 all-gather.10
  279.2 111.9 reduce-scatter.10
  394.5 61.5 all-gather.12
  472.8 111.9 reduce-scatter.12
  588.9 61.5 all-gather.14
  652.6 62.1 all-gather.16
  729.2 60.9 reduce-scatter.16
  796.3 61.4 all-gather.18
  873.4 60.9 reduce-scatter.18
  936.5 111.2 reduce-scatter.14
  1052.5 61.5 all-gather.20
  1128.4 60.9 reduce-scatter.20
  1192.9 61.4 all-gather.22
  1270.0 60.9 reduce-scatter.22
  1376.3 132.5 all-reduce.17
  1513.9 191.4 all-reduce.19
where the time goes:
time: 1740 us; the launch traced here: 1730 us
  waiting for transfers between devices  1320 us (76%)
  matrix products  140 us (8%)
  local copies, waits for them, and re-layouts  136 us (8%)
  other arithmetic  66.9 us (4%)
  blocking collectives  41.4 us (2%)
    reduce_scatter x4, waiting for transfers between devices, branch_sum(): lax.psum_scatter(jnp.einsum('lsc,cd->lsd', lhs_low, weight, preferred_ele...  440 us
    all_gather x4, waiting for transfers between devices, gather_grad(): lax.all_gather(grad_stream.astype(jnp.bfloat16), 'mp', axis=0, tiled=True)  241 us
    all_gather x4, waiting for transfers between devices, project_rows(): gathered = lax.all_gather(normed_low, 'mp', axis=0, tiled=True)  197 us
    psum x1, waiting for transfers between devices, shards(): stacked = lax.psum((stacked[0], stacked[1], stacked[2], stacked[3]), 'dp')  197 us
    reduce_scatter x4, waiting for transfers between devices, back_rows(): lax.psum_scatter(jnp.einsum('lsc,dc->lsd', grad_low, weight, preferred_el...  173 us
    psum x1, waiting for transfers between devices, shards(): lax.psum((small_stack[0], small_stack[1], small_stack[2]), ('dp', 'mp'))  74.7 us
    unnamed x225, local copies, waits for them, and re-layouts  43.9 us
    psum x1, blocking collectives, shards(): lax.psum((small_stack[0], small_stack[1], small_stack[2]), ('dp', 'mp'))  41.4 us
  transfers between devices with their start and end apart: 18, of which 17 were waited for; matrix products, arithmetic and copies ran while one was open for 11% of the time, Pallas kernels for 0%

commit v1 on v0

v1 whole, which is shorter than its diff:
```python
import jax
import jax.numpy as jnp
from jax import lax
from jax.sharding import PartitionSpec as P

BF = jnp.bfloat16
F32 = jnp.float32


def layer_norm(values, gain_vec, shift_vec):
    center = values - jnp.mean(values, axis=-1, keepdims=True)
    inv_std = lax.rsqrt(jnp.mean(center * center, axis=-1, keepdims=True) + 1e-05)
    normal = center * inv_std
    return (normal * gain_vec + shift_vec, normal, inv_std)


def norm_back(output_gradient, normal, inv_std, gain_vec):
    grad_normal = output_gradient * gain_vec
    mean_one = jnp.mean(grad_normal, axis=-1, keepdims=True)
    mean_two = jnp.mean(grad_normal * normal, axis=-1, keepdims=True)
    return inv_std * (grad_normal - mean_one - normal * mean_two)


def spread_band(band_rows):
    q_rows, window = band_rows.shape
    flipped = band_rows[:, ::-1]
    padded = jnp.concatenate([flipped, jnp.zeros((q_rows, q_rows + 1), band_rows.dtype)], axis=1)
    flat = jnp.concatenate([jnp.zeros((1,), band_rows.dtype), padded.reshape(-1)])
    return flat[: q_rows * (q_rows + window)].reshape(q_rows, q_rows + window)


def fold_band(matrix):
    q_rows, columns = matrix.shape
    window = columns - q_rows
    flat = jnp.concatenate([matrix.reshape(-1)[1:], jnp.zeros((q_rows + 1,), matrix.dtype)])
    return flat.reshape(q_rows, columns + 1)[:, :window][:, ::-1]


def dot_nt(lhs, rhs):
    return lax.dot_general(lhs, rhs, (((1,), (1,)), ((), ())), preferred_element_type=F32)


def dot_nn(lhs, rhs):
    return lax.dot_general(lhs, rhs, (((1,), (0,)), ((), ())), preferred_element_type=F32)


def dot_tn(lhs, rhs):
    return lax.dot_general(lhs, rhs, (((0,), (0,)), ((), ())), preferred_element_type=F32)


class Links:
    def __init__(self, dp, mp):
        self.dp = dp
        self.mp = mp
        self.dp_bits = [1 << k for k in range(1, dp.bit_length() - 1)]

    def swap(self, value, axis, bit):
        size = self.dp if axis == "dp" else self.mp
        return lax.ppermute(value, axis, [(i, i ^ bit) for i in range(size)])

    def gather_mp(self, piece):
        parts = [piece] + [self.swap(piece, "mp", p) for p in range(1, self.mp)]
        return jnp.stack(parts, axis=0)

    def scatter_mp(self, blocks):
        total = blocks[0].astype(F32)
        for p in range(1, self.mp):
            total = total + self.swap(blocks[p], "mp", p).astype(F32)
        return total.astype(BF)

    def gather_bits(self, value, bits):
        have = []
        for bit in bits:
            place = sum(1 for other in have if other > bit)
            value = jnp.stack([value, self.swap(value, "dp", bit)], axis=place)
            have.append(bit)
        return value

    def scatter_bits(self, value, bits):
        have = sorted(bits, reverse=True)
        for bit in bits:
            place = have.index(bit)
            keep = lax.index_in_dim(value, 0, place, keepdims=False)
            send = lax.index_in_dim(value, 1, place, keepdims=False)
            value = (keep.astype(F32) + self.swap(send, "dp", bit).astype(F32)).astype(BF)
            have.remove(bit)
        return value

    def gather(self, piece_a, piece_b):
        both = self.gather_mp(jnp.concatenate([piece_a, piece_b], axis=0))
        cut = piece_a.shape[0]
        out = []
        for value, bits in ((both[:, :cut], self.dp_bits), (both[:, cut:], self.dp_bits[::-1])):
            value = self.gather_bits(value, bits)
            value = value.reshape((-1,) + value.shape[-3:])
            out.append((value, self.swap(value, "dp", 1)))
        return out

    def reduce(self, halves_a, halves_b):
        parts = []
        for halves, bits in ((halves_a, self.dp_bits[::-1]), (halves_b, self.dp_bits)):
            own, other = halves
            value = (own.astype(F32) + self.swap(other, "dp", 1).astype(F32)).astype(BF)
            value = value.reshape((2,) * len(bits) + (self.mp,) + value.shape[1:])
            parts.append(self.scatter_bits(value, bits))
        return self.scatter_mp(jnp.concatenate(parts, axis=1))

    def regather(self, piece, index):
        bits = [1] + self.dp_bits
        value = self.gather_bits(piece, self.dp_bits)
        value = jnp.stack([value, self.swap(value, "dp", 1)], axis=len(self.dp_bits))
        value = value.reshape((self.dp,) + piece.shape)
        value = jnp.take(value, jnp.bitwise_xor(jnp.arange(self.dp), index), axis=0)
        value = jnp.transpose(value, (1, 0, 2, 3))
        return value.reshape(piece.shape[0], self.dp * piece.shape[1], piece.shape[2])

    def sum_all(self, value, axis):
        size = self.dp if axis == "dp" else self.mp
        bit = 1
        while bit < size:
            value = value + self.swap(value, axis, bit)
            bit *= 2
        return value


def gelu_tanh(values):
    return jax.nn.gelu(values, approximate=True)


def make_shards(dp, mp):
    links = Links(dp, mp)

    def shards(
        tokens,
        segments,
        qkv_weight,
        out_weight,
        up_weight,
        down_projection_weight,
        norm_gain,
        norm_bias,
        pos_bias,
        cotangent,
    ):
        seqs, block, width = tokens.shape
        layers = qkv_weight.shape[0]
        window = pos_bias.shape[2]
        channels = qkv_weight.shape[-1]
        hidden = up_weight.shape[-1]
        rows = seqs * block
        dp_index = lax.axis_index("dp")
        mp_index = lax.axis_index("mp")

        def own_piece(matrix):
            size = matrix.shape[-2] // dp
            return lax.dynamic_slice_in_dim(matrix, dp_index * size, size, axis=matrix.ndim - 2)

        gathered = []
        for layer in range(layers):
            qkv_rows = jnp.transpose(qkv_weight[layer], (0, 2, 1))
            attn = own_piece(jnp.concatenate([qkv_rows, out_weight[layer][None]], axis=0))
            up = own_piece(jnp.transpose(up_weight[layer])[None])
            down = own_piece(down_projection_weight[layer][None])
            pair_a, pair_b = links.gather(attn[:2], attn[2:])
            mats = []
            for pair in (pair_a, pair_b):
                for m in range(2):
                    mats.append(
                        jnp.concatenate([half[:, m].reshape(-1, width) for half in pair], axis=0)
                    )
            up_pair, down_pair = links.gather(up, down)
            ups = [half.reshape(-1, width) for half in up_pair]
            downs = [half.reshape(-1, width) for half in down_pair]
            gathered.append((mats, ups, downs))

        seg_pad = jnp.concatenate([jnp.full((seqs, window), -1, segments.dtype), segments], axis=1)
        seg_keys = lax.dynamic_slice_in_dim(seg_pad, mp_index * block, block + window, axis=1)
        seg_own = seg_keys[:, window:]
        same_doc = seg_own[:, :, None] == seg_keys[:, None, :]

        stream = tokens.reshape(rows, width).astype(F32)
        records = []
        for layer in range(layers):
            gains = norm_gain[layer]
            shifts = norm_bias[layer]
            (wq, wk, wv, wo), ups, downs = gathered[layer]
            normed, normal_a, inv_a = layer_norm(stream, gains[0], shifts[0])
            normed_a = normed.astype(BF)
            halo = lax.ppermute(normed_a, "mp", [(i, i + 1) for i in range(mp - 1)])
            both = jnp.concatenate(
                [halo.reshape(seqs, block, width), normed_a.reshape(seqs, block, width)], axis=1
            ).reshape(seqs * (window + block), width)
            queries = dot_nt(normed_a, wq)
            keys = dot_nt(both, wk)
            value_rows = dot_nt(both, wv)
            key_exp = jnp.exp(keys)
            keyvals = jnp.concatenate(
                [(key_exp * value_rows).astype(BF), key_exp.astype(BF)], axis=-1
            ).reshape(seqs, window + block, 2 * width)
            band_own = lax.dynamic_slice_in_dim(pos_bias[layer], mp_index * block, block, axis=0)
            spread = spread_band(jnp.exp(band_own))
            masked = jnp.where(same_doc, spread[None], 0.0)
            weights = masked.astype(BF)
            sums = jnp.einsum("sqk,skc->sqc", weights, keyvals, preferred_element_type=F32)
            sums = sums.reshape(rows, 2 * width)
            mixed = (jax.nn.sigmoid(queries) * sums[:, :width] / sums[:, width:]).astype(BF)
            stream = stream + dot_nn(mixed, wo)
            normed_two, normal_b, inv_b = layer_norm(stream, gains[1], shifts[1])
            normed_b = normed_two.astype(BF)
            pres = [dot_nt(normed_b, up) for up in ups]
            acts = [gelu_tanh(pre).astype(BF) for pre in pres]
            for act, down in zip(acts, downs):
                stream = stream + dot_nn(act, down)
            records.append(
                (
                    normal_a, inv_a, normed_a, both, queries, value_rows, key_exp, keyvals,
                    masked, weights, sums, mixed, normal_b, inv_b, normed_b, pres, acts,
                )
            )
        output = stream.astype(BF).reshape(seqs, block, width)

        grad = cotangent.reshape(rows, width)
        weight_out = [None] * layers
        small_out = [None] * layers
        for layer in reversed(range(layers)):
            gains = norm_gain[layer]
            (wq, wk, wv, wo), ups, downs = gathered[layer]
            (
                normal_a, inv_a, normed_a, both, queries, value_rows, key_exp, keyvals,
                masked, weights, sums, mixed, normal_b, inv_b, normed_b, pres, acts,
            ) = records[layer]
            grad_low = grad.astype(BF)
            down_grads = [dot_tn(act, grad_low).astype(BF) for act in acts]
            pre_grads = []
            for pre, down in zip(pres, downs):
                _, pull = jax.vjp(gelu_tanh, pre)
                pre_grads.append(pull(dot_nt(grad_low, down))[0].astype(BF))
            up_grads = [dot_tn(pre_grad, normed_b).astype(BF) for pre_grad in pre_grads]
            shape = (dp // 2 * mp, 1, hidden // dp, width)
            ff_piece = links.reduce(
                [item.reshape(shape) for item in up_grads], [item.reshape(shape) for item in down_grads]
            )
            grad_normed = sum(dot_nn(pre_grad, up) for pre_grad, up in zip(pre_grads, ups))
            grad = grad + norm_back(grad_normed, normal_b, inv_b, gains[1])
            gain_b = jnp.sum(grad_normed * normal_b, axis=0)
            shift_b = jnp.sum(grad_normed, axis=0)

            grad_low = grad.astype(BF)
            out_grad = dot_tn(mixed, grad_low).astype(BF)
            grad_mixed = dot_nt(grad_low, wo)
            numerator = sums[:, :width]
            denominator = sums[:, width:]
            sig = jax.nn.sigmoid(queries)
            grad_q = (grad_mixed * (numerator / denominator) * sig * (1.0 - sig)).astype(BF)
            scaled = grad_mixed * sig
            grad_num = (scaled / denominator).astype(BF)
            grad_den = (-scaled * numerator / (denominator * denominator)).astype(BF)
            grad_sums = jnp.concatenate([grad_num, grad_den], axis=-1).reshape(seqs, block, 2 * width)
            grad_kv = jnp.einsum("sqk,sqc->skc", weights, grad_sums, preferred_element_type=F32)
            grad_weights = jnp.einsum("sqc,skc->sqk", grad_sums, keyvals, preferred_element_type=F32)
            band_grad = fold_band(jnp.sum(grad_weights * masked, axis=0))
            grad_kv = grad_kv.reshape(seqs * (window + block), 2 * width)
            grad_carried = grad_kv[:, :width]
            grad_v = (grad_carried * key_exp).astype(BF)
            grad_k = ((grad_carried * value_rows + grad_kv[:, width:]) * key_exp).astype(BF)
            grad_both = (dot_nn(grad_k, wk) + dot_nn(grad_v, wv)).reshape(seqs, window + block, width)
            back = lax.ppermute(
                grad_both[:, :window].astype(BF), "mp", [(i + 1, i) for i in range(mp - 1)]
            )
            q_grad = dot_tn(grad_q, normed_a).astype(BF)
            k_grad = dot_tn(grad_k, both).astype(BF)
            v_grad = dot_tn(grad_v, both).astype(BF)
            shape = (2, dp // 2 * mp, channels // dp, width)

            def halves(first, second):
                return [
                    jnp.stack([first.reshape(shape)[c], second.reshape(shape)[c]], axis=1)
                    for c in range(2)
                ]

            attn_piece = links.reduce(halves(q_grad, k_grad), halves(v_grad, out_grad))
            grad_normed = dot_nn(grad_q, wq) + (grad_both[:, window:] + back.astype(F32)).reshape(
                rows, width
            )
            grad = grad + norm_back(grad_normed, normal_a, inv_a, gains[0])
            gain_a = jnp.sum(grad_normed * normal_a, axis=0)
            shift_a = jnp.sum(grad_normed, axis=0)
            ff_full = links.regather(ff_piece, dp_index).astype(F32)
            attn_full = links.regather(attn_piece, dp_index).astype(F32)
            weight_out[layer] = (
                jnp.transpose(attn_full[:3], (0, 2, 1)),
                attn_full[3],
                jnp.transpose(ff_full[0]),
                ff_full[1],
            )
            norms = jnp.stack([gain_a, gain_b, shift_a, shift_b]).reshape(-1, window)
            packed = links.sum_all(jnp.concatenate([band_grad, norms], axis=0), "dp")
            spread_out = lax.all_gather(packed[:block], "mp", axis=0, tiled=True)
            norm_sum = links.sum_all(packed[block:], "mp").reshape(4, width)
            small_out[layer] = (norm_sum[:2], norm_sum[2:], spread_out)

        grad_tokens = grad.reshape(seqs, block, width)
        big = tuple(jnp.stack([weight_out[l][k] for l in range(layers)]) for k in range(4))
        small = tuple(jnp.stack([small_out[l][k] for l in range(layers)]) for k in range(3))
        return (output, grad_tokens) + big + small

    return shards


def solution(mesh):
    placed = (
        P("dp", "mp", None),
        P("dp", None),
        P(None, None, None, "mp"),
        P(None, "mp", None),
        P(None, None, "mp"),
        P(None, "mp", None),
        P(),
        P(),
        P(),
        P("dp", "mp", None),
    )
    return jax.shard_map(
        make_shards(mesh.shape["dp"], mesh.shape["mp"]),
        mesh=mesh,
        in_specs=placed,
        out_specs=(
            P("dp", "mp", None),
            P("dp", "mp", None),
            P(None, None, None, "mp"),
            P(None, "mp", None),
            P(None, None, "mp"),
            P(None, "mp", None),
            P(),
            P(),
            P(),
        ),
        check_vma=False,
    )
```

time: 1740 us -> 790 us (0.45)
  waiting for transfers between devices: 1320 us -> 259 us
  starting transfers between devices: 2.39 us -> 119 us
  other arithmetic: 66.9 us -> 114 us
  blocking collectives: 41.4 us -> 0 us
    reduce_scatter x8 -> x0, waiting for transfers between devices: 613 us -> none  [the longest x4 440 us: branch_sum(): lax.psum_scatter(jnp.einsum('lsc,cd->lsd', lhs_low, weight, preferred_ele...]
    all_gather x8 -> x2, waiting for transfers between devices: 439 us -> 0.01 us  [shards(): spread_out = lax.all_gather(packed[:block], 'mp', axis=0, tiled=True)]
    psum x2 -> x0, waiting for transfers between devices: 271 us -> none  [the longest x1 197 us: shards(): stacked = lax.psum((stacked[0], stacked[1], stacked[2], stacked[3]), 'dp')]
    ppermute x0 -> x98, waiting for transfers between devices: none -> 259 us  [the longest x94 234 us: swap(): return lax.ppermute(value, axis, [(i, i ^ bit) for i in range(size)])]
    ppermute x0 -> x98, starting transfers between devices: none -> 119 us  [the longest x94 110 us: swap(): return lax.ppermute(value, axis, [(i, i ^ bit) for i in range(size)])]
    psum x1 -> x0, blocking collectives: 41.4 us -> none  [shards(): lax.psum((small_stack[0], small_stack[1], small_stack[2]), ('dp', 'mp'))]
    another operation x15 -> x49, other arithmetic: 14.7 us -> 51 us  [the longest x20 16.8 us: gather_bits(): value = jnp.stack([value, self.swap(value, 'dp', bit)], axis=place)]
    slice x3 -> x43, local copies, waits for them, and re-layouts: 4.2 us -> 39.1 us  [the longest x8 10.1 us: shards(): half[:, m].reshape(-1, width)]
  transfers between devices with their start and end apart: 18 -> 100, of which waited for: 17 -> 40; matrix products, arithmetic and copies ran while one was open for 11% -> 36% of each run, Pallas kernels for 0% -> 0%
where the time goes in v1:
time: 790 us; the launch traced here: 778 us
  waiting for transfers between devices  259 us (33%)
  matrix products  148 us (19%)
  local copies, waits for them, and re-layouts  120 us (15%)
  starting transfers between devices  119 us (15%)
  other arithmetic  114 us (14%)
  between operations  17.1 us (2%)
    ppermute x94, waiting for transfers between devices, swap(): return lax.ppermute(value, axis, [(i, i ^ bit) for i in range(size)])  234 us
    ppermute x94, starting transfers between devices, swap(): return lax.ppermute(value, axis, [(i, i ^ bit) for i in range(size)])  110 us
    dot_general x16, matrix products, dot_nt(): lax.dot_general(lhs, rhs, (((1,), (1,)), ((), ())), preferred_element_typ...  51.4 us
    dot_general x16, matrix products, dot_nn(): lax.dot_general(lhs, rhs, (((1,), (0,)), ((), ())), preferred_element_typ...  49.3 us
    dot_general x16, matrix products, dot_tn(): lax.dot_general(lhs, rhs, (((0,), (0,)), ((), ())), preferred_element_typ...  36.4 us
    unnamed x351, local copies, waits for them, and re-layouts  35.3 us
    another operation x20, other arithmetic, gather_bits(): value = jnp.stack([value, self.swap(value, 'dp', bit)], axis=place)  16.8 us
    ppermute x2, waiting for transfers between devices, shards(): halo = lax.ppermute(normed_a, 'mp', [(i, i + 1) for i in range(mp - 1)])  16.1 us
  transfers between devices with their start and end apart: 100, of which 40 were waited for; matrix products, arithmetic and copies ran while one was open for 36% of the time, Pallas kernels for 0%

profile of v1, /device:TPU:9, one launch (start us, length us, event | category | flops | bytes accessed | tf_op | source)
XLA Modules:
  0.0 777.9 jit_solution(11792302200769561507)
XLA Ops:
  45.9 10.3 %collective-permute-done.2 = bf16[4,24,768]{2,1,0:T(8,128)(2,1)} collective-permute-done((bf16[4,24,768]{2,1,0:T(8,128)(2,1)}, bf16[4,24,768]{2,1,0:T(8,128)(2,1)}, u32[]{:S(2)}, u32[]{:S(2)}) %collective-permute-start.2) | collective-permute-done | bytes 147488 | tf_op jit(solution)/shard_map/ppermute | solution.py:59
  67.8 4.4 collective-permute-start.30
  79.5 12.8 %collective-permute-done.30 = bf16[2,96,768]{2,1,0:T(8,128)(2,1)S(1)} collective-permute-done((bf16[2,96,768]{2,1,0:T(8,128)(2,1)S(1)}, bf16[2,96,768]{2,1,0:T(8,128)(2,1)S(1)}, u32[]{:S(2)}, u32[]{:S(2)}) %collective-permute-start.30) | collective-permute-done | bytes 294944 | tf_op jit(solution)/shard_map/ppermute | solution.py:59
  102.7 6.5 collective-permute-done.6
  110.6 4.4 collective-permute-done.15
  116.9 10.7 %collective-permute-done.34 = bf16[4,1,96,768]{3,2,0,1:T(8,128)(2,1)S(1)} collective-permute-done((bf16[4,1,96,768]{3,2,0,1:T(8,128)(2,1)S(1)}, bf16[4,1,96,768]{3,2,0,1:T(8,128)(2,1)S(1)}, u32[]{:S(2)}, u32[]{:S(2)}) %collective-permute-start.34) | collective-permute-done | bytes 589856 | tf_op jit(solution)/shard_map/ppermute | solution.py:59
  131.9 8.4 %collective-permute-done.4 = bf16[2,4,2,24,768]{4,3,2,1,0:T(8,128)(2,1)S(1)} collective-permute-done((bf16[2,4,2,24,768]{4,3,2,1,0:T(8,128)(2,1)S(1)}, bf16[2,4,2,24,768]{4,3,2,1,0:T(8,128)(2,1)S(1)}, u32[]{:S(2)}, u32[]{:S(2)}) %collective-permute-start.4) | collective-permute-done | bytes 589856 | tf_op jit(solution)/shard_map/ppermute | solution.py:59
  143.0 9.9 %collective-permute-done.23 = bf16[2,4,2,24,768]{4,3,2,1,0:T(8,128)(2,1)S(1)} collective-permute-done((bf16[2,4,2,24,768]{4,3,2,1,0:T(8,128)(2,1)S(1)}, bf16[2,4,2,24,768]{4,3,2,1,0:T(8,128)(2,1)S(1)}, u32[]{:S(2)}, u32[]{:S(2)}) %collective-permute-start.23) | collective-permute-done | bytes 589856 | tf_op jit(solution)/shard_map/ppermute | solution.py:59
  152.9 5.7 collective-permute-start.5
  164.5 8.2 %collective-permute-done.16 = bf16[2,4,1,96,768]{4,3,1,0,2:T(8,128)(2,1)S(1)} collective-permute-done((bf16[2,4,1,96,768]{4,3,1,0,2:T(8,128)(2,1)S(1)}, bf16[2,4,1,96,768]{4,3,1,0,2:T(8,128)(2,1)S(1)}, u32[]{:S(2)}, u32[]{:S(2)}) %collective-permute-start.16) | collective-permute-done | bytes 1179680 | tf_op jit(solution)/shard_map/ppermute | solution.py:59
  178.2 7.3 collective-permute-start.24
  196.5 4.8 copy.157
  212.0 4.8 fusion.186
  220.0 4.9 fusion.220
  236.9 9.6 %collective-permute-done.25 = bf16[512,768]{1,0:T(8,128)(2,1)S(1)} collective-permute-done((bf16[512,768]{1,0:T(8,128)(2,1)S(1)}, bf16[512,768]{1,0:T(8,128)(2,1)S(1)}, u32[]{:S(2)}, u32[]{:S(2)}) %collective-permute-start.25) | collective-permute-done | bytes 786464 | tf_op jit(solution)/shard_map/ppermute | solution.py:189
  254.3 4.7 copy.158
  268.6 4.2 fusion.225
  272.8 5.9 fusion.187
  278.7 4.6 fusion.24
  283.4 5.6 fusion.31
  293.2 3.6 multiply_reduce_fusion
  310.5 3.7 copy.159
  314.2 6.4 multiply_convert_fusion.3
  359.6 6.0 add_convert_fusion.4
  371.0 4.7 fusion.17
  375.6 5.5 fusion.10
  381.2 3.6 fusion.227
  401.6 3.8 copy.161
  405.5 5.5 multiply_convert_fusion.1
  444.1 4.4 convolution_convert_fusion.6
  460.5 9.1 %collective-permute-done.39 = bf16[2,256,768]{2,1,0:T(8,128)(2,1)S(1)} collective-permute-done((bf16[2,256,768]{2,1,0:T(8,128)(2,1)S(1)}, bf16[2,256,768]{2,1,0:T(8,128)(2,1)S(1)}, u32[]{:S(2)}, u32[]{:S(2)}) %collective-permute-start.39) | collective-permute-done | bytes 786464 | tf_op jit(solution)/shard_map/ppermute | solution.py:267
  473.2 3.7 collective-permute-done.95
  483.3 4.0 collective-permute-start.40
  507.2 13.1 %collective-permute-done.60 = bf16[4,24,768]{2,1,0:T(8,128)(2,1)S(1)} collective-permute-done((bf16[4,24,768]{2,1,0:T(8,128)(2,1)S(1)}, bf16[4,24,768]{2,1,0:T(8,128)(2,1)S(1)}, u32[]{:S(2)}, u32[]{:S(2)}) %collective-permute-start.60) | collective-permute-done | bytes 147488 | tf_op jit(solution)/shard_map/ppermute | solution.py:59
  531.8 11.6 %collective-permute-done.90 = f32[268,256]{1,0:T(8,128)S(1)} collective-permute-done((f32[268,256]{1,0:T(8,128)S(1)}, f32[268,256]{1,0:T(8,128)S(1)}, u32[]{:S(2)}, u32[]{:S(2)}) %collective-permute-start.90) | collective-permute-done | bytes 274464 | tf_op jit(solution)/shard_map/ppermute | solution.py:59
  568.5 17.4 %collective-permute-done.45 = bf16[4,2,24,768]{3,2,1,0:T(8,128)(2,1)S(1)} collective-permute-done((bf16[4,2,24,768]{3,2,1,0:T(8,128)(2,1)S(1)}, bf16[4,2,24,768]{3,2,1,0:T(8,128)(2,1)S(1)}, u32[]{:S(2)}, u32[]{:S(2)}) %collective-permute-start.45) | collective-permute-done | bytes 294944 | tf_op jit(solution)/shard_map/ppermute | solution.py:59
  600.4 7.2 collective-permute-done.78
  607.7 7.0 collective-permute-done.65
  616.2 16.6 %collective-permute-done.68 = bf16[2,4,1,96,768]{4,3,1,0,2:T(8,128)(2,1)S(1)} collective-permute-done((bf16[2,4,1,96,768]{4,3,1,0,2:T(8,128)(2,1)S(1)}, bf16[2,4,1,96,768]{4,3,1,0,2:T(8,128)(2,1)S(1)}, u32[]{:S(2)}, u32[]{:S(2)}) %collective-permute-start.68) | collective-permute-done | bytes 1179680 | tf_op jit(solution)/shard_map/ppermute | solution.py:59
  636.0 9.1 %collective-permute-done.66 = bf16[4,1,96,768]{3,2,0,1:T(8,128)(2,1)S(1)} collective-permute-done((bf16[4,1,96,768]{3,2,0,1:T(8,128)(2,1)S(1)}, bf16[4,1,96,768]{3,2,0,1:T(8,128)(2,1)S(1)}, u32[]{:S(2)}, u32[]{:S(2)}) %collective-permute-start.66) | collective-permute-done | bytes 589856 | tf_op jit(solution)/shard_map/ppermute | solution.py:59
  650.7 20.2 %collective-permute-done.84 = bf16[2,96,768]{2,1,0:T(8,128)(2,1)S(1)} collective-permute-done((bf16[2,96,768]{2,1,0:T(8,128)(2,1)S(1)}, bf16[2,96,768]{2,1,0:T(8,128)(2,1)S(1)}, u32[]{:S(2)}, u32[]{:S(2)}) %collective-permute-start.84) | collective-permute-done | bytes 294944 | tf_op jit(solution)/shard_map/ppermute | solution.py:59
  671.0 7.6 collective-permute-done.83
  678.6 4.5 collective-permute-start.62
  683.3 7.0 collective-permute-done.72
  713.3 6.5 collective-permute-done.86
  724.2 8.2 %collective-permute-done.74 = bf16[2,2,96,768]{3,2,1,0:T(8,128)(2,1)} collective-permute-done((bf16[2,2,96,768]{3,2,1,0:T(8,128)(2,1)}, bf16[2,2,96,768]{3,2,1,0:T(8,128)(2,1)}, u32[]{:S(2)}, u32[]{:S(2)}) %collective-permute-start.74) | collective-permute-done | bytes 589856 | tf_op jit(solution)/shard_map/ppermute | solution.py:59
  760.7 6.0 copy.150
  766.7 4.2 pad_maximum_fusion.1
  (816 shorter events, 412.8 us)
Async XLA Ops:
  7.2 729.0 %all-gather.5.cloned.1.call-start = ((), (), s32[]{:S(2)}) async-start(), calls=%async_computation.1 | async-start | bytes 1310720 | tf_op jit(solution)/shard_map/all_gather | solution.py:298
  16.2 56.2 %collective-permute-start.12 = (bf16[2,96,768]{2,1,0:T(8,128)(2,1)}, bf16[2,96,768]{2,1,0:T(8,128)(2,1)}, u32[]{:S(2)}, u32[]{:S(2)}) collective-permute-start(bf16[2,96,768]{2,1,0:T(8,128)(2,1)} %get-tuple-element.192), channel_id=1, source_target_pairs={{0,3},{1,2},{2,1},{3,0},{4,7},{5,6},{6,5},{7,4},{8,11},{9,10},{10,... | collective-permute-start | bytes 884744 | tf_op jit(solution)/shard_map/ppermute | solution.py:59
  17.5 54.9 %collective-permute-start.11 = (bf16[2,96,768]{2,1,0:T(8,128)(2,1)}, bf16[2,96,768]{2,1,0:T(8,128)(2,1)}, u32[]{:S(2)}, u32[]{:S(2)}) collective-permute-start(bf16[2,96,768]{2,1,0:T(8,128)(2,1)} %get-tuple-element.192), channel_id=1, source_target_pairs={{0,2},{1,3},{2,0},{3,1},{4,6},{5,7},{6,4},{7,5},{8,10},{9,11},{10,... | collective-permute-start | bytes 884744 | tf_op jit(solution)/shard_map/ppermute | solution.py:59
  20.9 35.3 %collective-permute-start.2 = (bf16[4,24,768]{2,1,0:T(8,128)(2,1)}, bf16[4,24,768]{2,1,0:T(8,128)(2,1)}, u32[]{:S(2)}, u32[]{:S(2)}) collective-permute-start(bf16[4,24,768]{2,1,0:T(8,128)(2,1)} %fusion.129), channel_id=1, source_target_pairs={{0,3},{1,2},{2,1},{3,0},{4,7},{5,6},{6,5},{7,4},{8,11},{9,10},{10,... | collective-permute-start | bytes 442376 | tf_op jit(solution)/shard_map/ppermute | solution.py:59
  23.3 35.0 %collective-permute-start.1 = (bf16[4,24,768]{2,1,0:T(8,128)(2,1)}, bf16[4,24,768]{2,1,0:T(8,128)(2,1)}, u32[]{:S(2)}, u32[]{:S(2)}) collective-permute-start(bf16[4,24,768]{2,1,0:T(8,128)(2,1)} %fusion.129), channel_id=1, source_target_pairs={{0,2},{1,3},{2,0},{3,1},{4,6},{5,7},{6,4},{7,5},{8,10},{9,11},{10,... | collective-permute-start | bytes 442376 | tf_op jit(solution)/shard_map/ppermute | solution.py:59
  24.2 37.2 %collective-permute-start = (bf16[4,24,768]{2,1,0:T(8,128)(2,1)}, bf16[4,24,768]{2,1,0:T(8,128)(2,1)}, u32[]{:S(2)}, u32[]{:S(2)}) collective-permute-start(bf16[4,24,768]{2,1,0:T(8,128)(2,1)} %fusion.129), channel_id=1, source_target_pairs={{0,1},{1,0},{2,3},{3,2},{4,5},{5,4},{6,7},{7,6},{8,9},{9,8},{10,11... | collective-permute-start | bytes 442376 | tf_op jit(solution)/shard_map/ppermute | solution.py:59
  72.5 36.7 %collective-permute-start.6 = (bf16[512,768]{1,0:T(8,128)(2,1)S(1)}, bf16[512,768]{1,0:T(8,128)(2,1)S(1)}, u32[]{:S(2)}, u32[]{:S(2)}) collective-permute-start(bf16[512,768]{1,0:T(8,128)(2,1)S(1)} %copy-done.80), channel_id=1, source_target_pairs={{0,1},{1,2},{2,3},{4,5},{5,6},{6,7},{8,9},{9,10},{10,11},{12,13},{... | collective-permute-start | bytes 2359304 | tf_op jit(solution)/shard_map/ppermute | solution.py:189
  98.2 29.4 %collective-permute-start.34 = (bf16[4,1,96,768]{3,2,0,1:T(8,128)(2,1)S(1)}, bf16[4,1,96,768]{3,2,0,1:T(8,128)(2,1)S(1)}, u32[]{:S(2)}, u32[]{:S(2)}) collective-permute-start(bf16[4,1,96,768]{3,2,0,1:T(8,128)(2,1)S(1)} %get-tuple-element.125), channel_id=1, source_target_pairs={{0,16},{4,20},{8,24},{12,28},{16,0},{20,4},{24,8},{28,12},{1,17},{... | collective-permute-start | bytes 1769480 | tf_op jit(solution)/shard_map/ppermute | solution.py:59
  102.4 26.7 %collective-permute-start.32 = (bf16[4,1,96,768]{3,2,0,1:T(8,128)(2,1)S(1)}, bf16[4,1,96,768]{3,2,0,1:T(8,128)(2,1)S(1)}, u32[]{:S(2)}, u32[]{:S(2)}) collective-permute-start(bf16[4,1,96,768]{3,2,0,1:T(8,128)(2,1)S(1)} %get-tuple-element.126), channel_id=1, source_target_pairs={{0,8},{4,12},{8,0},{12,4},{16,24},{20,28},{24,16},{28,20},{1,9},{5... | collective-permute-start | bytes 1769480 | tf_op jit(solution)/shard_map/ppermute | solution.py:59
  109.2 31.1 %collective-permute-start.4 = (bf16[2,4,2,24,768]{4,3,2,1,0:T(8,128)(2,1)S(1)}, bf16[2,4,2,24,768]{4,3,2,1,0:T(8,128)(2,1)S(1)}, u32[]{:S(2)}, u32[]{:S(2)}) collective-permute-start(bf16[2,4,2,24,768]{4,3,2,1,0:T(8,128)(2,1)S(1)} %get-tuple-element.184), channel_id=1, source_target_pairs={{0,16},{4,20},{8,24},{12,28},{16,0},{20,4},{24,8},{28,12},{1,17},{... | collective-permute-start | bytes 1769480 | tf_op jit(solution)/shard_map/ppermute | solution.py:59
  115.0 27.7 %collective-permute-start.8 = (bf16[2,4,2,24,768]{4,3,2,1,0:T(8,128)(2,1)S(1)}, bf16[2,4,2,24,768]{4,3,2,1,0:T(8,128)(2,1)S(1)}, u32[]{:S(2)}, u32[]{:S(2)}) collective-permute-start(bf16[2,4,2,24,768]{4,3,2,1,0:T(8,128)(2,1)S(1)} %get-tuple-element.178), channel_id=1, source_target_pairs={{0,8},{4,12},{8,0},{12,4},{16,24},{20,28},{24,16},{28,20},{1,9},{5... | collective-permute-start | bytes 1769480 | tf_op jit(solution)/shard_map/ppermute | solution.py:59
  115.4 37.5 %collective-permute-start.23 = (bf16[2,4,2,24,768]{4,3,2,1,0:T(8,128)(2,1)S(1)}, bf16[2,4,2,24,768]{4,3,2,1,0:T(8,128)(2,1)S(1)}, u32[]{:S(2)}, u32[]{:S(2)}) collective-permute-start(bf16[2,4,2,24,768]{4,3,2,1,0:T(8,128)(2,1)S(1)} %get-tuple-element.174), channel_id=1, source_target_pairs={{0,16},{4,20},{8,24},{12,28},{16,0},{20,4},{24,8},{28,12},{1,17},{... | collective-permute-start | bytes 1769480 | tf_op jit(solution)/shard_map/ppermute | solution.py:59
  127.7 32.1 %collective-permute-start.27 = (bf16[2,4,2,24,768]{4,3,2,1,0:T(8,128)(2,1)S(1)}, bf16[2,4,2,24,768]{4,3,2,1,0:T(8,128)(2,1)S(1)}, u32[]{:S(2)}, u32[]{:S(2)}) collective-permute-start(bf16[2,4,2,24,768]{4,3,2,1,0:T(8,128)(2,1)S(1)} %get-tuple-element.168), channel_id=1, source_target_pairs={{0,8},{4,12},{8,0},{12,4},{16,24},{20,28},{24,16},{28,20},{1,9},{5... | collective-permute-start | bytes 1769480 | tf_op jit(solution)/shard_map/ppermute | solution.py:59
  129.1 43.6 %collective-permute-start.16 = (bf16[2,4,1,96,768]{4,3,1,0,2:T(8,128)(2,1)S(1)}, bf16[2,4,1,96,768]{4,3,1,0,2:T(8,128)(2,1)S(1)}, u32[]{:S(2)}, u32[]{:S(2)}) collective-permute-start(bf16[2,4,1,96,768]{4,3,1,0,2:T(8,128)(2,1)S(1)} %get-tuple-element.144), channel_id=1, source_target_pairs={{0,8},{4,12},{8,0},{12,4},{16,24},{20,28},{24,16},{28,20},{1,9},{5... | collective-permute-start | bytes 3538952 | tf_op jit(solution)/shard_map/ppermute | solution.py:59
  140.3 37.9 %collective-permute-start.14 = (bf16[2,4,1,96,768]{4,3,1,2,0:T(8,128)(2,1)S(1)}, bf16[2,4,1,96,768]{4,3,1,2,0:T(8,128)(2,1)S(1)}, u32[]{:S(2)}, u32[]{:S(2)}) collective-permute-start(bf16[2,4,1,96,768]{4,3,1,2,0:T(8,128)(2,1)S(1)} %get-tuple-element.138), channel_id=1, source_target_pairs={{0,16},{4,20},{8,24},{12,28},{16,0},{20,4},{24,8},{28,12},{1,17},{... | collective-permute-start | bytes 3538952 | tf_op jit(solution)/shard_map/ppermute | solution.py:59
  142.7 85.4 %collective-permute-start.35 = (bf16[2,4,1,96,768]{4,3,1,0,2:T(8,128)(2,1)}, bf16[2,4,1,96,768]{4,3,1,0,2:T(8,128)(2,1)}, u32[]{:S(2)}, u32[]{:S(2)}) collective-permute-start(bf16[2,4,1,96,768]{4,3,1,0,2:T(8,128)(2,1)} %get-tuple-element.128), channel_id=1, source_target_pairs={{0,8},{4,12},{8,0},{12,4},{16,24},{20,28},{24,16},{28,20},{1,9},{5... | collective-permute-start | bytes 3538952 | tf_op jit(solution)/shard_map/ppermute | solution.py:59
  152.9 34.2 %collective-permute-start.5 = (bf16[16,2,24,768]{3,2,1,0:T(8,128)(2,1)S(1)}, bf16[16,2,24,768]{3,2,1,0:T(8,128)(2,1)S(1)}, u32[]{:S(2)}, u32[]{:S(2)}) collective-permute-start(bf16[16,2,24,768]{3,2,1,0:T(8,128)(2,1)S(1)} %bitcast.614), channel_id=1, source_target_pairs={{0,4},{4,0},{8,12},{12,8},{16,20},{20,16},{24,28},{28,24},{1,5},{5... | collective-permute-start | bytes 3538952 | tf_op jit(solution)/shard_map/ppermute | solution.py:59
  159.7 29.8 %collective-permute-start.9 = (bf16[16,2,24,768]{3,2,1,0:T(8,128)(2,1)S(1)}, bf16[16,2,24,768]{3,2,1,0:T(8,128)(2,1)S(1)}, u32[]{:S(2)}, u32[]{:S(2)}) collective-permute-start(bf16[16,2,24,768]{3,2,1,0:T(8,128)(2,1)S(1)} %bitcast.615), channel_id=1, source_target_pairs={{0,4},{4,0},{8,12},{12,8},{16,20},{20,16},{24,28},{28,24},{1,5},{5... | collective-permute-start | bytes 3538952 | tf_op jit(solution)/shard_map/ppermute | solution.py:59
  172.7 58.9 %collective-permute-start.33 = (bf16[2,4,1,96,768]{4,3,1,2,0:T(8,128)(2,1)}, bf16[2,4,1,96,768]{4,3,1,2,0:T(8,128)(2,1)}, u32[]{:S(2)}, u32[]{:S(2)}) collective-permute-start(bf16[2,4,1,96,768]{4,3,1,2,0:T(8,128)(2,1)} %get-tuple-element.122), channel_id=1, source_target_pairs={{0,16},{4,20},{8,24},{12,28},{16,0},{20,4},{24,8},{28,12},{1,17},{... | collective-permute-start | bytes 3538952 | tf_op jit(solution)/shard_map/ppermute | solution.py:59
  178.2 56.3 %collective-permute-start.24 = (bf16[16,2,24,768]{3,2,1,0:T(8,128)(2,1)}, bf16[16,2,24,768]{3,2,1,0:T(8,128)(2,1)}, u32[]{:S(2)}, u32[]{:S(2)}) collective-permute-start(bf16[16,2,24,768]{3,2,1,0:T(8,128)(2,1)} %bitcast.66), channel_id=1, source_target_pairs={{0,4},{4,0},{8,12},{12,8},{16,20},{20,16},{24,28},{28,24},{1,5},{5... | collective-permute-start | bytes 3538952 | tf_op jit(solution)/shard_map/ppermute | solution.py:59
  187.1 32.9 %collective-permute-start.18 = (bf16[16,1,96,768]{3,2,0,1:T(8,128)(2,1)}, bf16[16,1,96,768]{3,2,0,1:T(8,128)(2,1)}, u32[]{:S(2)}, u32[]{:S(2)}) collective-permute-start(bf16[16,1,96,768]{3,2,0,1:T(8,128)(2,1)} %bitcast.54), channel_id=1, source_target_pairs={{0,4},{4,0},{8,12},{12,8},{16,20},{20,16},{24,28},{28,24},{1,5},{5... | collective-permute-start | bytes 7077896 | tf_op jit(solution)/shard_map/ppermute | solution.py:59
  189.5 27.3 %collective-permute-start.17 = (bf16[16,1,96,768]{3,2,0,1:T(8,128)(2,1)}, bf16[16,1,96,768]{3,2,0,1:T(8,128)(2,1)}, u32[]{:S(2)}, u32[]{:S(2)}) collective-permute-start(bf16[16,1,96,768]{3,2,0,1:T(8,128)(2,1)} %bitcast.52), channel_id=1, source_target_pairs={{0,4},{4,0},{8,12},{12,8},{16,20},{20,16},{24,28},{28,24},{1,5},{5... | collective-permute-start | bytes 7077896 | tf_op jit(solution)/shard_map/ppermute | solution.py:59
  231.1 52.2 %collective-permute-start.37 = (bf16[16,1,96,768]{3,2,0,1:T(8,128)(2,1)}, bf16[16,1,96,768]{3,2,0,1:T(8,128)(2,1)}, u32[]{:S(2)}, u32[]{:S(2)}) collective-permute-start(bf16[16,1,96,768]{3,2,0,1:T(8,128)(2,1)} %bitcast.110), channel_id=1, source_target_pairs={{0,4},{4,0},{8,12},{12,8},{16,20},{20,16},{24,28},{28,24},{1,5},{5... | collective-permute-start | bytes 7077896 | tf_op jit(solution)/shard_map/ppermute | solution.py:59
  234.5 34.0 %collective-permute-start.36 = (bf16[16,1,96,768]{3,2,0,1:T(8,128)(2,1)}, bf16[16,1,96,768]{3,2,0,1:T(8,128)(2,1)}, u32[]{:S(2)}, u32[]{:S(2)}) collective-permute-start(bf16[16,1,96,768]{3,2,0,1:T(8,128)(2,1)} %bitcast.108), channel_id=1, source_target_pairs={{0,4},{4,0},{8,12},{12,8},{16,20},{20,16},{24,28},{28,24},{1,5},{5... | collective-permute-start | bytes 7077896 | tf_op jit(solution)/shard_map/ppermute | solution.py:59
  347.1 104.3 %collective-permute-start.52 = (bf16[16,2,24,768]{3,2,0,1:T(8,128)(2,1)}, bf16[16,2,24,768]{3,2,0,1:T(8,128)(2,1)}, u32[]{:S(2)}, u32[]{:S(2)}) collective-permute-start(bf16[16,2,24,768]{3,2,0,1:T(8,128)(2,1)} %pad_maximum_fusion.37), channel_id=1, source_target_pairs={{0,4},{4,0},{8,12},{12,8},{16,20},{20,16},{24,28},{28,24},{1,5},{5... | collective-permute-start | bytes 3538952 | tf_op jit(solution)/shard_map/ppermute | solution.py:59
  351.3 104.0 %collective-permute-start.55 = (bf16[16,2,24,768]{3,2,1,0:T(8,128)(2,1)}, bf16[16,2,24,768]{3,2,1,0:T(8,128)(2,1)}, u32[]{:S(2)}, u32[]{:S(2)}) collective-permute-start(bf16[16,2,24,768]{3,2,1,0:T(8,128)(2,1)} %pad_maximum_fusion.38), channel_id=1, source_target_pairs={{0,4},{4,0},{8,12},{12,8},{16,20},{20,16},{24,28},{28,24},{1,5},{5... | collective-permute-start | bytes 3538952 | tf_op jit(solution)/shard_map/ppermute | solution.py:59
  351.9 171.8 %collective-permute-start.76 = (bf16[16,1,96,768]{3,2,0,1:T(8,128)(2,1)}, bf16[16,1,96,768]{3,2,0,1:T(8,128)(2,1)}, u32[]{:S(2)}, u32[]{:S(2)}) collective-permute-start(bf16[16,1,96,768]{3,2,0,1:T(8,128)(2,1)} %bitcast.230), channel_id=1, source_target_pairs={{0,4},{4,0},{8,12},{12,8},{16,20},{20,16},{24,28},{28,24},{1,5},{5... | collective-permute-start | bytes 7077896 | tf_op jit(solution)/shard_map/ppermute | solution.py:59
  351.9 175.6 %collective-permute-start.79 = (bf16[16,1,96,768]{3,2,0,1:T(8,128)(2,1)}, bf16[16,1,96,768]{3,2,0,1:T(8,128)(2,1)}, u32[]{:S(2)}, u32[]{:S(2)}) collective-permute-start(bf16[16,1,96,768]{3,2,0,1:T(8,128)(2,1)} %bitcast.236), channel_id=1, source_target_pairs={{0,4},{4,0},{8,12},{12,8},{16,20},{20,16},{24,28},{28,24},{1,5},{5... | collective-permute-start | bytes 7077896 | tf_op jit(solution)/shard_map/ppermute | solution.py:59
  455.3 33.1 %collective-permute-start.53 = (bf16[2,4,2,24,768]{4,3,2,1,0:T(8,128)(2,1)}, bf16[2,4,2,24,768]{4,3,2,1,0:T(8,128)(2,1)}, u32[]{:S(2)}, u32[]{:S(2)}) collective-permute-start(bf16[2,4,2,24,768]{4,3,2,1,0:T(8,128)(2,1)} %bitcast.167), channel_id=1, source_target_pairs={{0,16},{4,20},{8,24},{12,28},{16,0},{20,4},{24,8},{28,12},{1,17},{... | collective-permute-start | bytes 1769480 | tf_op jit(solution)/shard_map/ppermute | solution.py:59
  459.2 30.5 %collective-permute-start.56 = (bf16[2,4,2,24,768]{4,3,2,1,0:T(8,128)(2,1)}, bf16[2,4,2,24,768]{4,3,2,1,0:T(8,128)(2,1)S(1)}, u32[]{:S(2)}, u32[]{:S(2)}) collective-permute-start(bf16[2,4,2,24,768]{4,3,2,1,0:T(8,128)(2,1)} %slice_bitcast_fusion.14), channel_id=1, source_target_pairs={{0,8},{4,12},{8,0},{12,4},{16,24},{20,28},{24,16},{28,20},{1,9},{5... | collective-permute-start | bytes 1769480 | tf_op jit(solution)/shard_map/ppermute | solution.py:59
  482.8 253.4 %all-gather.3.cloned.1.call-start = ((), (), s32[]{:S(2)}) async-start(), calls=%async_computation | async-start | bytes 1310720 | tf_op jit(solution)/shard_map/all_gather | solution.py:298
  520.3 67.9 %collective-permute-start.64 = (bf16[16,1,96,768]{3,2,0,1:T(8,128)(2,1)}, bf16[16,1,96,768]{3,2,0,1:T(8,128)(2,1)}, u32[]{:S(2)}, u32[]{:S(2)}) collective-permute-start(bf16[16,1,96,768]{3,2,0,1:T(8,128)(2,1)} %bitcast.201), channel_id=1, source_target_pairs={{0,4},{4,0},{8,12},{12,8},{16,20},{20,16},{24,28},{28,24},{1,5},{5... | collective-permute-start | bytes 7077896 | tf_op jit(solution)/shard_map/ppermute | solution.py:59
  521.6 71.2 %collective-permute-start.67 = (bf16[16,1,96,768]{3,2,0,1:T(8,128)(2,1)}, bf16[16,1,96,768]{3,2,0,1:T(8,128)(2,1)}, u32[]{:S(2)}, u32[]{:S(2)}) collective-permute-start(bf16[16,1,96,768]{3,2,0,1:T(8,128)(2,1)} %bitcast.207), channel_id=1, source_target_pairs={{0,4},{4,0},{8,12},{12,8},{16,20},{20,16},{24,28},{28,24},{1,5},{5... | collective-permute-start | bytes 7077896 | tf_op jit(solution)/shard_map/ppermute | solution.py:59
  522.2 35.4 %collective-permute-start.41 = (bf16[2,4,2,24,768]{4,3,2,1,0:T(8,128)(2,1)}, bf16[2,4,2,24,768]{4,3,2,1,0:T(8,128)(2,1)}, u32[]{:S(2)}, u32[]{:S(2)}) collective-permute-start(bf16[2,4,2,24,768]{4,3,2,1,0:T(8,128)(2,1)} %bitcast.131), channel_id=1, source_target_pairs={{0,16},{4,20},{8,24},{12,28},{16,0},{20,4},{24,8},{28,12},{1,17},{... | collective-permute-start | bytes 1769480 | tf_op jit(solution)/shard_map/ppermute | solution.py:59
  523.7 37.4 %collective-permute-start.44 = (bf16[2,4,2,24,768]{4,3,2,1,0:T(8,128)(2,1)}, bf16[2,4,2,24,768]{4,3,2,1,0:T(8,128)(2,1)}, u32[]{:S(2)}, u32[]{:S(2)}) collective-permute-start(bf16[2,4,2,24,768]{4,3,2,1,0:T(8,128)(2,1)} %slice_bitcast_fusion.16), channel_id=1, source_target_pairs={{0,8},{4,12},{8,0},{12,4},{16,24},{20,28},{24,16},{28,20},{1,9},{5... | collective-permute-start | bytes 1769480 | tf_op jit(solution)/shard_map/ppermute | solution.py:59
  555.7 41.0 %collective-permute-start.77 = (bf16[2,4,1,96,768]{4,3,1,2,0:T(8,128)(2,1)}, bf16[2,4,1,96,768]{4,3,1,2,0:T(8,128)(2,1)}, u32[]{:S(2)}, u32[]{:S(2)}) collective-permute-start(bf16[2,4,1,96,768]{4,3,1,2,0:T(8,128)(2,1)} %bitcast.666), channel_id=1, source_target_pairs={{0,16},{4,20},{8,24},{12,28},{16,0},{20,4},{24,8},{28,12},{1,17},{... | collective-permute-start | bytes 3538952 | tf_op jit(solution)/shard_map/ppermute | solution.py:59
  566.2 33.5 %collective-permute-start.80 = (bf16[2,4,1,96,768]{4,3,1,0,2:T(8,128)(2,1)}, bf16[2,4,1,96,768]{4,3,1,0,2:T(8,128)(2,1)S(1)}, u32[]{:S(2)}, u32[]{:S(2)}) collective-permute-start(bf16[2,4,1,96,768]{4,3,1,0,2:T(8,128)(2,1)} %slice_bitcast_fusion), channel_id=1, source_target_pairs={{0,8},{4,12},{8,0},{12,4},{16,24},{20,28},{24,16},{28,20},{1,9},{5... | collective-permute-start | bytes 3538952 | tf_op jit(solution)/shard_map/ppermute | solution.py:59
  586.9 60.0 %collective-permute-start.48 = (bf16[4,24,768]{2,1,0:T(8,128)(2,1)S(1)}, bf16[4,24,768]{2,1,0:T(8,128)(2,1)S(1)}, u32[]{:S(2)}, u32[]{:S(2)}) collective-permute-start(bf16[4,24,768]{2,1,0:T(8,128)(2,1)S(1)} %get-tuple-element.160), channel_id=1, source_target_pairs={{0,3},{1,2},{2,1},{3,0},{4,7},{5,6},{6,5},{7,4},{8,11},{9,10},{10,... | collective-permute-start | bytes 442376 | tf_op jit(solution)/shard_map/ppermute | solution.py:59
  588.2 60.1 %collective-permute-start.47 = (bf16[4,24,768]{2,1,0:T(8,128)(2,1)S(1)}, bf16[4,24,768]{2,1,0:T(8,128)(2,1)S(1)}, u32[]{:S(2)}, u32[]{:S(2)}) collective-permute-start(bf16[4,24,768]{2,1,0:T(8,128)(2,1)S(1)} %get-tuple-element.161), channel_id=1, source_target_pairs={{0,2},{1,3},{2,0},{3,1},{4,6},{5,7},{6,4},{7,5},{8,10},{9,11},{10,... | collective-permute-start | bytes 442376 | tf_op jit(solution)/shard_map/ppermute | solution.py:59
  599.7 33.1 %collective-permute-start.68 = (bf16[2,4,1,96,768]{4,3,1,0,2:T(8,128)(2,1)S(1)}, bf16[2,4,1,96,768]{4,3,1,0,2:T(8,128)(2,1)S(1)}, u32[]{:S(2)}, u32[]{:S(2)}) collective-permute-start(bf16[2,4,1,96,768]{4,3,1,0,2:T(8,128)(2,1)S(1)} %slice_bitcast_fusion.2), channel_id=1, source_target_pairs={{0,8},{4,12},{8,0},{12,4},{16,24},{20,28},{24,16},{28,20},{1,9},{5... | collective-permute-start | bytes 3538952 | tf_op jit(solution)/shard_map/ppermute | solution.py:59
  607.6 40.8 %collective-permute-start.46 = (bf16[4,24,768]{2,1,0:T(8,128)(2,1)S(1)}, bf16[4,24,768]{2,1,0:T(8,128)(2,1)S(1)}, u32[]{:S(2)}, u32[]{:S(2)}) collective-permute-start(bf16[4,24,768]{2,1,0:T(8,128)(2,1)S(1)} %get-tuple-element.159), channel_id=1, source_target_pairs={{0,1},{1,0},{2,3},{3,2},{4,5},{5,4},{6,7},{7,6},{8,9},{9,8},{10,11... | collective-permute-start | bytes 442376 | tf_op jit(solution)/shard_map/ppermute | solution.py:59
  645.1 25.9 %collective-permute-start.84 = (bf16[2,96,768]{2,1,0:T(8,128)(2,1)S(1)}, bf16[2,96,768]{2,1,0:T(8,128)(2,1)S(1)}, u32[]{:S(2)}, u32[]{:S(2)}) collective-permute-start(bf16[2,96,768]{2,1,0:T(8,128)(2,1)S(1)} %get-tuple-element.99), channel_id=1, source_target_pairs={{0,3},{1,2},{2,1},{3,0},{4,7},{5,6},{6,5},{7,4},{8,11},{9,10},{10,... | collective-permute-start | bytes 884744 | tf_op jit(solution)/shard_map/ppermute | solution.py:59
  645.3 33.3 %collective-permute-start.83 = (bf16[2,96,768]{2,1,0:T(8,128)(2,1)S(1)}, bf16[2,96,768]{2,1,0:T(8,128)(2,1)S(1)}, u32[]{:S(2)}, u32[]{:S(2)}) collective-permute-start(bf16[2,96,768]{2,1,0:T(8,128)(2,1)S(1)} %get-tuple-element.100), channel_id=1, source_target_pairs={{0,2},{1,3},{2,0},{3,1},{4,6},{5,7},{6,4},{7,5},{8,10},{9,11},{10,... | collective-permute-start | bytes 884744 | tf_op jit(solution)/shard_map/ppermute | solution.py:59
  646.9 36.1 %collective-permute-start.82 = (bf16[2,96,768]{2,1,0:T(8,128)(2,1)S(1)}, bf16[2,96,768]{2,1,0:T(8,128)(2,1)S(1)}, u32[]{:S(2)}, u32[]{:S(2)}) collective-permute-start(bf16[2,96,768]{2,1,0:T(8,128)(2,1)S(1)} %get-tuple-element.98), channel_id=1, source_target_pairs={{0,1},{1,0},{2,3},{3,2},{4,5},{5,4},{6,7},{7,6},{8,9},{9,8},{10,11... | collective-permute-start | bytes 884744 | tf_op jit(solution)/shard_map/ppermute | solution.py:59
  648.3 42.0 %collective-permute-start.72 = (bf16[2,96,768]{2,1,0:T(8,128)(2,1)S(1)}, bf16[2,96,768]{2,1,0:T(8,128)(2,1)S(1)}, u32[]{:S(2)}, u32[]{:S(2)}) collective-permute-start(bf16[2,96,768]{2,1,0:T(8,128)(2,1)S(1)} %get-tuple-element.94), channel_id=1, source_target_pairs={{0,3},{1,2},{2,1},{3,0},{4,7},{5,6},{6,5},{7,4},{8,11},{9,10},{10,... | collective-permute-start | bytes 884744 | tf_op jit(solution)/shard_map/ppermute | solution.py:59
  648.4 45.9 %collective-permute-start.71 = (bf16[2,96,768]{2,1,0:T(8,128)(2,1)S(1)}, bf16[2,96,768]{2,1,0:T(8,128)(2,1)S(1)}, u32[]{:S(2)}, u32[]{:S(2)}) collective-permute-start(bf16[2,96,768]{2,1,0:T(8,128)(2,1)S(1)} %get-tuple-element.95), channel_id=1, source_target_pairs={{0,2},{1,3},{2,0},{3,1},{4,6},{5,7},{6,4},{7,5},{8,10},{9,11},{10,... | collective-permute-start | bytes 884744 | tf_op jit(solution)/shard_map/ppermute | solution.py:59
  704.3 28.2 %collective-permute-start.74 = (bf16[2,2,96,768]{3,2,1,0:T(8,128)(2,1)}, bf16[2,2,96,768]{3,2,1,0:T(8,128)(2,1)}, u32[]{:S(2)}, u32[]{:S(2)}) collective-permute-start(bf16[2,2,96,768]{3,2,1,0:T(8,128)(2,1)} %get-tuple-element.154), channel_id=1, source_target_pairs={{0,16},{4,20},{8,24},{12,28},{16,0},{20,4},{24,8},{28,12},{1,17},{... | collective-permute-start | bytes 1769480 | tf_op jit(solution)/shard_map/ppermute | solution.py:59
  708.5 30.8 %collective-permute-start.51 = (bf16[2,2,4,24,768]{4,3,2,1,0:T(8,128)(2,1)}, bf16[2,2,4,24,768]{4,3,2,1,0:T(8,128)(2,1)}, u32[]{:S(2)}, u32[]{:S(2)}) collective-permute-start(bf16[2,2,4,24,768]{4,3,2,1,0:T(8,128)(2,1)} %get-tuple-element.158), channel_id=1, source_target_pairs={{0,4},{4,0},{8,12},{12,8},{16,20},{20,16},{24,28},{28,24},{1,5},{5... | collective-permute-start | bytes 1769480 | tf_op jit(solution)/shard_map/ppermute | solution.py:59
  (223 other events, 1984.4 us)
Sparse Core Ops, SparseCore 0:
  482.9 35.6 all-gather.4
  554.9 30.7 all-gather.2

commit v2 on v1

v2 whole, which is shorter than its diff:
```python
import functools

import jax
import jax.numpy as jnp
from jax import lax
from jax.experimental import pallas as pl
from jax.experimental.pallas import tpu as pltpu
from jax.sharding import PartitionSpec as P

BF = jnp.bfloat16
F32 = jnp.float32
VMEM_LIMIT = 58 * 1024 * 1024
TOKEN = (8, 128)
GELU_A = 0.7978845608028654
GELU_B = 0.044715


def dot_nt(lhs, rhs):
    return lax.dot_general(lhs, rhs, (((1,), (1,)), ((), ())), preferred_element_type=F32)


def dot_nn(lhs, rhs):
    return lax.dot_general(lhs, rhs, (((1,), (0,)), ((), ())), preferred_element_type=F32)


def dot_tn(lhs, rhs):
    return lax.dot_general(lhs, rhs, (((0,), (0,)), ((), ())), preferred_element_type=F32)


def normalize(values):
    center = values - jnp.mean(values, axis=-1, keepdims=True)
    inv_std = lax.rsqrt(jnp.mean(center * center, axis=-1, keepdims=True) + 1e-05)
    return center * inv_std, inv_std


def norm_back(grad_out, normal, inv_std, gain):
    grad_normal = grad_out * gain
    mean_one = jnp.mean(grad_normal, axis=-1, keepdims=True)
    mean_two = jnp.mean(grad_normal * normal, axis=-1, keepdims=True)
    return inv_std * (grad_normal - mean_one - normal * mean_two)


def whole(shape):
    return pl.BlockSpec(shape, lambda *_: (0,) * len(shape))


def call(order, body, grid, in_specs, out_specs, out_shape, scratch=(), prefetch=0, name=None):
    first = prefetch + len(in_specs)
    second = first + 1 + len(out_specs)
    anywhere = pl.BlockSpec(memory_space=pl.ANY)

    def with_token(*refs):
        return body(*refs[:first], *refs[first + 1 : second], *refs[second + 1 :])

    kernel = pl.pallas_call(
        with_token,
        grid_spec=pltpu.PrefetchScalarGridSpec(
            num_scalar_prefetch=prefetch,
            grid=grid,
            in_specs=list(in_specs) + [anywhere],
            out_specs=list(out_specs) + [anywhere],
            scratch_shapes=list(scratch),
        ),
        out_shape=list(out_shape) + [shape_of(TOKEN, jnp.int32)],
        input_output_aliases={first: len(out_specs)},
        compiler_params=pltpu.CompilerParams(
            dimension_semantics=("arbitrary",) * len(grid), vmem_limit_bytes=VMEM_LIMIT
        ),
        cost_estimate=pl.CostEstimate(flops=0, bytes_accessed=0, transcendentals=0),
        name=name,
    )

    def run(*operands):
        *results, order.token = kernel(*operands, order.token)
        return results

    return run


def shape_of(shape, dtype):
    return jax.ShapeDtypeStruct(shape, dtype)


def tie(*arrays):
    count = len(arrays)
    return pl.pallas_call(
        lambda *refs: None,
        out_shape=[shape_of(a.shape, a.dtype) for a in arrays],
        in_specs=[pl.BlockSpec(memory_space=pl.ANY)] * count,
        out_specs=[pl.BlockSpec(memory_space=pl.ANY)] * count,
        input_output_aliases={i: i for i in range(count)},
        cost_estimate=pl.CostEstimate(flops=0, bytes_accessed=0, transcendentals=0),
        name="tie",
    )(*arrays)


def enter_kernel(order, tokens, gain, shift):
    rows, width = tokens.shape

    def body(t_ref, g_ref, s_ref, x_ref, n_ref):
        x = t_ref[...].astype(F32)
        x_ref[...] = x
        normal, _ = normalize(x)
        n_ref[...] = (normal * g_ref[...] + s_ref[...]).astype(BF)

    return call(
        order,
        body,
        (1,),
        [whole((rows, width)), whole((1, width)), whole((1, width))],
        [whole((rows, width)), whole((rows, width))],
        [shape_of((rows, width), F32), shape_of((rows, width), BF)],
        name="enter",
    )(tokens, gain, shift)


def attn_forward(order, top, x, normed, halo, weights, band_rev, seg_q, seg_k, gain, shift):
    rows, width = x.shape
    seqs, block, _ = seg_q.shape
    keys = seg_k.shape[2]
    window = keys - block
    quarter = weights[0].shape[1]
    half = 2 * quarter

    def body(top_ref, x_ref, n_ref, h_ref, oa, ob, ta, tb, band_ref, sq_ref, sk_ref, g_ref, s_ref,
             sg_ref, ratio_ref, rden_ref, v_ref, kexp_ref, mixed_ref, masked_ref, x1_ref, nb_ref, both_ref, mix):
        step = pl.program_id(0)

        @pl.when(step == 0)
        def _():
            for s in range(seqs):
                both_ref[s * keys : s * keys + window] = h_ref[s * block : (s + 1) * block]
                both_ref[s * keys + window : (s + 1) * keys] = n_ref[s * block : (s + 1) * block]
            band = jnp.concatenate([jnp.exp(band_ref[...]), jnp.zeros((block, block), F32)], axis=1)
            spread = pltpu.roll(band, 1, axis=1, stride=1, stride_axis=0)
            for s in range(seqs):
                masked = jnp.where(sq_ref[s] == sk_ref[s], spread, 0.0)
                masked_ref[s] = masked
                mix[s] = masked.astype(BF)
            x1_ref[...] = x_ref[...]

        def part(wa, wb):
            def mat(m):
                return jnp.concatenate([wa[top_ref[0] ^ m], wb[top_ref[0] ^ m]], axis=0)

            both = both_ref[...]
            q = dot_nt(n_ref[...], mat(0))
            kexp = jnp.exp(dot_nt(both, mat(1)))
            v = dot_nt(both, mat(2))
            v_ref[...] = v
            kexp_ref[...] = kexp
            carried = (kexp * v).astype(BF)
            wsum = kexp.astype(BF)
            sg = jax.nn.sigmoid(q)
            sg_ref[...] = sg
            mixed = []
            for s in range(seqs):
                num = dot_nn(mix[s], carried[s * keys : (s + 1) * keys])
                den = dot_nn(mix[s], wsum[s * keys : (s + 1) * keys])
                rden = 1.0 / den
                ratio = num * rden
                here = slice(s * block, (s + 1) * block)
                rden_ref[here] = rden
                ratio_ref[here] = ratio
                mixed.append((sg[here] * ratio).astype(BF))
            mixed = jnp.concatenate(mixed, axis=0)
            mixed_ref[...] = mixed
            x1_ref[...] += dot_nn(mixed, mat(3))

        @pl.when(step == 0)
        def _():
            part(oa, ob)

        @pl.when(step == 1)
        def _():
            part(ta, tb)
            normal, _ = normalize(x1_ref[...])
            nb_ref[...] = (normal * g_ref[...] + s_ref[...]).astype(BF)

    def col(n):
        return pl.BlockSpec((n, half), lambda i, *_: (0, i))

    return call(
        order,
        body,
        (2,),
        [whole((rows, width))] * 3
        + [whole((4, quarter, width))] * 4
        + [whole((block, window)), whole((seqs, block, 1)), whole((seqs, 1, keys)), whole((1, width)), whole((1, width))],
        [col(rows)] * 3 + [col(seqs * keys)] * 2 + [col(rows)]
        + [whole((seqs, block, keys)), whole((rows, width)), whole((rows, width)), whole((seqs * keys, width))],
        [shape_of((rows, width), F32)] * 3
        + [shape_of((seqs * keys, width), F32)] * 2
        + [
            shape_of((rows, width), BF),
            shape_of((seqs, block, keys), F32),
            shape_of((rows, width), F32),
            shape_of((rows, width), BF),
            shape_of((seqs * keys, width), BF),
        ],
        [pltpu.VMEM((seqs, block, keys), BF)],
        prefetch=1,
        name="attn_fwd",
    )(top, x, normed, halo, *weights, band_rev, seg_q, seg_k, gain, shift)


def gelu_both(pre):
    square = pre * pre
    th = jnp.tanh(GELU_A * pre * (1.0 + GELU_B * square))
    upper = 0.5 * (1.0 + th)
    slope = upper + 0.5 * GELU_A * pre * (1.0 - th * th) * (1.0 + 3.0 * GELU_B * square)
    return pre * upper, slope


def chunk_specs(chunk, width, per_half):
    own = pl.BlockSpec((chunk, width), lambda i, *_: (jnp.minimum(i, per_half - 1), 0))
    other = pl.BlockSpec((chunk, width), lambda i, *_: (jnp.maximum(i - per_half, 0), 0))
    return own, other


def ff_forward(order, x1, normed, ups, downs, gain, shift):
    rows, width = x1.shape
    half = ups[0].shape[0]
    per_half = 2
    chunk = half // per_half
    steps = 2 * per_half

    def body(x_ref, n_ref, u0, u1, d0, d1, g_ref, s_ref, act_ref, slope_ref, x2_ref, next_ref):
        step = pl.program_id(0)

        @pl.when(step == 0)
        def _():
            x2_ref[...] = x_ref[...]

        def part(u, d):
            act, slope = gelu_both(dot_nt(n_ref[...], u[...]))
            act = act.astype(BF)
            act_ref[...] = act
            slope_ref[...] = slope.astype(BF)
            x2_ref[...] += dot_nn(act, d[...])

        pl.when(step < per_half)(lambda: part(u0, d0))
        pl.when(step >= per_half)(lambda: part(u1, d1))

        @pl.when(step == steps - 1)
        def _():
            normal, _ = normalize(x2_ref[...])
            next_ref[...] = (normal * g_ref[...] + s_ref[...]).astype(BF)

    own, other = chunk_specs(chunk, width, per_half)
    col = pl.BlockSpec((rows, chunk), lambda i: (0, i))
    return call(
        order,
        body,
        (steps,),
        [whole((rows, width))] * 2 + [own, other, own, other] + [whole((1, width))] * 2,
        [col, col, whole((rows, width)), whole((rows, width))],
        [
            shape_of((rows, 2 * half), BF),
            shape_of((rows, 2 * half), BF),
            shape_of((rows, width), F32),
            shape_of((rows, width), BF),
        ],
        name="ff_fwd",
    )(x1, normed, *ups, *downs, gain, shift)


def ff_backward(order, x1, normed, ups, downs, grad, gain, saved):
    rows, width = x1.shape
    half = ups[0].shape[0]
    per_half = 2
    chunk = half // per_half
    steps = 2 * per_half
    fresh = saved is None

    def body(x_ref, n_ref, u0, u1, d0, d1, grad_ref, g_ref, *rest):
        if fresh:
            (out_ref, gu0, gu1, gd0, gd1, g1_ref, ga_ref, gg_ref, gs_ref, low, dn, x2) = rest
        else:
            (act_ref, slope_ref, gu0, gu1, gd0, gd1, g1_ref, ga_ref, gg_ref, gs_ref, low, dn) = rest
        step = pl.program_id(0)

        @pl.when(step == 0)
        def _():
            low[...] = grad_ref[...].astype(BF)
            dn[...] = jnp.zeros_like(dn)
            if fresh:
                x2[...] = x_ref[...]

        def part(u, d, gu, gd):
            if fresh:
                act, slope = gelu_both(dot_nt(n_ref[...], u[...]))
                act = act.astype(BF)
                x2[...] += dot_nn(act, d[...])
            else:
                act, slope = act_ref[...], slope_ref[...].astype(F32)
            pre_grad = (dot_nt(low[...], d[...]) * slope).astype(BF)
            dn[...] += dot_nn(pre_grad, u[...])
            gd[...] = dot_tn(act, low[...]).astype(BF)
            gu[...] = dot_tn(pre_grad, n_ref[...]).astype(BF)

        pl.when(step < per_half)(lambda: part(u0, d0, gu0, gd0))
        pl.when(step >= per_half)(lambda: part(u1, d1, gu1, gd1))

        @pl.when(step == steps - 1)
        def _():
            if fresh:
                out_ref[...] = x2[...].astype(BF)
            normal, inv = normalize(x_ref[...])
            total = dn[...]
            g1 = grad_ref[...] + norm_back(total, normal, inv, g_ref[...])
            g1_ref[...] = g1
            ga_ref[...] = g1.astype(BF)
            gg_ref[...] = jnp.sum(total * normal, axis=0, keepdims=True)
            gs_ref[...] = jnp.sum(total, axis=0, keepdims=True)

    own, other = chunk_specs(chunk, width, per_half)
    col = pl.BlockSpec((rows, chunk), lambda i: (0, i))
    out_specs = [own, other, own, other] + [whole((rows, width))] * 2 + [whole((1, width))] * 2
    out_shape = (
        [shape_of((half, width), BF)] * 4
        + [shape_of((rows, width), F32), shape_of((rows, width), BF)]
        + [shape_of((1, width), F32)] * 2
    )
    scratch = [pltpu.VMEM((rows, width), BF), pltpu.VMEM((rows, width), F32)]
    if fresh:
        out_specs = [whole((rows, width))] + out_specs
        out_shape = [shape_of((rows, width), BF)] + out_shape
        scratch.append(pltpu.VMEM((rows, width), F32))
    return call(
        order,
        body,
        (steps,),
        [whole((rows, width))] * 2 + [own, other, own, other] + [whole((rows, width)), whole((1, width))]
        + ([] if fresh else [col, col]),
        out_specs,
        out_shape,
        scratch,
        name="ff_bwd",
    )(x1, normed, *ups, *downs, grad, gain, *(() if fresh else saved))


def attn_backward(order, top, grad_low, weights, sg, ratio, rden, v, kexp, masked):
    rows, width = grad_low.shape
    seqs, block, keys = masked.shape
    window = keys - block
    quarter = weights[0].shape[1]
    half = 2 * quarter

    def body(top_ref, ga_ref, oa, ob, ta, tb, sg_ref, ratio_ref, rden_ref, v_ref, kexp_ref, masked_ref,
             gq_ref, gk_ref, gv_ref, band_ref, own_ref, halo_ref, mix_t, wgrad, dn):
        step = pl.program_id(0)

        @pl.when(step == 0)
        def _():
            for s in range(seqs):
                mix_t[s] = masked_ref[s].T.astype(BF)
            wgrad[...] = jnp.zeros_like(wgrad)
            dn[...] = jnp.zeros_like(dn)

        def part(wa, wb):
            def mat(m):
                return jnp.concatenate([wa[top_ref[0] ^ m], wb[top_ref[0] ^ m]], axis=0)

            gm = dot_nt(ga_ref[...], mat(3))
            sig = sg_ref[...]
            rat = ratio_ref[...]
            scaled = gm * sig
            gq = (scaled * rat * (1.0 - sig)).astype(BF)
            gq_ref[...] = gq
            gnum_f = scaled * rden_ref[...]
            gnum = gnum_f.astype(BF)
            gden = (-gnum_f * rat).astype(BF)
            wq, wk, wv = mat(0), mat(1), mat(2)
            dq = dot_nn(gq, wq)
            for s in range(seqs):
                here = slice(s * block, (s + 1) * block)
                there = slice(s * keys, (s + 1) * keys)
                vv = v_ref[there]
                ke = kexp_ref[there]
                gcar = dot_nn(mix_t[s], gnum[here])
                gsum = dot_nn(mix_t[s], gden[here])
                gv = (gcar * ke).astype(BF)
                gk = ((gcar * vv + gsum) * ke).astype(BF)
                gk_ref[there] = gk
                gv_ref[there] = gv
                wgrad[s] += dot_nt(gnum[here], (ke * vv).astype(BF)) + dot_nt(gden[here], ke.astype(BF))
                dkv = dot_nn(gk, wk) + dot_nn(gv, wv)
                dn[s * keys : s * keys + window] += dkv[:window]
                dn[s * keys + window : (s + 1) * keys] += dkv[window:] + dq[here]

        @pl.when(step == 0)
        def _():
            part(oa, ob)

        @pl.when(step == 1)
        def _():
            part(ta, tb)
            total = wgrad[0] * masked_ref[0]
            for s in range(1, seqs):
                total = total + wgrad[s] * masked_ref[s]
            lane_row = lax.broadcasted_iota(jnp.int32, (block, keys), 0) + 1
            bit = 1
            while bit <= block:
                rolled = pltpu.roll(total, keys - bit, axis=1)
                total = jnp.where((lane_row & bit) != 0, rolled, total)
                bit *= 2
            band_ref[...] = total[:, :window]
            for s in range(seqs):
                halo_ref[s * block : (s + 1) * block] = dn[s * keys : s * keys + window].astype(BF)
                own_ref[s * block : (s + 1) * block] = dn[s * keys + window : (s + 1) * keys]

    def col(n):
        return pl.BlockSpec((n, half), lambda i, *_: (0, i))

    return call(
        order,
        body,
        (2,),
        [whole((rows, width))]
        + [whole((4, quarter, width))] * 4
        + [col(rows)] * 3 + [col(seqs * keys)] * 2 + [whole((seqs, block, keys))],
        [col(rows), col(seqs * keys), col(seqs * keys), whole((block, window)), whole((rows, width)), whole((rows, width))],
        [
            shape_of((rows, width), BF),
            shape_of((seqs * keys, width), BF),
            shape_of((seqs * keys, width), BF),
            shape_of((block, window), F32),
            shape_of((rows, width), F32),
            shape_of((rows, width), BF),
        ],
        [
            pltpu.VMEM((seqs, keys, block), BF),
            pltpu.VMEM((seqs, block, keys), F32),
            pltpu.VMEM((seqs * keys, width), F32),
        ],
        prefetch=1,
        name="attn_bwd",
    )(top, grad_low, *weights, sg, ratio, rden, v, kexp, masked)


def attn_weight_grads(order, top, gq, gk, gv, mixed, normed, both, grad_low):
    rows, width = gq.shape
    keyrows = both.shape[0]
    half = width // 2
    quarter = half // 2

    def body(top_ref, gq_ref, gk_ref, gv_ref, mixed_ref, n_ref, b_ref, ga_ref, oa, ob, ta, tb):
        step = pl.program_id(0)
        mat = lax.rem(step, 4)

        def store(value):
            low = value.astype(BF)

            @pl.when(step < 4)
            def _():
                oa[0] = low[:quarter]
                ob[0] = low[quarter:]

            @pl.when(step >= 4)
            def _():
                ta[0] = low[:quarter]
                tb[0] = low[quarter:]

        pl.when(mat == 0)(lambda: store(dot_tn(gq_ref[...], n_ref[...])))
        pl.when(mat == 1)(lambda: store(dot_tn(gk_ref[...], b_ref[...])))
        pl.when(mat == 2)(lambda: store(dot_tn(gv_ref[...], b_ref[...])))
        pl.when(mat == 3)(lambda: store(dot_tn(mixed_ref[...], ga_ref[...])))

    def col(n):
        return pl.BlockSpec((n, half), lambda i, *_: (0, i // 4))

    own = pl.BlockSpec((1, quarter, width), lambda i, t: (jnp.minimum(i, 3) ^ t[0], 0, 0))
    other = pl.BlockSpec((1, quarter, width), lambda i, t: (jnp.maximum(i - 4, 0) ^ t[0], 0, 0))
    return call(
        order,
        body,
        (8,),
        [col(rows), col(keyrows), col(keyrows), col(rows), whole((rows, width)), whole((keyrows, width)), whole((rows, width))],
        [own, own, other, other],
        [shape_of((4, quarter, width), BF)] * 4,
        prefetch=1,
        name="attn_wgrad",
    )(top, gq, gk, gv, mixed, normed, both, grad_low)


def leave_attn(order, x, grad, own, back, gain):
    rows, width = x.shape

    def body(x_ref, g_ref, o_ref, b_ref, gain_ref, out_ref, gg_ref, gs_ref):
        normal, inv = normalize(x_ref[...])
        total = o_ref[...] + b_ref[...].astype(F32)
        out_ref[...] = g_ref[...] + norm_back(total, normal, inv, gain_ref[...])
        gg_ref[...] = jnp.sum(total * normal, axis=0, keepdims=True)
        gs_ref[...] = jnp.sum(total, axis=0, keepdims=True)

    return call(
        order,
        body,
        (1,),
        [whole((rows, width))] * 4 + [whole((1, width))],
        [whole((rows, width)), whole((1, width)), whole((1, width))],
        [shape_of((rows, width), F32)] + [shape_of((1, width), F32)] * 2,
        name="leave",
    )(x, grad, own, back, gain)


class Order:
    def __init__(self):
        self.token = jnp.zeros(TOKEN, jnp.int32)

    def pin(self, *arrays):
        *arrays, self.token = tie(*arrays, self.token)
        return arrays


class Links:
    def __init__(self, order, dp, mp):
        self.order = order
        self.dp = dp
        self.mp = mp
        bits = [1 << k for k in range(1, dp.bit_length() - 1)]
        self.routes = (bits, bits[::-1])

    def swap(self, value, axis, bit):
        size = self.dp if axis == "dp" else self.mp
        return lax.ppermute(value, axis, [(i, i ^ bit) for i in range(size)])


class Spread:
    def __init__(self, links, values):
        self.links = links
        self.values = list(values)
        self.phase = 0
        self.have = [[], []]

    def start(self):
        self.values = self.links.order.pin(*self.values)
        self.coming = [
            self.links.swap(value, "dp", route[self.phase])
            for value, route in zip(self.values, self.links.routes)
        ]

    def wait(self):
        coming = self.links.order.pin(*self.coming)
        for k in range(2):
            bit = self.links.routes[k][self.phase]
            place = sum(1 for other in self.have[k] if other > bit)
            self.values[k] = jnp.stack([self.values[k], coming[k]], axis=place)
            self.have[k].append(bit)
        self.phase += 1

    def wait_all(self):
        self.wait()
        while self.phase < len(self.links.routes[0]):
            self.start()
            self.wait()

    def start_cores(self):
        self.values = self.links.order.pin(*self.values)
        self.coming = [self.links.swap(value, "dp", 1) for value in self.values]

    def wait_cores(self):
        return self.values + self.links.order.pin(*self.coming)


class Gather(Spread):
    def __init__(self, links, piece_a, piece_b):
        super().__init__(links, ())
        self.cut = piece_a.shape[0]
        self.piece = jnp.concatenate([piece_a, piece_b], axis=0)

    def start_mp(self):
        (self.piece,) = self.links.order.pin(self.piece)
        self.coming_mp = [self.links.swap(self.piece, "mp", p) for p in range(1, self.links.mp)]

    def wait_mp(self):
        parts = [self.piece] + self.links.order.pin(*self.coming_mp)
        self.values = [
            jnp.stack([part[: self.cut] for part in parts]),
            jnp.stack([part[self.cut :] for part in parts]),
        ]


class Reduce:
    def __init__(self, links, halves):
        self.links = links
        self.halves = halves
        self.phase = 0

    def start_cores(self):
        others = self.links.order.pin(*self.halves[2:])
        self.coming = [self.links.swap(other, "dp", 1) for other in others]

    def wait_cores(self):
        coming = self.links.order.pin(*self.coming)
        mp = self.links.mp
        self.have = [sorted(route, reverse=True) for route in self.links.routes]
        self.values = []
        for own, other in zip(self.halves[:2], coming):
            total = (own.astype(F32) + other.astype(F32)).astype(BF)
            groups = self.links.dp // 2
            rows = total.size // total.shape[-1] // groups // mp
            self.values.append(total.reshape((2,) * len(self.have[0]) + (mp, rows, total.shape[-1])))

    def start(self):
        sends, self.keeps = [], []
        for k in range(2):
            place = self.have[k].index(self.links.routes[1 - k][self.phase])
            self.keeps.append(lax.index_in_dim(self.values[k], 0, place, keepdims=False))
            sends.append(lax.index_in_dim(self.values[k], 1, place, keepdims=False))
        sends = self.links.order.pin(*sends)
        self.coming = [
            self.links.swap(sends[k], "dp", self.links.routes[1 - k][self.phase]) for k in range(2)
        ]

    def wait(self):
        coming = self.links.order.pin(*self.coming)
        for k in range(2):
            self.values[k] = (self.keeps[k].astype(F32) + coming[k].astype(F32)).astype(BF)
            self.have[k].remove(self.links.routes[1 - k][self.phase])
        self.phase += 1

    def wait_all(self):
        self.wait()
        while self.phase < len(self.links.routes[0]):
            self.start()
            self.wait()

    def start_mp(self):
        blocks = [jnp.concatenate([value[p] for value in self.values], axis=0) for p in range(self.links.mp)]
        self.kept = blocks[0]
        sends = self.links.order.pin(*blocks[1:])
        self.coming = [self.links.swap(send, "mp", p + 1) for p, send in enumerate(sends)]

    def wait_mp(self):
        total = self.kept.astype(F32)
        for part in self.links.order.pin(*self.coming):
            total = total + part.astype(F32)
        return total.astype(BF)


def make_shards(dp, mp):
    def shards(
        tokens,
        segments,
        qkv_weight,
        out_weight,
        up_weight,
        down_projection_weight,
        norm_gain,
        norm_bias,
        pos_bias,
        cotangent,
    ):
        seqs, block, width = tokens.shape
        layers = qkv_weight.shape[0]
        window = pos_bias.shape[2]
        channels = qkv_weight.shape[-1]
        hidden = up_weight.shape[-1]
        rows = seqs * block
        dp_index = lax.axis_index("dp")
        mp_index = lax.axis_index("mp")
        order = Order()
        links = Links(order, dp, mp)
        attn_rows = 4 * channels // dp
        ff_rows = hidden // dp
        top = (dp_index // 2 // (dp // 8)).astype(jnp.int32).reshape(1)

        def picks(count, offset, length):
            return (
                lax.broadcasted_iota(jnp.int32, (count, length), 0) + offset
                == lax.broadcasted_iota(jnp.int32, (count, length), 1)
            ).astype(BF)

        attn_pick = picks(attn_rows, dp_index * attn_rows, 4 * channels)
        ff_pick = picks(ff_rows, dp_index * ff_rows, hidden)

        def attn_gather(layer):
            piece = jnp.einsum(
                "rmc,mdc->rd",
                attn_pick[:, : 3 * channels].reshape(attn_rows, 3, channels),
                qkv_weight[layer],
                preferred_element_type=F32,
            ) + dot_nn(attn_pick[:, 3 * channels :], out_weight[layer])
            piece = piece.astype(BF)
            return Gather(links, piece[: attn_rows // 2], piece[attn_rows // 2 :])

        def ff_gather(layer):
            return Gather(
                links,
                dot_nt(ff_pick, up_weight[layer]).astype(BF),
                dot_nn(ff_pick, down_projection_weight[layer]).astype(BF),
            )

        def attn_mats(parts):
            return [part.reshape(4, -1, width) for part in parts]

        def ff_mats(parts):
            flat = [part.reshape(-1, width) for part in parts]
            return (flat[0], flat[2]), (flat[1], flat[3])

        def forward_halo(value):
            return lax.ppermute(value, "mp", [(i, i + 1) for i in range(mp - 1)])

        def backward_halo(value):
            return lax.ppermute(value, "mp", [(i + 1, i) for i in range(mp - 1)])

        gains = norm_gain.reshape(layers, 2, 1, width)
        shifts = norm_bias.reshape(layers, 2, 1, width)

        attn0 = attn_gather(0)
        attn0.start_mp()
        ff0 = ff_gather(0)
        ff0.start_mp()
        x, normed = enter_kernel(order, tokens.reshape(rows, width), gains[0, 0], shifts[0, 0])
        (normed,) = order.pin(normed)
        halo = forward_halo(normed)
        attn0.wait_mp()
        attn0.start()
        attn1 = attn_gather(1)
        attn1.start_mp()
        ff1 = ff_gather(1)
        ff1.start_mp()

        seg_pad = jnp.concatenate([jnp.full((seqs, window), -1, segments.dtype), segments], axis=1)
        seg_keys = lax.dynamic_slice_in_dim(seg_pad, mp_index * block, block + window, axis=1)
        seg_q = seg_keys[:, window:].reshape(seqs, block, 1)
        seg_k = seg_keys.reshape(seqs, 1, block + window)
        band_rev = lax.dynamic_slice_in_dim(pos_bias, mp_index * block, block, axis=1)[:, :, ::-1]

        attn0.wait()
        attn0.start()
        ff0.wait_mp()
        ff0.start()
        attn0.wait_all()
        attn0.start_cores()
        w_attn0 = attn_mats(attn0.wait_cores())
        ff0.wait()
        ff0.start()
        (halo,) = order.pin(halo)

        def attn(layer, x, normed, halo, w_attn):
            sg, ratio, rden, v, kexp, mixed, masked, x1, normed_b, both = attn_forward(
                order, top, x, normed, halo, w_attn, band_rev[layer], seg_q, seg_k,
                gains[layer, 1], shifts[layer, 1],
            )
            return x1, normed_b, (sg, ratio, rden, v, kexp, masked), (mixed, normed, both)

        x1_0, normed_b0, saved0, rows0 = attn(0, x, normed, halo, w_attn0)
        attn1.wait_mp()
        attn1.start()
        ff0.wait_all()
        ff0.start_cores()
        ups0, downs0 = ff_mats(ff0.wait_cores())
        attn1.wait()
        attn1.start()
        act0, slope0, x2, normed2 = ff_forward(
            order, x1_0, normed_b0, ups0, downs0, gains[1, 0], shifts[1, 0]
        )
        (normed2,) = order.pin(normed2)
        halo2 = forward_halo(normed2)
        ff1.wait_mp()
        ff1.start()
        attn1.wait_all()
        attn1.start_cores()
        w_attn1 = attn_mats(attn1.wait_cores())
        ff1.wait()
        ff1.start()
        (halo2,) = order.pin(halo2)
        x1_1, normed_b1, saved1, rows1 = attn(1, x2, normed2, halo2, w_attn1)
        ff1.wait_all()
        ff1.start_cores()
        ups1, downs1 = ff_mats(ff1.wait_cores())

        output, gu0, gu1, gd0, gd1, grad1, grad1_low, gain_b1, shift_b1 = ff_backward(
            order, x1_1, normed_b1, ups1, downs1, cotangent.reshape(rows, width), gains[1, 1], None
        )
        r_ff1 = Reduce(links, [gu0, gd0, gu1, gd1])
        r_ff1.start_cores()
        r_ff1.wait_cores()
        r_ff1.start()

        def attn_back(grad_low, w_attn, saved, kept):
            gq, gk, gv, band, dn_own, dn_halo = attn_backward(order, top, grad_low, w_attn, *saved)
            (dn_halo,) = order.pin(dn_halo)
            back = backward_halo(dn_halo)
            halves = attn_weight_grads(order, top, gq, gk, gv, *kept, grad_low)
            return band, dn_own, back, Reduce(links, halves)

        band1, dn_own1, back1, r_attn1 = attn_back(grad1_low, w_attn1, saved1, rows1)
        r_attn1.start_cores()
        r_attn1.wait_cores()
        r_attn1.start()
        (back1,) = order.pin(back1)
        grad2, gain_a1, shift_a1 = leave_attn(order, x2, grad1, dn_own1, back1, gains[1, 0])
        r_ff1.wait()
        r_ff1.start()
        gu0, gu1, gd0, gd1, grad3, grad3_low, gain_b0, shift_b0 = ff_backward(
            order, x1_0, normed_b0, ups0, downs0, grad2, gains[0, 1], (act0, slope0)
        )
        r_ff0 = Reduce(links, [gu0, gd0, gu1, gd1])
        r_ff0.start_cores()
        r_attn1.wait()
        r_attn1.start()
        r_ff0.wait_cores()
        r_ff0.start()
        r_ff1.wait_all()
        band0, dn_own0, back0, r_attn0 = attn_back(grad3_low, w_attn0, saved0, rows0)
        r_ff1.start_mp()
        r_attn0.start_cores()
        r_attn0.wait_cores()
        r_attn0.start()
        r_attn1.wait_all()
        r_attn1.start_mp()
        (back0,) = order.pin(back0)
        grad4, gain_a0, shift_a0 = leave_attn(order, x, grad3, dn_own0, back0, gains[0, 0])
        norms = jnp.concatenate(
            [gain_a0, gain_b0, shift_a0, shift_b0, gain_a1, gain_b1, shift_a1, shift_b1], axis=0
        ).reshape(-1, window)
        packed = jnp.concatenate([band0, band1, norms], axis=0)
        packed = lax.psum(packed, "dp")
        r_ff0.wait()
        r_ff0.start()
        r_attn0.wait()
        r_attn0.start()

        def halves_of(*pieces):
            joined = jnp.concatenate(pieces, axis=0)
            middle = joined.shape[0] // 2
            return joined[:middle], joined[middle:]

        back_1 = Spread(links, halves_of(r_attn1.wait_mp(), r_ff1.wait_mp()))
        r_ff0.wait_all()
        r_ff0.start_mp()
        back_1.start()
        r_attn0.wait_all()
        r_attn0.start_mp()
        back_1.wait()
        back_1.start()
        (packed,) = order.pin(packed)
        packed = lax.all_gather(packed, "mp", axis=0, tiled=False)
        back_1.wait_all()
        back_1.start_cores()
        full_1 = back_1.wait_cores()
        back_0 = Spread(links, halves_of(r_ff0.wait_mp(), r_attn0.wait_mp()))
        back_0.start()

        owner = jnp.bitwise_xor(jnp.arange(dp), dp_index)

        def results(full, attn_first):
            parts = [
                jnp.concatenate(
                    [half.reshape(dp // 2, 1, -1, width) for half in (full[k], full[2 + k])], axis=1
                )
                for k in range(2)
            ]
            value = jnp.concatenate(parts, axis=2).reshape(dp, -1, width)
            if attn_first:
                attn_part, up_part, down_part = jnp.split(value, [attn_rows, attn_rows + ff_rows], axis=1)
            else:
                up_part, down_part, attn_part = jnp.split(value, [ff_rows, 2 * ff_rows], axis=1)

            def places(count):
                spots = (owner[:, None] * count + jnp.arange(count)[None, :]).reshape(-1, 1)
                return (spots == jnp.arange(dp * count)[None, :]).astype(BF)

            attn_place = places(attn_rows).reshape(-1, 4, channels)
            ff_place = places(ff_rows)
            attn_part = attn_part.reshape(-1, width)
            return (
                jnp.einsum("pd,pmc->mdc", attn_part, attn_place[:, :3], preferred_element_type=F32),
                dot_tn(attn_place[:, 3], attn_part),
                dot_tn(up_part.reshape(-1, width), ff_place),
                dot_tn(ff_place, down_part.reshape(-1, width)),
            )

        out1 = results(full_1, True)
        back_0.wait()
        back_0.start()
        back_0.wait_all()
        back_0.start_cores()
        out0 = results(back_0.wait_cores(), False)
        big = tuple(jnp.stack([out0[k], out1[k]]) for k in range(4))
        band_sum = jnp.transpose(packed[:, : layers * block].reshape(mp, layers, block, window), (1, 0, 2, 3))
        band_sum = band_sum.reshape(layers, mp * block, window)[:, :, ::-1]
        norm_sum = jnp.sum(packed[:, layers * block :], axis=0).reshape(layers, 4, width)
        return (
            (output.reshape(tokens.shape), grad4.reshape(tokens.shape))
            + big
            + (norm_sum[:, :2], norm_sum[:, 2:], band_sum)
        )

    return shards


def solution(mesh):
    placed = (
        P("dp", "mp", None),
        P("dp", None),
        P(None, None, None, "mp"),
        P(None, "mp", None),
        P(None, None, "mp"),
        P(None, "mp", None),
        P(),
        P(),
        P(),
        P("dp", "mp", None),
    )
    return jax.shard_map(
        make_shards(mesh.shape["dp"], mesh.shape["mp"]),
        mesh=mesh,
        in_specs=placed,
        out_specs=(
            P("dp", "mp", None),
            P("dp", "mp", None),
            P(None, None, None, "mp"),
            P(None, "mp", None),
            P(None, None, "mp"),
            P(None, "mp", None),
            P(),
            P(),
            P(),
        ),
        check_vma=False,
    )
```

time: 790 us -> 746 us (0.944)
  Pallas kernels: 0 us -> 156 us
  matrix products: 148 us -> 23.7 us
  local copies, waits for them, and re-layouts: 120 us -> 87.3 us
  starting transfers between devices: 119 us -> 88.6 us
    pallas_call x0 -> x97, Pallas kernels: none -> 156 us  [the longest x12 156 us: run(): *results, order.token = kernel(*operands, order.token)]
    ppermute x94 -> x84, waiting for transfers between devices: 234 us -> 167 us  [swap(): return lax.ppermute(value, axis, [(i, i ^ bit) for i in range(size)])]
    psum x0 -> x1, waiting for transfers between devices: none -> 57.2 us  [shards(): packed = lax.psum(packed, 'dp')]
    dot_general x16 -> x2, matrix products: 51.4 us -> 2.43 us  [dot_nt(): lax.dot_general(lhs, rhs, (((1,), (1,)), ((), ())), preferred_element_typ...]
    dot_general x16 -> x4, matrix products: 49.3 us -> 5.13 us  [dot_nn(): lax.dot_general(lhs, rhs, (((1,), (0,)), ((), ())), preferred_element_typ...]
    ppermute x94 -> x84, starting transfers between devices: 110 us -> 77.3 us  [swap(): return lax.ppermute(value, axis, [(i, i ^ bit) for i in range(size)])]
    slice x49 -> x10, local copies, waits for them, and re-layouts: 42.5 us -> 14.5 us  [the longest x3 6.74 us: attn(): band_rev[layer]]
    dot_general x16 -> x6, matrix products: 36.4 us -> 11.3 us  [dot_tn(): lax.dot_general(lhs, rhs, (((0,), (0,)), ((), ())), preferred_element_typ...]
  transfers between devices with their start and end apart: 100 -> 90, of which waited for: 40 -> 38; matrix products, arithmetic and copies ran while one was open for 36% -> 17% of each run, Pallas kernels for 0% -> 8%
where the time goes in v2:
time: 746 us; the launch traced here: 739 us
  waiting for transfers between devices  255 us (34%)
  Pallas kernels  156 us (21%)
  other arithmetic  113 us (15%)
  starting transfers between devices  88.6 us (12%)
  local copies, waits for them, and re-layouts  87.3 us (12%)
  matrix products  23.7 us (3%)
  between operations  15.8 us (2%)
    ppermute x84, waiting for transfers between devices, swap(): return lax.ppermute(value, axis, [(i, i ^ bit) for i in range(size)])  167 us
    pallas_call x12, Pallas kernels, run(): *results, order.token = kernel(*operands, order.token)  156 us
    ppermute x84, starting transfers between devices, swap(): return lax.ppermute(value, axis, [(i, i ^ bit) for i in range(size)])  77.3 us
    psum x1, waiting for transfers between devices, shards(): packed = lax.psum(packed, 'dp')  57.2 us
    another operation x24, other arithmetic, wait(): self.values[k] = jnp.stack([self.values[k], coming[k]], axis=place)  46.7 us
    unnamed x294, local copies, waits for them, and re-layouts  27.9 us
    convert_element_type x16, other arithmetic, wait(): (self.keeps[k].astype(F32) + coming[k].astype(F32)).astype(BF)  17.8 us
    ppermute x2, waiting for transfers between devices, backward_halo(): return lax.ppermute(value, 'mp', [(i + 1, i) for i in range(mp - 1)])  17.4 us
  transfers between devices with their start and end apart: 90, of which 38 were waited for; matrix products, arithmetic and copies ran while one was open for 17% of the time, Pallas kernels for 8%

profile of v2, /device:TPU:9, one launch (start us, length us, event | category | flops | bytes accessed | tf_op | source)
XLA Modules:
  0.0 739.3 jit_solution(7092191130234206730)
XLA Ops:
  36.1 3.4 collective-permute-done.7.refs_0_
  44.8 6.3 collective-permute-done.3.refs_2_
  59.1 7.0 collective-permute-done.11.refs_0_
  71.3 3.0 collective-permute-start.13
  75.9 3.8 collective-permute-start
  83.1 6.1 collective-permute-done.10.refs_1_
  97.5 3.1 slice.438
  103.3 14.8 %attn_fwd.2 = (f32[512,768]{1,0:T(8,128)}, f32[512,768]{1,0:T(8,128)}, f32[512,768]{1,0:T(8,128)}, f32[1024,768]{1,0:T(8,128)}, f32[1024,768]{1,0:T(8,128)}, /*i...) custom-call(s32[1]{0:T(128)} %bitcast.refs_0_, ...), custom_call_target="tpu_custom_call", output_to_operand_aliasing={{10}: (13, {})} | custom-call | tf_op jit(solution)/shard_map/attn_fwd/pallas_call | solution.py:74
  125.3 3.1 pad_maximum_fusion.4.refs_1_
  129.9 3.0 collective-permute-start.20
  134.3 5.6 collective-permute-done.20.refs_0_
  146.7 14.3 %ff_fwd.1 = (bf16[512,3072]{1,0:T(8,128)(2,1)}, bf16[512,3072]{1,0:T(8,128)(2,1)}, f32[512,768]{1,0:T(8,128)}, bf16[512,768]{1,0:T(8,128)(2,1)}, s32[8,128]{1,0:T(8,128)}) custom-call(f32[512,768]{1,0:T(8,128)} %get-tuple-element.389.refs_0_, bf16[512,768]{1,0:T(8,128)(2,1)} %get-tuple-element.390.refs_1_, ...), custom_call_target="tpu_custom_call", output_to_operand_aliasing={{4}: (8, {})} | custom-call | tf_op jit(solution)/shard_map/ff_fwd/pallas_call | solution.py:74
  161.0 7.1 collective-permute-done.27.refs_2_
  173.4 9.8 %collective-permute-done.30.refs_0_ = bf16[2,4,48,768]{3,2,1,0:T(8,128)(2,1)S(1)} collective-permute-done((bf16[2,4,48,768]{3,2,1,0:T(8,128)(2,1)S(1)}, bf16[2,4,48,768]{3,2,1,0:T(8,128)(2,1)S(1)}, u32[]{:S(2)}, u32[]{:S(2)}) %collective-permute-start.30) | collective-permute-done | bytes 589856 | tf_op jit(solution)/shard_map/ppermute | solution.py:527
  194.8 8.6 %collective-permute-done.28.refs_0_ = bf16[4,96,768]{2,1,0:T(8,128)(2,1)} collective-permute-done((bf16[4,96,768]{2,1,0:T(8,128)(2,1)S(1)}, bf16[4,96,768]{2,1,0:T(8,128)(2,1)}, u32[]{:S(2)}, u32[]{:S(2)}) %collective-permute-start.28) | collective-permute-done | bytes 589856 | tf_op jit(solution)/shard_map/ppermute | solution.py:527
  210.3 3.0 collective-permute-start.24
  215.1 13.5 %collective-permute-done.24.refs_0_ = bf16[512,768]{1,0:T(8,128)(2,1)} collective-permute-done((bf16[512,768]{1,0:T(8,128)(2,1)S(1)}, bf16[512,768]{1,0:T(8,128)(2,1)}, u32[]{:S(2)}, u32[]{:S(2)}) %collective-permute-start.24) | collective-permute-done | bytes 786464 | tf_op jit(solution)/shard_map/ppermute | solution.py:704
  228.6 14.9 %attn_fwd.3 = (f32[512,768]{1,0:T(8,128)}, f32[512,768]{1,0:T(8,128)}, f32[512,768]{1,0:T(8,128)}, f32[1024,768]{1,0:T(8,128)}, f32[1024,768]{1,0:T(8,128)}, /*i...) custom-call(s32[1]{0:T(128)} %bitcast.refs_0_, ...), custom_call_target="tpu_custom_call", output_to_operand_aliasing={{10}: (13, {})} | custom-call | tf_op jit(solution)/shard_map/attn_fwd/pallas_call | solution.py:74
  245.5 3.0 pad_maximum_fusion.6.refs_1_
  250.2 3.7 collective-permute-start.36
  253.9 7.7 %collective-permute-done.36.refs_0_ = bf16[2,2,4,96,768]{4,3,2,1,0:T(8,128)(2,1)S(1)} collective-permute-done((bf16[2,2,4,96,768]{4,3,2,1,0:T(8,128)(2,1)}, bf16[2,2,4,96,768]{4,3,2,1,0:T(8,128)(2,1)S(1)}, u32[]{:S(2)}, u32[]{:S(2)}) %collective-permute-start.36) | collective-permute-done | bytes 2359328 | tf_op jit(solution)/shard_map/ppermute | solution.py:527
  263.0 25.7 %ff_bwd.2 = (bf16[512,768]{1,0:T(8,128)(2,1)}, bf16[1536,768]{1,0:T(8,128)(2,1)}, bf16[1536,768]{1,0:T(8,128)(2,1)}, bf16[1536,768]{1,0:T(8,128)(2,1)}, bf16[153...) custom-call(f32[512,768]{1,0:T(8,128)} %get-tuple-element.445.refs_0, ...), custom_call_target="tpu_custom_call", output_to_operand_aliasing={{9}: (8, {})} | custom-call | tf_op jit(solution)/shard_map/ff_bwd/pallas_call | solution.py:74
  289.3 6.3 collective-permute-done.38.refs_0_
  297.0 3.1 add_convert_fusion.2
  304.4 16.0 %attn_bwd.2 = (bf16[512,768]{1,0:T(8,128)(2,1)}, bf16[1024,768]{1,0:T(8,128)(2,1)}, bf16[1024,768]{1,0:T(8,128)(2,1)}, f32[256,256]{1,0:T(8,128)}, f32[512,768]{...) custom-call(s32[1]{0:T(128)} %bitcast.refs_0_, ...), custom_call_target="tpu_custom_call", output_to_operand_aliasing={{6}: (12, {})} | custom-call | tf_op jit(solution)/shard_map/attn_bwd/pallas_call | solution.py:74
  320.4 11.4 %attn_wgrad.2 = (bf16[4,192,768]{2,1,0:T(8,128)(2,1)}, bf16[4,192,768]{2,1,0:T(8,128)(2,1)}, bf16[4,192,768]{2,1,0:T(8,128)(2,1)}, bf16[4,192,768]{2,1,0:T(8,128)(2,1)}, s32[8,128]{1,0:T(8,128)}) custom-call(s32[1]{0:T(128)} %bitcast.refs_0_, bf16[512,768]{1,0:T(8,128)(2,1)} %get-tuple-element.484.refs_1_, ...), custom_call_target="tpu_custom_call", output_to_operand_aliasing={{4}: (8, {})} | custom-call | tf_op jit(solution)/shard_map/attn_wgrad/pallas_call | solution.py:74
  342.4 11.4 %collective-permute-done.40.refs_0_ = bf16[512,768]{1,0:T(8,128)(2,1)} collective-permute-done((bf16[512,768]{1,0:T(8,128)(2,1)}, bf16[512,768]{1,0:T(8,128)(2,1)}, u32[]{:S(2)}, u32[]{:S(2)}) %collective-permute-start.40) | collective-permute-done | bytes 786464 | tf_op jit(solution)/shard_map/ppermute | solution.py:707
  353.8 4.9 leave.2
  365.7 19.8 %ff_bwd.3 = (bf16[1536,768]{1,0:T(8,128)(2,1)}, bf16[1536,768]{1,0:T(8,128)(2,1)}, bf16[1536,768]{1,0:T(8,128)(2,1)}, bf16[1536,768]{1,0:T(8,128)(2,1)}, f32[512...) custom-call(f32[512,768]{1,0:T(8,128)} %get-tuple-element.389.refs_0, ...), custom_call_target="tpu_custom_call", output_to_operand_aliasing={{8}: (10, {})} | custom-call | tf_op jit(solution)/shard_map/ff_bwd/pallas_call | solution.py:74
  388.8 12.8 %collective-permute-done.49.refs_0_ = bf16[2,4,48,768]{3,2,1,0:T(8,128)(2,1)} collective-permute-done((bf16[2,4,48,768]{3,2,1,0:T(8,128)(2,1)}, bf16[2,4,48,768]{3,2,1,0:T(8,128)(2,1)}, u32[]{:S(2)}, u32[]{:S(2)}) %collective-permute-start.49) | collective-permute-done | bytes 589856 | tf_op jit(solution)/shard_map/ppermute | solution.py:527
  409.4 3.1 add_convert_fusion
  422.6 15.8 %attn_bwd.3 = (bf16[512,768]{1,0:T(8,128)(2,1)}, bf16[1024,768]{1,0:T(8,128)(2,1)}, bf16[1024,768]{1,0:T(8,128)(2,1)}, f32[256,256]{1,0:T(8,128)}, f32[512,768]{...) custom-call(s32[1]{0:T(128)} %bitcast.refs_0_, ...), custom_call_target="tpu_custom_call", output_to_operand_aliasing={{6}: (12, {})} | custom-call | tf_op jit(solution)/shard_map/attn_bwd/pallas_call | solution.py:74
  438.5 11.3 %attn_wgrad.3 = (bf16[4,192,768]{2,1,0:T(8,128)(2,1)}, bf16[4,192,768]{2,1,0:T(8,128)(2,1)}, bf16[4,192,768]{2,1,0:T(8,128)(2,1)}, bf16[4,192,768]{2,1,0:T(8,128)(2,1)}, s32[8,128]{1,0:T(8,128)}) custom-call(s32[1]{0:T(128)} %bitcast.refs_0_, bf16[512,768]{1,0:T(8,128)(2,1)} %get-tuple-element.549.refs_1_, ...), custom_call_target="tpu_custom_call", output_to_operand_aliasing={{4}: (8, {})} | custom-call | tf_op jit(solution)/shard_map/attn_wgrad/pallas_call | solution.py:74
  467.9 6.0 collective-permute-done.51.refs_0_
  473.9 4.9 leave.3
  478.8 8.0 %collective-permute-done.56.refs_0_ = bf16[2,4,96,768]{3,2,1,0:T(8,128)(2,1)} collective-permute-done((bf16[2,4,96,768]{3,2,1,0:T(8,128)(2,1)}, bf16[2,4,96,768]{3,2,1,0:T(8,128)(2,1)}, u32[]{:S(2)}, u32[]{:S(2)}) %collective-permute-start.56) | collective-permute-done | bytes 1179680 | tf_op jit(solution)/shard_map/ppermute | solution.py:527
  496.0 6.1 collective-permute-done.66.refs_0_
  509.3 3.5 collective-permute-done.60.refs_0_
  512.9 4.7 collective-permute-done.61.refs_1_
  517.5 14.1 %collective-permute-done.62.refs_2_ = bf16[192,768]{1,0:T(8,128)(2,1)S(1)} collective-permute-done((bf16[192,768]{1,0:T(8,128)(2,1)}, bf16[192,768]{1,0:T(8,128)(2,1)S(1)}, u32[]{:S(2)}, u32[]{:S(2)}) %collective-permute-start.62) | collective-permute-done | bytes 294944 | tf_op jit(solution)/shard_map/ppermute | solution.py:527
  556.4 57.2 %all-reduce.3.cloned.1.call-done.refs_0_ = f32[536,256]{1,0:T(8,128)} async-done(((f32[536,256]{1,0:T(8,128)}), f32[536,256]{1,0:T(8,128)}) %all-reduce.3.cloned.1.call-update) | async-done | bytes 548880 | tf_op jit(solution)/shard_map/psum | solution.py:822
  624.5 5.7 collective-permute-done.68.refs_0_
  633.9 19.0 %collective-permute-done.70.refs_2_ = bf16[192,768]{1,0:T(8,128)(2,1)S(1)} collective-permute-done((bf16[192,768]{1,0:T(8,128)(2,1)S(1)}, bf16[192,768]{1,0:T(8,128)(2,1)S(1)}, u32[]{:S(2)}, u32[]{:S(2)}) %collective-permute-start.70) | collective-permute-done | bytes 294944 | tf_op jit(solution)/shard_map/ppermute | solution.py:527
  655.2 4.1 collective-permute-done.81.refs_2_
  664.6 2.9 collective-permute-done.82.refs_0_
  675.9 5.4 collective-permute-done.84.refs_0_
  685.6 3.9 collective-permute-start.86
  720.1 11.6 %rev.4 = f32[2,1024,256]{2,1,0:T(8,128)} reverse(f32[2,1024,256]{2,1,0:T(8,128)S(1)} %bitcast.483), dimensions={2} | reverse | bytes 4194304 | tf_op jit(solution)/shard_map/rev | solution.py:886
  (691 shorter events, 280.3 us)
Async XLA Ops:
  7.2 606.4 %all-reduce.3.cloned.1.call-start = ((), (), s32[]{:S(2)}) async-start(), calls=%async_computation | async-start | bytes 1097728 | tf_op jit(solution)/shard_map/psum | solution.py:822
  10.4 17.0 %collective-permute-start.4 = (bf16[96,768]{1,0:T(8,128)(2,1)}, bf16[96,768]{1,0:T(8,128)(2,1)S(1)}, u32[]{:S(2)}, u32[]{:S(2)}) collective-permute-start(bf16[96,768]{1,0:T(8,128)(2,1)} %get-tuple-element.350), channel_id=1, source_target_pairs={{0,1},{1,0},{2,3},{3,2},{4,5},{5,4},{6,7},{7,6},{8,9},{9,8},{10,11... | collective-permute-start | bytes 442376 | tf_op jit(solution)/shard_map/ppermute | solution.py:527
  10.4 17.4 %collective-permute-start.5 = (bf16[96,768]{1,0:T(8,128)(2,1)}, bf16[96,768]{1,0:T(8,128)(2,1)S(1)}, u32[]{:S(2)}, u32[]{:S(2)}) collective-permute-start(bf16[96,768]{1,0:T(8,128)(2,1)} %get-tuple-element.350), channel_id=1, source_target_pairs={{0,2},{1,3},{2,0},{3,1},{4,6},{5,7},{6,4},{7,5},{8,10},{9,11},{10,... | collective-permute-start | bytes 442376 | tf_op jit(solution)/shard_map/ppermute | solution.py:527
  12.9 14.9 %collective-permute-start.6 = (bf16[96,768]{1,0:T(8,128)(2,1)}, bf16[96,768]{1,0:T(8,128)(2,1)S(1)}, u32[]{:S(2)}, u32[]{:S(2)}) collective-permute-start(bf16[96,768]{1,0:T(8,128)(2,1)} %get-tuple-element.350), channel_id=1, source_target_pairs={{0,3},{1,2},{2,1},{3,0},{4,7},{5,6},{6,5},{7,4},{8,11},{9,10},{10,... | collective-permute-start | bytes 442376 | tf_op jit(solution)/shard_map/ppermute | solution.py:527
  17.4 27.4 %collective-permute-start.1 = (bf16[192,768]{1,0:T(8,128)(2,1)}, bf16[192,768]{1,0:T(8,128)(2,1)S(1)}, u32[]{:S(2)}, u32[]{:S(2)}) collective-permute-start(bf16[192,768]{1,0:T(8,128)(2,1)} %get-tuple-element.349), channel_id=1, source_target_pairs={{0,1},{1,0},{2,3},{3,2},{4,5},{5,4},{6,7},{7,6},{8,9},{9,8},{10,11... | collective-permute-start | bytes 884744 | tf_op jit(solution)/shard_map/ppermute | solution.py:527
  18.5 26.3 %collective-permute-start.2 = (bf16[192,768]{1,0:T(8,128)(2,1)}, bf16[192,768]{1,0:T(8,128)(2,1)S(1)}, u32[]{:S(2)}, u32[]{:S(2)}) collective-permute-start(bf16[192,768]{1,0:T(8,128)(2,1)} %get-tuple-element.349), channel_id=1, source_target_pairs={{0,2},{1,3},{2,0},{3,1},{4,6},{5,7},{6,4},{7,5},{8,10},{9,11},{10,... | collective-permute-start | bytes 884744 | tf_op jit(solution)/shard_map/ppermute | solution.py:527
  27.5 23.6 %collective-permute-start.3 = (bf16[192,768]{1,0:T(8,128)(2,1)S(1)}, bf16[192,768]{1,0:T(8,128)(2,1)S(1)}, u32[]{:S(2)}, u32[]{:S(2)}) collective-permute-start(bf16[192,768]{1,0:T(8,128)(2,1)S(1)} %copy-done.55), channel_id=1, source_target_pairs={{0,3},{1,2},{2,1},{3,0},{4,7},{5,6},{6,5},{7,4},{8,11},{9,10},{10,... | collective-permute-start | bytes 884744 | tf_op jit(solution)/shard_map/ppermute | solution.py:527
  74.4 14.8 %collective-permute-start.10 = (bf16[4,96,768]{2,1,0:T(8,128)(2,1)}, bf16[4,96,768]{2,1,0:T(8,128)(2,1)}, u32[]{:S(2)}, u32[]{:S(2)}) collective-permute-start(bf16[4,96,768]{2,1,0:T(8,128)(2,1)} %get-tuple-element.370), channel_id=1, source_target_pairs={{0,16},{4,20},{8,24},{12,28},{16,0},{20,4},{24,8},{28,12},{1,17},{... | collective-permute-start | bytes 1769480 | tf_op jit(solution)/shard_map/ppermute | solution.py:527
  74.6 14.6 %collective-permute-start.9 = (bf16[4,96,768]{2,1,0:T(8,128)(2,1)}, bf16[4,96,768]{2,1,0:T(8,128)(2,1)}, u32[]{:S(2)}, u32[]{:S(2)}) collective-permute-start(bf16[4,96,768]{2,1,0:T(8,128)(2,1)} %get-tuple-element.369), channel_id=1, source_target_pairs={{0,8},{4,12},{8,0},{12,4},{16,24},{20,28},{24,16},{28,20},{1,9},{5... | collective-permute-start | bytes 1769480 | tf_op jit(solution)/shard_map/ppermute | solution.py:527
  75.9 27.4 %collective-permute-start = (bf16[512,768]{1,0:T(8,128)(2,1)S(1)}, bf16[512,768]{1,0:T(8,128)(2,1)}, u32[]{:S(2)}, u32[]{:S(2)}) collective-permute-start(bf16[512,768]{1,0:T(8,128)(2,1)S(1)} %copy-done.19), channel_id=1, source_target_pairs={{0,1},{1,2},{2,3},{4,5},{5,6},{6,7},{8,9},{9,10},{10,11},{12,13},{... | collective-permute-start | bytes 2359304 | tf_op jit(solution)/shard_map/ppermute | solution.py:704
  93.7 29.5 %collective-permute-start.15 = (bf16[2,4,96,768]{3,2,1,0:T(8,128)(2,1)}, bf16[2,4,96,768]{3,2,1,0:T(8,128)(2,1)S(1)}, u32[]{:S(2)}, u32[]{:S(2)}) collective-permute-start(bf16[2,4,96,768]{3,2,1,0:T(8,128)(2,1)} %get-tuple-element.391), channel_id=1, source_target_pairs={{0,16},{4,20},{8,24},{12,28},{16,0},{20,4},{24,8},{28,12},{1,17},{... | collective-permute-start | bytes 3538952 | tf_op jit(solution)/shard_map/ppermute | solution.py:527
  94.8 28.4 %collective-permute-start.16 = (bf16[2,4,96,768]{3,2,1,0:T(8,128)(2,1)}, bf16[2,4,96,768]{3,2,1,0:T(8,128)(2,1)S(1)}, u32[]{:S(2)}, u32[]{:S(2)}) collective-permute-start(bf16[2,4,96,768]{3,2,1,0:T(8,128)(2,1)} %get-tuple-element.392), channel_id=1, source_target_pairs={{0,8},{4,12},{8,0},{12,4},{16,24},{20,28},{24,16},{28,20},{1,9},{5... | collective-permute-start | bytes 3538952 | tf_op jit(solution)/shard_map/ppermute | solution.py:527
  100.6 17.5 %collective-permute-start.17 = (bf16[96,768]{1,0:T(8,128)(2,1)S(1)}, bf16[96,768]{1,0:T(8,128)(2,1)S(1)}, u32[]{:S(2)}, u32[]{:S(2)}) collective-permute-start(bf16[96,768]{1,0:T(8,128)(2,1)S(1)} %copy-done.85), channel_id=1, source_target_pairs={{0,1},{1,0},{2,3},{3,2},{4,5},{5,4},{6,7},{7,6},{8,9},{9,8},{10,11... | collective-permute-start | bytes 442376 | tf_op jit(solution)/shard_map/ppermute | solution.py:527
  100.6 17.5 %collective-permute-start.18 = (bf16[96,768]{1,0:T(8,128)(2,1)S(1)}, bf16[96,768]{1,0:T(8,128)(2,1)}, u32[]{:S(2)}, u32[]{:S(2)}) collective-permute-start(bf16[96,768]{1,0:T(8,128)(2,1)S(1)} %copy-done.85), channel_id=1, source_target_pairs={{0,2},{1,3},{2,0},{3,1},{4,6},{5,7},{6,4},{7,5},{8,10},{9,11},{10,... | collective-permute-start | bytes 442376 | tf_op jit(solution)/shard_map/ppermute | solution.py:527
  103.2 14.9 %collective-permute-start.19 = (bf16[96,768]{1,0:T(8,128)(2,1)S(1)}, bf16[96,768]{1,0:T(8,128)(2,1)S(1)}, u32[]{:S(2)}, u32[]{:S(2)}) collective-permute-start(bf16[96,768]{1,0:T(8,128)(2,1)S(1)} %copy-done.85), channel_id=1, source_target_pairs={{0,3},{1,2},{2,1},{3,0},{4,7},{5,6},{6,5},{7,4},{8,11},{9,10},{10,... | collective-permute-start | bytes 442376 | tf_op jit(solution)/shard_map/ppermute | solution.py:527
  133.5 27.5 %collective-permute-start.25 = (bf16[192,768]{1,0:T(8,128)(2,1)S(1)}, bf16[192,768]{1,0:T(8,128)(2,1)S(1)}, u32[]{:S(2)}, u32[]{:S(2)}) collective-permute-start(bf16[192,768]{1,0:T(8,128)(2,1)S(1)} %copy-done.54), channel_id=1, source_target_pairs={{0,1},{1,0},{2,3},{3,2},{4,5},{5,4},{6,7},{7,6},{8,9},{9,8},{10,11... | collective-permute-start | bytes 884744 | tf_op jit(solution)/shard_map/ppermute | solution.py:527
  139.9 21.1 %collective-permute-start.26 = (bf16[192,768]{1,0:T(8,128)(2,1)S(1)}, bf16[192,768]{1,0:T(8,128)(2,1)}, u32[]{:S(2)}, u32[]{:S(2)}) collective-permute-start(bf16[192,768]{1,0:T(8,128)(2,1)S(1)} %copy-done.54), channel_id=1, source_target_pairs={{0,2},{1,3},{2,0},{3,1},{4,6},{5,7},{6,4},{7,5},{8,10},{9,11},{10,... | collective-permute-start | bytes 884744 | tf_op jit(solution)/shard_map/ppermute | solution.py:527
  141.7 26.4 %collective-permute-start.27 = (bf16[192,768]{1,0:T(8,128)(2,1)S(1)}, bf16[192,768]{1,0:T(8,128)(2,1)}, u32[]{:S(2)}, u32[]{:S(2)}) collective-permute-start(bf16[192,768]{1,0:T(8,128)(2,1)S(1)} %copy-done.54), channel_id=1, source_target_pairs={{0,3},{1,2},{2,1},{3,0},{4,7},{5,6},{6,5},{7,4},{8,11},{9,10},{10,... | collective-permute-start | bytes 884744 | tf_op jit(solution)/shard_map/ppermute | solution.py:527
  169.2 14.0 %collective-permute-start.30 = (bf16[2,4,48,768]{3,2,1,0:T(8,128)(2,1)S(1)}, bf16[2,4,48,768]{3,2,1,0:T(8,128)(2,1)S(1)}, u32[]{:S(2)}, u32[]{:S(2)}) collective-permute-start(bf16[2,4,48,768]{3,2,1,0:T(8,128)(2,1)S(1)} %copy-done.27), channel_id=1, source_target_pairs={{0,16},{4,20},{8,24},{12,28},{16,0},{20,4},{24,8},{28,12},{1,17},{... | collective-permute-start | bytes 1769480 | tf_op jit(solution)/shard_map/ppermute | solution.py:527
  207.9 35.6 %collective-permute-start.34 = (bf16[2,4,96,768]{3,2,1,0:T(8,128)(2,1)}, bf16[2,4,96,768]{3,2,1,0:T(8,128)(2,1)S(1)}, u32[]{:S(2)}, u32[]{:S(2)}) collective-permute-start(bf16[2,4,96,768]{3,2,1,0:T(8,128)(2,1)} %get-tuple-element.447), channel_id=1, source_target_pairs={{0,16},{4,20},{8,24},{12,28},{16,0},{20,4},{24,8},{28,12},{1,17},{... | collective-permute-start | bytes 3538952 | tf_op jit(solution)/shard_map/ppermute | solution.py:527
  209.1 34.4 %collective-permute-start.35 = (bf16[2,4,96,768]{3,2,1,0:T(8,128)(2,1)}, bf16[2,4,96,768]{3,2,1,0:T(8,128)(2,1)S(1)}, u32[]{:S(2)}, u32[]{:S(2)}) collective-permute-start(bf16[2,4,96,768]{3,2,1,0:T(8,128)(2,1)} %get-tuple-element.448), channel_id=1, source_target_pairs={{0,8},{4,12},{8,0},{12,4},{16,24},{20,28},{24,16},{28,20},{1,9},{5... | collective-permute-start | bytes 3538952 | tf_op jit(solution)/shard_map/ppermute | solution.py:527
  210.3 18.3 %collective-permute-start.24 = (bf16[512,768]{1,0:T(8,128)(2,1)S(1)}, bf16[512,768]{1,0:T(8,128)(2,1)}, u32[]{:S(2)}, u32[]{:S(2)}) collective-permute-start(bf16[512,768]{1,0:T(8,128)(2,1)S(1)} %copy-done.18), channel_id=1, source_target_pairs={{0,1},{1,2},{2,3},{4,5},{5,6},{6,7},{8,9},{9,10},{10,11},{12,13},{... | collective-permute-start | bytes 2359304 | tf_op jit(solution)/shard_map/ppermute | solution.py:704
  332.3 27.5 %collective-permute-start.43 = (bf16[2,4,96,768]{3,2,1,0:T(8,128)(2,1)}, bf16[2,4,96,768]{3,2,1,0:T(8,128)(2,1)S(1)}, u32[]{:S(2)}, u32[]{:S(2)}) collective-permute-start(bf16[2,4,96,768]{3,2,1,0:T(8,128)(2,1)} %get-tuple-element.507), channel_id=1, source_target_pairs={{0,16},{4,20},{8,24},{12,28},{16,0},{20,4},{24,8},{28,12},{1,17},{... | collective-permute-start | bytes 3538952 | tf_op jit(solution)/shard_map/ppermute | solution.py:527
  332.6 27.3 %collective-permute-start.44 = (bf16[2,4,96,768]{3,2,1,0:T(8,128)(2,1)}, bf16[2,4,96,768]{3,2,1,0:T(8,128)(2,1)}, u32[]{:S(2)}, u32[]{:S(2)}) collective-permute-start(bf16[2,4,96,768]{3,2,1,0:T(8,128)(2,1)} %get-tuple-element.508), channel_id=1, source_target_pairs={{0,8},{4,12},{8,0},{12,4},{16,24},{20,28},{24,16},{28,20},{1,9},{5... | collective-permute-start | bytes 3538952 | tf_op jit(solution)/shard_map/ppermute | solution.py:527
  333.5 20.3 %collective-permute-start.40 = (bf16[512,768]{1,0:T(8,128)(2,1)}, bf16[512,768]{1,0:T(8,128)(2,1)}, u32[]{:S(2)}, u32[]{:S(2)}) collective-permute-start(bf16[512,768]{1,0:T(8,128)(2,1)} %get-tuple-element.483), channel_id=1, source_target_pairs={{1,0},{2,1},{3,2},{5,4},{6,5},{7,6},{9,8},{10,9},{11,10},{13,12},{... | collective-permute-start | bytes 2359304 | tf_op jit(solution)/shard_map/ppermute | solution.py:707
  385.5 22.4 %collective-permute-start.47 = (bf16[1536,768]{1,0:T(8,128)(2,1)}, bf16[1536,768]{1,0:T(8,128)(2,1)S(1)}, u32[]{:S(2)}, u32[]{:S(2)}) collective-permute-start(bf16[1536,768]{1,0:T(8,128)(2,1)} %get-tuple-element.528), channel_id=1, source_target_pairs={{0,4},{4,0},{8,12},{12,8},{16,20},{20,16},{24,28},{28,24},{1,5},{5... | collective-permute-start | bytes 7077896 | tf_op jit(solution)/shard_map/ppermute | solution.py:527
  386.7 21.3 %collective-permute-start.48 = (bf16[1536,768]{1,0:T(8,128)(2,1)}, bf16[1536,768]{1,0:T(8,128)(2,1)}, u32[]{:S(2)}, u32[]{:S(2)}) collective-permute-start(bf16[1536,768]{1,0:T(8,128)(2,1)} %get-tuple-element.529), channel_id=1, source_target_pairs={{0,4},{4,0},{8,12},{12,8},{16,20},{20,16},{24,28},{28,24},{1,5},{5... | collective-permute-start | bytes 7077896 | tf_op jit(solution)/shard_map/ppermute | solution.py:527
  386.8 14.8 %collective-permute-start.49 = (bf16[2,4,48,768]{3,2,1,0:T(8,128)(2,1)}, bf16[2,4,48,768]{3,2,1,0:T(8,128)(2,1)}, u32[]{:S(2)}, u32[]{:S(2)}) collective-permute-start(bf16[2,4,48,768]{3,2,1,0:T(8,128)(2,1)} %get-tuple-element.530), channel_id=1, source_target_pairs={{0,16},{4,20},{8,24},{12,28},{16,0},{20,4},{24,8},{28,12},{1,17},{... | collective-permute-start | bytes 1769480 | tf_op jit(solution)/shard_map/ppermute | solution.py:527
  387.3 14.8 %collective-permute-start.50 = (bf16[2,4,48,768]{3,2,1,0:T(8,128)(2,1)}, bf16[2,4,48,768]{3,2,1,0:T(8,128)(2,1)}, u32[]{:S(2)}, u32[]{:S(2)}) collective-permute-start(bf16[2,4,48,768]{3,2,1,0:T(8,128)(2,1)} %get-tuple-element.531), channel_id=1, source_target_pairs={{0,8},{4,12},{8,0},{12,4},{16,24},{20,28},{24,16},{28,20},{1,9},{5... | collective-permute-start | bytes 1769480 | tf_op jit(solution)/shard_map/ppermute | solution.py:527
  388.2 28.3 %collective-permute-start.45 = (bf16[4,96,768]{2,1,0:T(8,128)(2,1)}, bf16[4,96,768]{2,1,0:T(8,128)(2,1)}, u32[]{:S(2)}, u32[]{:S(2)}) collective-permute-start(bf16[4,96,768]{2,1,0:T(8,128)(2,1)} %get-tuple-element.522), channel_id=1, source_target_pairs={{0,8},{4,12},{8,0},{12,4},{16,24},{20,28},{24,16},{28,20},{1,9},{5... | collective-permute-start | bytes 1769480 | tf_op jit(solution)/shard_map/ppermute | solution.py:527
  401.6 14.9 %collective-permute-start.46 = (bf16[4,96,768]{2,1,0:T(8,128)(2,1)}, bf16[4,96,768]{2,1,0:T(8,128)(2,1)}, u32[]{:S(2)}, u32[]{:S(2)}) collective-permute-start(bf16[4,96,768]{2,1,0:T(8,128)(2,1)} %get-tuple-element.523), channel_id=1, source_target_pairs={{0,16},{4,20},{8,24},{12,28},{16,0},{20,4},{24,8},{28,12},{1,17},{... | collective-permute-start | bytes 1769480 | tf_op jit(solution)/shard_map/ppermute | solution.py:527
  453.7 20.2 %collective-permute-start.51 = (bf16[512,768]{1,0:T(8,128)(2,1)}, bf16[512,768]{1,0:T(8,128)(2,1)}, u32[]{:S(2)}, u32[]{:S(2)}) collective-permute-start(bf16[512,768]{1,0:T(8,128)(2,1)} %get-tuple-element.546), channel_id=1, source_target_pairs={{1,0},{2,1},{3,2},{5,4},{6,5},{7,6},{9,8},{10,9},{11,10},{13,12},{... | collective-permute-start | bytes 2359304 | tf_op jit(solution)/shard_map/ppermute | solution.py:707
  456.0 30.8 %collective-permute-start.56 = (bf16[2,4,96,768]{3,2,1,0:T(8,128)(2,1)}, bf16[2,4,96,768]{3,2,1,0:T(8,128)(2,1)}, u32[]{:S(2)}, u32[]{:S(2)}) collective-permute-start(bf16[2,4,96,768]{3,2,1,0:T(8,128)(2,1)} %get-tuple-element.577), channel_id=1, source_target_pairs={{0,16},{4,20},{8,24},{12,28},{16,0},{20,4},{24,8},{28,12},{1,17},{... | collective-permute-start | bytes 3538952 | tf_op jit(solution)/shard_map/ppermute | solution.py:527
  457.2 29.6 %collective-permute-start.57 = (bf16[2,4,96,768]{3,2,1,0:T(8,128)(2,1)}, bf16[2,4,96,768]{3,2,1,0:T(8,128)(2,1)}, u32[]{:S(2)}, u32[]{:S(2)}) collective-permute-start(bf16[2,4,96,768]{3,2,1,0:T(8,128)(2,1)} %get-tuple-element.578), channel_id=1, source_target_pairs={{0,8},{4,12},{8,0},{12,4},{16,24},{20,28},{24,16},{28,20},{1,9},{5... | collective-permute-start | bytes 3538952 | tf_op jit(solution)/shard_map/ppermute | solution.py:527
  490.9 14.3 %collective-permute-start.63 = (bf16[96,768]{1,0:T(8,128)(2,1)}, bf16[96,768]{1,0:T(8,128)(2,1)}, u32[]{:S(2)}, u32[]{:S(2)}) collective-permute-start(bf16[96,768]{1,0:T(8,128)(2,1)} %get-tuple-element.588), channel_id=1, source_target_pairs={{0,1},{1,0},{2,3},{3,2},{4,5},{5,4},{6,7},{7,6},{8,9},{9,8},{10,11... | collective-permute-start | bytes 442376 | tf_op jit(solution)/shard_map/ppermute | solution.py:527
  490.9 14.4 %collective-permute-start.64 = (bf16[96,768]{1,0:T(8,128)(2,1)}, bf16[96,768]{1,0:T(8,128)(2,1)}, u32[]{:S(2)}, u32[]{:S(2)}) collective-permute-start(bf16[96,768]{1,0:T(8,128)(2,1)} %get-tuple-element.589), channel_id=1, source_target_pairs={{0,2},{1,3},{2,0},{3,1},{4,6},{5,7},{6,4},{7,5},{8,10},{9,11},{10,... | collective-permute-start | bytes 442376 | tf_op jit(solution)/shard_map/ppermute | solution.py:527
  493.1 14.2 %collective-permute-start.65 = (bf16[96,768]{1,0:T(8,128)(2,1)}, bf16[96,768]{1,0:T(8,128)(2,1)}, u32[]{:S(2)}, u32[]{:S(2)}) collective-permute-start(bf16[96,768]{1,0:T(8,128)(2,1)} %get-tuple-element.590), channel_id=1, source_target_pairs={{0,3},{1,2},{2,1},{3,0},{4,7},{5,6},{6,5},{7,4},{8,11},{9,10},{10,... | collective-permute-start | bytes 442376 | tf_op jit(solution)/shard_map/ppermute | solution.py:527
  502.0 30.3 %collective-permute-start.58 = (bf16[4,96,768]{2,1,0:T(8,128)(2,1)}, bf16[4,96,768]{2,1,0:T(8,128)(2,1)}, u32[]{:S(2)}, u32[]{:S(2)}) collective-permute-start(bf16[4,96,768]{2,1,0:T(8,128)(2,1)} %get-tuple-element.583), channel_id=1, source_target_pairs={{0,8},{4,12},{8,0},{12,4},{16,24},{20,28},{24,16},{28,20},{1,9},{5... | collective-permute-start | bytes 1769480 | tf_op jit(solution)/shard_map/ppermute | solution.py:527
  502.6 29.8 %collective-permute-start.59 = (bf16[4,96,768]{2,1,0:T(8,128)(2,1)}, bf16[4,96,768]{2,1,0:T(8,128)(2,1)}, u32[]{:S(2)}, u32[]{:S(2)}) collective-permute-start(bf16[4,96,768]{2,1,0:T(8,128)(2,1)} %get-tuple-element.584), channel_id=1, source_target_pairs={{0,16},{4,20},{8,24},{12,28},{16,0},{20,4},{24,8},{28,12},{1,17},{... | collective-permute-start | bytes 1769480 | tf_op jit(solution)/shard_map/ppermute | solution.py:527
  507.3 24.3 %collective-permute-start.62 = (bf16[192,768]{1,0:T(8,128)(2,1)}, bf16[192,768]{1,0:T(8,128)(2,1)S(1)}, u32[]{:S(2)}, u32[]{:S(2)}) collective-permute-start(bf16[192,768]{1,0:T(8,128)(2,1)} %get-tuple-element.587), channel_id=1, source_target_pairs={{0,3},{1,2},{2,1},{3,0},{4,7},{5,6},{6,5},{7,4},{8,11},{9,10},{10,... | collective-permute-start | bytes 884744 | tf_op jit(solution)/shard_map/ppermute | solution.py:527
  553.8 59.7 %collective-permute-start.75 = (bf16[2,144,768]{2,1,0:T(8,128)(2,1)}, bf16[2,144,768]{2,1,0:T(8,128)(2,1)S(1)}, u32[]{:S(2)}, u32[]{:S(2)}) collective-permute-start(bf16[2,144,768]{2,1,0:T(8,128)(2,1)} %get-tuple-element.625), channel_id=1, source_target_pairs={{0,16},{4,20},{8,24},{12,28},{16,0},{20,4},{24,8},{28,12},{1,17},{... | collective-permute-start | bytes 1327112 | tf_op jit(solution)/shard_map/ppermute | solution.py:527
  554.2 59.3 %collective-permute-start.76 = (bf16[2,144,768]{2,1,0:T(8,128)(2,1)}, bf16[2,144,768]{2,1,0:T(8,128)(2,1)S(1)}, u32[]{:S(2)}, u32[]{:S(2)}) collective-permute-start(bf16[2,144,768]{2,1,0:T(8,128)(2,1)} %get-tuple-element.626), channel_id=1, source_target_pairs={{0,8},{4,12},{8,0},{12,4},{16,24},{20,28},{24,16},{28,20},{1,9},{5... | collective-permute-start | bytes 1327112 | tf_op jit(solution)/shard_map/ppermute | solution.py:527
  556.3 161.0 %all-gather.3.cloned.1.call-start = ((), (), s32[]{:S(2)}) async-start(), calls=%async_computation.1 | async-start | bytes 2744320 | tf_op jit(solution)/shard_map/all_gather | solution.py:842
  618.7 15.2 %collective-permute-start.69 = (bf16[192,768]{1,0:T(8,128)(2,1)S(1)}, bf16[192,768]{1,0:T(8,128)(2,1)S(1)}, u32[]{:S(2)}, u32[]{:S(2)}) collective-permute-start(bf16[192,768]{1,0:T(8,128)(2,1)S(1)} %copy-done.99), channel_id=1, source_target_pairs={{0,2},{1,3},{2,0},{3,1},{4,6},{5,7},{6,4},{7,5},{8,10},{9,11},{10,... | collective-permute-start | bytes 884744 | tf_op jit(solution)/shard_map/ppermute | solution.py:527
  620.9 32.0 %collective-permute-start.70 = (bf16[192,768]{1,0:T(8,128)(2,1)S(1)}, bf16[192,768]{1,0:T(8,128)(2,1)S(1)}, u32[]{:S(2)}, u32[]{:S(2)}) collective-permute-start(bf16[192,768]{1,0:T(8,128)(2,1)S(1)} %copy-done.98), channel_id=1, source_target_pairs={{0,3},{1,2},{2,1},{3,0},{4,7},{5,6},{6,5},{7,4},{8,11},{9,10},{10,... | collective-permute-start | bytes 884744 | tf_op jit(solution)/shard_map/ppermute | solution.py:527
  621.3 33.7 %collective-permute-start.79 = (bf16[96,768]{1,0:T(8,128)(2,1)}, bf16[96,768]{1,0:T(8,128)(2,1)}, u32[]{:S(2)}, u32[]{:S(2)}) collective-permute-start(bf16[96,768]{1,0:T(8,128)(2,1)} %get-tuple-element.649), channel_id=1, source_target_pairs={{0,1},{1,0},{2,3},{3,2},{4,5},{5,4},{6,7},{7,6},{8,9},{9,8},{10,11... | collective-permute-start | bytes 442376 | tf_op jit(solution)/shard_map/ppermute | solution.py:527
  622.5 32.7 %collective-permute-start.80 = (bf16[96,768]{1,0:T(8,128)(2,1)}, bf16[96,768]{1,0:T(8,128)(2,1)}, u32[]{:S(2)}, u32[]{:S(2)}) collective-permute-start(bf16[96,768]{1,0:T(8,128)(2,1)} %get-tuple-element.650), channel_id=1, source_target_pairs={{0,2},{1,3},{2,0},{3,1},{4,6},{5,7},{6,4},{7,5},{8,10},{9,11},{10,... | collective-permute-start | bytes 442376 | tf_op jit(solution)/shard_map/ppermute | solution.py:527
  630.3 29.0 %collective-permute-start.81 = (bf16[96,768]{1,0:T(8,128)(2,1)}, bf16[96,768]{1,0:T(8,128)(2,1)S(1)}, u32[]{:S(2)}, u32[]{:S(2)}) collective-permute-start(bf16[96,768]{1,0:T(8,128)(2,1)} %get-tuple-element.651), channel_id=1, source_target_pairs={{0,3},{1,2},{2,1},{3,0},{4,7},{5,6},{6,5},{7,4},{8,11},{9,10},{10,... | collective-permute-start | bytes 442376 | tf_op jit(solution)/shard_map/ppermute | solution.py:527
  (189 other events, 1036.8 us)
Sparse Core Ops, SparseCore 0:
  556.5 57.0 all-reduce.2
  664.7 46.6 all-gather.2

commit v3 on v2

--- a/solution.py
+++ b/solution.py
@@ -114,7 +114,21 @@
     )(tokens, gain, shift)
 
 
-def attn_forward(order, top, x, normed, halo, weights, band_rev, seg_q, seg_k, gain, shift):
+def reverse_lanes(values):
+    count = values.shape[1]
+    flip = (
+        lax.broadcasted_iota(jnp.int32, (count, count), 0)
+        + lax.broadcasted_iota(jnp.int32, (count, count), 1)
+        == count - 1
+    ).astype(BF)
+    high = values.astype(BF)
+    rest = values - high.astype(F32)
+    middle = rest.astype(BF)
+    last = (rest - middle.astype(F32)).astype(BF)
+    return (dot_nn(high, flip) + dot_nn(middle, flip)) + dot_nn(last, flip)
+
+
+def attn_forward(order, layer, place, x, normed, halo, weights, pos_bias, seg_q, seg_k, gain, shift):
     rows, width = x.shape
     seqs, block, _ = seg_q.shape
     keys = seg_k.shape[2]
@@ -122,16 +136,14 @@
     quarter = weights[0].shape[1]
     half = 2 * quarter
 
-    def body(top_ref, x_ref, n_ref, h_ref, oa, ob, ta, tb, band_ref, sq_ref, sk_ref, g_ref, s_ref,
-             sg_ref, ratio_ref, rden_ref, v_ref, kexp_ref, mixed_ref, masked_ref, x1_ref, nb_ref, both_ref, mix):
+    def body(place_ref, x_ref, n_ref, h_ref, oa, ob, ta, tb, band_ref, sq_ref, sk_ref, g_ref, s_ref,
+             sg_ref, ratio_ref, rden_ref, v_ref, wsum_ref, car_ref, mixed_ref, masked_ref, x1_ref, nb_ref, mix):
         step = pl.program_id(0)
 
         @pl.when(step == 0)
         def _():
-            for s in range(seqs):
-                both_ref[s * keys : s * keys + window] = h_ref[s * block : (s + 1) * block]
-                both_ref[s * keys + window : (s + 1) * keys] = n_ref[s * block : (s + 1) * block]
-            band = jnp.concatenate([jnp.exp(band_ref[...]), jnp.zeros((block, block), F32)], axis=1)
+            band = reverse_lanes(jnp.exp(band_ref[0]))
+            band = jnp.concatenate([band, jnp.zeros((block, block), F32)], axis=1)
             spread = pltpu.roll(band, 1, axis=1, stride=1, stride_axis=0)
             for s in range(seqs):
                 masked = jnp.where(sq_ref[s] == sk_ref[s], spread, 0.0)
@@ -141,27 +153,31 @@
 
         def part(wa, wb):
             def mat(m):
-                return jnp.concatenate([wa[top_ref[0] ^ m], wb[top_ref[0] ^ m]], axis=0)
-
-            both = both_ref[...]
-            q = dot_nt(n_ref[...], mat(0))
-            kexp = jnp.exp(dot_nt(both, mat(1)))
-            v = dot_nt(both, mat(2))
-            v_ref[...] = v
-            kexp_ref[...] = kexp
-            carried = (kexp * v).astype(BF)
-            wsum = kexp.astype(BF)
+                return jnp.concatenate([wa[place_ref[0] ^ m], wb[place_ref[0] ^ m]], axis=0)
+
+            wq, wk, wv = mat(0), mat(1), mat(2)
+            q = dot_nt(n_ref[...], wq)
             sg = jax.nn.sigmoid(q)
-            sg_ref[...] = sg
+            sg_ref[...] = sg.astype(BF)
+            carried, wsum = [], []
+            for r, source in enumerate((h_ref, n_ref)):
+                here = slice(r * rows, (r + 1) * rows)
+                kexp = jnp.exp(dot_nt(source[...], wk))
+                v = dot_nt(source[...], wv)
+                v_ref[here] = v.astype(BF)
+                wsum.append(kexp.astype(BF))
+                carried.append((kexp * v).astype(BF))
+                wsum_ref[here] = wsum[r]
+                car_ref[here] = carried[r]
             mixed = []
             for s in range(seqs):
-                num = dot_nn(mix[s], carried[s * keys : (s + 1) * keys])
-                den = dot_nn(mix[s], wsum[s * keys : (s + 1) * keys])
+                here = slice(s * block, (s + 1) * block)
+                num = dot_nn(mix[s, :, :window], carried[0][here]) + dot_nn(mix[s, :, window:], carried[1][here])
+                den = dot_nn(mix[s, :, :window], wsum[0][here]) + dot_nn(mix[s, :, window:], wsum[1][here])
                 rden = 1.0 / den
                 ratio = num * rden
-                here = slice(s * block, (s + 1) * block)
-                rden_ref[here] = rden
-                ratio_ref[here] = ratio
+                rden_ref[here] = rden.astype(BF)
+                ratio_ref[here] = ratio.astype(BF)
                 mixed.append((sg[here] * ratio).astype(BF))
             mixed = jnp.concatenate(mixed, axis=0)
             mixed_ref[...] = mixed
@@ -186,30 +202,29 @@
         (2,),
         [whole((rows, width))] * 3
         + [whole((4, quarter, width))] * 4
-        + [whole((block, window)), whole((seqs, block, 1)), whole((seqs, 1, keys)), whole((1, width)), whole((1, width))],
-        [col(rows)] * 3 + [col(seqs * keys)] * 2 + [col(rows)]
-        + [whole((seqs, block, keys)), whole((rows, width)), whole((rows, width)), whole((seqs * keys, width))],
-        [shape_of((rows, width), F32)] * 3
-        + [shape_of((seqs * keys, width), F32)] * 2
+        + [pl.BlockSpec((1, block, window), lambda i, place: (layer, place[1], 0))]
+        + [whole((seqs, block, 1)), whole((seqs, 1, keys)), whole((1, width)), whole((1, width))],
+        [col(rows)] * 3 + [col(2 * rows)] * 3 + [col(rows)]
+        + [whole((seqs, block, keys)), whole((rows, width)), whole((rows, width))],
+        [shape_of((rows, width), BF)] * 3
+        + [shape_of((2 * rows, width), BF)] * 3
         + [
             shape_of((rows, width), BF),
             shape_of((seqs, block, keys), F32),
             shape_of((rows, width), F32),
             shape_of((rows, width), BF),
-            shape_of((seqs * keys, width), BF),
         ],
         [pltpu.VMEM((seqs, block, keys), BF)],
         prefetch=1,
         name="attn_fwd",
-    )(top, x, normed, halo, *weights, band_rev, seg_q, seg_k, gain, shift)
+    )(place, x, normed, halo, *weights, pos_bias, seg_q, seg_k, gain, shift)
 
 
 def gelu_both(pre):
     square = pre * pre
-    th = jnp.tanh(GELU_A * pre * (1.0 + GELU_B * square))
-    upper = 0.5 * (1.0 + th)
-    slope = upper + 0.5 * GELU_A * pre * (1.0 - th * th) * (1.0 + 3.0 * GELU_B * square)
-    return pre * upper, slope
+    upper = 0.5 + 0.5 * jnp.tanh(pre * (GELU_A + (GELU_A * GELU_B) * square))
+    act = pre * upper
+    return act, upper + act * (1.0 - upper) * (2.0 * GELU_A + (6.0 * GELU_A * GELU_B) * square)
 
 
 def chunk_specs(chunk, width, per_half):
@@ -340,14 +355,14 @@
     )(x1, normed, *ups, *downs, grad, gain, *(() if fresh else saved))
 
 
-def attn_backward(order, top, grad_low, weights, sg, ratio, rden, v, kexp, masked):
+def attn_backward(order, place, grad_low, weights, sg, ratio, rden, v, wsum, carried, masked):
     rows, width = grad_low.shape
     seqs, block, keys = masked.shape
     window = keys - block
     quarter = weights[0].shape[1]
     half = 2 * quarter
 
-    def body(top_ref, ga_ref, oa, ob, ta, tb, sg_ref, ratio_ref, rden_ref, v_ref, kexp_ref, masked_ref,
+    def body(place_ref, ga_ref, oa, ob, ta, tb, sg_ref, ratio_ref, rden_ref, v_ref, wsum_ref, car_ref, masked_ref,
              gq_ref, gk_ref, gv_ref, band_ref, own_ref, halo_ref, mix_t, wgrad, dn):
         step = pl.program_id(0)
 
@@ -360,34 +375,33 @@
 
         def part(wa, wb):
             def mat(m):
-                return jnp.concatenate([wa[top_ref[0] ^ m], wb[top_ref[0] ^ m]], axis=0)
+                return jnp.concatenate([wa[place_ref[0] ^ m], wb[place_ref[0] ^ m]], axis=0)
 
             gm = dot_nt(ga_ref[...], mat(3))
-            sig = sg_ref[...]
-            rat = ratio_ref[...]
+            sig = sg_ref[...].astype(F32)
+            rat = ratio_ref[...].astype(F32)
             scaled = gm * sig
             gq = (scaled * rat * (1.0 - sig)).astype(BF)
             gq_ref[...] = gq
-            gnum_f = scaled * rden_ref[...]
+            gnum_f = scaled * rden_ref[...].astype(F32)
             gnum = gnum_f.astype(BF)
             gden = (-gnum_f * rat).astype(BF)
             wq, wk, wv = mat(0), mat(1), mat(2)
-            dq = dot_nn(gq, wq)
-            for s in range(seqs):
-                here = slice(s * block, (s + 1) * block)
-                there = slice(s * keys, (s + 1) * keys)
-                vv = v_ref[there]
-                ke = kexp_ref[there]
-                gcar = dot_nn(mix_t[s], gnum[here])
-                gsum = dot_nn(mix_t[s], gden[here])
-                gv = (gcar * ke).astype(BF)
-                gk = ((gcar * vv + gsum) * ke).astype(BF)
-                gk_ref[there] = gk
-                gv_ref[there] = gv
-                wgrad[s] += dot_nt(gnum[here], (ke * vv).astype(BF)) + dot_nt(gden[here], ke.astype(BF))
-                dkv = dot_nn(gk, wk) + dot_nn(gv, wv)
-                dn[s * keys : s * keys + window] += dkv[:window]
-                dn[s * keys + window : (s + 1) * keys] += dkv[window:] + dq[here]
+            dn[rows:] += dot_nn(gq, wq)
+            for r in range(2):
+                for s in range(seqs):
+                    here = slice(s * block, (s + 1) * block)
+                    there = slice(r * rows + s * block, r * rows + (s + 1) * block)
+                    cols = slice(r * window, r * window + block)
+                    ke = wsum_ref[there].astype(F32)
+                    gcar = dot_nn(mix_t[s, cols], gnum[here])
+                    gsum = dot_nn(mix_t[s, cols], gden[here])
+                    gv = (gcar * ke).astype(BF)
+                    gk = ((gcar * v_ref[there].astype(F32) + gsum) * ke).astype(BF)
+                    gk_ref[there] = gk
+                    gv_ref[there] = gv
+                    wgrad[s, :, cols] += dot_nt(gnum[here], car_ref[there]) + dot_nt(gden[here], wsum_ref[there])
+                    dn[there] += dot_nn(gk, wk) + dot_nn(gv, wv)
 
         @pl.when(step == 0)
         def _():
@@ -405,10 +419,9 @@
                 rolled = pltpu.roll(total, keys - bit, axis=1)
                 total = jnp.where((lane_row & bit) != 0, rolled, total)
                 bit *= 2
-            band_ref[...] = total[:, :window]
-            for s in range(seqs):
-                halo_ref[s * block : (s + 1) * block] = dn[s * keys : s * keys + window].astype(BF)
-                own_ref[s * block : (s + 1) * block] = dn[s * keys + window : (s + 1) * keys]
+            band_ref[...] = reverse_lanes(total[:, :window])
+            halo_ref[...] = dn[:rows].astype(BF)
+            own_ref[...] = dn[rows:]
 
     def col(n):
         return pl.BlockSpec((n, half), lambda i, *_: (0, i))
@@ -419,12 +432,12 @@
         (2,),
         [whole((rows, width))]
         + [whole((4, quarter, width))] * 4
-        + [col(rows)] * 3 + [col(seqs * keys)] * 2 + [whole((seqs, block, keys))],
-        [col(rows), col(seqs * keys), col(seqs * keys), whole((block, window)), whole((rows, width)), whole((rows, width))],
+        + [col(rows)] * 3 + [col(2 * rows)] * 3 + [whole((seqs, block, keys))],
+        [col(rows), col(2 * rows), col(2 * rows), whole((block, window)), whole((rows, width)), whole((rows, width))],
         [
             shape_of((rows, width), BF),
-            shape_of((seqs * keys, width), BF),
-            shape_of((seqs * keys, width), BF),
+            shape_of((2 * rows, width), BF),
+            shape_of((2 * rows, width), BF),
             shape_of((block, window), F32),
             shape_of((rows, width), F32),
             shape_of((rows, width), BF),
@@ -432,20 +445,19 @@
         [
             pltpu.VMEM((seqs, keys, block), BF),
             pltpu.VMEM((seqs, block, keys), F32),
-            pltpu.VMEM((seqs * keys, width), F32),
+            pltpu.VMEM((2 * rows, width), F32),
         ],
         prefetch=1,
         name="attn_bwd",
-    )(top, grad_low, *weights, sg, ratio, rden, v, kexp, masked)
-
-
-def attn_weight_grads(order, top, gq, gk, gv, mixed, normed, both, grad_low):
+    )(place, grad_low, *weights, sg, ratio, rden, v, wsum, carried, masked)
+
+
+def attn_weight_grads(order, place, gq, gk, gv, mixed, normed, halo, grad_low):
     rows, width = gq.shape
-    keyrows = both.shape[0]
     half = width // 2
     quarter = half // 2
 
-    def body(top_ref, gq_ref, gk_ref, gv_ref, mixed_ref, n_ref, b_ref, ga_ref, oa, ob, ta, tb):
+    def body(place_ref, gq_ref, gk_ref, gv_ref, mixed_ref, n_ref, h_ref, ga_ref, oa, ob, ta, tb):
         step = pl.program_id(0)
         mat = lax.rem(step, 4)
 
@@ -462,9 +474,12 @@
                 ta[0] = low[:quarter]
                 tb[0] = low[quarter:]
 
+        def keys_grad(ref):
+            return dot_tn(ref[:rows], h_ref[...]) + dot_tn(ref[rows:], n_ref[...])
+
         pl.when(mat == 0)(lambda: store(dot_tn(gq_ref[...], n_ref[...])))
-        pl.when(mat == 1)(lambda: store(dot_tn(gk_ref[...], b_ref[...])))
-        pl.when(mat == 2)(lambda: store(dot_tn(gv_ref[...], b_ref[...])))
+        pl.when(mat == 1)(lambda: store(keys_grad(gk_ref)))
+        pl.when(mat == 2)(lambda: store(keys_grad(gv_ref)))
         pl.when(mat == 3)(lambda: store(dot_tn(mixed_ref[...], ga_ref[...])))
 
     def col(n):
@@ -476,12 +491,12 @@
         order,
         body,
         (8,),
-        [col(rows), col(keyrows), col(keyrows), col(rows), whole((rows, width)), whole((keyrows, width)), whole((rows, width))],
+        [col(rows), col(2 * rows), col(2 * rows), col(rows)] + [whole((rows, width))] * 3,
         [own, own, other, other],
         [shape_of((4, quarter, width), BF)] * 4,
         prefetch=1,
         name="attn_wgrad",
-    )(top, gq, gk, gv, mixed, normed, both, grad_low)
+    )(place, gq, gk, gv, mixed, normed, halo, grad_low)
 
 
 def leave_attn(order, x, grad, own, back, gain):
@@ -503,6 +518,69 @@
         [shape_of((rows, width), F32)] + [shape_of((1, width), F32)] * 2,
         name="leave",
     )(x, grad, own, back, gain)
+
+
+def finish_layer(order, layer, layers, place, parts, channels, hidden, mp_rows, previous):
+    groups, count, width = parts[0].shape
+    piece = count * 2 // 3
+    small = piece // 2
+    total = 2 * groups * piece
+
+    def body(place_ref, oa, ob, ta, tb, *rest):
+        qkv_ref, out_ref, up_ref, down_ref, attn, up = rest[-6:]
+        for core, (pa, pb) in enumerate(((oa, ob), (ta, tb))):
+            for p in range(groups):
+                owner = 2 * (place_ref[2] ^ p) + (place_ref[3] ^ core)
+                start = pl.multiple_of(owner * piece, piece)
+                up[pl.ds(start, piece)] = pa[p, :piece].astype(F32)
+                down_ref[0, pl.ds(start, piece)] = pb[p, :piece].astype(F32)
+                attn[pl.ds(start, small)] = pa[p, piece:].astype(F32)
+                attn[pl.ds(pl.multiple_of(owner * piece + small, small), small)] = pb[p, piece:].astype(F32)
+        up_ref[0] = up[...].T
+        for m in range(3):
+            qkv_ref[0, m] = attn[m * channels : (m + 1) * channels].T
+        out_ref[0] = attn[3 * channels :]
+
+    shapes = [
+        (layers, 3, width, channels),
+        (layers, channels, width),
+        (layers, width, hidden),
+        (layers, hidden, width),
+    ]
+
+    def here(shape):
+        return pl.BlockSpec((1,) + shape[1:], lambda i, *_: (layer,) + (0,) * (len(shape) - 1))
+
+    first = len(parts) + 1
+    extra = list(previous) if previous is not None else []
+    order_in = first + len(extra)
+    anywhere = pl.BlockSpec(memory_space=pl.ANY)
+
+    def with_token(*refs):
+        ins = refs[: first + len(extra)]
+        outs = refs[order_in + 1 : order_in + 5]
+        return body(*ins[:first], *outs, *refs[order_in + 6 :])
+
+    aliases = {first + k: k for k in range(len(extra))}
+    aliases[order_in] = 4
+    *results, order.token = pl.pallas_call(
+        with_token,
+        grid_spec=pltpu.PrefetchScalarGridSpec(
+            num_scalar_prefetch=1,
+            grid=(1,),
+            in_specs=[whole(part.shape) for part in parts] + [anywhere] * (len(extra) + 1),
+            out_specs=[here(shape) for shape in shapes] + [anywhere],
+            scratch_shapes=[pltpu.VMEM((total, width), F32)] * 2,
+        ),
+        out_shape=[shape_of(shape, F32) for shape in shapes] + [shape_of(TOKEN, jnp.int32)],
+        input_output_aliases=aliases,
+        compiler_params=pltpu.CompilerParams(
+            dimension_semantics=("arbitrary",), vmem_limit_bytes=VMEM_LIMIT
+        ),
+        cost_estimate=pl.CostEstimate(flops=0, bytes_accessed=0, transcendentals=0),
+        name="finish",
+    )(place, *parts, *extra, order.token)
+    return results
 
 
 class Order:
@@ -665,7 +743,8 @@
         links = Links(order, dp, mp)
         attn_rows = 4 * channels // dp
         ff_rows = hidden // dp
-        top = (dp_index // 2 // (dp // 8)).astype(jnp.int32).reshape(1)
+        group = dp_index // 2
+        place = jnp.stack([group // (dp // 8), mp_index, group, dp_index % 2]).astype(jnp.int32)
 
         def picks(count, offset, length):
             return (
@@ -676,19 +755,17 @@
         attn_pick = picks(attn_rows, dp_index * attn_rows, 4 * channels)
         ff_pick = picks(ff_rows, dp_index * ff_rows, hidden)
 
-        def attn_gather(layer):
+        def attn_piece(layer):
             piece = jnp.einsum(
                 "rmc,mdc->rd",
                 attn_pick[:, : 3 * channels].reshape(attn_rows, 3, channels),
                 qkv_weight[layer],
                 preferred_element_type=F32,
             ) + dot_nn(attn_pick[:, 3 * channels :], out_weight[layer])
-            piece = piece.astype(BF)
-            return Gather(links, piece[: attn_rows // 2], piece[attn_rows // 2 :])
-
-        def ff_gather(layer):
-            return Gather(
-                links,
+            return piece.astype(BF)
+
+        def ff_pieces(layer):
+            return (
                 dot_nt(ff_pick, up_weight[layer]).astype(BF),
                 dot_nn(ff_pick, down_projection_weight[layer]).astype(BF),
             )
@@ -700,6 +777,12 @@
             flat = [part.reshape(-1, width) for part in parts]
             return (flat[0], flat[2]), (flat[1], flat[3])
 
+        def relative(gathered):
+            by_dp = jnp.take(gathered, jnp.bitwise_xor(jnp.arange(dp), dp_index), axis=0)
+            both = jnp.take(by_dp, jnp.bitwise_xor(jnp.arange(mp), mp_index), axis=1)
+            both = both.reshape((dp // 2, 2) + gathered.shape[1:])
+            return both[:, 0], both[:, 1]
+
         def forward_halo(value):
             return lax.ppermute(value, "mp", [(i, i + 1) for i in range(mp - 1)])
 
@@ -708,70 +791,63 @@
 
         gains = norm_gain.reshape(layers, 2, 1, width)
         shifts = norm_bias.reshape(layers, 2, 1, width)
-
-        attn0 = attn_gather(0)
+        middle = attn_rows // 2
+
+        piece = attn_piece(0)
+        attn0 = Gather(links, piece[:middle], piece[middle:])
         attn0.start_mp()
-        ff0 = ff_gather(0)
+        ff0 = Gather(links, *ff_pieces(0))
         ff0.start_mp()
         x, normed = enter_kernel(order, tokens.reshape(rows, width), gains[0, 0], shifts[0, 0])
         (normed,) = order.pin(normed)
         halo = forward_halo(normed)
-        attn0.wait_mp()
-        attn0.start()
-        attn1 = attn_gather(1)
-        attn1.start_mp()
-        ff1 = ff_gather(1)
-        ff1.start_mp()
+        (later,) = order.pin(jnp.concatenate((attn_piece(1),) + ff_pieces(1), axis=0))
+        later = lax.all_gather(later, ("dp", "mp"), axis=0, tiled=False)
 
         seg_pad = jnp.concatenate([jnp.full((seqs, window), -1, segments.dtype), segments], axis=1)
         seg_keys = lax.dynamic_slice_in_dim(seg_pad, mp_index * block, block + window, axis=1)
         seg_q = seg_keys[:, window:].reshape(seqs, block, 1)
         seg_k = seg_keys.reshape(seqs, 1, block + window)
-        band_rev = lax.dynamic_slice_in_dim(pos_bias, mp_index * block, block, axis=1)[:, :, ::-1]
-
+
+        attn0.wait_mp()
+        attn0.start()
+        ff0.wait_mp()
         attn0.wait()
         attn0.start()
-        ff0.wait_mp()
         ff0.start()
         attn0.wait_all()
         attn0.start_cores()
-        w_attn0 = attn_mats(attn0.wait_cores())
         ff0.wait()
         ff0.start()
+        w_attn0 = attn_mats(attn0.wait_cores())
         (halo,) = order.pin(halo)
 
         def attn(layer, x, normed, halo, w_attn):
-            sg, ratio, rden, v, kexp, mixed, masked, x1, normed_b, both = attn_forward(
-                order, top, x, normed, halo, w_attn, band_rev[layer], seg_q, seg_k,
+            sg, ratio, rden, v, wsum, carried, mixed, masked, x1, normed_b = attn_forward(
+                order, layer, place, x, normed, halo, w_attn, pos_bias, seg_q, seg_k,
                 gains[layer, 1], shifts[layer, 1],
             )
-            return x1, normed_b, (sg, ratio, rden, v, kexp, masked), (mixed, normed, both)
+            return x1, normed_b, (sg, ratio, rden, v, wsum, carried, masked), (mixed, normed, halo)
 
         x1_0, normed_b0, saved0, rows0 = attn(0, x, normed, halo, w_attn0)
-        attn1.wait_mp()
-        attn1.start()
         ff0.wait_all()
         ff0.start_cores()
         ups0, downs0 = ff_mats(ff0.wait_cores())
-        attn1.wait()
-        attn1.start()
         act0, slope0, x2, normed2 = ff_forward(
             order, x1_0, normed_b0, ups0, downs0, gains[1, 0], shifts[1, 0]
         )
         (normed2,) = order.pin(normed2)
         halo2 = forward_halo(normed2)
-        ff1.wait_mp()
-        ff1.start()
-        attn1.wait_all()
-        attn1.start_cores()
-        w_attn1 = attn_mats(attn1.wait_cores())
-        ff1.wait()
-        ff1.start()
+        (later,) = order.pin(later)
+        later = later.reshape((dp, mp) + later.shape[1:])
+        own, other = relative(later)
+        cuts = [middle, attn_rows, attn_rows + ff_rows]
+        own_a, own_b, own_up, own_down = jnp.split(own, cuts, axis=2)
+        other_a, other_b, other_up, other_down = jnp.split(other, cuts, axis=2)
+        w_attn1 = attn_mats([own_a, own_b, other_a, other_b])
+        ups1, downs1 = ff_mats([own_up, own_down, other_up, other_down])
         (halo2,) = order.pin(halo2)
         x1_1, normed_b1, saved1, rows1 = attn(1, x2, normed2, halo2, w_attn1)
-        ff1.wait_all()
-        ff1.start_cores()
-        ups1, downs1 = ff_mats(ff1.wait_cores())
 
         output, gu0, gu1, gd0, gd1, grad1, grad1_low, gain_b1, shift_b1 = ff_backward(
             order, x1_1, normed_b1, ups1, downs1, cotangent.reshape(rows, width), gains[1, 1], None
@@ -780,114 +856,154 @@
         r_ff1.start_cores()
         r_ff1.wait_cores()
         r_ff1.start()
-
-        def attn_back(grad_low, w_attn, saved, kept):
-            gq, gk, gv, band, dn_own, dn_halo = attn_backward(order, top, grad_low, w_attn, *saved)
-            (dn_halo,) = order.pin(dn_halo)
-            back = backward_halo(dn_halo)
-            halves = attn_weight_grads(order, top, gq, gk, gv, *kept, grad_low)
-            return band, dn_own, back, Reduce(links, halves)
-
-        band1, dn_own1, back1, r_attn1 = attn_back(grad1_low, w_attn1, saved1, rows1)
+        gq, gk, gv, band1, dn_own1, back1 = attn_backward(order, place, grad1_low, w_attn1, *saved1)
+        (back1,) = order.pin(back1)
+        back1 = backward_halo(back1)
+        r_attn1 = Reduce(links, attn_weight_grads(order, place, gq, gk, gv, *rows1, grad1_low))
+        r_ff1.wait()
+        r_ff1.start()
         r_attn1.start_cores()
+        (back1,) = order.pin(back1)
+        grad2, gain_a1, shift_a1 = leave_attn(order, x2, grad1, dn_own1, back1, gains[1, 0])
         r_attn1.wait_cores()
         r_attn1.start()
-        (back1,) = order.pin(back1)
-        grad2, gain_a1, shift_a1 = leave_attn(order, x2, grad1, dn_own1, back1, gains[1, 0])
-        r_ff1.wait()
-        r_ff1.start()
+        (band1,) = order.pin(band1)
+        band1 = lax.psum(band1, "dp")
+
         gu0, gu1, gd0, gd1, grad3, grad3_low, gain_b0, shift_b0 = ff_backward(
             order, x1_0, normed_b0, ups0, downs0, grad2, gains[0, 1], (act0, slope0)
         )
         r_ff0 = Reduce(links, [gu0, gd0, gu1, gd1])
         r_ff0.start_cores()
+        r_ff1.wait_all()
+        r_ff1.start_mp()
         r_attn1.wait()
         r_attn1.start()
         r_ff0.wait_cores()
         r_ff0.start()
-        r_ff1.wait_all()
-        band0, dn_own0, back0, r_attn0 = attn_back(grad3_low, w_attn0, saved0, rows0)
-        r_ff1.start_mp()
+        gq, gk, gv, band0, dn_own0, back0 = attn_backward(order, place, grad3_low, w_attn0, *saved0)
+        (back0,) = order.pin(back0)
+        back0 = backward_halo(back0)
+        r_attn1.wait_all()
+        r_attn1.start_mp()
+        r_attn0 = Reduce(links, attn_weight_grads(order, place, gq, gk, gv, *rows0, grad3_low))
         r_attn0.start_cores()
+        r_ff0.wait()
+        r_ff0.start()
         r_attn0.wait_cores()
         r_attn0.start()
-        r_attn1.wait_all()
-        r_attn1.start_mp()
         (back0,) = order.pin(back0)
         grad4, gain_a0, shift_a0 = leave_attn(order, x, grad3, dn_own0, back0, gains[0, 0])
         norms = jnp.concatenate(
             [gain_a0, gain_b0, shift_a0, shift_b0, gain_a1, gain_b1, shift_a1, shift_b1], axis=0
         ).reshape(-1, window)
-        packed = jnp.concatenate([band0, band1, norms], axis=0)
-        packed = lax.psum(packed, "dp")
-        r_ff0.wait()
-        r_ff0.start()
+        small = jnp.concatenate([band0, norms], axis=0)
+
+        class Small:
+            def __init__(self, value):
+                self.value = value
+                self.bit = 1
+
+            def start(self):
+                (self.value,) = order.pin(self.value)
+                self.coming = links.swap(self.value, "dp", self.bit)
+
+            def wait(self):
+                (coming,) = order.pin(self.coming)
+                self.value = self.value + coming
+                self.bit *= 2
+
+        def spread_of(attn_sum, ff_sum):
+            half = ff_sum.shape[0] // 2
+            return Spread(
+                links,
+                [
+                    jnp.concatenate([ff_sum[:half], attn_sum[:middle]], axis=0),
+                    jnp.concatenate([ff_sum[half:], attn_sum[middle:]], axis=0),
+                ],
+            )
+
+        small = Small(small)
+        small.start()
+        ff1_sum = r_ff1.wait_mp()
+        r_ff0.wait_all()
+        r_ff0.start_mp()
+        small.wait()
+        small.start()
+        attn1_sum = r_attn1.wait_mp()
+        back_1 = spread_of(attn1_sum, ff1_sum)
+        back_1.start()
         r_attn0.wait()
         r_attn0.start()
-
-        def halves_of(*pieces):
-            joined = jnp.concatenate(pieces, axis=0)
-            middle = joined.shape[0] // 2
-            return joined[:middle], joined[middle:]
-
-        back_1 = Spread(links, halves_of(r_attn1.wait_mp(), r_ff1.wait_mp()))
-        r_ff0.wait_all()
-        r_ff0.start_mp()
+        small.wait()
+        while small.bit < dp:
+            small.start()
+            small.wait()
+        (band1,) = order.pin(band1)
+        (low_small,) = order.pin(jnp.concatenate([small.value, band1], axis=0).astype(BF))
+        small_parts = [links.swap(low_small, "mp", p) for p in range(1, mp)]
+        back_1.wait()
         back_1.start()
         r_attn0.wait_all()
         r_attn0.start_mp()
-        back_1.wait()
-        back_1.start()
-        (packed,) = order.pin(packed)
-        packed = lax.all_gather(packed, "mp", axis=0, tiled=False)
         back_1.wait_all()
         back_1.start_cores()
+        ff0_sum = r_ff0.wait_mp()
         full_1 = back_1.wait_cores()
-        back_0 = Spread(links, halves_of(r_ff0.wait_mp(), r_attn0.wait_mp()))
+        attn0_sum = r_attn0.wait_mp()
+        back_0 = spread_of(attn0_sum, ff0_sum)
         back_0.start()
 
-        owner = jnp.bitwise_xor(jnp.arange(dp), dp_index)
-
-        def results(full, attn_first):
-            parts = [
-                jnp.concatenate(
-                    [half.reshape(dp // 2, 1, -1, width) for half in (full[k], full[2 + k])], axis=1
-                )
-                for k in range(2)
+        def finish(layer, full, previous):
+            full = [part.reshape(dp // 2, -1, width) for part in full]
+            if middle % 16 == 0:
+                return finish_layer(order, layer, layers, place, full, channels, hidden, attn_rows, previous)
+            owner = jnp.bitwise_xor(jnp.arange(dp), dp_index)
+            part_a, part_b = [
+                jnp.stack([full[k], full[2 + k]], axis=1).reshape(dp, -1, width) for k in range(2)
             ]
-            value = jnp.concatenate(parts, axis=2).reshape(dp, -1, width)
-            if attn_first:
-                attn_part, up_part, down_part = jnp.split(value, [attn_rows, attn_rows + ff_rows], axis=1)
-            else:
-                up_part, down_part, attn_part = jnp.split(value, [ff_rows, 2 * ff_rows], axis=1)
-
-            def places(count):
+
+            def rows_of(value):
+                return value.reshape(-1, width)
+
+            def place_of(count):
                 spots = (owner[:, None] * count + jnp.arange(count)[None, :]).reshape(-1, 1)
                 return (spots == jnp.arange(dp * count)[None, :]).astype(BF)
 
-            attn_place = places(attn_rows).reshape(-1, 4, channels)
-            ff_place = places(ff_rows)
-            attn_part = attn_part.reshape(-1, width)
-            return (
+            attn_part = rows_of(jnp.concatenate([part_a[:, ff_rows:], part_b[:, ff_rows:]], axis=1))
+            attn_place = place_of(attn_rows).reshape(-1, 4, channels)
+            ff_place = place_of(ff_rows)
+            values = (
                 jnp.einsum("pd,pmc->mdc", attn_part, attn_place[:, :3], preferred_element_type=F32),
                 dot_tn(attn_place[:, 3], attn_part),
-                dot_tn(up_part.reshape(-1, width), ff_place),
-                dot_tn(ff_place, down_part.reshape(-1, width)),
+                dot_tn(rows_of(part_a[:, :ff_rows]), ff_place),
+                dot_tn(ff_place, rows_of(part_b[:, :ff_rows])),
             )
-
-        out1 = results(full_1, True)
+            if previous is None:
+                previous = [jnp.zeros((layers,) + value.shape, F32) for value in values]
+            return [
+                lax.dynamic_update_index_in_dim(kept, value, layer, 0)
+                for kept, value in zip(previous, values)
+            ]
+
+        big = finish(1, full_1, None)
         back_0.wait()
         back_0.start()
+        small_parts = [low_small] + order.pin(*small_parts)
+        small_all = jnp.stack([part.astype(F32) for part in small_parts])
+        pairs = small_all[:, block:-block]
+        while pairs.shape[0] > 1:
+            pairs = pairs[0::2] + pairs[1::2]
+        norm_sum = pairs[0].reshape(layers, 4, width)
+        bands = jnp.stack([small_all[:, :block], small_all[:, -block:]])
+        band_sum = jnp.take(bands, jnp.bitwise_xor(jnp.arange(mp), mp_index), axis=1)
+        band_sum = band_sum.reshape(layers, mp * block, window)
         back_0.wait_all()
         back_0.start_cores()
-        out0 = results(back_0.wait_cores(), False)
-        big = tuple(jnp.stack([out0[k], out1[k]]) for k in range(4))
-        band_sum = jnp.transpose(packed[:, : layers * block].reshape(mp, layers, block, window), (1, 0, 2, 3))
-        band_sum = band_sum.reshape(layers, mp * block, window)[:, :, ::-1]
-        norm_sum = jnp.sum(packed[:, layers * block :], axis=0).reshape(layers, 4, width)
+        big = finish(0, back_0.wait_cores(), big)
         return (
             (output.reshape(tokens.shape), grad4.reshape(tokens.shape))
-            + big
+            + tuple(big)
             + (norm_sum[:, :2], norm_sum[:, 2:], band_sum)
         )
 

time: 746 us -> 761 us (1.020)
  local copies, waits for them, and re-layouts: 87.3 us -> 115 us
  waiting for transfers between devices: 255 us -> 237 us
  matrix products: 23.7 us -> 6.21 us
  Pallas kernels: 156 us -> 170 us
  starting transfers between devices: 88.6 us -> 97.4 us
    ppermute x84 -> x72, waiting for transfers between devices: 167 us -> 124 us  [swap(): return lax.ppermute(value, axis, [(i, i ^ bit) for i in range(size)])]
    gather x0 -> x6, local copies, waits for them, and re-layouts: none -> 36.4 us  [the longest x3 20.6 us: relative(): both = jnp.take(by_dp, jnp.bitwise_xor(jnp.arange(mp), mp_index), axis=1)]
    ppermute x2, waiting for transfers between devices: 17.4 us -> 47.2 us  [backward_halo(): return lax.ppermute(value, 'mp', [(i + 1, i) for i in range(mp - 1)])]
    another operation x24 -> x16, other arithmetic: 46.7 us -> 29.6 us  [wait(): self.values[k] = jnp.stack([self.values[k], coming[k]], axis=place)]
    pallas_call x0 -> x2, Pallas kernels: none -> 14.7 us  [finish_layer(): pl.pallas_call(with_token, grid_spec=pltpu.PrefetchScalarGridSpec(num_sca...]
    dot_general x10 -> x2, matrix products: 16.1 us -> 3.3 us  [attn_piece(): jnp.einsum('rmc,mdc->rd', attn_pick[:, :3 * channels].reshape(attn_rows,...]
    rev x1 -> x0, local copies, waits for them, and re-layouts: 11.6 us -> none  [shards(): band_sum = band_sum.reshape(layers, mp * block, window)[:, :, ::-1]]
    psum x1, waiting for transfers between devices: 57.2 us -> 46 us  [shards(): band1 = lax.psum(band1, 'dp')]
  transfers between devices with their start and end apart: 90 -> 78, of which waited for: 38 -> 25; matrix products, arithmetic and copies ran while one was open for 17% -> 22% of each run, Pallas kernels for 8% -> 16%
where the time goes in v3:
time: 761 us; the launch traced here: 754 us
  waiting for transfers between devices  237 us (31%)
  Pallas kernels  170 us (22%)
  local copies, waits for them, and re-layouts  115 us (15%)
  other arithmetic  113 us (15%)
  starting transfers between devices  97.4 us (13%)
  between operations  15.9 us (2%)
    pallas_call x12, Pallas kernels, run(): *results, order.token = kernel(*operands, order.token)  156 us
    ppermute x72, waiting for transfers between devices, swap(): return lax.ppermute(value, axis, [(i, i ^ bit) for i in range(size)])  124 us
    ppermute x72, starting transfers between devices, swap(): return lax.ppermute(value, axis, [(i, i ^ bit) for i in range(size)])  81.9 us
    ppermute x2, waiting for transfers between devices, backward_halo(): return lax.ppermute(value, 'mp', [(i + 1, i) for i in range(mp - 1)])  47.2 us
    psum x1, waiting for transfers between devices, shards(): band1 = lax.psum(band1, 'dp')  46 us
    unnamed x222, local copies, waits for them, and re-layouts  36.6 us
    another operation x16, other arithmetic, wait(): self.values[k] = jnp.stack([self.values[k], coming[k]], axis=place)  29.6 us
    gather x3, local copies, waits for them, and re-layouts, relative(): both = jnp.take(by_dp, jnp.bitwise_xor(jnp.arange(mp), mp_index), axis=1)  20.6 us
  transfers between devices with their start and end apart: 78, of which 25 were waited for; matrix products, arithmetic and copies ran while one was open for 22% of the time, Pallas kernels for 16%

profile of v3, /device:TPU:9, one launch (start us, length us, event | category | flops | bytes accessed | tf_op | source)
XLA Modules:
  0.0 754.0 jit_solution(8309536154247849052)
XLA Ops:
  15.6 2.7 enter.1
  28.2 9.5 %collective-permute-done.3.refs_2_ = bf16[96,768]{1,0:T(8,128)(2,1)S(1)} collective-permute-done((bf16[96,768]{1,0:T(8,128)(2,1)S(1)}, bf16[96,768]{1,0:T(8,128)(2,1)S(1)}, u32[]{:S(2)}, u32[]{:S(2)}) %collective-permute-start.3) | collective-permute-done | bytes 147488 | tf_op jit(solution)/shard_map/ppermute | solution.py:605
  45.1 17.1 %collective-permute-done.7.refs_1_ = bf16[192,768]{1,0:T(8,128)(2,1)S(1)} collective-permute-done((bf16[192,768]{1,0:T(8,128)(2,1)S(1)}, bf16[192,768]{1,0:T(8,128)(2,1)S(1)}, u32[]{:S(2)}, u32[]{:S(2)}) %collective-permute-start.7) | collective-permute-done | bytes 294944 | tf_op jit(solution)/shard_map/ppermute | solution.py:605
  62.2 9.4 %collective-permute-done.8.refs_2_ = bf16[192,768]{1,0:T(8,128)(2,1)S(1)} collective-permute-done((bf16[192,768]{1,0:T(8,128)(2,1)S(1)}, bf16[192,768]{1,0:T(8,128)(2,1)S(1)}, u32[]{:S(2)}, u32[]{:S(2)}) %collective-permute-start.8) | collective-permute-done | bytes 294944 | tf_op jit(solution)/shard_map/ppermute | solution.py:605
  83.7 4.5 collective-permute-done.10.refs_1_
  93.1 13.5 %collective-permute-start.11 = (bf16[2,2,4,48,768]{4,3,2,1,0:T(8,128)(2,1)}, bf16[2,2,4,48,768]{4,3,2,1,0:T(8,128)(2,1)S(1)}, u32[]{:S(2)}, u32[]{:S(2)}) collective-permute-start(bf16[2,2,4,48,768]{4,3,2,1,0:T(8,128)(2,1)} %get-tuple-element.360), channel_id=1, source_target_pairs={{0,4},{4,0},{8,12},{12,8},{16,20},{20,16},{24,28},{28,24},{1,5},{5... | collective-permute-start | bytes 3538952 | tf_op jit(solution)/shard_map/ppermute | solution.py:605
  112.2 6.0 collective-permute-start
  121.9 19.2 %collective-permute-done.refs_0_ = bf16[512,768]{1,0:T(8,128)(2,1)S(1)} collective-permute-done((bf16[512,768]{1,0:T(8,128)(2,1)}, bf16[512,768]{1,0:T(8,128)(2,1)S(1)}, u32[]{:S(2)}, u32[]{:S(2)}) %collective-permute-start) | collective-permute-done | bytes 786464 | tf_op jit(solution)/shard_map/ppermute | solution.py:787
  142.0 14.6 %attn_fwd.2 = (bf16[512,768]{1,0:T(8,128)(2,1)}, bf16[512,768]{1,0:T(8,128)(2,1)}, bf16[512,768]{1,0:T(8,128)(2,1)}, bf16[1024,768]{1,0:T(8,128)(2,1)}, bf16[102...) custom-call(s32[4]{0:T(128)} %pad_add_fusion.refs_0_, ...), custom_call_target="tpu_custom_call", output_to_operand_aliasing={{10}: (13, {})} | custom-call | tf_op jit(solution)/shard_map/attn_fwd/pallas_call | solution.py:74
  158.1 3.0 pad_maximum_fusion.2.refs_1_
  161.1 2.9 pad_maximum_fusion.1.refs_0_
  164.0 6.3 collective-permute-start.17
  170.4 7.6 %collective-permute-done.17.refs_0_ = bf16[2,2,4,96,768]{4,3,2,1,0:T(8,128)(2,1)S(1)} collective-permute-done((bf16[2,2,4,96,768]{4,3,2,1,0:T(8,128)(2,1)}, bf16[2,2,4,96,768]{4,3,2,1,0:T(8,128)(2,1)S(1)}, u32[]{:S(2)}, u32[]{:S(2)}) %collective-permute-start.17) | collective-permute-done | bytes 2359328 | tf_op jit(solution)/shard_map/ppermute | solution.py:605
  179.5 13.6 %ff_fwd.1 = (bf16[512,3072]{1,0:T(8,128)(2,1)}, bf16[512,3072]{1,0:T(8,128)(2,1)}, f32[512,768]{1,0:T(8,128)}, bf16[512,768]{1,0:T(8,128)(2,1)}, s32[8,128]{1,0:T(8,128)}) custom-call(f32[512,768]{1,0:T(8,128)} %get-tuple-element.374.refs_0_, bf16[512,768]{1,0:T(8,128)(2,1)} %get-tuple-element.375.refs_1_, ...), custom_call_target="tpu_custom_call", output_to_operand_aliasing={{4}: (8, {})} | custom-call | tf_op jit(solution)/shard_map/ff_fwd/pallas_call | solution.py:74
  193.1 4.1 collective-permute-start.19
  197.3 12.0 %gather_fusion = bf16[8,4,288,768]{3,2,1,0:T(8,128)(2,1)} fusion(bf16[8,4,288,768]{3,2,1,0:T(8,128)(2,1)} %bitcast.360, s32[1024]{0:T(1024)S(1)} %pad_clamp_fusion.1), kind=kCustom, calls=%fused_computation | custom fusion | bytes 28311584 | tf_op jit(solution)/shard_map/jit(_take)/gather | solution.py:781
  209.2 7.0 broadcast_select_fusion
  216.2 5.7 fusion.62
  221.9 7.5 gather_fusion.2
  229.4 7.4 gather_fusion.3
  236.8 7.2 pad_maximum_fusion
  258.2 14.6 %attn_fwd.3 = (bf16[512,768]{1,0:T(8,128)(2,1)}, bf16[512,768]{1,0:T(8,128)(2,1)}, bf16[512,768]{1,0:T(8,128)(2,1)}, bf16[1024,768]{1,0:T(8,128)(2,1)}, bf16[102...) custom-call(s32[4]{0:T(128)} %pad_add_fusion.refs_0_, ...), custom_call_target="tpu_custom_call", output_to_operand_aliasing={{10}: (13, {})} | custom-call | tf_op jit(solution)/shard_map/attn_fwd/pallas_call | solution.py:74
  272.8 25.4 %ff_bwd.2 = (bf16[512,768]{1,0:T(8,128)(2,1)}, bf16[1536,768]{1,0:T(8,128)(2,1)}, bf16[1536,768]{1,0:T(8,128)(2,1)}, bf16[1536,768]{1,0:T(8,128)(2,1)}, bf16[153...) custom-call(f32[512,768]{1,0:T(8,128)} %get-tuple-element.398.refs_0, ...), custom_call_target="tpu_custom_call", output_to_operand_aliasing={{9}: (8, {})} | custom-call | tf_op jit(solution)/shard_map/ff_bwd/pallas_call | solution.py:74
  299.0 6.9 collective-permute-done.20.refs_0_
  307.3 3.1 add_convert_fusion.2
  316.5 16.0 %attn_bwd.2 = (bf16[512,768]{1,0:T(8,128)(2,1)}, bf16[1024,768]{1,0:T(8,128)(2,1)}, bf16[1024,768]{1,0:T(8,128)(2,1)}, f32[256,256]{1,0:T(8,128)}, f32[512,768]{...) custom-call(s32[4]{0:T(128)} %pad_add_fusion.refs_0_, ...), custom_call_target="tpu_custom_call", output_to_operand_aliasing={{6}: (13, {})} | custom-call | tf_op jit(solution)/shard_map/attn_bwd/pallas_call | solution.py:74
  332.5 11.7 %attn_wgrad.2 = (bf16[4,192,768]{2,1,0:T(8,128)(2,1)}, bf16[4,192,768]{2,1,0:T(8,128)(2,1)}, bf16[4,192,768]{2,1,0:T(8,128)(2,1)}, bf16[4,192,768]{2,1,0:T(8,128)(2,1)}, s32[8,128]{1,0:T(8,128)}) custom-call(s32[4]{0:T(128)} %pad_add_fusion.refs_0_, bf16[512,768]{1,0:T(8,128)(2,1)} %get-tuple-element.427.refs_1_, ...), custom_call_target="tpu_custom_call", output_to_operand_aliasing={{4}: (8, {})} | custom-call | tf_op jit(solution)/shard_map/attn_wgrad/pallas_call | solution.py:74
  354.5 17.3 %collective-permute-done.22.refs_0_ = bf16[512,768]{1,0:T(8,128)(2,1)} collective-permute-done((bf16[512,768]{1,0:T(8,128)(2,1)}, bf16[512,768]{1,0:T(8,128)(2,1)}, u32[]{:S(2)}, u32[]{:S(2)}) %collective-permute-start.22) | collective-permute-done | bytes 786464 | tf_op jit(solution)/shard_map/ppermute | solution.py:790
  371.8 4.9 leave.2
  383.9 19.6 %ff_bwd.3 = (bf16[1536,768]{1,0:T(8,128)(2,1)}, bf16[1536,768]{1,0:T(8,128)(2,1)}, bf16[1536,768]{1,0:T(8,128)(2,1)}, bf16[1536,768]{1,0:T(8,128)(2,1)}, f32[512...) custom-call(f32[512,768]{1,0:T(8,128)} %get-tuple-element.374.refs_0, ...), custom_call_target="tpu_custom_call", output_to_operand_aliasing={{8}: (10, {})} | custom-call | tf_op jit(solution)/shard_map/ff_bwd/pallas_call | solution.py:74
  420.6 3.1 add_convert_fusion
  428.9 15.7 %attn_bwd.3 = (bf16[512,768]{1,0:T(8,128)(2,1)}, bf16[1024,768]{1,0:T(8,128)(2,1)}, bf16[1024,768]{1,0:T(8,128)(2,1)}, f32[256,256]{1,0:T(8,128)}, f32[512,768]{...) custom-call(s32[4]{0:T(128)} %pad_add_fusion.refs_0_, ...), custom_call_target="tpu_custom_call", output_to_operand_aliasing={{6}: (13, {})} | custom-call | tf_op jit(solution)/shard_map/attn_bwd/pallas_call | solution.py:74
  450.2 11.7 %attn_wgrad.3 = (bf16[4,192,768]{2,1,0:T(8,128)(2,1)}, bf16[4,192,768]{2,1,0:T(8,128)(2,1)}, bf16[4,192,768]{2,1,0:T(8,128)(2,1)}, bf16[4,192,768]{2,1,0:T(8,128)(2,1)}, s32[8,128]{1,0:T(8,128)}) custom-call(s32[4]{0:T(128)} %pad_add_fusion.refs_0_, bf16[512,768]{1,0:T(8,128)(2,1)} %get-tuple-element.495.refs_1_, ...), custom_call_target="tpu_custom_call", output_to_operand_aliasing={{4}: (8, {})} | custom-call | tf_op jit(solution)/shard_map/attn_wgrad/pallas_call | solution.py:74
  469.9 3.3 collective-permute-start.33
  478.8 29.9 %collective-permute-done.33.refs_0_ = bf16[512,768]{1,0:T(8,128)(2,1)} collective-permute-done((bf16[512,768]{1,0:T(8,128)(2,1)}, bf16[512,768]{1,0:T(8,128)(2,1)}, u32[]{:S(2)}, u32[]{:S(2)}) %collective-permute-start.33) | collective-permute-done | bytes 786464 | tf_op jit(solution)/shard_map/ppermute | solution.py:790
  508.8 4.9 leave.3
  524.6 5.5 collective-permute-done.40.refs_0_
  546.2 6.9 collective-permute-done.56.refs_1_
  560.0 3.1 collective-permute-done.54.refs_0_
  573.8 46.0 %all-reduce.3.cloned.1.call-done.refs_0_ = f32[256,256]{1,0:T(8,128)} async-done(((f32[256,256]{1,0:T(8,128)}), f32[256,256]{1,0:T(8,128)}) %all-reduce.3.cloned.1.call-update) | async-done | bytes 262160 | tf_op jit(solution)/shard_map/psum | solution.py:871
  632.8 6.7 collective-permute-done.58.refs_0_
  648.7 9.1 %collective-permute-done.45.refs_0_ = bf16[192,768]{1,0:T(8,128)(2,1)S(1)} collective-permute-done((bf16[192,768]{1,0:T(8,128)(2,1)S(1)}, bf16[192,768]{1,0:T(8,128)(2,1)S(1)}, u32[]{:S(2)}, u32[]{:S(2)}) %collective-permute-start.45) | collective-permute-done | bytes 294944 | tf_op jit(solution)/shard_map/ppermute | solution.py:605
  661.5 18.9 %collective-permute-done.47.refs_2_ = bf16[192,768]{1,0:T(8,128)(2,1)S(1)} collective-permute-done((bf16[192,768]{1,0:T(8,128)(2,1)S(1)}, bf16[192,768]{1,0:T(8,128)(2,1)S(1)}, u32[]{:S(2)}, u32[]{:S(2)}) %collective-permute-start.47) | collective-permute-done | bytes 294944 | tf_op jit(solution)/shard_map/ppermute | solution.py:605
  693.6 7.4 finish.2
  706.7 8.7 %collective-permute-done.73.refs_2_ = bf16[536,256]{1,0:T(8,128)(2,1)S(1)} collective-permute-done((bf16[536,256]{1,0:T(8,128)(2,1)S(1)}, bf16[536,256]{1,0:T(8,128)(2,1)S(1)}, u32[]{:S(2)}, u32[]{:S(2)}) %collective-permute-start.73) | collective-permute-done | bytes 274464 | tf_op jit(solution)/shard_map/ppermute | solution.py:605
  723.1 3.3 collective-permute-start.74
  733.8 7.3 finish.3
  741.1 5.6 copy.296
  (584 shorter events, 240.7 us)
Async XLA Ops:
  7.2 190.0 %all-gather.3.cloned.1.call-start = ((), (), s32[]{:S(2)}) async-start(), calls=%async_computation.1 | async-start | bytes 14598144 | tf_op jit(solution)/shard_map/all_gather | solution.py:805
  19.1 600.6 %all-reduce.3.cloned.1.call-start = ((), (), s32[]{:S(2)}) async-start(), calls=%async_computation | async-start | bytes 524288 | tf_op jit(solution)/shard_map/psum | solution.py:871
  21.7 15.9 %collective-permute-start.3 = (bf16[96,768]{1,0:T(8,128)(2,1)S(1)}, bf16[96,768]{1,0:T(8,128)(2,1)S(1)}, u32[]{:S(2)}, u32[]{:S(2)}) collective-permute-start(bf16[96,768]{1,0:T(8,128)(2,1)S(1)} %copy-done.62), channel_id=1, source_target_pairs={{0,3},{1,2},{2,1},{3,0},{4,7},{5,6},{6,5},{7,4},{8,11},{9,10},{10,... | collective-permute-start | bytes 442376 | tf_op jit(solution)/shard_map/ppermute | solution.py:605
  21.9 23.2 %collective-permute-start.6 = (bf16[192,768]{1,0:T(8,128)(2,1)S(1)}, bf16[192,768]{1,0:T(8,128)(2,1)S(1)}, u32[]{:S(2)}, u32[]{:S(2)}) collective-permute-start(bf16[192,768]{1,0:T(8,128)(2,1)S(1)} %copy-done.34), channel_id=1, source_target_pairs={{0,1},{1,0},{2,3},{3,2},{4,5},{5,4},{6,7},{7,6},{8,9},{9,8},{10,11... | collective-permute-start | bytes 884744 | tf_op jit(solution)/shard_map/ppermute | solution.py:605
  23.0 39.1 %collective-permute-start.7 = (bf16[192,768]{1,0:T(8,128)(2,1)S(1)}, bf16[192,768]{1,0:T(8,128)(2,1)S(1)}, u32[]{:S(2)}, u32[]{:S(2)}) collective-permute-start(bf16[192,768]{1,0:T(8,128)(2,1)S(1)} %copy-done.34), channel_id=1, source_target_pairs={{0,2},{1,3},{2,0},{3,1},{4,6},{5,7},{6,4},{7,5},{8,10},{9,11},{10,... | collective-permute-start | bytes 884744 | tf_op jit(solution)/shard_map/ppermute | solution.py:605
  25.2 46.4 %collective-permute-start.8 = (bf16[192,768]{1,0:T(8,128)(2,1)S(1)}, bf16[192,768]{1,0:T(8,128)(2,1)S(1)}, u32[]{:S(2)}, u32[]{:S(2)}) collective-permute-start(bf16[192,768]{1,0:T(8,128)(2,1)S(1)} %copy-done.34), channel_id=1, source_target_pairs={{0,3},{1,2},{2,1},{3,0},{4,7},{5,6},{6,5},{7,4},{8,11},{9,10},{10,... | collective-permute-start | bytes 884744 | tf_op jit(solution)/shard_map/ppermute | solution.py:605
  42.6 31.8 %collective-permute-start.4 = (bf16[4,48,768]{2,1,0:T(8,128)(2,1)}, bf16[4,48,768]{2,1,0:T(8,128)(2,1)S(1)}, u32[]{:S(2)}, u32[]{:S(2)}) collective-permute-start(bf16[4,48,768]{2,1,0:T(8,128)(2,1)} %get-tuple-element.342), channel_id=1, source_target_pairs={{0,8},{4,12},{8,0},{12,4},{16,24},{20,28},{24,16},{28,20},{1,9},{5... | collective-permute-start | bytes 884744 | tf_op jit(solution)/shard_map/ppermute | solution.py:605
  43.5 30.9 %collective-permute-start.5 = (bf16[4,48,768]{2,1,0:T(8,128)(2,1)}, bf16[4,48,768]{2,1,0:T(8,128)(2,1)S(1)}, u32[]{:S(2)}, u32[]{:S(2)}) collective-permute-start(bf16[4,48,768]{2,1,0:T(8,128)(2,1)} %get-tuple-element.343), channel_id=1, source_target_pairs={{0,16},{4,20},{8,24},{12,28},{16,0},{20,4},{24,8},{28,12},{1,17},{... | collective-permute-start | bytes 884744 | tf_op jit(solution)/shard_map/ppermute | solution.py:605
  83.0 23.7 %collective-permute-start.13 = (bf16[4,96,768]{2,1,0:T(8,128)(2,1)}, bf16[4,96,768]{2,1,0:T(8,128)(2,1)S(1)}, u32[]{:S(2)}, u32[]{:S(2)}) collective-permute-start(bf16[4,96,768]{2,1,0:T(8,128)(2,1)} %get-tuple-element.362), channel_id=1, source_target_pairs={{0,8},{4,12},{8,0},{12,4},{16,24},{20,28},{24,16},{28,20},{1,9},{5... | collective-permute-start | bytes 1769480 | tf_op jit(solution)/shard_map/ppermute | solution.py:605
  83.2 23.4 %collective-permute-start.14 = (bf16[4,96,768]{2,1,0:T(8,128)(2,1)}, bf16[4,96,768]{2,1,0:T(8,128)(2,1)}, u32[]{:S(2)}, u32[]{:S(2)}) collective-permute-start(bf16[4,96,768]{2,1,0:T(8,128)(2,1)} %get-tuple-element.363), channel_id=1, source_target_pairs={{0,16},{4,20},{8,24},{12,28},{16,0},{20,4},{24,8},{28,12},{1,17},{... | collective-permute-start | bytes 1769480 | tf_op jit(solution)/shard_map/ppermute | solution.py:605
  93.1 27.3 %collective-permute-start.11 = (bf16[2,2,4,48,768]{4,3,2,1,0:T(8,128)(2,1)}, bf16[2,2,4,48,768]{4,3,2,1,0:T(8,128)(2,1)S(1)}, u32[]{:S(2)}, u32[]{:S(2)}) collective-permute-start(bf16[2,2,4,48,768]{4,3,2,1,0:T(8,128)(2,1)} %get-tuple-element.360), channel_id=1, source_target_pairs={{0,4},{4,0},{8,12},{12,8},{16,20},{20,16},{24,28},{28,24},{1,5},{5... | collective-permute-start | bytes 3538952 | tf_op jit(solution)/shard_map/ppermute | solution.py:605
  110.9 45.6 %collective-permute-start.15 = (bf16[2,4,96,768]{3,2,1,0:T(8,128)(2,1)}, bf16[2,4,96,768]{3,2,1,0:T(8,128)(2,1)}, u32[]{:S(2)}, u32[]{:S(2)}) collective-permute-start(bf16[2,4,96,768]{3,2,1,0:T(8,128)(2,1)} %get-tuple-element.376), channel_id=1, source_target_pairs={{0,16},{4,20},{8,24},{12,28},{16,0},{20,4},{24,8},{28,12},{1,17},{... | collective-permute-start | bytes 3538952 | tf_op jit(solution)/shard_map/ppermute | solution.py:605
  112.2 44.4 %collective-permute-start.16 = (bf16[2,4,96,768]{3,2,1,0:T(8,128)(2,1)}, bf16[2,4,96,768]{3,2,1,0:T(8,128)(2,1)}, u32[]{:S(2)}, u32[]{:S(2)}) collective-permute-start(bf16[2,4,96,768]{3,2,1,0:T(8,128)(2,1)} %get-tuple-element.377), channel_id=1, source_target_pairs={{0,8},{4,12},{8,0},{12,4},{16,24},{20,28},{24,16},{28,20},{1,9},{5... | collective-permute-start | bytes 3538952 | tf_op jit(solution)/shard_map/ppermute | solution.py:605
  112.2 28.9 %collective-permute-start = (bf16[512,768]{1,0:T(8,128)(2,1)}, bf16[512,768]{1,0:T(8,128)(2,1)S(1)}, u32[]{:S(2)}, u32[]{:S(2)}) collective-permute-start(bf16[512,768]{1,0:T(8,128)(2,1)} %get-tuple-element.334.refs_2_.refs_5_), channel_id=1, source_target_pairs={{0,1},{1,2},{2,3},{4,5},{5,6},{6,7},{8,9},{9,10},{10,11},{12,13},{... | collective-permute-start | bytes 2359304 | tf_op jit(solution)/shard_map/ppermute | solution.py:787
  193.1 64.1 %collective-permute-start.19 = (bf16[512,768]{1,0:T(8,128)(2,1)}, bf16[512,768]{1,0:T(8,128)(2,1)S(1)}, u32[]{:S(2)}, u32[]{:S(2)}) collective-permute-start(bf16[512,768]{1,0:T(8,128)(2,1)} %get-tuple-element.391.refs_2_.refs_5_), channel_id=1, source_target_pairs={{0,1},{1,2},{2,3},{4,5},{5,6},{6,7},{8,9},{9,10},{10,11},{12,13},{... | collective-permute-start | bytes 2359304 | tf_op jit(solution)/shard_map/ppermute | solution.py:787
  314.7 29.5 %collective-permute-start.23 = (bf16[2,4,96,768]{3,2,1,0:T(8,128)(2,1)}, bf16[2,4,96,768]{3,2,1,0:T(8,128)(2,1)S(1)}, u32[]{:S(2)}, u32[]{:S(2)}) collective-permute-start(bf16[2,4,96,768]{3,2,1,0:T(8,128)(2,1)} %get-tuple-element.434), channel_id=1, source_target_pairs={{0,16},{4,20},{8,24},{12,28},{16,0},{20,4},{24,8},{28,12},{1,17},{... | collective-permute-start | bytes 3538952 | tf_op jit(solution)/shard_map/ppermute | solution.py:605
  314.8 29.5 %collective-permute-start.24 = (bf16[2,4,96,768]{3,2,1,0:T(8,128)(2,1)}, bf16[2,4,96,768]{3,2,1,0:T(8,128)(2,1)}, u32[]{:S(2)}, u32[]{:S(2)}) collective-permute-start(bf16[2,4,96,768]{3,2,1,0:T(8,128)(2,1)} %get-tuple-element.435), channel_id=1, source_target_pairs={{0,8},{4,12},{8,0},{12,4},{16,24},{20,28},{24,16},{28,20},{1,9},{5... | collective-permute-start | bytes 3538952 | tf_op jit(solution)/shard_map/ppermute | solution.py:605
  350.0 26.7 %collective-permute-start.25 = (bf16[4,192,768]{2,1,0:T(8,128)(2,1)}, bf16[4,192,768]{2,1,0:T(8,128)(2,1)S(1)}, u32[]{:S(2)}, u32[]{:S(2)}) collective-permute-start(bf16[4,192,768]{2,1,0:T(8,128)(2,1)} %get-tuple-element.449), channel_id=1, source_target_pairs={{0,4},{4,0},{8,12},{12,8},{16,20},{20,16},{24,28},{28,24},{1,5},{5... | collective-permute-start | bytes 3538952 | tf_op jit(solution)/shard_map/ppermute | solution.py:605
  351.0 25.7 %collective-permute-start.26 = (bf16[4,192,768]{2,1,0:T(8,128)(2,1)}, bf16[4,192,768]{2,1,0:T(8,128)(2,1)S(1)}, u32[]{:S(2)}, u32[]{:S(2)}) collective-permute-start(bf16[4,192,768]{2,1,0:T(8,128)(2,1)} %get-tuple-element.450), channel_id=1, source_target_pairs={{0,4},{4,0},{8,12},{12,8},{16,20},{20,16},{24,28},{28,24},{1,5},{5... | collective-permute-start | bytes 3538952 | tf_op jit(solution)/shard_map/ppermute | solution.py:605
  351.0 20.8 %collective-permute-start.22 = (bf16[512,768]{1,0:T(8,128)(2,1)}, bf16[512,768]{1,0:T(8,128)(2,1)}, u32[]{:S(2)}, u32[]{:S(2)}) collective-permute-start(bf16[512,768]{1,0:T(8,128)(2,1)} %get-tuple-element.426), channel_id=1, source_target_pairs={{1,0},{2,1},{3,2},{5,4},{6,5},{7,6},{9,8},{10,9},{11,10},{13,12},{... | collective-permute-start | bytes 2359304 | tf_op jit(solution)/shard_map/ppermute | solution.py:790
  353.1 52.3 %collective-permute-start.31 = (bf16[4,96,768]{2,1,0:T(8,128)(2,1)}, bf16[4,96,768]{2,1,0:T(8,128)(2,1)}, u32[]{:S(2)}, u32[]{:S(2)}) collective-permute-start(bf16[4,96,768]{2,1,0:T(8,128)(2,1)} %get-tuple-element.475), channel_id=1, source_target_pairs={{0,8},{4,12},{8,0},{12,4},{16,24},{20,28},{24,16},{28,20},{1,9},{5... | collective-permute-start | bytes 1769480 | tf_op jit(solution)/shard_map/ppermute | solution.py:605
  353.1 52.3 %collective-permute-start.32 = (bf16[4,96,768]{2,1,0:T(8,128)(2,1)}, bf16[4,96,768]{2,1,0:T(8,128)(2,1)}, u32[]{:S(2)}, u32[]{:S(2)}) collective-permute-start(bf16[4,96,768]{2,1,0:T(8,128)(2,1)} %get-tuple-element.476), channel_id=1, source_target_pairs={{0,16},{4,20},{8,24},{12,28},{16,0},{20,4},{24,8},{28,12},{1,17},{... | collective-permute-start | bytes 1769480 | tf_op jit(solution)/shard_map/ppermute | solution.py:605
  382.6 29.1 %collective-permute-start.29 = (bf16[2,4,48,768]{3,2,1,0:T(8,128)(2,1)}, bf16[2,4,48,768]{3,2,1,0:T(8,128)(2,1)}, u32[]{:S(2)}, u32[]{:S(2)}) collective-permute-start(bf16[2,4,48,768]{3,2,1,0:T(8,128)(2,1)} %get-tuple-element.473), channel_id=1, source_target_pairs={{0,16},{4,20},{8,24},{12,28},{16,0},{20,4},{24,8},{28,12},{1,17},{... | collective-permute-start | bytes 1769480 | tf_op jit(solution)/shard_map/ppermute | solution.py:605
  383.9 27.9 %collective-permute-start.30 = (bf16[2,4,48,768]{3,2,1,0:T(8,128)(2,1)}, bf16[2,4,48,768]{3,2,1,0:T(8,128)(2,1)}, u32[]{:S(2)}, u32[]{:S(2)}) collective-permute-start(bf16[2,4,48,768]{3,2,1,0:T(8,128)(2,1)} %get-tuple-element.474), channel_id=1, source_target_pairs={{0,8},{4,12},{8,0},{12,4},{16,24},{20,28},{24,16},{28,20},{1,9},{5... | collective-permute-start | bytes 1769480 | tf_op jit(solution)/shard_map/ppermute | solution.py:605
  403.5 15.6 %collective-permute-start.27 = (bf16[1536,768]{1,0:T(8,128)(2,1)}, bf16[1536,768]{1,0:T(8,128)(2,1)S(1)}, u32[]{:S(2)}, u32[]{:S(2)}) collective-permute-start(bf16[1536,768]{1,0:T(8,128)(2,1)} %get-tuple-element.471), channel_id=1, source_target_pairs={{0,4},{4,0},{8,12},{12,8},{16,20},{20,16},{24,28},{28,24},{1,5},{5... | collective-permute-start | bytes 7077896 | tf_op jit(solution)/shard_map/ppermute | solution.py:605
  417.4 27.2 %collective-permute-start.34 = (bf16[4,48,768]{2,1,0:T(8,128)(2,1)}, bf16[4,48,768]{2,1,0:T(8,128)(2,1)}, u32[]{:S(2)}, u32[]{:S(2)}) collective-permute-start(bf16[4,48,768]{2,1,0:T(8,128)(2,1)} %get-tuple-element.499), channel_id=1, source_target_pairs={{0,8},{4,12},{8,0},{12,4},{16,24},{20,28},{24,16},{28,20},{1,9},{5... | collective-permute-start | bytes 884744 | tf_op jit(solution)/shard_map/ppermute | solution.py:605
  418.9 25.7 %collective-permute-start.35 = (bf16[4,48,768]{2,1,0:T(8,128)(2,1)}, bf16[4,48,768]{2,1,0:T(8,128)(2,1)}, u32[]{:S(2)}, u32[]{:S(2)}) collective-permute-start(bf16[4,48,768]{2,1,0:T(8,128)(2,1)} %get-tuple-element.500), channel_id=1, source_target_pairs={{0,16},{4,20},{8,24},{12,28},{16,0},{20,4},{24,8},{28,12},{1,17},{... | collective-permute-start | bytes 884744 | tf_op jit(solution)/shard_map/ppermute | solution.py:605
  427.6 35.9 %collective-permute-start.38 = (bf16[2,4,96,768]{3,2,1,0:T(8,128)(2,1)}, bf16[2,4,96,768]{3,2,1,0:T(8,128)(2,1)S(1)}, u32[]{:S(2)}, u32[]{:S(2)}) collective-permute-start(bf16[2,4,96,768]{3,2,1,0:T(8,128)(2,1)} %get-tuple-element.512), channel_id=1, source_target_pairs={{0,16},{4,20},{8,24},{12,28},{16,0},{20,4},{24,8},{28,12},{1,17},{... | collective-permute-start | bytes 3538952 | tf_op jit(solution)/shard_map/ppermute | solution.py:605
  428.9 35.9 %collective-permute-start.39 = (bf16[2,4,96,768]{3,2,1,0:T(8,128)(2,1)}, bf16[2,4,96,768]{3,2,1,0:T(8,128)(2,1)}, u32[]{:S(2)}, u32[]{:S(2)}) collective-permute-start(bf16[2,4,96,768]{3,2,1,0:T(8,128)(2,1)} %get-tuple-element.513), channel_id=1, source_target_pairs={{0,8},{4,12},{8,0},{12,4},{16,24},{20,28},{24,16},{28,20},{1,9},{5... | collective-permute-start | bytes 3538952 | tf_op jit(solution)/shard_map/ppermute | solution.py:605
  463.5 56.4 %collective-permute-start.42 = (bf16[192,768]{1,0:T(8,128)(2,1)}, bf16[192,768]{1,0:T(8,128)(2,1)}, u32[]{:S(2)}, u32[]{:S(2)}) collective-permute-start(bf16[192,768]{1,0:T(8,128)(2,1)} %get-tuple-element.529), channel_id=1, source_target_pairs={{0,1},{1,0},{2,3},{3,2},{4,5},{5,4},{6,7},{7,6},{8,9},{9,8},{10,11... | collective-permute-start | bytes 884744 | tf_op jit(solution)/shard_map/ppermute | solution.py:605
  463.5 56.4 %collective-permute-start.43 = (bf16[192,768]{1,0:T(8,128)(2,1)}, bf16[192,768]{1,0:T(8,128)(2,1)}, u32[]{:S(2)}, u32[]{:S(2)}) collective-permute-start(bf16[192,768]{1,0:T(8,128)(2,1)} %get-tuple-element.530), channel_id=1, source_target_pairs={{0,2},{1,3},{2,0},{3,1},{4,6},{5,7},{6,4},{7,5},{8,10},{9,11},{10,... | collective-permute-start | bytes 884744 | tf_op jit(solution)/shard_map/ppermute | solution.py:605
  464.7 55.6 %collective-permute-start.44 = (bf16[192,768]{1,0:T(8,128)(2,1)}, bf16[192,768]{1,0:T(8,128)(2,1)}, u32[]{:S(2)}, u32[]{:S(2)}) collective-permute-start(bf16[192,768]{1,0:T(8,128)(2,1)} %get-tuple-element.531), channel_id=1, source_target_pairs={{0,3},{1,2},{2,1},{3,0},{4,7},{5,6},{6,5},{7,4},{8,11},{9,10},{10,... | collective-permute-start | bytes 884744 | tf_op jit(solution)/shard_map/ppermute | solution.py:605
  469.9 38.9 %collective-permute-start.33 = (bf16[512,768]{1,0:T(8,128)(2,1)}, bf16[512,768]{1,0:T(8,128)(2,1)}, u32[]{:S(2)}, u32[]{:S(2)}) collective-permute-start(bf16[512,768]{1,0:T(8,128)(2,1)} %get-tuple-element.494), channel_id=1, source_target_pairs={{1,0},{2,1},{3,2},{5,4},{6,5},{7,6},{9,8},{10,9},{11,10},{13,12},{... | collective-permute-start | bytes 2359304 | tf_op jit(solution)/shard_map/ppermute | solution.py:790
  519.8 22.3 %collective-permute-start.48 = (bf16[96,768]{1,0:T(8,128)(2,1)}, bf16[96,768]{1,0:T(8,128)(2,1)}, u32[]{:S(2)}, u32[]{:S(2)}) collective-permute-start(bf16[96,768]{1,0:T(8,128)(2,1)} %get-tuple-element.553), channel_id=1, source_target_pairs={{0,1},{1,0},{2,3},{3,2},{4,5},{5,4},{6,7},{7,6},{8,9},{9,8},{10,11... | collective-permute-start | bytes 442376 | tf_op jit(solution)/shard_map/ppermute | solution.py:605
  519.9 22.3 %collective-permute-start.49 = (bf16[96,768]{1,0:T(8,128)(2,1)}, bf16[96,768]{1,0:T(8,128)(2,1)}, u32[]{:S(2)}, u32[]{:S(2)}) collective-permute-start(bf16[96,768]{1,0:T(8,128)(2,1)} %get-tuple-element.554), channel_id=1, source_target_pairs={{0,2},{1,3},{2,0},{3,1},{4,6},{5,7},{6,4},{7,5},{8,10},{9,11},{10,... | collective-permute-start | bytes 442376 | tf_op jit(solution)/shard_map/ppermute | solution.py:605
  520.3 21.8 %collective-permute-start.50 = (bf16[96,768]{1,0:T(8,128)(2,1)}, bf16[96,768]{1,0:T(8,128)(2,1)}, u32[]{:S(2)}, u32[]{:S(2)}) collective-permute-start(bf16[96,768]{1,0:T(8,128)(2,1)} %get-tuple-element.555), channel_id=1, source_target_pairs={{0,3},{1,2},{2,1},{3,0},{4,7},{5,6},{6,5},{7,4},{8,11},{9,10},{10,... | collective-permute-start | bytes 442376 | tf_op jit(solution)/shard_map/ppermute | solution.py:605
  566.7 54.7 %collective-permute-start.52 = (bf16[144,768]{1,0:T(8,128)(2,1)S(1)}, bf16[144,768]{1,0:T(8,128)(2,1)S(1)}, u32[]{:S(2)}, u32[]{:S(2)}) collective-permute-start(bf16[144,768]{1,0:T(8,128)(2,1)S(1)} %copy-done.55), channel_id=1, source_target_pairs={{0,8},{4,12},{8,0},{12,4},{16,24},{20,28},{24,16},{28,20},{1,9},{5... | collective-permute-start | bytes 663560 | tf_op jit(solution)/shard_map/ppermute | solution.py:605
  568.3 53.2 %collective-permute-start.53 = (bf16[144,768]{1,0:T(8,128)(2,1)S(1)}, bf16[144,768]{1,0:T(8,128)(2,1)S(1)}, u32[]{:S(2)}, u32[]{:S(2)}) collective-permute-start(bf16[144,768]{1,0:T(8,128)(2,1)S(1)} %copy-done.53), channel_id=1, source_target_pairs={{0,16},{4,20},{8,24},{12,28},{16,0},{20,4},{24,8},{28,12},{1,17},{... | collective-permute-start | bytes 663560 | tf_op jit(solution)/shard_map/ppermute | solution.py:605
  568.5 57.2 %collective-permute-start.60 = (bf16[4,48,768]{2,1,0:T(8,128)(2,1)}, bf16[4,48,768]{2,1,0:T(8,128)(2,1)S(1)}, u32[]{:S(2)}, u32[]{:S(2)}) collective-permute-start(bf16[4,48,768]{2,1,0:T(8,128)(2,1)} %get-tuple-element.590), channel_id=1, source_target_pairs={{0,8},{4,12},{8,0},{12,4},{16,24},{20,28},{24,16},{28,20},{1,9},{5... | collective-permute-start | bytes 884744 | tf_op jit(solution)/shard_map/ppermute | solution.py:605
  568.6 57.2 %collective-permute-start.61 = (bf16[4,48,768]{2,1,0:T(8,128)(2,1)}, bf16[4,48,768]{2,1,0:T(8,128)(2,1)S(1)}, u32[]{:S(2)}, u32[]{:S(2)}) collective-permute-start(bf16[4,48,768]{2,1,0:T(8,128)(2,1)} %get-tuple-element.591), channel_id=1, source_target_pairs={{0,16},{4,20},{8,24},{12,28},{16,0},{20,4},{24,8},{28,12},{1,17},{... | collective-permute-start | bytes 884744 | tf_op jit(solution)/shard_map/ppermute | solution.py:605
  643.5 40.2 %collective-permute-start.65 = (bf16[2,2,144,768]{3,2,1,0:T(8,128)(2,1)}, bf16[2,2,144,768]{3,2,1,0:T(8,128)(2,1)S(1)}, u32[]{:S(2)}, u32[]{:S(2)}) collective-permute-start(bf16[2,2,144,768]{3,2,1,0:T(8,128)(2,1)} %get-tuple-element.607), channel_id=1, source_target_pairs={{0,4},{4,0},{8,12},{12,8},{16,20},{20,16},{24,28},{28,24},{1,5},{5... | collective-permute-start | bytes 2654216 | tf_op jit(solution)/shard_map/ppermute | solution.py:605
  646.1 37.7 %collective-permute-start.66 = (bf16[2,2,144,768]{3,2,1,0:T(8,128)(2,1)}, bf16[2,2,144,768]{3,2,1,0:T(8,128)(2,1)S(1)}, u32[]{:S(2)}, u32[]{:S(2)}) collective-permute-start(bf16[2,2,144,768]{3,2,1,0:T(8,128)(2,1)} %get-tuple-element.608), channel_id=1, source_target_pairs={{0,4},{4,0},{8,12},{12,8},{16,20},{20,16},{24,28},{28,24},{1,5},{5... | collective-permute-start | bytes 2654216 | tf_op jit(solution)/shard_map/ppermute | solution.py:605
  648.5 32.0 %collective-permute-start.47 = (bf16[192,768]{1,0:T(8,128)(2,1)S(1)}, bf16[192,768]{1,0:T(8,128)(2,1)S(1)}, u32[]{:S(2)}, u32[]{:S(2)}) collective-permute-start(bf16[192,768]{1,0:T(8,128)(2,1)S(1)} %copy-done.72), channel_id=1, source_target_pairs={{0,3},{1,2},{2,1},{3,0},{4,7},{5,6},{6,5},{7,4},{8,11},{9,10},{10,... | collective-permute-start | bytes 884744 | tf_op jit(solution)/shard_map/ppermute | solution.py:605
  657.8 27.1 %collective-permute-start.62 = (bf16[96,768]{1,0:T(8,128)(2,1)}, bf16[96,768]{1,0:T(8,128)(2,1)S(1)}, u32[]{:S(2)}, u32[]{:S(2)}) collective-permute-start(bf16[96,768]{1,0:T(8,128)(2,1)} %get-tuple-element.604), channel_id=1, source_target_pairs={{0,1},{1,0},{2,3},{3,2},{4,5},{5,4},{6,7},{7,6},{8,9},{9,8},{10,11... | collective-permute-start | bytes 442376 | tf_op jit(solution)/shard_map/ppermute | solution.py:605
  661.4 23.5 %collective-permute-start.63 = (bf16[96,768]{1,0:T(8,128)(2,1)}, bf16[96,768]{1,0:T(8,128)(2,1)S(1)}, u32[]{:S(2)}, u32[]{:S(2)}) collective-permute-start(bf16[96,768]{1,0:T(8,128)(2,1)} %get-tuple-element.605), channel_id=1, source_target_pairs={{0,2},{1,3},{2,0},{3,1},{4,6},{5,7},{6,4},{7,5},{8,10},{9,11},{10,... | collective-permute-start | bytes 442376 | tf_op jit(solution)/shard_map/ppermute | solution.py:605
  690.8 15.8 %collective-permute-start.71 = (bf16[536,256]{1,0:T(8,128)(2,1)S(1)}, bf16[536,256]{1,0:T(8,128)(2,1)S(1)}, u32[]{:S(2)}, u32[]{:S(2)}) collective-permute-start(bf16[536,256]{1,0:T(8,128)(2,1)S(1)} %copy-done.27), channel_id=1, source_target_pairs={{0,1},{1,0},{2,3},{3,2},{4,5},{5,4},{6,7},{7,6},{8,9},{9,8},{10,11... | collective-permute-start | bytes 823304 | tf_op jit(solution)/shard_map/ppermute | solution.py:605
  690.8 15.8 %collective-permute-start.72 = (bf16[536,256]{1,0:T(8,128)(2,1)S(1)}, bf16[536,256]{1,0:T(8,128)(2,1)S(1)}, u32[]{:S(2)}, u32[]{:S(2)}) collective-permute-start(bf16[536,256]{1,0:T(8,128)(2,1)S(1)} %copy-done.27), channel_id=1, source_target_pairs={{0,2},{1,3},{2,0},{3,1},{4,6},{5,7},{6,4},{7,5},{8,10},{9,11},{10,... | collective-permute-start | bytes 823304 | tf_op jit(solution)/shard_map/ppermute | solution.py:605
  693.2 22.2 %collective-permute-start.73 = (bf16[536,256]{1,0:T(8,128)(2,1)S(1)}, bf16[536,256]{1,0:T(8,128)(2,1)S(1)}, u32[]{:S(2)}, u32[]{:S(2)}) collective-permute-start(bf16[536,256]{1,0:T(8,128)(2,1)S(1)} %copy-done.27), channel_id=1, source_target_pairs={{0,3},{1,2},{2,1},{3,0},{4,7},{5,6},{6,5},{7,4},{8,11},{9,10},{10,... | collective-permute-start | bytes 823304 | tf_op jit(solution)/shard_map/ppermute | solution.py:605
  (140 other events, 883.8 us)
Sparse Core Ops, SparseCore 0:
  19.3 146.6 all-gather.2
  566.9 52.8 all-reduce.2

commit v4 on v3

--- a/solution.py
+++ b/solution.py
@@ -5,7 +5,7 @@
 from jax import lax
 from jax.experimental import pallas as pl
 from jax.experimental.pallas import tpu as pltpu
-from jax.sharding import PartitionSpec as P
+from jax.sharding import Mesh, PartitionSpec as P
 
 BF = jnp.bfloat16
 F32 = jnp.float32
@@ -128,16 +128,38 @@
     return (dot_nn(high, flip) + dot_nn(middle, flip)) + dot_nn(last, flip)
 
 
+def attn_specs(weights):
+    if len(weights) == 4:
+        return [whole(w.shape) for w in weights]
+    groups, _, mp, count, width = weights[0].shape
+    return [pl.BlockSpec((groups, 1, mp, count // 3, width), lambda i, place: (0, place[3] ^ i, 0, 0, 0))]
+
+
+def by_half(step, refs, place_ref, part):
+    if len(refs) == 1:
+        width = refs[0].shape[-1]
+        part(lambda m: refs[0][m, 0].reshape(-1, width))
+        return
+    for half in range(2):
+        wa, wb = refs[2 * half], refs[2 * half + 1]
+
+        def mat(m, wa=wa, wb=wb):
+            return jnp.concatenate([wa[place_ref[0] ^ m], wb[place_ref[0] ^ m]], axis=0)
+
+        pl.when(step == half)(functools.partial(part, mat))
+
+
 def attn_forward(order, layer, place, x, normed, halo, weights, pos_bias, seg_q, seg_k, gain, shift):
     rows, width = x.shape
     seqs, block, _ = seg_q.shape
     keys = seg_k.shape[2]
     window = keys - block
-    quarter = weights[0].shape[1]
-    half = 2 * quarter
-
-    def body(place_ref, x_ref, n_ref, h_ref, oa, ob, ta, tb, band_ref, sq_ref, sk_ref, g_ref, s_ref,
-             sg_ref, ratio_ref, rden_ref, v_ref, wsum_ref, car_ref, mixed_ref, masked_ref, x1_ref, nb_ref, mix):
+    half = width // 2
+
+    def body(place_ref, x_ref, n_ref, h_ref, *rest):
+        w_refs, rest = rest[: len(weights)], rest[len(weights) :]
+        (band_ref, sq_ref, sk_ref, g_ref, s_ref, sg_ref, ratio_ref, rden_ref, v_ref, wsum_ref, car_ref, mixed_ref,
+         masked_ref, x1_ref, nb_ref, mix) = rest
         step = pl.program_id(0)
 
         @pl.when(step == 0)
@@ -151,10 +173,7 @@
                 mix[s] = masked.astype(BF)
             x1_ref[...] = x_ref[...]
 
-        def part(wa, wb):
-            def mat(m):
-                return jnp.concatenate([wa[place_ref[0] ^ m], wb[place_ref[0] ^ m]], axis=0)
-
+        def part(mat):
             wq, wk, wv = mat(0), mat(1), mat(2)
             q = dot_nt(n_ref[...], wq)
             sg = jax.nn.sigmoid(q)
@@ -183,13 +202,10 @@
             mixed_ref[...] = mixed
             x1_ref[...] += dot_nn(mixed, mat(3))
 
-        @pl.when(step == 0)
-        def _():
-            part(oa, ob)
+        by_half(step, w_refs, place_ref, part)
 
         @pl.when(step == 1)
         def _():
-            part(ta, tb)
             normal, _ = normalize(x1_ref[...])
             nb_ref[...] = (normal * g_ref[...] + s_ref[...]).astype(BF)
 
@@ -201,7 +217,7 @@
         body,
         (2,),
         [whole((rows, width))] * 3
-        + [whole((4, quarter, width))] * 4
+        + attn_specs(weights)
         + [pl.BlockSpec((1, block, window), lambda i, place: (layer, place[1], 0))]
         + [whole((seqs, block, 1)), whole((seqs, 1, keys)), whole((1, width)), whole((1, width))],
         [col(rows)] * 3 + [col(2 * rows)] * 3 + [col(rows)]
@@ -280,90 +296,126 @@
     )(x1, normed, *ups, *downs, gain, shift)
 
 
-def ff_backward(order, x1, normed, ups, downs, grad, gain, saved):
+def ff_specs(weights, side, chunk):
+    if len(weights) == 4:
+        width = weights[0].shape[1]
+        spec = pl.BlockSpec((chunk, width), lambda i, *_: (i, 0))
+        return [weights[side], weights[2 + side]], [spec, spec]
+    groups, _, mp, count, width = weights[0].shape
+    rows = count // 3
+    per = chunk // (mp * rows)
+
+    def spec(which):
+        return pl.BlockSpec((per, 1, mp, rows, width), lambda i, place: (i, place[3] ^ side, 0, which, 0))
+
+    return [weights[0], weights[0]], [spec(1), spec(2)]
+
+
+def ff_backward(order, place, x1, normed, weights, side, groups, grad, gain, saved, before):
     rows, width = x1.shape
-    half = ups[0].shape[0]
-    per_half = 2
-    chunk = half // per_half
-    steps = 2 * per_half
+    steps = 2
+    half = 2 * width
+    chunk = half // steps
+    operands, w_specs = ff_specs(weights, side, chunk)
+    group_rows = half // groups
+    per = chunk // group_rows
     fresh = saved is None
-
-    def body(x_ref, n_ref, u0, u1, d0, d1, grad_ref, g_ref, *rest):
-        if fresh:
-            (out_ref, gu0, gu1, gd0, gd1, g1_ref, ga_ref, gg_ref, gs_ref, low, dn, x2) = rest
+    last = before is not None
+    relative = len(weights) == 4
+
+    def body(place_ref, x_ref, n_ref, u_ref, d_ref, grad_ref, g_ref, *rest):
+        rest = list(rest)
+        act_ref, slope_ref = (None, None) if fresh else (rest.pop(0), rest.pop(0))
+        dn_in = rest.pop(0) if last else None
+        x2_in = rest.pop(0) if last and fresh else None
+        wg_ref = rest.pop(0)
+        if last:
+            g1_ref, ga_ref, gg_ref, gs_ref = rest[:4]
+            rest = rest[4:]
+            out_ref = rest.pop(0) if fresh else None
+            low, dn = rest[0], rest[1]
+            x2 = rest[2] if fresh else None
         else:
-            (act_ref, slope_ref, gu0, gu1, gd0, gd1, g1_ref, ga_ref, gg_ref, gs_ref, low, dn) = rest
+            dn = rest.pop(0)
+            x2 = rest.pop(0) if fresh else None
+            low = rest[0]
         step = pl.program_id(0)
 
         @pl.when(step == 0)
         def _():
             low[...] = grad_ref[...].astype(BF)
-            dn[...] = jnp.zeros_like(dn)
+            dn[...] = dn_in[...] if last else jnp.zeros_like(dn)
             if fresh:
-                x2[...] = x_ref[...]
-
-        def part(u, d, gu, gd):
-            if fresh:
-                act, slope = gelu_both(dot_nt(n_ref[...], u[...]))
-                act = act.astype(BF)
-                x2[...] += dot_nn(act, d[...])
-            else:
-                act, slope = act_ref[...], slope_ref[...].astype(F32)
-            pre_grad = (dot_nt(low[...], d[...]) * slope).astype(BF)
-            dn[...] += dot_nn(pre_grad, u[...])
-            gd[...] = dot_tn(act, low[...]).astype(BF)
-            gu[...] = dot_tn(pre_grad, n_ref[...]).astype(BF)
-
-        pl.when(step < per_half)(lambda: part(u0, d0, gu0, gd0))
-        pl.when(step >= per_half)(lambda: part(u1, d1, gu1, gd1))
-
-        @pl.when(step == steps - 1)
-        def _():
-            if fresh:
-                out_ref[...] = x2[...].astype(BF)
-            normal, inv = normalize(x_ref[...])
-            total = dn[...]
-            g1 = grad_ref[...] + norm_back(total, normal, inv, g_ref[...])
-            g1_ref[...] = g1
-            ga_ref[...] = g1.astype(BF)
-            gg_ref[...] = jnp.sum(total * normal, axis=0, keepdims=True)
-            gs_ref[...] = jnp.sum(total, axis=0, keepdims=True)
-
-    own, other = chunk_specs(chunk, width, per_half)
-    col = pl.BlockSpec((rows, chunk), lambda i: (0, i))
-    out_specs = [own, other, own, other] + [whole((rows, width))] * 2 + [whole((1, width))] * 2
-    out_shape = (
-        [shape_of((half, width), BF)] * 4
-        + [shape_of((rows, width), F32), shape_of((rows, width), BF)]
-        + [shape_of((1, width), F32)] * 2
-    )
-    scratch = [pltpu.VMEM((rows, width), BF), pltpu.VMEM((rows, width), F32)]
-    if fresh:
-        out_specs = [whole((rows, width))] + out_specs
-        out_shape = [shape_of((rows, width), BF)] + out_shape
-        scratch.append(pltpu.VMEM((rows, width), F32))
+                x2[...] = x2_in[...] if last else x_ref[...]
+
+        u = u_ref[...].reshape(chunk, width)
+        d = d_ref[...].reshape(chunk, width)
+        if fresh:
+            act, slope = gelu_both(dot_nt(n_ref[...], u))
+            act = act.astype(BF)
+            x2[...] += dot_nn(act, d)
+        else:
+            act, slope = act_ref[...], slope_ref[...].astype(F32)
+        pre_grad = (dot_nt(low[...], d) * slope).astype(BF)
+        dn[...] += dot_nn(pre_grad, u)
+        for which, value in ((0, dot_tn(pre_grad, n_ref[...])), (1, dot_tn(act, low[...]))):
+            value = value.astype(BF)
+            for k in range(per):
+                spot = (place_ref[5] ^ k) if relative else k
+                wg_ref[spot, which] = value[k * group_rows : (k + 1) * group_rows]
+
+        if last:
+
+            @pl.when(step == steps - 1)
+            def _():
+                if fresh:
+                    out_ref[...] = x2[...].astype(BF)
+                normal, inv = normalize(x_ref[...])
+                total = dn[...]
+                g1 = grad_ref[...] + norm_back(total, normal, inv, g_ref[...])
+                g1_ref[...] = g1
+                ga_ref[...] = g1.astype(BF)
+                gg_ref[...] = jnp.sum(total * normal, axis=0, keepdims=True)
+                gs_ref[...] = jnp.sum(total, axis=0, keepdims=True)
+
+    full = whole((rows, width))
+    col = pl.BlockSpec((rows, chunk), lambda i, *_: (0, steps * side + i))
+    wg = pl.BlockSpec((per, 2, group_rows, width), lambda i, place: ((place[4] ^ i) if relative else i, 0, 0, 0))
+    in_specs = [full, full] + w_specs + [full, whole((1, width))]
+    operands = [x1, normed] + operands + [grad, gain]
+    if not fresh:
+        in_specs += [col, col]
+        operands += list(saved)
+    out_specs, out_shape = [wg], [shape_of((groups, 2, group_rows, width), BF)]
+    scratch = [pltpu.VMEM((rows, width), BF)]
+    sums = [shape_of((rows, width), F32)] * (2 if fresh else 1)
+    if last:
+        in_specs += [full] * len(sums)
+        operands += list(before)
+        out_specs += [full, full, whole((1, width)), whole((1, width))]
+        out_shape += [shape_of((rows, width), F32), shape_of((rows, width), BF)] + [shape_of((1, width), F32)] * 2
+        if fresh:
+            out_specs.append(full)
+            out_shape.append(shape_of((rows, width), BF))
+        scratch += [pltpu.VMEM((rows, width), F32)] * len(sums)
+    else:
+        out_specs += [full] * len(sums)
+        out_shape += sums
     return call(
-        order,
-        body,
-        (steps,),
-        [whole((rows, width))] * 2 + [own, other, own, other] + [whole((rows, width)), whole((1, width))]
-        + ([] if fresh else [col, col]),
-        out_specs,
-        out_shape,
-        scratch,
-        name="ff_bwd",
-    )(x1, normed, *ups, *downs, grad, gain, *(() if fresh else saved))
+        order, body, (steps,), in_specs, out_specs, out_shape, scratch, prefetch=1, name="ff_bwd"
+    )(place, *operands)
 
 
 def attn_backward(order, place, grad_low, weights, sg, ratio, rden, v, wsum, carried, masked):
     rows, width = grad_low.shape
     seqs, block, keys = masked.shape
     window = keys - block
-    quarter = weights[0].shape[1]
-    half = 2 * quarter
-
-    def body(place_ref, ga_ref, oa, ob, ta, tb, sg_ref, ratio_ref, rden_ref, v_ref, wsum_ref, car_ref, masked_ref,
-             gq_ref, gk_ref, gv_ref, band_ref, own_ref, halo_ref, mix_t, wgrad, dn):
+    half = width // 2
+
+    def body(place_ref, ga_ref, *rest):
+        w_refs, rest = rest[: len(weights)], rest[len(weights) :]
+        (sg_ref, ratio_ref, rden_ref, v_ref, wsum_ref, car_ref, masked_ref,
+         gq_ref, gk_ref, gv_ref, band_ref, own_ref, halo_ref, mix_t, wgrad, dn) = rest
         step = pl.program_id(0)
 
         @pl.when(step == 0)
@@ -373,10 +425,7 @@
             wgrad[...] = jnp.zeros_like(wgrad)
             dn[...] = jnp.zeros_like(dn)
 
-        def part(wa, wb):
-            def mat(m):
-                return jnp.concatenate([wa[place_ref[0] ^ m], wb[place_ref[0] ^ m]], axis=0)
-
+        def part(mat):
             gm = dot_nt(ga_ref[...], mat(3))
             sig = sg_ref[...].astype(F32)
             rat = ratio_ref[...].astype(F32)
@@ -403,13 +452,10 @@
                     wgrad[s, :, cols] += dot_nt(gnum[here], car_ref[there]) + dot_nt(gden[here], wsum_ref[there])
                     dn[there] += dot_nn(gk, wk) + dot_nn(gv, wv)
 
-        @pl.when(step == 0)
-        def _():
-            part(oa, ob)
+        by_half(step, w_refs, place_ref, part)
 
         @pl.when(step == 1)
         def _():
-            part(ta, tb)
             total = wgrad[0] * masked_ref[0]
             for s in range(1, seqs):
                 total = total + wgrad[s] * masked_ref[s]
@@ -431,7 +477,7 @@
         body,
         (2,),
         [whole((rows, width))]
-        + [whole((4, quarter, width))] * 4
+        + attn_specs(weights)
         + [col(rows)] * 3 + [col(2 * rows)] * 3 + [whole((seqs, block, keys))],
         [col(rows), col(2 * rows), col(2 * rows), whole((block, window)), whole((rows, width)), whole((rows, width))],
         [
@@ -452,7 +498,7 @@
     )(place, grad_low, *weights, sg, ratio, rden, v, wsum, carried, masked)
 
 
-def attn_weight_grads(order, place, gq, gk, gv, mixed, normed, halo, grad_low):
+def attn_weight_grads(order, place, gq, gk, gv, mixed, normed, halo, grad_low, mp, mixed_rows):
     rows, width = gq.shape
     half = width // 2
     quarter = half // 2
@@ -464,15 +510,18 @@
         def store(value):
             low = value.astype(BF)
 
-            @pl.when(step < 4)
-            def _():
-                oa[0] = low[:quarter]
-                ob[0] = low[quarter:]
-
-            @pl.when(step >= 4)
-            def _():
-                ta[0] = low[:quarter]
-                tb[0] = low[quarter:]
+            def put(a_ref, b_ref):
+                if not mixed_rows:
+                    a_ref[0] = low[:quarter]
+                    b_ref[0] = low[quarter:]
+                    return
+                piece = quarter // mp
+                for z in range(mp):
+                    a_ref[0, z * piece : (z + 1) * piece] = low[2 * z * piece : (2 * z + 1) * piece]
+                    b_ref[0, z * piece : (z + 1) * piece] = low[(2 * z + 1) * piece : (2 * z + 2) * piece]
+
+            pl.when(step < 4)(lambda: put(oa, ob))
+            pl.when(step >= 4)(lambda: put(ta, tb))
 
         def keys_grad(ref):
             return dot_tn(ref[:rows], h_ref[...]) + dot_tn(ref[rows:], n_ref[...])
@@ -521,28 +570,53 @@
 
 
 def finish_layer(order, layer, layers, place, parts, channels, hidden, mp_rows, previous):
-    groups, count, width = parts[0].shape
-    piece = count * 2 // 3
+    width = parts[0].shape[-1]
+    piece = mp_rows
     small = piece // 2
-    total = 2 * groups * piece
-
-    def body(place_ref, oa, ob, ta, tb, *rest):
-        qkv_ref, out_ref, up_ref, down_ref, attn, up = rest[-6:]
-        for core, (pa, pb) in enumerate(((oa, ob), (ta, tb))):
-            for p in range(groups):
-                owner = 2 * (place_ref[2] ^ p) + (place_ref[3] ^ core)
-                start = pl.multiple_of(owner * piece, piece)
-                up[pl.ds(start, piece)] = pa[p, :piece].astype(F32)
-                down_ref[0, pl.ds(start, piece)] = pb[p, :piece].astype(F32)
-                attn[pl.ds(start, small)] = pa[p, piece:].astype(F32)
-                attn[pl.ds(pl.multiple_of(owner * piece + small, small), small)] = pb[p, piece:].astype(F32)
+    total = 4 * channels
+
+    def body(place_ref, *rest):
+        p_refs, (qkv_ref, out_ref, up_ref, down_ref, up) = rest[: len(parts)], rest[len(parts) :]
+
+        def put(owner, count, shift, value):
+            start = owner * piece + shift
+            mat = start // channels
+            inner = pl.multiple_of(start - mat * channels, small)
+
+            @pl.when(mat < 3)
+            def _():
+                qkv_ref[0, jnp.minimum(mat, 2), pl.ds(inner, count)] = value
+
+            @pl.when(mat == 3)
+            def _():
+                out_ref[0, pl.ds(inner, count)] = value
+
+        if len(parts) == 1:
+            for owner in range(total // piece):
+                here = slice(owner * piece, (owner + 1) * piece)
+                mat = owner * piece // channels
+                inner = slice(owner * piece - mat * channels, owner * piece - mat * channels + piece)
+                value = p_refs[0][owner, :piece].astype(F32)
+                if mat < 3:
+                    qkv_ref[0, mat, inner] = value
+                else:
+                    out_ref[0, inner] = value
+                up[here] = p_refs[0][owner, piece : 2 * piece].astype(F32)
+                down_ref[0, here] = p_refs[0][owner, 2 * piece :].astype(F32)
+        else:
+            for core in range(2):
+                pa, pb = p_refs[2 * core], p_refs[2 * core + 1]
+                for p in range(pa.shape[0]):
+                    owner = 2 * (place_ref[2] ^ p) + (place_ref[3] ^ core)
+                    start = pl.multiple_of(owner * piece, piece)
+                    up[pl.ds(start, piece)] = pa[p, :piece].astype(F32)
+                    down_ref[0, pl.ds(start, piece)] = pb[p, :piece].astype(F32)
+                    put(owner, small, 0, pa[p, piece:].astype(F32))
+                    put(owner, small, small, pb[p, piece:].astype(F32))
         up_ref[0] = up[...].T
-        for m in range(3):
-            qkv_ref[0, m] = attn[m * channels : (m + 1) * channels].T
-        out_ref[0] = attn[3 * channels :]
 
     shapes = [
-        (layers, 3, width, channels),
+        (layers, 3, channels, width),
         (layers, channels, width),
         (layers, width, hidden),
         (layers, hidden, width),
@@ -570,7 +644,7 @@
             grid=(1,),
             in_specs=[whole(part.shape) for part in parts] + [anywhere] * (len(extra) + 1),
             out_specs=[here(shape) for shape in shapes] + [anywhere],
-            scratch_shapes=[pltpu.VMEM((total, width), F32)] * 2,
+            scratch_shapes=[pltpu.VMEM((total, width), F32)],
         ),
         out_shape=[shape_of(shape, F32) for shape in shapes] + [shape_of(TOKEN, jnp.int32)],
         input_output_aliases=aliases,
@@ -583,6 +657,9 @@
     return results
 
 
+DP = ("g", "c")
+
+
 class Order:
     def __init__(self):
         self.token = jnp.zeros(TOKEN, jnp.int32)
@@ -601,7 +678,7 @@
         self.routes = (bits, bits[::-1])
 
     def swap(self, value, axis, bit):
-        size = self.dp if axis == "dp" else self.mp
+        size = self.dp if axis == DP else self.mp
         return lax.ppermute(value, axis, [(i, i ^ bit) for i in range(size)])
 
 
@@ -615,7 +692,7 @@
     def start(self):
         self.values = self.links.order.pin(*self.values)
         self.coming = [
-            self.links.swap(value, "dp", route[self.phase])
+            self.links.swap(value, DP, route[self.phase])
             for value, route in zip(self.values, self.links.routes)
         ]
 
@@ -636,7 +713,7 @@
 
     def start_cores(self):
         self.values = self.links.order.pin(*self.values)
-        self.coming = [self.links.swap(value, "dp", 1) for value in self.values]
+        self.coming = [self.links.swap(value, DP, 1) for value in self.values]
 
     def wait_cores(self):
         return self.values + self.links.order.pin(*self.coming)
@@ -668,7 +745,7 @@
 
     def start_cores(self):
         others = self.links.order.pin(*self.halves[2:])
-        self.coming = [self.links.swap(other, "dp", 1) for other in others]
+        self.coming = [self.links.swap(other, DP, 1) for other in others]
 
     def wait_cores(self):
         coming = self.links.order.pin(*self.coming)
@@ -689,7 +766,7 @@
             sends.append(lax.index_in_dim(self.values[k], 1, place, keepdims=False))
         sends = self.links.order.pin(*sends)
         self.coming = [
-            self.links.swap(sends[k], "dp", self.links.routes[1 - k][self.phase]) for k in range(2)
+            self.links.swap(sends[k], DP, self.links.routes[1 - k][self.phase]) for k in range(2)
         ]
 
     def wait(self):
@@ -704,14 +781,45 @@
         while self.phase < len(self.links.routes[0]):
             self.start()
             self.wait()
-
-    def start_mp(self):
-        blocks = [jnp.concatenate([value[p] for value in self.values], axis=0) for p in range(self.links.mp)]
-        self.kept = blocks[0]
-        sends = self.links.order.pin(*blocks[1:])
-        self.coming = [self.links.swap(send, "mp", p + 1) for p, send in enumerate(sends)]
-
-    def wait_mp(self):
+        return self.values
+
+
+class ReduceWide:
+    def __init__(self, links, own, other):
+        self.links = links
+        self.own = own
+        self.other = other
+
+    def start_cores(self):
+        (self.other,) = self.links.order.pin(self.other)
+        self.coming = self.links.swap(self.other, DP, 1)
+
+    def wait_cores(self):
+        (coming,) = self.links.order.pin(self.coming)
+        total = (self.own.astype(F32) + coming.astype(F32)).astype(BF)
+        (total,) = self.links.order.pin(total)
+        self.sums = lax.psum_scatter(total, "g", scatter_dimension=0, tiled=True)
+
+    def wait(self):
+        (sums,) = self.links.order.pin(self.sums)
+        return sums.reshape(2, self.links.mp, -1, sums.shape[-1])
+
+
+class ReduceMp:
+    def __init__(self, links, arrays, index):
+        self.links = links
+        joined = jnp.concatenate(arrays, axis=1)
+        if index is None:
+            blocks = [joined[p] for p in range(links.mp)]
+        else:
+            blocks = [
+                lax.dynamic_index_in_dim(joined, jnp.bitwise_xor(index, p), 0, keepdims=False)
+                for p in range(links.mp)
+            ]
+        self.kept, *sends = links.order.pin(*blocks)
+        self.coming = [links.swap(send, "mp", p + 1) for p, send in enumerate(sends)]
+
+    def wait(self):
         total = self.kept.astype(F32)
         for part in self.links.order.pin(*self.coming):
             total = total + part.astype(F32)
@@ -737,14 +845,17 @@
         channels = qkv_weight.shape[-1]
         hidden = up_weight.shape[-1]
         rows = seqs * block
-        dp_index = lax.axis_index("dp")
+        group = lax.axis_index("g")
+        core = lax.axis_index("c")
+        dp_index = group * 2 + core
         mp_index = lax.axis_index("mp")
         order = Order()
         links = Links(order, dp, mp)
         attn_rows = 4 * channels // dp
         ff_rows = hidden // dp
-        group = dp_index // 2
-        place = jnp.stack([group // (dp // 8), mp_index, group, dp_index % 2]).astype(jnp.int32)
+        groups = dp // 2
+        per = max(1, width // (mp * ff_rows))
+        place = jnp.stack([group // (groups // 4), mp_index, group, core, group // per, group % per]).astype(jnp.int32)
 
         def picks(count, offset, length):
             return (
@@ -752,17 +863,17 @@
                 == lax.broadcasted_iota(jnp.int32, (count, length), 1)
             ).astype(BF)
 
-        attn_pick = picks(attn_rows, dp_index * attn_rows, 4 * channels)
         ff_pick = picks(ff_rows, dp_index * ff_rows, hidden)
 
         def attn_piece(layer):
-            piece = jnp.einsum(
-                "rmc,mdc->rd",
-                attn_pick[:, : 3 * channels].reshape(attn_rows, 3, channels),
-                qkv_weight[layer],
-                preferred_element_type=F32,
-            ) + dot_nn(attn_pick[:, 3 * channels :], out_weight[layer])
-            return piece.astype(BF)
+            by_channel = jnp.transpose(qkv_weight[layer], (0, 2, 1)).reshape(3 * channels, width)
+            start = dp_index * attn_rows
+            inner = start - 3 * channels
+            return jnp.where(
+                inner < 0,
+                lax.dynamic_slice_in_dim(by_channel, jnp.minimum(start, 3 * channels - attn_rows), attn_rows),
+                lax.dynamic_slice_in_dim(out_weight[layer], jnp.maximum(inner, 0), attn_rows),
+            )
 
         def ff_pieces(layer):
             return (
@@ -792,17 +903,17 @@
         gains = norm_gain.reshape(layers, 2, 1, width)
         shifts = norm_bias.reshape(layers, 2, 1, width)
         middle = attn_rows // 2
+        in_blocks = middle % 16 == 0
 
         piece = attn_piece(0)
         attn0 = Gather(links, piece[:middle], piece[middle:])
         attn0.start_mp()
-        ff0 = Gather(links, *ff_pieces(0))
-        ff0.start_mp()
         x, normed = enter_kernel(order, tokens.reshape(rows, width), gains[0, 0], shifts[0, 0])
         (normed,) = order.pin(normed)
         halo = forward_halo(normed)
-        (later,) = order.pin(jnp.concatenate((attn_piece(1),) + ff_pieces(1), axis=0))
-        later = lax.all_gather(later, ("dp", "mp"), axis=0, tiled=False)
+        ff0 = Gather(links, *ff_pieces(0))
+        ff0.start_mp()
+        later = jnp.concatenate((attn_piece(1),) + ff_pieces(1), axis=0)
 
         seg_pad = jnp.concatenate([jnp.full((seqs, window), -1, segments.dtype), segments], axis=1)
         seg_keys = lax.dynamic_slice_in_dim(seg_pad, mp_index * block, block + window, axis=1)
@@ -811,9 +922,11 @@
 
         attn0.wait_mp()
         attn0.start()
-        ff0.wait_mp()
+        (later,) = order.pin(later)
+        later = lax.all_gather(later, ("g", "c", "mp"), axis=0, tiled=False)
         attn0.wait()
         attn0.start()
+        ff0.wait_mp()
         ff0.start()
         attn0.wait_all()
         attn0.start_cores()
@@ -839,57 +952,58 @@
         (normed2,) = order.pin(normed2)
         halo2 = forward_halo(normed2)
         (later,) = order.pin(later)
-        later = later.reshape((dp, mp) + later.shape[1:])
-        own, other = relative(later)
-        cuts = [middle, attn_rows, attn_rows + ff_rows]
-        own_a, own_b, own_up, own_down = jnp.split(own, cuts, axis=2)
-        other_a, other_b, other_up, other_down = jnp.split(other, cuts, axis=2)
-        w_attn1 = attn_mats([own_a, own_b, other_a, other_b])
-        ups1, downs1 = ff_mats([own_up, own_down, other_up, other_down])
+        if in_blocks:
+            w_attn1 = w_ff1 = [later.reshape((groups, 2, mp) + later.shape[1:])]
+        else:
+            own, other = relative(later.reshape((dp, mp) + later.shape[1:]))
+            cuts = [middle, attn_rows, attn_rows + ff_rows]
+            own_a, own_b, own_up, own_down = jnp.split(own, cuts, axis=2)
+            other_a, other_b, other_up, other_down = jnp.split(other, cuts, axis=2)
+            w_attn1 = attn_mats([own_a, own_b, other_a, other_b])
+            w_ff1 = sum(ff_mats([own_up, own_down, other_up, other_down]), ())
         (halo2,) = order.pin(halo2)
         x1_1, normed_b1, saved1, rows1 = attn(1, x2, normed2, halo2, w_attn1)
 
-        output, gu0, gu1, gd0, gd1, grad1, grad1_low, gain_b1, shift_b1 = ff_backward(
-            order, x1_1, normed_b1, ups1, downs1, cotangent.reshape(rows, width), gains[1, 1], None
+        def ff_back(layer, x1, normed_b, weights, grad, saved):
+            args = (order, place, x1, normed_b, weights)
+            kept = (groups, grad, gains[layer, 1], saved)
+            wg_other, *before = ff_backward(*args, 1, *kept, None)
+            wide = ReduceWide(links, None, wg_other)
+            wide.start_cores()
+            wide.own, *rest = ff_backward(*args, 0, *kept, before)
+            return wide, rest
+
+        wide1, (grad1, grad1_low, gain_b1, shift_b1, output) = ff_back(
+            1, x1_1, normed_b1, w_ff1, cotangent.reshape(rows, width), None
         )
-        r_ff1 = Reduce(links, [gu0, gd0, gu1, gd1])
-        r_ff1.start_cores()
-        r_ff1.wait_cores()
-        r_ff1.start()
+        wide1.wait_cores()
         gq, gk, gv, band1, dn_own1, back1 = attn_backward(order, place, grad1_low, w_attn1, *saved1)
         (back1,) = order.pin(back1)
         back1 = backward_halo(back1)
-        r_attn1 = Reduce(links, attn_weight_grads(order, place, gq, gk, gv, *rows1, grad1_low))
-        r_ff1.wait()
-        r_ff1.start()
+        r_attn1 = Reduce(
+            links, attn_weight_grads(order, place, gq, gk, gv, *rows1, grad1_low, mp, in_blocks)
+        )
+        (back1,) = order.pin(back1)
         r_attn1.start_cores()
-        (back1,) = order.pin(back1)
         grad2, gain_a1, shift_a1 = leave_attn(order, x2, grad1, dn_own1, back1, gains[1, 0])
         r_attn1.wait_cores()
         r_attn1.start()
-        (band1,) = order.pin(band1)
-        band1 = lax.psum(band1, "dp")
-
-        gu0, gu1, gd0, gd1, grad3, grad3_low, gain_b0, shift_b0 = ff_backward(
-            order, x1_0, normed_b0, ups0, downs0, grad2, gains[0, 1], (act0, slope0)
+        wide0, (grad3, grad3_low, gain_b0, shift_b0) = ff_back(
+            0, x1_0, normed_b0, ups0 + downs0, grad2, (act0, slope0)
         )
-        r_ff0 = Reduce(links, [gu0, gd0, gu1, gd1])
-        r_ff0.start_cores()
-        r_ff1.wait_all()
-        r_ff1.start_mp()
+        wide0.wait_cores()
         r_attn1.wait()
         r_attn1.start()
-        r_ff0.wait_cores()
-        r_ff0.start()
         gq, gk, gv, band0, dn_own0, back0 = attn_backward(order, place, grad3_low, w_attn0, *saved0)
+        attn1_sum = r_attn1.wait_all()
         (back0,) = order.pin(back0)
         back0 = backward_halo(back0)
-        r_attn1.wait_all()
-        r_attn1.start_mp()
-        r_attn0 = Reduce(links, attn_weight_grads(order, place, gq, gk, gv, *rows0, grad3_low))
+        r_attn0 = Reduce(
+            links, attn_weight_grads(order, place, gq, gk, gv, *rows0, grad3_low, mp, False)
+        )
         r_attn0.start_cores()
-        r_ff0.wait()
-        r_ff0.start()
+        up1, down1 = wide1.wait()
+        mp1 = ReduceMp(links, attn1_sum + [up1, down1], mp_index if in_blocks else None)
         r_attn0.wait_cores()
         r_attn0.start()
         (back0,) = order.pin(back0)
@@ -897,71 +1011,48 @@
         norms = jnp.concatenate(
             [gain_a0, gain_b0, shift_a0, shift_b0, gain_a1, gain_b1, shift_a1, shift_b1], axis=0
         ).reshape(-1, window)
-        small = jnp.concatenate([band0, norms], axis=0)
-
-        class Small:
-            def __init__(self, value):
-                self.value = value
-                self.bit = 1
-
-            def start(self):
-                (self.value,) = order.pin(self.value)
-                self.coming = links.swap(self.value, "dp", self.bit)
-
-            def wait(self):
-                (coming,) = order.pin(self.coming)
-                self.value = self.value + coming
-                self.bit *= 2
-
-        def spread_of(attn_sum, ff_sum):
-            half = ff_sum.shape[0] // 2
-            return Spread(
-                links,
-                [
-                    jnp.concatenate([ff_sum[:half], attn_sum[:middle]], axis=0),
-                    jnp.concatenate([ff_sum[half:], attn_sum[middle:]], axis=0),
-                ],
-            )
-
-        small = Small(small)
-        small.start()
-        ff1_sum = r_ff1.wait_mp()
-        r_ff0.wait_all()
-        r_ff0.start_mp()
-        small.wait()
-        small.start()
-        attn1_sum = r_attn1.wait_mp()
-        back_1 = spread_of(attn1_sum, ff1_sum)
-        back_1.start()
+        small = jnp.concatenate([band0, band1, norms], axis=0).astype(BF)
+
+        def small_start(bit):
+            (here,) = order.pin(small)
+            return here, links.swap(here, DP, bit)
+
+        def small_wait(pair):
+            (coming,) = order.pin(pair[1])
+            return (pair[0].astype(F32) + coming.astype(F32)).astype(BF)
+
+        bits = [1 << k for k in range(dp.bit_length() - 1)]
+        pair = small_start(bits[0])
         r_attn0.wait()
+        small = small_wait(pair)
         r_attn0.start()
-        small.wait()
-        while small.bit < dp:
-            small.start()
-            small.wait()
-        (band1,) = order.pin(band1)
-        (low_small,) = order.pin(jnp.concatenate([small.value, band1], axis=0).astype(BF))
-        small_parts = [links.swap(low_small, "mp", p) for p in range(1, mp)]
-        back_1.wait()
-        back_1.start()
-        r_attn0.wait_all()
-        r_attn0.start_mp()
-        back_1.wait_all()
-        back_1.start_cores()
-        ff0_sum = r_ff0.wait_mp()
-        full_1 = back_1.wait_cores()
-        attn0_sum = r_attn0.wait_mp()
-        back_0 = spread_of(attn0_sum, ff0_sum)
-        back_0.start()
+        pair = small_start(bits[1])
+        sum1 = mp1.wait()
+        (sum1,) = order.pin(sum1)
+        full1 = lax.all_gather(sum1, DP, axis=0, tiled=False)
+        attn0_sum = r_attn0.wait_all()
+        small = small_wait(pair)
+        for bit in bits[2:]:
+            small = small_wait(small_start(bit))
+        up0, down0 = wide0.wait()
+        mp0 = ReduceMp(links, attn0_sum + [up0, down0], None)
+        (small,) = order.pin(small)
+        small_parts = [links.swap(small, "mp", p) for p in range(1, mp)]
+        (full1,) = order.pin(full1)
 
         def finish(layer, full, previous):
-            full = [part.reshape(dp // 2, -1, width) for part in full]
-            if middle % 16 == 0:
+            if in_blocks:
                 return finish_layer(order, layer, layers, place, full, channels, hidden, attn_rows, previous)
-            owner = jnp.bitwise_xor(jnp.arange(dp), dp_index)
-            part_a, part_b = [
-                jnp.stack([full[k], full[2 + k]], axis=1).reshape(dp, -1, width) for k in range(2)
-            ]
+            if len(full) == 1:
+                owner = jnp.arange(dp)
+                attn_part, up_part, down_part = jnp.split(full[0], [attn_rows, attn_rows + ff_rows], axis=1)
+            else:
+                owner = jnp.bitwise_xor(jnp.arange(dp), dp_index)
+                part_a, part_b = [
+                    jnp.stack([full[k], full[2 + k]], axis=1).reshape(dp, -1, width) for k in range(2)
+                ]
+                attn_part = jnp.concatenate([part_a[:, ff_rows:], part_b[:, ff_rows:]], axis=1)
+                up_part, down_part = part_a[:, :ff_rows], part_b[:, :ff_rows]
 
             def rows_of(value):
                 return value.reshape(-1, width)
@@ -970,14 +1061,13 @@
                 spots = (owner[:, None] * count + jnp.arange(count)[None, :]).reshape(-1, 1)
                 return (spots == jnp.arange(dp * count)[None, :]).astype(BF)
 
-            attn_part = rows_of(jnp.concatenate([part_a[:, ff_rows:], part_b[:, ff_rows:]], axis=1))
             attn_place = place_of(attn_rows).reshape(-1, 4, channels)
             ff_place = place_of(ff_rows)
             values = (
-                jnp.einsum("pd,pmc->mdc", attn_part, attn_place[:, :3], preferred_element_type=F32),
-                dot_tn(attn_place[:, 3], attn_part),
-                dot_tn(rows_of(part_a[:, :ff_rows]), ff_place),
-                dot_tn(ff_place, rows_of(part_b[:, :ff_rows])),
+                jnp.einsum("pd,pmc->mcd", rows_of(attn_part), attn_place[:, :3], preferred_element_type=F32),
+                dot_tn(attn_place[:, 3], rows_of(attn_part)),
+                dot_tn(rows_of(up_part), ff_place),
+                dot_tn(ff_place, rows_of(down_part)),
             )
             if previous is None:
                 previous = [jnp.zeros((layers,) + value.shape, F32) for value in values]
@@ -986,34 +1076,53 @@
                 for kept, value in zip(previous, values)
             ]
 
-        big = finish(1, full_1, None)
-        back_0.wait()
-        back_0.start()
-        small_parts = [low_small] + order.pin(*small_parts)
-        small_all = jnp.stack([part.astype(F32) for part in small_parts])
-        pairs = small_all[:, block:-block]
+        big = finish(1, [full1], None)
+        sum0 = mp0.wait()
+        spread0 = Spread(
+            links,
+            [
+                jnp.concatenate([sum0[attn_rows : attn_rows + ff_rows], sum0[:middle]], axis=0),
+                jnp.concatenate([sum0[attn_rows + ff_rows :], sum0[middle:attn_rows]], axis=0),
+            ],
+        )
+        spread0.start()
+        small_parts = [small] + order.pin(*small_parts)
+        spread0.wait()
+        spread0.start()
+        small_all = jnp.stack(small_parts)
+        pairs = small_all[:, 2 * block :].astype(F32)
         while pairs.shape[0] > 1:
             pairs = pairs[0::2] + pairs[1::2]
         norm_sum = pairs[0].reshape(layers, 4, width)
-        bands = jnp.stack([small_all[:, :block], small_all[:, -block:]])
-        band_sum = jnp.take(bands, jnp.bitwise_xor(jnp.arange(mp), mp_index), axis=1)
-        band_sum = band_sum.reshape(layers, mp * block, window)
-        back_0.wait_all()
-        back_0.start_cores()
-        big = finish(0, back_0.wait_cores(), big)
+        bands = jnp.take(
+            small_all[:, : 2 * block].astype(F32), jnp.bitwise_xor(jnp.arange(mp), mp_index), axis=0
+        ).reshape(mp, layers, block, window)
+        band_sum = jnp.transpose(bands, (1, 0, 2, 3)).reshape(layers, mp * block, window)
+        spread0.wait_all()
+        spread0.start_cores()
+        full0 = [part.reshape(groups, -1, width) for part in spread0.wait_cores()]
+        qkv_out, out_out, up_out, down_out = finish(0, full0, big)
         return (
-            (output.reshape(tokens.shape), grad4.reshape(tokens.shape))
-            + tuple(big)
-            + (norm_sum[:, :2], norm_sum[:, 2:], band_sum)
+            output.reshape(tokens.shape),
+            grad4.reshape(tokens.shape),
+            jnp.transpose(qkv_out, (0, 1, 3, 2)),
+            out_out,
+            up_out,
+            down_out,
+            norm_sum[:, :2],
+            norm_sum[:, 2:],
+            band_sum,
         )
 
     return shards
 
 
 def solution(mesh):
+    dp, mp = mesh.shape["dp"], mesh.shape["mp"]
+    inner = Mesh(mesh.devices.reshape(dp // 2, 2, mp), DP + ("mp",))
     placed = (
-        P("dp", "mp", None),
-        P("dp", None),
+        P(DP, "mp", None),
+        P(DP, None),
         P(None, None, None, "mp"),
         P(None, "mp", None),
         P(None, None, "mp"),
@@ -1021,15 +1130,15 @@
         P(),
         P(),
         P(),
-        P("dp", "mp", None),
+        P(DP, "mp", None),
     )
     return jax.shard_map(
-        make_shards(mesh.shape["dp"], mesh.shape["mp"]),
-        mesh=mesh,
+        make_shards(dp, mp),
+        mesh=inner,
         in_specs=placed,
         out_specs=(
-            P("dp", "mp", None),
-            P("dp", "mp", None),
+            P(DP, "mp", None),
+            P(DP, "mp", None),
             P(None, None, None, "mp"),
             P(None, "mp", None),
             P(None, None, "mp"),

time: 761 us -> 626 us (0.82)
  local copies, waits for them, and re-layouts: 115 us -> 51.1 us
  other arithmetic: 113 us -> 68.1 us
  starting transfers between devices: 97.4 us -> 64.8 us
  Pallas kernels: 170 us -> 179 us
    psum x1 -> x0, waiting for transfers between devices: 46 us -> none  [shards(): band1 = lax.psum(band1, 'dp')]
    ppermute x72 -> x50, waiting for transfers between devices: 124 us -> 166 us  [swap(): return lax.ppermute(value, axis, [(i, i ^ bit) for i in range(size)])]
    ppermute x2, waiting for transfers between devices: 47.2 us -> 12.4 us  [backward_halo(): return lax.ppermute(value, 'mp', [(i + 1, i) for i in range(mp - 1)])]
    gather x6 -> x1, local copies, waits for them, and re-layouts: 36.4 us -> 2.32 us  [shards(): jnp.take(small_all[:, :2 * block].astype(F32), jnp.bitwise_xor(jnp.arange...]
    ppermute x2, waiting for transfers between devices: 19.2 us -> 51.9 us  [forward_halo(): return lax.ppermute(value, 'mp', [(i, i + 1) for i in range(mp - 1)])]
    ppermute x72 -> x50, starting transfers between devices: 81.9 us -> 52.8 us  [swap(): return lax.ppermute(value, axis, [(i, i ^ bit) for i in range(size)])]
    convert_element_type x4 -> x9, other arithmetic: 4.95 us -> 22.9 us  [the longest x2 14.2 us: wait_cores(): total = (self.own.astype(F32) + coming.astype(F32)).astype(BF)]
    unnamed x222 -> x188, local copies, waits for them, and re-layouts: 36.6 us -> 23 us
  transfers between devices with their start and end apart: 78 -> 58, of which waited for: 25 -> 28; matrix products, arithmetic and copies ran while one was open for 22% -> 13% of each run, Pallas kernels for 16% -> 23%
where the time goes in v4:
time: 626 us; the launch traced here: 620 us
  waiting for transfers between devices  237 us (38%)
  Pallas kernels  179 us (29%)
  other arithmetic  68.1 us (11%)
  starting transfers between devices  64.8 us (10%)
  local copies, waits for them, and re-layouts  51.1 us (8%)
  between operations  15 us (2%)
    pallas_call x14, Pallas kernels, run(): *results, order.token = kernel(*operands, order.token)  167 us
    ppermute x50, waiting for transfers between devices, swap(): return lax.ppermute(value, axis, [(i, i ^ bit) for i in range(size)])  166 us
    ppermute x50, starting transfers between devices, swap(): return lax.ppermute(value, axis, [(i, i ^ bit) for i in range(size)])  52.8 us
    ppermute x2, waiting for transfers between devices, forward_halo(): return lax.ppermute(value, 'mp', [(i, i + 1) for i in range(mp - 1)])  51.9 us
    another operation x12, other arithmetic, wait(): self.values[k] = jnp.stack([self.values[k], coming[k]], axis=place)  24.3 us
    unnamed x188, local copies, waits for them, and re-layouts  23 us
    convert_element_type x2, other arithmetic, wait_cores(): total = (self.own.astype(F32) + coming.astype(F32)).astype(BF)  14.2 us
  transfers between devices with their start and end apart: 58, of which 28 were waited for; matrix products, arithmetic and copies ran while one was open for 13% of the time, Pallas kernels for 23%

profile of v4, /device:TPU:9, one launch (start us, length us, event | category | flops | bytes accessed | tf_op | source)
XLA Modules:
  0.0 620.4 jit_solution(7836934407815490229)
XLA Ops:
  10.3 2.5 collective-permute-start.2
  19.9 2.7 enter.1
  23.3 2.4 collective-permute-done.3.refs_2_
  44.8 12.6 %collective-permute-done.10.refs_2_ = bf16[192,768]{1,0:T(8,128)(2,1)S(1)} collective-permute-done((bf16[192,768]{1,0:T(8,128)(2,1)S(1)}, bf16[192,768]{1,0:T(8,128)(2,1)S(1)}, u32[]{:S(2)}, u32[]{:S(2)}) %collective-permute-start.10) | collective-permute-done | bytes 294944 | tf_op jit(solution)/shard_map/ppermute | solution.py:682
  57.4 12.2 %collective-permute-done.9.refs_1_ = bf16[192,768]{1,0:T(8,128)(2,1)S(1)} collective-permute-done((bf16[192,768]{1,0:T(8,128)(2,1)S(1)}, bf16[192,768]{1,0:T(8,128)(2,1)S(1)}, u32[]{:S(2)}, u32[]{:S(2)}) %collective-permute-start.9) | collective-permute-done | bytes 294944 | tf_op jit(solution)/shard_map/ppermute | solution.py:682
  81.6 16.2 %collective-permute-done.13.refs_0_ = bf16[4,96,768]{2,1,0:T(8,128)(2,1)S(1)} collective-permute-done((bf16[4,96,768]{2,1,0:T(8,128)(2,1)}, bf16[4,96,768]{2,1,0:T(8,128)(2,1)S(1)}, u32[]{:S(2)}, u32[]{:S(2)}) %collective-permute-start.13) | collective-permute-done | bytes 589856 | tf_op jit(solution)/shard_map/ppermute | solution.py:682
  103.6 3.5 collective-permute-start
  110.7 35.2 %collective-permute-done.refs_0_ = bf16[512,768]{1,0:T(8,128)(2,1)S(1)} collective-permute-done((bf16[512,768]{1,0:T(8,128)(2,1)}, bf16[512,768]{1,0:T(8,128)(2,1)S(1)}, u32[]{:S(2)}, u32[]{:S(2)}) %collective-permute-start) | collective-permute-done | bytes 786464 | tf_op jit(solution)/shard_map/ppermute | solution.py:898
  146.7 14.7 %attn_fwd.2 = (bf16[512,768]{1,0:T(8,128)(2,1)}, bf16[512,768]{1,0:T(8,128)(2,1)}, bf16[512,768]{1,0:T(8,128)(2,1)}, bf16[1024,768]{1,0:T(8,128)(2,1)}, bf16[102...) custom-call(s32[6]{0:T(128)} %stack.207.refs_0_, ...), custom_call_target="tpu_custom_call", output_to_operand_aliasing={{10}: (13, {})} | custom-call | tf_op jit(solution)/shard_map/attn_fwd/pallas_call | solution.py:74
  162.7 3.0 pad_maximum_fusion.1.refs_1_
  165.7 3.1 pad_maximum_fusion.refs_0_
  170.0 8.2 %collective-permute-done.17.refs_0_ = bf16[2,2,4,96,768]{4,3,2,1,0:T(8,128)(2,1)S(1)} collective-permute-done((bf16[2,2,4,96,768]{4,3,2,1,0:T(8,128)(2,1)}, bf16[2,2,4,96,768]{4,3,2,1,0:T(8,128)(2,1)S(1)}, u32[]{:S(2)}, u32[]{:S(2)}) %collective-permute-start.17) | collective-permute-done | bytes 2359328 | tf_op jit(solution)/shard_map/ppermute | solution.py:682
  179.6 13.6 %ff_fwd.1 = (bf16[512,3072]{1,0:T(8,128)(2,1)}, bf16[512,3072]{1,0:T(8,128)(2,1)}, f32[512,768]{1,0:T(8,128)}, bf16[512,768]{1,0:T(8,128)(2,1)}, s32[8,128]{1,0:T(8,128)}) custom-call(f32[512,768]{1,0:T(8,128)} %get-tuple-element.323.refs_0_.refs_1_, bf16[512,768]{1,0:T(8,128)(2,1)} %get-tuple-element.324.refs_1_.refs_2_, ...), custom_call_target="tpu_custom_call", output_to_operand_aliasing={{4}: (8, {})} | custom-call | tf_op jit(solution)/shard_map/ff_fwd/pallas_call | solution.py:74
  193.2 4.3 collective-permute-start.19
  197.6 16.8 %collective-permute-done.19.refs_0_ = bf16[512,768]{1,0:T(8,128)(2,1)S(1)} collective-permute-done((bf16[512,768]{1,0:T(8,128)(2,1)}, bf16[512,768]{1,0:T(8,128)(2,1)S(1)}, u32[]{:S(2)}, u32[]{:S(2)}) %collective-permute-start.19) | collective-permute-done | bytes 786464 | tf_op jit(solution)/shard_map/ppermute | solution.py:898
  215.2 14.2 %attn_fwd.3 = (bf16[512,768]{1,0:T(8,128)(2,1)}, bf16[512,768]{1,0:T(8,128)(2,1)}, bf16[512,768]{1,0:T(8,128)(2,1)}, bf16[1024,768]{1,0:T(8,128)(2,1)}, bf16[102...) custom-call(s32[6]{0:T(128)} %stack.207.refs_0_, ...), custom_call_target="tpu_custom_call", output_to_operand_aliasing={{10}: (10, {})} | custom-call | tf_op jit(solution)/shard_map/attn_fwd/pallas_call | solution.py:74
  229.5 13.6 %ff_bwd.4 = (bf16[4,2,384,768]{3,2,1,0:T(8,128)(2,1)}, f32[512,768]{1,0:T(8,128)}, f32[512,768]{1,0:T(8,128)}, s32[8,128]{1,0:T(8,128)}) custom-call(s32[6]{0:T(128)} %stack.207.refs_0_, f32[512,768]{1,0:T(8,128)} %get-tuple-element.347.refs_1_, bf16[512,768]{1,0:T(8,128)(2,1)} %get-tuple-element.348.refs_2_, ...), custom_call_target="tpu_custom_call", output_to_operand_aliasing={{3}: (7, {})} | custom-call | tf_op jit(solution)/shard_map/ff_bwd/pallas_call | solution.py:74
  244.0 16.9 %ff_bwd.5 = (bf16[4,2,384,768]{3,2,1,0:T(8,128)(2,1)}, f32[512,768]{1,0:T(8,128)}, bf16[512,768]{1,0:T(8,128)(2,1)}, f32[1,768]{1,0:T(1,128)}, f32[1,768]{1,0:T(...) custom-call(s32[6]{0:T(128)} %stack.207.refs_0_, ...), custom_call_target="tpu_custom_call", output_to_operand_aliasing={{6}: (9, {})} | custom-call | tf_op jit(solution)/shard_map/ff_bwd/pallas_call | solution.py:74
  260.9 7.1 %add_convert_fusion.1.refs_0_ = bf16[4,2,384,768]{3,2,1,0:T(8,128)(2,1)} fusion(bf16[4,2,384,768]{3,2,1,0:T(8,128)(2,1)} %get-tuple-element.368, bf16[4,2,384,768]{3,2,1,0:T(8,128)(2,1)} %get-tuple-element.365), kind=kLoop, calls=%fused_computation.2 | loop fusion | flops 9437184 | bytes 14155776 | tf_op jit(solution)/shard_map/convert_element_type | solution.py:799
  268.1 15.8 %attn_bwd.2 = (bf16[512,768]{1,0:T(8,128)(2,1)}, bf16[1024,768]{1,0:T(8,128)(2,1)}, bf16[1024,768]{1,0:T(8,128)(2,1)}, f32[256,256]{1,0:T(8,128)}, f32[512,768]{...) custom-call(s32[6]{0:T(128)} %stack.207.refs_0_, ...), custom_call_target="tpu_custom_call", output_to_operand_aliasing={{6}: (10, {})} | custom-call | tf_op jit(solution)/shard_map/attn_bwd/pallas_call | solution.py:74
  285.8 12.2 %attn_wgrad.2 = (bf16[4,192,768]{2,1,0:T(8,128)(2,1)}, bf16[4,192,768]{2,1,0:T(8,128)(2,1)}, bf16[4,192,768]{2,1,0:T(8,128)(2,1)}, bf16[4,192,768]{2,1,0:T(8,128)(2,1)}, s32[8,128]{1,0:T(8,128)}) custom-call(s32[6]{0:T(128)} %stack.207.refs_0_, bf16[512,768]{1,0:T(8,128)(2,1)} %get-tuple-element.375.refs_1_, ...), custom_call_target="tpu_custom_call", output_to_operand_aliasing={{4}: (8, {})} | custom-call | tf_op jit(solution)/shard_map/attn_wgrad/pallas_call | solution.py:74
  298.0 7.7 %collective-permute-done.21.refs_0_ = bf16[512,768]{1,0:T(8,128)(2,1)S(1)} collective-permute-done((bf16[512,768]{1,0:T(8,128)(2,1)}, bf16[512,768]{1,0:T(8,128)(2,1)S(1)}, u32[]{:S(2)}, u32[]{:S(2)}) %collective-permute-start.21) | collective-permute-done | bytes 786464 | tf_op jit(solution)/shard_map/ppermute | solution.py:901
  307.2 4.9 leave.2
  317.7 11.8 %ff_bwd.6 = (bf16[4,2,384,768]{3,2,1,0:T(8,128)(2,1)}, f32[512,768]{1,0:T(8,128)}, s32[8,128]{1,0:T(8,128)}) custom-call(s32[6]{0:T(128)} %stack.207.refs_0_, f32[512,768]{1,0:T(8,128)} %get-tuple-element.323.refs_0_.refs_1_, bf16[512,768]{1,0:T(8,128)(2,1)} %get-tuple-element.324.refs_1_.refs_2_, ...), custom_call_target="tpu_custom_call", output_to_operand_aliasing={{2}: (9, {})} | custom-call | tf_op jit(solution)/shard_map/ff_bwd/pallas_call | solution.py:74
  330.0 14.4 %ff_bwd.7 = (bf16[4,2,384,768]{3,2,1,0:T(8,128)(2,1)}, f32[512,768]{1,0:T(8,128)}, bf16[512,768]{1,0:T(8,128)(2,1)}, f32[1,768]{1,0:T(1,128)}, f32[1,768]{1,0:T(1,128)}, /*index=5*/s32[8,128]{1,0:T(8,128)}) custom-call(s32[6]{0:T(128)} %stack.207.refs_0_, f32[512,768]{1,0:T(8,128)} %get-tuple-element.323.refs_0_.refs_1_, ...), custom_call_target="tpu_custom_call", output_to_operand_aliasing={{5}: (10, {})} | custom-call | tf_op jit(solution)/shard_map/ff_bwd/pallas_call | solution.py:74
  344.4 7.1 %add_convert_fusion.refs_0_ = bf16[4,2,384,768]{3,2,1,0:T(8,128)(2,1)} fusion(bf16[4,2,384,768]{3,2,1,0:T(8,128)(2,1)} %get-tuple-element.416, bf16[4,2,384,768]{3,2,1,0:T(8,128)(2,1)} %get-tuple-element.413), kind=kLoop, calls=%fused_computation.1 | loop fusion | flops 9437184 | bytes 14155776 | tf_op jit(solution)/shard_map/convert_element_type | solution.py:799
  353.4 21.2 %collective-permute-done.24.refs_0_ = bf16[2,4,48,768]{3,2,1,0:T(8,128)(2,1)S(1)} collective-permute-done((bf16[2,4,48,768]{3,2,1,0:T(8,128)(2,1)}, bf16[2,4,48,768]{3,2,1,0:T(8,128)(2,1)S(1)}, u32[]{:S(2)}, u32[]{:S(2)}) %collective-permute-start.24) | collective-permute-done | bytes 589856 | tf_op jit(solution)/shard_map/ppermute | solution.py:682
  381.9 15.6 %attn_bwd.3 = (bf16[512,768]{1,0:T(8,128)(2,1)}, bf16[1024,768]{1,0:T(8,128)(2,1)}, bf16[1024,768]{1,0:T(8,128)(2,1)}, f32[256,256]{1,0:T(8,128)}, f32[512,768]{...) custom-call(s32[6]{0:T(128)} %stack.207.refs_0_, ...), custom_call_target="tpu_custom_call", output_to_operand_aliasing={{6}: (13, {})} | custom-call | tf_op jit(solution)/shard_map/attn_bwd/pallas_call | solution.py:74
  398.4 11.8 %attn_wgrad.3 = (bf16[4,192,768]{2,1,0:T(8,128)(2,1)}, bf16[4,192,768]{2,1,0:T(8,128)(2,1)}, bf16[4,192,768]{2,1,0:T(8,128)(2,1)}, bf16[4,192,768]{2,1,0:T(8,128)(2,1)}, s32[8,128]{1,0:T(8,128)}) custom-call(s32[6]{0:T(128)} %stack.207.refs_0_, bf16[512,768]{1,0:T(8,128)(2,1)} %get-tuple-element.430.refs_1_, ...), custom_call_target="tpu_custom_call", output_to_operand_aliasing={{4}: (8, {})} | custom-call | tf_op jit(solution)/shard_map/attn_wgrad/pallas_call | solution.py:74
  410.2 2.4 collective-permute-start.30
  429.0 4.8 collective-permute-done.29.refs_0_
  433.8 4.9 leave.3
  442.0 2.6 collective-permute-start.38
  450.1 11.1 %collective-permute-done.37.refs_0_ = bf16[288,768]{1,0:T(8,128)(2,1)} collective-permute-done((bf16[288,768]{1,0:T(8,128)(2,1)}, bf16[288,768]{1,0:T(8,128)(2,1)}, u32[]{:S(2)}, u32[]{:S(2)}) %collective-permute-start.37) | collective-permute-done | bytes 442400 | tf_op jit(solution)/shard_map/ppermute | solution.py:682
  461.2 11.9 %collective-permute-done.38.refs_1_ = bf16[288,768]{1,0:T(8,128)(2,1)} collective-permute-done((bf16[288,768]{1,0:T(8,128)(2,1)}, bf16[288,768]{1,0:T(8,128)(2,1)}, u32[]{:S(2)}, u32[]{:S(2)}) %collective-permute-start.38) | collective-permute-done | bytes 442400 | tf_op jit(solution)/shard_map/ppermute | solution.py:682
  473.1 10.4 %collective-permute-done.39.refs_2_ = bf16[288,768]{1,0:T(8,128)(2,1)} collective-permute-done((bf16[288,768]{1,0:T(8,128)(2,1)}, bf16[288,768]{1,0:T(8,128)(2,1)}, u32[]{:S(2)}, u32[]{:S(2)}) %collective-permute-start.39) | collective-permute-done | bytes 442400 | tf_op jit(solution)/shard_map/ppermute | solution.py:682
  483.5 2.3 add_convert_fusion.7.refs_0_
  488.6 4.7 collective-permute-done.35.refs_0_
  494.4 7.4 %collective-permute-done.40.refs_0_ = bf16[536,256]{1,0:T(8,128)(2,1)S(1)} collective-permute-done((bf16[536,256]{1,0:T(8,128)(2,1)S(1)}, bf16[536,256]{1,0:T(8,128)(2,1)S(1)}, u32[]{:S(2)}, u32[]{:S(2)}) %collective-permute-start.40) | collective-permute-done | bytes 274464 | tf_op jit(solution)/shard_map/ppermute | solution.py:682
  505.6 4.2 collective-permute-done.41.refs_0_
  513.3 2.8 collective-permute-start.43
  519.6 6.5 %all-gather.7.cloned.1.call-done = bf16[2304,768]{1,0:T(8,128)(2,1)} async-done(((bf16[288,768]{1,0:T(8,128)(2,1)}), bf16[2304,768]{1,0:T(8,128)(2,1)}) %all-gather.7.cloned.1.call-update) | async-done | bytes 3538960 | tf_op jit(solution)/shard_map/all_gather | solution.py:1032
  526.1 6.1 finish.2
  533.7 28.9 %collective-permute-done.44.refs_2_ = bf16[288,768]{1,0:T(8,128)(2,1)S(1)} collective-permute-done((bf16[288,768]{1,0:T(8,128)(2,1)}, bf16[288,768]{1,0:T(8,128)(2,1)S(1)}, u32[]{:S(2)}, u32[]{:S(2)}) %collective-permute-start.44) | collective-permute-done | bytes 442400 | tf_op jit(solution)/shard_map/ppermute | solution.py:682
  568.5 5.8 collective-permute-done.49.refs_2_
  585.4 2.4 collective-permute-done.50.refs_0_
  592.3 10.6 %collective-permute-start.52 = (bf16[2,2,144,768]{3,2,1,0:T(8,128)(2,1)}, bf16[2,2,144,768]{3,2,1,0:T(8,128)(2,1)S(1)}, u32[]{:S(2)}, u32[]{:S(2)}) collective-permute-start(bf16[2,2,144,768]{3,2,1,0:T(8,128)(2,1)} %get-tuple-element.530), channel_id=1, source_target_pairs={{0,4},{4,0},{8,12},{12,8},{16,20},{20,16},{24,28},{28,24},{1,5},{5... | collective-permute-start | bytes 2654216 | tf_op jit(solution)/shard_map/ppermute | solution.py:682
  607.4 6.3 %finish.3 = (f32[2,3,192,768]{3,2,1,0:T(8,128)}, f32[2,192,768]{2,1,0:T(8,128)}, f32[2,768,768]{2,1,0:T(8,128)}, f32[2,768,768]{2,1,0:T(8,128)}, s32[8,128]{1,0:T(8,128)}) custom-call(s32[6]{0:T(128)} %stack.207.refs_0_, bf16[4,144,768]{2,1,0:T(8,128)(2,1)} %bitcast.250, ...), custom_call_target="tpu_custom_call", output_to_operand_aliasing={{0}: (5, {}), {1}: (6, {}), {2}: (7, {}), {3}: (8, {}), {4}... | custom-call | tf_op jit(solution)/shard_map/finish/pallas_call | solution.py:640
  (445 shorter events, 144.2 us)
Async XLA Ops:
  7.2 190.4 %all-gather.5.cloned.1.call-start = ((), (), s32[]{:S(2)}) async-start(), calls=%async_computation.2 | async-start | bytes 14598144 | tf_op jit(solution)/shard_map/all_gather | solution.py:926
  10.3 13.0 %collective-permute-start.1 = (bf16[96,768]{1,0:T(8,128)(2,1)}, bf16[96,768]{1,0:T(8,128)(2,1)S(1)}, u32[]{:S(2)}, u32[]{:S(2)}) collective-permute-start(bf16[96,768]{1,0:T(8,128)(2,1)} %get-tuple-element.283), channel_id=1, source_target_pairs={{0,1},{1,0},{2,3},{3,2},{4,5},{5,4},{6,7},{7,6},{8,9},{9,8},{10,11... | collective-permute-start | bytes 442376 | tf_op jit(solution)/shard_map/ppermute | solution.py:682
  10.3 13.0 %collective-permute-start.2 = (bf16[96,768]{1,0:T(8,128)(2,1)}, bf16[96,768]{1,0:T(8,128)(2,1)S(1)}, u32[]{:S(2)}, u32[]{:S(2)}) collective-permute-start(bf16[96,768]{1,0:T(8,128)(2,1)} %get-tuple-element.283), channel_id=1, source_target_pairs={{0,2},{1,3},{2,0},{3,1},{4,6},{5,7},{6,4},{7,5},{8,10},{9,11},{10,... | collective-permute-start | bytes 442376 | tf_op jit(solution)/shard_map/ppermute | solution.py:682
  12.8 12.9 %collective-permute-start.3 = (bf16[96,768]{1,0:T(8,128)(2,1)}, bf16[96,768]{1,0:T(8,128)(2,1)S(1)}, u32[]{:S(2)}, u32[]{:S(2)}) collective-permute-start(bf16[96,768]{1,0:T(8,128)(2,1)} %get-tuple-element.283), channel_id=1, source_target_pairs={{0,3},{1,2},{2,1},{3,0},{4,7},{5,6},{6,5},{7,4},{8,11},{9,10},{10,... | collective-permute-start | bytes 442376 | tf_op jit(solution)/shard_map/ppermute | solution.py:682
  30.8 386.7 %reduce-scatter.7.cloned.1.call-start = ((), (), s32[]{:S(2)}) async-start(), calls=%async_computation.4 | async-start | bytes 5898240
  33.4 24.0 %collective-permute-start.10 = (bf16[192,768]{1,0:T(8,128)(2,1)S(1)}, bf16[192,768]{1,0:T(8,128)(2,1)S(1)}, u32[]{:S(2)}, u32[]{:S(2)}) collective-permute-start(bf16[192,768]{1,0:T(8,128)(2,1)S(1)} %copy-done.24), channel_id=1, source_target_pairs={{0,3},{1,2},{2,1},{3,0},{4,7},{5,6},{6,5},{7,4},{8,11},{9,10},{10,... | collective-permute-start | bytes 884744 | tf_op jit(solution)/shard_map/ppermute | solution.py:682
  34.8 22.5 %collective-permute-start.8 = (bf16[192,768]{1,0:T(8,128)(2,1)S(1)}, bf16[192,768]{1,0:T(8,128)(2,1)S(1)}, u32[]{:S(2)}, u32[]{:S(2)}) collective-permute-start(bf16[192,768]{1,0:T(8,128)(2,1)S(1)} %copy-done.24), channel_id=1, source_target_pairs={{0,1},{1,0},{2,3},{3,2},{4,5},{5,4},{6,7},{7,6},{8,9},{9,8},{10,11... | collective-permute-start | bytes 884744 | tf_op jit(solution)/shard_map/ppermute | solution.py:682
  35.5 34.1 %collective-permute-start.9 = (bf16[192,768]{1,0:T(8,128)(2,1)S(1)}, bf16[192,768]{1,0:T(8,128)(2,1)S(1)}, u32[]{:S(2)}, u32[]{:S(2)}) collective-permute-start(bf16[192,768]{1,0:T(8,128)(2,1)S(1)} %copy-done.24), channel_id=1, source_target_pairs={{0,2},{1,3},{2,0},{3,1},{4,6},{5,7},{6,4},{7,5},{8,10},{9,11},{10,... | collective-permute-start | bytes 884744 | tf_op jit(solution)/shard_map/ppermute | solution.py:682
  43.2 32.4 %collective-permute-start.6 = (bf16[2,4,48,768]{3,2,1,0:T(8,128)(2,1)}, bf16[2,4,48,768]{3,2,1,0:T(8,128)(2,1)S(1)}, u32[]{:S(2)}, u32[]{:S(2)}) collective-permute-start(bf16[2,4,48,768]{3,2,1,0:T(8,128)(2,1)} %get-tuple-element.297), channel_id=1, source_target_pairs={{0,16},{4,20},{8,24},{12,28},{16,0},{20,4},{24,8},{28,12},{1,17},{... | collective-permute-start | bytes 1769480 | tf_op jit(solution)/shard_map/ppermute | solution.py:682
  44.4 31.2 %collective-permute-start.7 = (bf16[2,4,48,768]{3,2,1,0:T(8,128)(2,1)}, bf16[2,4,48,768]{3,2,1,0:T(8,128)(2,1)S(1)}, u32[]{:S(2)}, u32[]{:S(2)}) collective-permute-start(bf16[2,4,48,768]{3,2,1,0:T(8,128)(2,1)} %get-tuple-element.298), channel_id=1, source_target_pairs={{0,8},{4,12},{8,0},{12,4},{16,24},{20,28},{24,16},{28,20},{1,9},{5... | collective-permute-start | bytes 1769480 | tf_op jit(solution)/shard_map/ppermute | solution.py:682
  75.1 22.6 %collective-permute-start.13 = (bf16[4,96,768]{2,1,0:T(8,128)(2,1)}, bf16[4,96,768]{2,1,0:T(8,128)(2,1)S(1)}, u32[]{:S(2)}, u32[]{:S(2)}) collective-permute-start(bf16[4,96,768]{2,1,0:T(8,128)(2,1)} %get-tuple-element.311), channel_id=1, source_target_pairs={{0,8},{4,12},{8,0},{12,4},{16,24},{20,28},{24,16},{28,20},{1,9},{5... | collective-permute-start | bytes 1769480 | tf_op jit(solution)/shard_map/ppermute | solution.py:682
  75.4 22.4 %collective-permute-start.14 = (bf16[4,96,768]{2,1,0:T(8,128)(2,1)}, bf16[4,96,768]{2,1,0:T(8,128)(2,1)}, u32[]{:S(2)}, u32[]{:S(2)}) collective-permute-start(bf16[4,96,768]{2,1,0:T(8,128)(2,1)} %get-tuple-element.312), channel_id=1, source_target_pairs={{0,16},{4,20},{8,24},{12,28},{16,0},{20,4},{24,8},{28,12},{1,17},{... | collective-permute-start | bytes 1769480 | tf_op jit(solution)/shard_map/ppermute | solution.py:682
  80.0 29.2 %collective-permute-start.11 = (bf16[2,2,4,48,768]{4,3,2,1,0:T(8,128)(2,1)}, bf16[2,2,4,48,768]{4,3,2,1,0:T(8,128)(2,1)S(1)}, u32[]{:S(2)}, u32[]{:S(2)}) collective-permute-start(bf16[2,2,4,48,768]{4,3,2,1,0:T(8,128)(2,1)} %get-tuple-element.309), channel_id=1, source_target_pairs={{0,4},{4,0},{8,12},{12,8},{16,20},{20,16},{24,28},{28,24},{1,5},{5... | collective-permute-start | bytes 3538952 | tf_op jit(solution)/shard_map/ppermute | solution.py:682
  81.6 27.7 %collective-permute-start.12 = (bf16[2,2,4,48,768]{4,3,2,1,0:T(8,128)(2,1)}, bf16[2,2,4,48,768]{4,3,2,1,0:T(8,128)(2,1)S(1)}, u32[]{:S(2)}, u32[]{:S(2)}) collective-permute-start(bf16[2,2,4,48,768]{4,3,2,1,0:T(8,128)(2,1)} %get-tuple-element.310), channel_id=1, source_target_pairs={{0,4},{4,0},{8,12},{12,8},{16,20},{20,16},{24,28},{28,24},{1,5},{5... | collective-permute-start | bytes 3538952 | tf_op jit(solution)/shard_map/ppermute | solution.py:682
  102.0 59.4 %collective-permute-start.15 = (bf16[2,4,96,768]{3,2,1,0:T(8,128)(2,1)}, bf16[2,4,96,768]{3,2,1,0:T(8,128)(2,1)}, u32[]{:S(2)}, u32[]{:S(2)}) collective-permute-start(bf16[2,4,96,768]{3,2,1,0:T(8,128)(2,1)} %get-tuple-element.325), channel_id=1, source_target_pairs={{0,16},{4,20},{8,24},{12,28},{16,0},{20,4},{24,8},{28,12},{1,17},{... | collective-permute-start | bytes 3538952 | tf_op jit(solution)/shard_map/ppermute | solution.py:682
  103.3 58.1 %collective-permute-start.16 = (bf16[2,4,96,768]{3,2,1,0:T(8,128)(2,1)}, bf16[2,4,96,768]{3,2,1,0:T(8,128)(2,1)}, u32[]{:S(2)}, u32[]{:S(2)}) collective-permute-start(bf16[2,4,96,768]{3,2,1,0:T(8,128)(2,1)} %get-tuple-element.326), channel_id=1, source_target_pairs={{0,8},{4,12},{8,0},{12,4},{16,24},{20,28},{24,16},{28,20},{1,9},{5... | collective-permute-start | bytes 3538952 | tf_op jit(solution)/shard_map/ppermute | solution.py:682
  103.6 42.2 %collective-permute-start = (bf16[512,768]{1,0:T(8,128)(2,1)}, bf16[512,768]{1,0:T(8,128)(2,1)S(1)}, u32[]{:S(2)}, u32[]{:S(2)}) collective-permute-start(bf16[512,768]{1,0:T(8,128)(2,1)} %get-tuple-element.282.refs_2_.refs_5_), channel_id=1, source_target_pairs={{0,1},{1,2},{2,3},{4,5},{5,6},{6,7},{8,9},{9,10},{10,11},{12,13},{... | collective-permute-start | bytes 2359304 | tf_op jit(solution)/shard_map/ppermute | solution.py:898
  168.8 9.4 %collective-permute-start.17 = (bf16[2,2,4,96,768]{4,3,2,1,0:T(8,128)(2,1)}, bf16[2,2,4,96,768]{4,3,2,1,0:T(8,128)(2,1)S(1)}, u32[]{:S(2)}, u32[]{:S(2)}) collective-permute-start(bf16[2,2,4,96,768]{4,3,2,1,0:T(8,128)(2,1)} %get-tuple-element.331), channel_id=1, source_target_pairs={{0,4},{4,0},{8,12},{12,8},{16,20},{20,16},{24,28},{28,24},{1,5},{5... | collective-permute-start | bytes 7077896 | tf_op jit(solution)/shard_map/ppermute | solution.py:682
  170.0 8.9 %collective-permute-start.18 = (bf16[2,2,4,96,768]{4,3,2,1,0:T(8,128)(2,1)}, bf16[2,2,4,96,768]{4,3,2,1,0:T(8,128)(2,1)}, u32[]{:S(2)}, u32[]{:S(2)}) collective-permute-start(bf16[2,2,4,96,768]{4,3,2,1,0:T(8,128)(2,1)} %get-tuple-element.332), channel_id=1, source_target_pairs={{0,4},{4,0},{8,12},{12,8},{16,20},{20,16},{24,28},{28,24},{1,5},{5... | collective-permute-start | bytes 7077896 | tf_op jit(solution)/shard_map/ppermute | solution.py:682
  193.2 21.1 %collective-permute-start.19 = (bf16[512,768]{1,0:T(8,128)(2,1)}, bf16[512,768]{1,0:T(8,128)(2,1)S(1)}, u32[]{:S(2)}, u32[]{:S(2)}) collective-permute-start(bf16[512,768]{1,0:T(8,128)(2,1)} %get-tuple-element.340.refs_2_.refs_5_), channel_id=1, source_target_pairs={{0,1},{1,2},{2,3},{4,5},{5,6},{6,7},{8,9},{9,10},{10,11},{12,13},{... | collective-permute-start | bytes 2359304 | tf_op jit(solution)/shard_map/ppermute | solution.py:898
  243.1 17.8 %collective-permute-start.20 = (bf16[4,2,384,768]{3,2,1,0:T(8,128)(2,1)}, bf16[4,2,384,768]{3,2,1,0:T(8,128)(2,1)}, u32[]{:S(2)}, u32[]{:S(2)}) collective-permute-start(bf16[4,2,384,768]{3,2,1,0:T(8,128)(2,1)} %get-tuple-element.366), channel_id=1, source_target_pairs={{0,4},{4,0},{8,12},{12,8},{16,20},{20,16},{24,28},{28,24},{1,5},{5... | collective-permute-start | bytes 14155784 | tf_op jit(solution)/shard_map/ppermute | solution.py:682
  268.1 242.5 %reduce-scatter.9.cloned.1.call-start = ((), (), s32[]{:S(2)}) async-start(), calls=%async_computation.5 | async-start | bytes 5898240
  283.9 21.8 %collective-permute-start.21 = (bf16[512,768]{1,0:T(8,128)(2,1)}, bf16[512,768]{1,0:T(8,128)(2,1)S(1)}, u32[]{:S(2)}, u32[]{:S(2)}) collective-permute-start(bf16[512,768]{1,0:T(8,128)(2,1)} %get-tuple-element.374), channel_id=1, source_target_pairs={{1,0},{2,1},{3,2},{5,4},{6,5},{7,6},{9,8},{10,9},{11,10},{13,12},{... | collective-permute-start | bytes 2359304 | tf_op jit(solution)/shard_map/ppermute | solution.py:901
  329.5 14.9 %collective-permute-start.26 = (bf16[4,2,384,768]{3,2,1,0:T(8,128)(2,1)}, bf16[4,2,384,768]{3,2,1,0:T(8,128)(2,1)}, u32[]{:S(2)}, u32[]{:S(2)}) collective-permute-start(bf16[4,2,384,768]{3,2,1,0:T(8,128)(2,1)} %get-tuple-element.414), channel_id=1, source_target_pairs={{0,4},{4,0},{8,12},{12,8},{16,20},{20,16},{24,28},{28,24},{1,5},{5... | collective-permute-start | bytes 14155784 | tf_op jit(solution)/shard_map/ppermute | solution.py:682
  351.5 174.5 %all-gather.7.cloned.1.call-start = ((), (), s32[]{:S(2)}) async-start(), calls=%async_computation.3 | async-start | bytes 3981312 | tf_op jit(solution)/shard_map/all_gather | solution.py:1032
  351.6 23.0 %collective-permute-start.24 = (bf16[2,4,48,768]{3,2,1,0:T(8,128)(2,1)}, bf16[2,4,48,768]{3,2,1,0:T(8,128)(2,1)S(1)}, u32[]{:S(2)}, u32[]{:S(2)}) collective-permute-start(bf16[2,4,48,768]{3,2,1,0:T(8,128)(2,1)} %get-tuple-element.411), channel_id=1, source_target_pairs={{0,16},{4,20},{8,24},{12,28},{16,0},{20,4},{24,8},{28,12},{1,17},{... | collective-permute-start | bytes 1769480 | tf_op jit(solution)/shard_map/ppermute | solution.py:682
  352.6 23.5 %collective-permute-start.25 = (bf16[2,4,48,768]{3,2,1,0:T(8,128)(2,1)S(1)}, bf16[2,4,48,768]{3,2,1,0:T(8,128)(2,1)S(1)}, u32[]{:S(2)}, u32[]{:S(2)}) collective-permute-start(bf16[2,4,48,768]{3,2,1,0:T(8,128)(2,1)S(1)} %copy-done.46), channel_id=1, source_target_pairs={{0,8},{4,12},{8,0},{12,4},{16,24},{20,28},{24,16},{28,20},{1,9},{5... | collective-permute-start | bytes 1769480 | tf_op jit(solution)/shard_map/ppermute | solution.py:682
  380.6 17.0 %collective-permute-start.27 = (bf16[4,48,768]{2,1,0:T(8,128)(2,1)}, bf16[4,48,768]{2,1,0:T(8,128)(2,1)S(1)}, u32[]{:S(2)}, u32[]{:S(2)}) collective-permute-start(bf16[4,48,768]{2,1,0:T(8,128)(2,1)} %get-tuple-element.425), channel_id=1, source_target_pairs={{0,8},{4,12},{8,0},{12,4},{16,24},{20,28},{24,16},{28,20},{1,9},{5... | collective-permute-start | bytes 884744 | tf_op jit(solution)/shard_map/ppermute | solution.py:682
  381.9 15.7 %collective-permute-start.28 = (bf16[4,48,768]{2,1,0:T(8,128)(2,1)}, bf16[4,48,768]{2,1,0:T(8,128)(2,1)S(1)}, u32[]{:S(2)}, u32[]{:S(2)}) collective-permute-start(bf16[4,48,768]{2,1,0:T(8,128)(2,1)} %get-tuple-element.426), channel_id=1, source_target_pairs={{0,16},{4,20},{8,24},{12,28},{16,0},{20,4},{24,8},{28,12},{1,17},{... | collective-permute-start | bytes 884744 | tf_op jit(solution)/shard_map/ppermute | solution.py:682
  410.2 10.2 %collective-permute-start.30 = (bf16[4,192,768]{2,1,0:T(8,128)(2,1)}, bf16[4,192,768]{2,1,0:T(8,128)(2,1)S(1)}, u32[]{:S(2)}, u32[]{:S(2)}) collective-permute-start(bf16[4,192,768]{2,1,0:T(8,128)(2,1)} %get-tuple-element.439), channel_id=1, source_target_pairs={{0,4},{4,0},{8,12},{12,8},{16,20},{20,16},{24,28},{28,24},{1,5},{5... | collective-permute-start | bytes 3538952 | tf_op jit(solution)/shard_map/ppermute | solution.py:682
  412.6 7.8 %collective-permute-start.31 = (bf16[4,192,768]{2,1,0:T(8,128)(2,1)}, bf16[4,192,768]{2,1,0:T(8,128)(2,1)S(1)}, u32[]{:S(2)}, u32[]{:S(2)}) collective-permute-start(bf16[4,192,768]{2,1,0:T(8,128)(2,1)} %get-tuple-element.440), channel_id=1, source_target_pairs={{0,4},{4,0},{8,12},{12,8},{16,20},{20,16},{24,28},{28,24},{1,5},{5... | collective-permute-start | bytes 3538952 | tf_op jit(solution)/shard_map/ppermute | solution.py:682
  412.6 21.1 %collective-permute-start.29 = (bf16[512,768]{1,0:T(8,128)(2,1)}, bf16[512,768]{1,0:T(8,128)(2,1)}, u32[]{:S(2)}, u32[]{:S(2)}) collective-permute-start(bf16[512,768]{1,0:T(8,128)(2,1)} %get-tuple-element.429), channel_id=1, source_target_pairs={{1,0},{2,1},{3,2},{5,4},{6,5},{7,6},{9,8},{10,9},{11,10},{13,12},{... | collective-permute-start | bytes 2359304 | tf_op jit(solution)/shard_map/ppermute | solution.py:901
  426.0 18.7 %collective-permute-start.32 = (bf16[2,4,48,768]{3,2,1,0:T(8,128)(2,1)}, bf16[2,4,48,768]{3,2,1,0:T(8,128)(2,1)S(1)}, u32[]{:S(2)}, u32[]{:S(2)}) collective-permute-start(bf16[2,4,48,768]{3,2,1,0:T(8,128)(2,1)} %get-tuple-element.456), channel_id=1, source_target_pairs={{0,16},{4,20},{8,24},{12,28},{16,0},{20,4},{24,8},{28,12},{1,17},{... | collective-permute-start | bytes 1769480 | tf_op jit(solution)/shard_map/ppermute | solution.py:682
  427.2 17.5 %collective-permute-start.33 = (bf16[2,4,48,768]{3,2,1,0:T(8,128)(2,1)}, bf16[2,4,48,768]{3,2,1,0:T(8,128)(2,1)S(1)}, u32[]{:S(2)}, u32[]{:S(2)}) collective-permute-start(bf16[2,4,48,768]{3,2,1,0:T(8,128)(2,1)} %get-tuple-element.457), channel_id=1, source_target_pairs={{0,8},{4,12},{8,0},{12,4},{16,24},{20,28},{24,16},{28,20},{1,9},{5... | collective-permute-start | bytes 1769480 | tf_op jit(solution)/shard_map/ppermute | solution.py:682
  442.0 19.2 %collective-permute-start.37 = (bf16[288,768]{1,0:T(8,128)(2,1)}, bf16[288,768]{1,0:T(8,128)(2,1)}, u32[]{:S(2)}, u32[]{:S(2)}) collective-permute-start(bf16[288,768]{1,0:T(8,128)(2,1)} %get-tuple-element.478), channel_id=1, source_target_pairs={{0,1},{1,0},{2,3},{3,2},{4,5},{5,4},{6,7},{7,6},{8,9},{9,8},{10,11... | collective-permute-start | bytes 1327112 | tf_op jit(solution)/shard_map/ppermute | solution.py:682
  442.0 31.1 %collective-permute-start.38 = (bf16[288,768]{1,0:T(8,128)(2,1)}, bf16[288,768]{1,0:T(8,128)(2,1)}, u32[]{:S(2)}, u32[]{:S(2)}) collective-permute-start(bf16[288,768]{1,0:T(8,128)(2,1)} %get-tuple-element.479), channel_id=1, source_target_pairs={{0,2},{1,3},{2,0},{3,1},{4,6},{5,7},{6,4},{7,5},{8,10},{9,11},{10,... | collective-permute-start | bytes 1327112 | tf_op jit(solution)/shard_map/ppermute | solution.py:682
  444.7 38.8 %collective-permute-start.39 = (bf16[288,768]{1,0:T(8,128)(2,1)}, bf16[288,768]{1,0:T(8,128)(2,1)}, u32[]{:S(2)}, u32[]{:S(2)}) collective-permute-start(bf16[288,768]{1,0:T(8,128)(2,1)} %get-tuple-element.480), channel_id=1, source_target_pairs={{0,3},{1,2},{2,1},{3,0},{4,7},{5,6},{6,5},{7,4},{8,11},{9,10},{10,... | collective-permute-start | bytes 1327112 | tf_op jit(solution)/shard_map/ppermute | solution.py:682
  487.8 14.0 %collective-permute-start.40 = (bf16[536,256]{1,0:T(8,128)(2,1)S(1)}, bf16[536,256]{1,0:T(8,128)(2,1)S(1)}, u32[]{:S(2)}, u32[]{:S(2)}) collective-permute-start(bf16[536,256]{1,0:T(8,128)(2,1)S(1)} %copy-done.36), channel_id=1, source_target_pairs={{0,8},{4,12},{8,0},{12,4},{16,24},{20,28},{24,16},{28,20},{1,9},{5... | collective-permute-start | bytes 823304 | tf_op jit(solution)/shard_map/ppermute | solution.py:682
  513.3 18.9 %collective-permute-start.42 = (bf16[288,768]{1,0:T(8,128)(2,1)}, bf16[288,768]{1,0:T(8,128)(2,1)S(1)}, u32[]{:S(2)}, u32[]{:S(2)}) collective-permute-start(bf16[288,768]{1,0:T(8,128)(2,1)} %get-tuple-element.502), channel_id=1, source_target_pairs={{0,1},{1,0},{2,3},{3,2},{4,5},{5,4},{6,7},{7,6},{8,9},{9,8},{10,11... | collective-permute-start | bytes 1327112 | tf_op jit(solution)/shard_map/ppermute | solution.py:682
  513.3 20.4 %collective-permute-start.43 = (bf16[288,768]{1,0:T(8,128)(2,1)}, bf16[288,768]{1,0:T(8,128)(2,1)S(1)}, u32[]{:S(2)}, u32[]{:S(2)}) collective-permute-start(bf16[288,768]{1,0:T(8,128)(2,1)} %get-tuple-element.503), channel_id=1, source_target_pairs={{0,2},{1,3},{2,0},{3,1},{4,6},{5,7},{6,4},{7,5},{8,10},{9,11},{10,... | collective-permute-start | bytes 1327112 | tf_op jit(solution)/shard_map/ppermute | solution.py:682
  516.1 46.5 %collective-permute-start.44 = (bf16[288,768]{1,0:T(8,128)(2,1)}, bf16[288,768]{1,0:T(8,128)(2,1)S(1)}, u32[]{:S(2)}, u32[]{:S(2)}) collective-permute-start(bf16[288,768]{1,0:T(8,128)(2,1)} %get-tuple-element.504), channel_id=1, source_target_pairs={{0,3},{1,2},{2,1},{3,0},{4,7},{5,6},{6,5},{7,4},{8,11},{9,10},{10,... | collective-permute-start | bytes 1327112 | tf_op jit(solution)/shard_map/ppermute | solution.py:682
  516.9 51.5 %collective-permute-start.47 = (bf16[536,256]{1,0:T(8,128)(2,1)}, bf16[536,256]{1,0:T(8,128)(2,1)S(1)}, u32[]{:S(2)}, u32[]{:S(2)}) collective-permute-start(bf16[536,256]{1,0:T(8,128)(2,1)} %get-tuple-element.518), channel_id=1, source_target_pairs={{0,1},{1,0},{2,3},{3,2},{4,5},{5,4},{6,7},{7,6},{8,9},{9,8},{10,11... | collective-permute-start | bytes 823304 | tf_op jit(solution)/shard_map/ppermute | solution.py:682
  518.1 50.3 %collective-permute-start.48 = (bf16[536,256]{1,0:T(8,128)(2,1)}, bf16[536,256]{1,0:T(8,128)(2,1)S(1)}, u32[]{:S(2)}, u32[]{:S(2)}) collective-permute-start(bf16[536,256]{1,0:T(8,128)(2,1)} %get-tuple-element.518), channel_id=1, source_target_pairs={{0,2},{1,3},{2,0},{3,1},{4,6},{5,7},{6,4},{7,5},{8,10},{9,11},{10,... | collective-permute-start | bytes 823304 | tf_op jit(solution)/shard_map/ppermute | solution.py:682
  532.2 42.0 %collective-permute-start.49 = (bf16[536,256]{1,0:T(8,128)(2,1)S(1)}, bf16[536,256]{1,0:T(8,128)(2,1)S(1)}, u32[]{:S(2)}, u32[]{:S(2)}) collective-permute-start(bf16[536,256]{1,0:T(8,128)(2,1)S(1)} %copy-done.17), channel_id=1, source_target_pairs={{0,3},{1,2},{2,1},{3,0},{4,7},{5,6},{6,5},{7,4},{8,11},{9,10},{10,... | collective-permute-start | bytes 823304 | tf_op jit(solution)/shard_map/ppermute | solution.py:682
  566.3 8.7 %collective-permute-start.45 = (bf16[144,768]{1,0:T(8,128)(2,1)}, bf16[144,768]{1,0:T(8,128)(2,1)S(1)}, u32[]{:S(2)}, u32[]{:S(2)}) collective-permute-start(bf16[144,768]{1,0:T(8,128)(2,1)} %get-tuple-element.516), channel_id=1, source_target_pairs={{0,8},{4,12},{8,0},{12,4},{16,24},{20,28},{24,16},{28,20},{1,9},{5... | collective-permute-start | bytes 663560 | tf_op jit(solution)/shard_map/ppermute | solution.py:682
  567.0 7.9 %collective-permute-start.46 = (bf16[144,768]{1,0:T(8,128)(2,1)}, bf16[144,768]{1,0:T(8,128)(2,1)S(1)}, u32[]{:S(2)}, u32[]{:S(2)}) collective-permute-start(bf16[144,768]{1,0:T(8,128)(2,1)} %get-tuple-element.517), channel_id=1, source_target_pairs={{0,16},{4,20},{8,24},{12,28},{16,0},{20,4},{24,8},{28,12},{1,17},{... | collective-permute-start | bytes 663560 | tf_op jit(solution)/shard_map/ppermute | solution.py:682
  579.3 8.5 %collective-permute-start.50 = (bf16[2,144,768]{2,1,0:T(8,128)(2,1)}, bf16[2,144,768]{2,1,0:T(8,128)(2,1)}, u32[]{:S(2)}, u32[]{:S(2)}) collective-permute-start(bf16[2,144,768]{2,1,0:T(8,128)(2,1)} %get-tuple-element.524), channel_id=1, source_target_pairs={{0,16},{4,20},{8,24},{12,28},{16,0},{20,4},{24,8},{28,12},{1,17},{... | collective-permute-start | bytes 1327112 | tf_op jit(solution)/shard_map/ppermute | solution.py:682
  592.3 14.1 %collective-permute-start.52 = (bf16[2,2,144,768]{3,2,1,0:T(8,128)(2,1)}, bf16[2,2,144,768]{3,2,1,0:T(8,128)(2,1)S(1)}, u32[]{:S(2)}, u32[]{:S(2)}) collective-permute-start(bf16[2,2,144,768]{3,2,1,0:T(8,128)(2,1)} %get-tuple-element.530), channel_id=1, source_target_pairs={{0,4},{4,0},{8,12},{12,8},{16,20},{20,16},{24,28},{28,24},{1,5},{5... | collective-permute-start | bytes 2654216 | tf_op jit(solution)/shard_map/ppermute | solution.py:682
  (104 other events, 470.7 us)
Sparse Core Ops, SparseCore 0:
  30.9 148.5 all-gather.4
  268.2 57.5 reduce-scatter.6
  351.6 69.9 reduce-scatter.8
  486.0 40.0 all-gather.6

commit v5 on v4

--- a/solution.py
+++ b/solution.py
@@ -296,114 +296,114 @@
     )(x1, normed, *ups, *downs, gain, shift)
 
 
-def ff_specs(weights, side, chunk):
+def ff_specs(weights, chunk):
     if len(weights) == 4:
-        width = weights[0].shape[1]
-        spec = pl.BlockSpec((chunk, width), lambda i, *_: (i, 0))
-        return [weights[side], weights[2 + side]], [spec, spec]
+        half, width = weights[0].shape
+        own, other = chunk_specs(chunk, width, half // chunk)
+        return list(weights), [own, other, own, other]
     groups, _, mp, count, width = weights[0].shape
     rows = count // 3
     per = chunk // (mp * rows)
+    steps = groups // per
 
     def spec(which):
-        return pl.BlockSpec((per, 1, mp, rows, width), lambda i, place: (i, place[3] ^ side, 0, which, 0))
+        return pl.BlockSpec(
+            (per, 1, mp, rows, width), lambda i, place: (i % steps, place[3] ^ (i // steps), 0, which, 0)
+        )
 
     return [weights[0], weights[0]], [spec(1), spec(2)]
 
 
-def ff_backward(order, place, x1, normed, weights, side, groups, grad, gain, saved, before):
+def ff_backward(order, place, x1, normed, weights, groups, grad, gain, saved):
     rows, width = x1.shape
-    steps = 2
+    chunk = width
     half = 2 * width
-    chunk = half // steps
-    operands, w_specs = ff_specs(weights, side, chunk)
+    per_half = half // chunk
+    steps = 2 * per_half
+    operands, w_specs = ff_specs(weights, chunk)
     group_rows = half // groups
     per = chunk // group_rows
     fresh = saved is None
-    last = before is not None
     relative = len(weights) == 4
 
-    def body(place_ref, x_ref, n_ref, u_ref, d_ref, grad_ref, g_ref, *rest):
+    def body(place_ref, x_ref, n_ref, *rest):
         rest = list(rest)
+        w_refs = [rest.pop(0) for _ in operands]
+        grad_ref, g_ref = rest.pop(0), rest.pop(0)
         act_ref, slope_ref = (None, None) if fresh else (rest.pop(0), rest.pop(0))
-        dn_in = rest.pop(0) if last else None
-        x2_in = rest.pop(0) if last and fresh else None
-        wg_ref = rest.pop(0)
-        if last:
-            g1_ref, ga_ref, gg_ref, gs_ref = rest[:4]
-            rest = rest[4:]
-            out_ref = rest.pop(0) if fresh else None
-            low, dn = rest[0], rest[1]
-            x2 = rest[2] if fresh else None
-        else:
-            dn = rest.pop(0)
-            x2 = rest.pop(0) if fresh else None
-            low = rest[0]
+        wg_ref, g1_ref, ga_ref, gg_ref, gs_ref = rest[:5]
+        out_ref, (low, dn, x2) = (rest[5], rest[6:]) if fresh else (None, (rest[5], rest[6], None))
         step = pl.program_id(0)
 
         @pl.when(step == 0)
         def _():
             low[...] = grad_ref[...].astype(BF)
-            dn[...] = dn_in[...] if last else jnp.zeros_like(dn)
+            dn[...] = jnp.zeros_like(dn)
             if fresh:
-                x2[...] = x2_in[...] if last else x_ref[...]
-
-        u = u_ref[...].reshape(chunk, width)
-        d = d_ref[...].reshape(chunk, width)
-        if fresh:
-            act, slope = gelu_both(dot_nt(n_ref[...], u))
-            act = act.astype(BF)
-            x2[...] += dot_nn(act, d)
+                x2[...] = x_ref[...]
+
+        def part(u_ref, d_ref):
+            u = u_ref[...].reshape(chunk, width)
+            d = d_ref[...].reshape(chunk, width)
+            if fresh:
+                act, slope = gelu_both(dot_nt(n_ref[...], u))
+                act = act.astype(BF)
+                x2[...] += dot_nn(act, d)
+            else:
+                act, slope = act_ref[...], slope_ref[...].astype(F32)
+            pre_grad = (dot_nt(low[...], d) * slope).astype(BF)
+            dn[...] += dot_nn(pre_grad, u)
+            for which, value in ((0, dot_tn(pre_grad, n_ref[...])), (1, dot_tn(act, low[...]))):
+                value = value.astype(BF)
+                for k in range(per):
+                    spot = (place_ref[5] ^ k) if relative else k
+                    wg_ref[spot, 0, which] = value[k * group_rows : (k + 1) * group_rows]
+
+        if relative:
+            pl.when(step < per_half)(lambda: part(w_refs[0], w_refs[2]))
+            pl.when(step >= per_half)(lambda: part(w_refs[1], w_refs[3]))
         else:
-            act, slope = act_ref[...], slope_ref[...].astype(F32)
-        pre_grad = (dot_nt(low[...], d) * slope).astype(BF)
-        dn[...] += dot_nn(pre_grad, u)
-        for which, value in ((0, dot_tn(pre_grad, n_ref[...])), (1, dot_tn(act, low[...]))):
-            value = value.astype(BF)
-            for k in range(per):
-                spot = (place_ref[5] ^ k) if relative else k
-                wg_ref[spot, which] = value[k * group_rows : (k + 1) * group_rows]
-
-        if last:
-
-            @pl.when(step == steps - 1)
-            def _():
-                if fresh:
-                    out_ref[...] = x2[...].astype(BF)
-                normal, inv = normalize(x_ref[...])
-                total = dn[...]
-                g1 = grad_ref[...] + norm_back(total, normal, inv, g_ref[...])
-                g1_ref[...] = g1
-                ga_ref[...] = g1.astype(BF)
-                gg_ref[...] = jnp.sum(total * normal, axis=0, keepdims=True)
-                gs_ref[...] = jnp.sum(total, axis=0, keepdims=True)
+            part(*w_refs)
+
+        @pl.when(step == steps - 1)
+        def _():
+            if fresh:
+                out_ref[...] = x2[...].astype(BF)
+            normal, inv = normalize(x_ref[...])
+            total = dn[...]
+            g1 = grad_ref[...] + norm_back(total, normal, inv, g_ref[...])
+            g1_ref[...] = g1
+            ga_ref[...] = g1.astype(BF)
+            gg_ref[...] = jnp.sum(total * normal, axis=0, keepdims=True)
+            gs_ref[...] = jnp.sum(total, axis=0, keepdims=True)
 
     full = whole((rows, width))
-    col = pl.BlockSpec((rows, chunk), lambda i, *_: (0, steps * side + i))
-    wg = pl.BlockSpec((per, 2, group_rows, width), lambda i, place: ((place[4] ^ i) if relative else i, 0, 0, 0))
-    in_specs = [full, full] + w_specs + [full, whole((1, width))]
-    operands = [x1, normed] + operands + [grad, gain]
-    if not fresh:
-        in_specs += [col, col]
-        operands += list(saved)
-    out_specs, out_shape = [wg], [shape_of((groups, 2, group_rows, width), BF)]
-    scratch = [pltpu.VMEM((rows, width), BF)]
-    sums = [shape_of((rows, width), F32)] * (2 if fresh else 1)
-    if last:
-        in_specs += [full] * len(sums)
-        operands += list(before)
-        out_specs += [full, full, whole((1, width)), whole((1, width))]
-        out_shape += [shape_of((rows, width), F32), shape_of((rows, width), BF)] + [shape_of((1, width), F32)] * 2
-        if fresh:
-            out_specs.append(full)
-            out_shape.append(shape_of((rows, width), BF))
-        scratch += [pltpu.VMEM((rows, width), F32)] * len(sums)
-    else:
-        out_specs += [full] * len(sums)
-        out_shape += sums
+    col = pl.BlockSpec((rows, chunk), lambda i, *_: (0, i))
+    wg = pl.BlockSpec(
+        (per, 1, 2, group_rows, width),
+        lambda i, place: (
+            (place[4] ^ (i % per_half)) if relative else i % per_half, place[3] ^ (i // per_half), 0, 0, 0,
+        ),
+    )
     return call(
-        order, body, (steps,), in_specs, out_specs, out_shape, scratch, prefetch=1, name="ff_bwd"
-    )(place, *operands)
+        order,
+        body,
+        (steps,),
+        [full, full] + w_specs + [full, whole((1, width))] + ([] if fresh else [col, col]),
+        [wg, full, full, whole((1, width)), whole((1, width))] + ([full] if fresh else []),
+        [
+            shape_of((groups, 2, 2, group_rows, width), BF),
+            shape_of((rows, width), F32),
+            shape_of((rows, width), BF),
+            shape_of((1, width), F32),
+            shape_of((1, width), F32),
+        ]
+        + ([shape_of((rows, width), BF)] if fresh else []),
+        [pltpu.VMEM((rows, width), BF), pltpu.VMEM((rows, width), F32)]
+        + ([pltpu.VMEM((rows, width), F32)] if fresh else []),
+        prefetch=1,
+        name="ff_bwd",
+    )(place, x1, normed, *operands, grad, gain, *(() if fresh else saved))
 
 
 def attn_backward(order, place, grad_low, weights, sg, ratio, rden, v, wsum, carried, masked):
@@ -785,20 +785,10 @@
 
 
 class ReduceWide:
-    def __init__(self, links, own, other):
+    def __init__(self, links, grads):
         self.links = links
-        self.own = own
-        self.other = other
-
-    def start_cores(self):
-        (self.other,) = self.links.order.pin(self.other)
-        self.coming = self.links.swap(self.other, DP, 1)
-
-    def wait_cores(self):
-        (coming,) = self.links.order.pin(self.coming)
-        total = (self.own.astype(F32) + coming.astype(F32)).astype(BF)
-        (total,) = self.links.order.pin(total)
-        self.sums = lax.psum_scatter(total, "g", scatter_dimension=0, tiled=True)
+        (grads,) = links.order.pin(grads.reshape((links.dp,) + grads.shape[2:]))
+        self.sums = lax.psum_scatter(grads, DP, scatter_dimension=0, tiled=True)
 
     def wait(self):
         (sums,) = self.links.order.pin(self.sums)
@@ -908,12 +898,11 @@
         piece = attn_piece(0)
         attn0 = Gather(links, piece[:middle], piece[middle:])
         attn0.start_mp()
-        x, normed = enter_kernel(order, tokens.reshape(rows, width), gains[0, 0], shifts[0, 0])
-        (normed,) = order.pin(normed)
-        halo = forward_halo(normed)
+        (later,) = order.pin(jnp.concatenate((attn_piece(1),) + ff_pieces(1), axis=0))
+        later = lax.all_gather(later, ("g", "c", "mp"), axis=0, tiled=False)
         ff0 = Gather(links, *ff_pieces(0))
         ff0.start_mp()
-        later = jnp.concatenate((attn_piece(1),) + ff_pieces(1), axis=0)
+        x, normed = enter_kernel(order, tokens.reshape(rows, width), gains[0, 0], shifts[0, 0])
 
         seg_pad = jnp.concatenate([jnp.full((seqs, window), -1, segments.dtype), segments], axis=1)
         seg_keys = lax.dynamic_slice_in_dim(seg_pad, mp_index * block, block + window, axis=1)
@@ -922,12 +911,12 @@
 
         attn0.wait_mp()
         attn0.start()
-        (later,) = order.pin(later)
-        later = lax.all_gather(later, ("g", "c", "mp"), axis=0, tiled=False)
         attn0.wait()
         attn0.start()
         ff0.wait_mp()
         ff0.start()
+        (normed,) = order.pin(normed)
+        halo = forward_halo(normed)
         attn0.wait_all()
         attn0.start_cores()
         ff0.wait()
@@ -965,18 +954,15 @@
         x1_1, normed_b1, saved1, rows1 = attn(1, x2, normed2, halo2, w_attn1)
 
         def ff_back(layer, x1, normed_b, weights, grad, saved):
-            args = (order, place, x1, normed_b, weights)
-            kept = (groups, grad, gains[layer, 1], saved)
-            wg_other, *before = ff_backward(*args, 1, *kept, None)
-            wide = ReduceWide(links, None, wg_other)
-            wide.start_cores()
-            wide.own, *rest = ff_backward(*args, 0, *kept, before)
-            return wide, rest
-
-        wide1, (grad1, grad1_low, gain_b1, shift_b1, output) = ff_back(
+            grads, *rest = ff_backward(
+                order, place, x1, normed_b, weights, groups, grad, gains[layer, 1], saved
+            )
+            return grads, rest
+
+        ff_grads1, (grad1, grad1_low, gain_b1, shift_b1, output) = ff_back(
             1, x1_1, normed_b1, w_ff1, cotangent.reshape(rows, width), None
         )
-        wide1.wait_cores()
+        wide1 = ReduceWide(links, ff_grads1)
         gq, gk, gv, band1, dn_own1, back1 = attn_backward(order, place, grad1_low, w_attn1, *saved1)
         (back1,) = order.pin(back1)
         back1 = backward_halo(back1)
@@ -988,22 +974,25 @@
         grad2, gain_a1, shift_a1 = leave_attn(order, x2, grad1, dn_own1, back1, gains[1, 0])
         r_attn1.wait_cores()
         r_attn1.start()
-        wide0, (grad3, grad3_low, gain_b0, shift_b0) = ff_back(
+        ff_grads0, (grad3, grad3_low, gain_b0, shift_b0) = ff_back(
             0, x1_0, normed_b0, ups0 + downs0, grad2, (act0, slope0)
         )
-        wide0.wait_cores()
         r_attn1.wait()
+        wide0 = ReduceWide(links, ff_grads0)
         r_attn1.start()
+        up1, down1 = wide1.wait()
+        attn1_sum = r_attn1.wait_all()
+        mp1 = ReduceMp(links, attn1_sum + [up1, down1], mp_index if in_blocks else None)
         gq, gk, gv, band0, dn_own0, back0 = attn_backward(order, place, grad3_low, w_attn0, *saved0)
-        attn1_sum = r_attn1.wait_all()
-        (back0,) = order.pin(back0)
-        back0 = backward_halo(back0)
         r_attn0 = Reduce(
             links, attn_weight_grads(order, place, gq, gk, gv, *rows0, grad3_low, mp, False)
         )
+        sum1 = mp1.wait()
         r_attn0.start_cores()
-        up1, down1 = wide1.wait()
-        mp1 = ReduceMp(links, attn1_sum + [up1, down1], mp_index if in_blocks else None)
+        (back0,) = order.pin(back0)
+        back0 = backward_halo(back0)
+        (sum1,) = order.pin(sum1)
+        full1 = lax.all_gather(sum1, DP, axis=0, tiled=False)
         r_attn0.wait_cores()
         r_attn0.start()
         (back0,) = order.pin(back0)
@@ -1022,20 +1011,15 @@
             return (pair[0].astype(F32) + coming.astype(F32)).astype(BF)
 
         bits = [1 << k for k in range(dp.bit_length() - 1)]
+        r_attn0.wait()
+        r_attn0.start()
         pair = small_start(bits[0])
-        r_attn0.wait()
-        small = small_wait(pair)
-        r_attn0.start()
-        pair = small_start(bits[1])
-        sum1 = mp1.wait()
-        (sum1,) = order.pin(sum1)
-        full1 = lax.all_gather(sum1, DP, axis=0, tiled=False)
         attn0_sum = r_attn0.wait_all()
         small = small_wait(pair)
-        for bit in bits[2:]:
-            small = small_wait(small_start(bit))
         up0, down0 = wide0.wait()
         mp0 = ReduceMp(links, attn0_sum + [up0, down0], None)
+        for bit in bits[1:]:
+            small = small_wait(small_start(bit))
         (small,) = order.pin(small)
         small_parts = [links.swap(small, "mp", p) for p in range(1, mp)]
         (full1,) = order.pin(full1)

time: 626 us -> 579 us (0.925)
  waiting for transfers between devices: 237 us -> 205 us
  other arithmetic: 68.1 us -> 55.8 us
  Pallas kernels: 179 us -> 170 us
  starting transfers between devices: 64.8 us -> 72.9 us
    ppermute x50 -> x48, waiting for transfers between devices: 166 us -> 149 us  [swap(): return lax.ppermute(value, axis, [(i, i ^ bit) for i in range(size)])]
    ppermute x2, waiting for transfers between devices: 51.9 us -> 37.7 us  [forward_halo(): return lax.ppermute(value, 'mp', [(i, i + 1) for i in range(mp - 1)])]
    convert_element_type x2 -> x0, other arithmetic: 14.2 us -> none  [wait_cores(): total = (self.own.astype(F32) + coming.astype(F32)).astype(BF)]
    pallas_call x14 -> x12, Pallas kernels: 167 us -> 158 us  [run(): *results, order.token = kernel(*operands, order.token)]
    all_gather x1, waiting for transfers between devices: 6.48 us -> 0.01 us  [shards(): full1 = lax.all_gather(sum1, DP, axis=0, tiled=False)]
    ppermute x50 -> x48, starting transfers between devices: 52.8 us -> 59.2 us  [swap(): return lax.ppermute(value, axis, [(i, i ^ bit) for i in range(size)])]
    unnamed x188 -> x182, local copies, waits for them, and re-layouts: 23 us -> 24.9 us
  transfers between devices with their start and end apart: 58 -> 56, of which waited for: 28 -> 28; matrix products, arithmetic and copies ran while one was open for 13% -> 13% of each run, Pallas kernels for 23% -> 22%
where the time goes in v5:
time: 579 us; the launch traced here: 573 us
  waiting for transfers between devices  205 us (35%)
  Pallas kernels  170 us (29%)
  starting transfers between devices  72.9 us (13%)
  other arithmetic  55.8 us (10%)
  local copies, waits for them, and re-layouts  50.9 us (9%)
  between operations  15.3 us (3%)
    pallas_call x12, Pallas kernels, run(): *results, order.token = kernel(*operands, order.token)  158 us
    ppermute x48, waiting for transfers between devices, swap(): return lax.ppermute(value, axis, [(i, i ^ bit) for i in range(size)])  149 us
    ppermute x48, starting transfers between devices, swap(): return lax.ppermute(value, axis, [(i, i ^ bit) for i in range(size)])  59.2 us
    ppermute x2, waiting for transfers between devices, forward_halo(): return lax.ppermute(value, 'mp', [(i, i + 1) for i in range(mp - 1)])  37.7 us
    unnamed x182, local copies, waits for them, and re-layouts  24.9 us
    another operation x12, other arithmetic, wait(): self.values[k] = jnp.stack([self.values[k], coming[k]], axis=place)  24.1 us
    ppermute x2, waiting for transfers between devices, backward_halo(): return lax.ppermute(value, 'mp', [(i + 1, i) for i in range(mp - 1)])  14.8 us
    pallas_call x2, Pallas kernels, finish_layer(): pl.pallas_call(with_token, grid_spec=pltpu.PrefetchScalarGridSpec(num_sca...  12.4 us
  transfers between devices with their start and end apart: 56, of which 28 were waited for; matrix products, arithmetic and copies ran while one was open for 13% of the time, Pallas kernels for 22%

profile of v5, /device:TPU:9, one launch (start us, length us, event | category | flops | bytes accessed | tf_op | source)
XLA Modules:
  0.0 573.0 jit_solution(7110088629127396092)
XLA Ops:
  13.6 2.5 collective-permute-start.4
  19.8 2.7 enter.1
  22.5 11.1 %collective-permute-done.5.refs_2_ = bf16[96,768]{1,0:T(8,128)(2,1)S(1)} collective-permute-done((bf16[96,768]{1,0:T(8,128)(2,1)S(1)}, bf16[96,768]{1,0:T(8,128)(2,1)S(1)}, u32[]{:S(2)}, u32[]{:S(2)}) %collective-permute-start.5) | collective-permute-done | bytes 147488 | tf_op jit(solution)/shard_map/ppermute | solution.py:682
  41.0 4.2 collective-permute-start.1
  51.6 22.1 %collective-permute-done.1.refs_1_ = bf16[192,768]{1,0:T(8,128)(2,1)S(1)} collective-permute-done((bf16[192,768]{1,0:T(8,128)(2,1)S(1)}, bf16[192,768]{1,0:T(8,128)(2,1)S(1)}, u32[]{:S(2)}, u32[]{:S(2)}) %collective-permute-start.1) | collective-permute-done | bytes 294944 | tf_op jit(solution)/shard_map/ppermute | solution.py:682
  73.7 15.3 %collective-permute-done.2.refs_2_ = bf16[192,768]{1,0:T(8,128)(2,1)S(1)} collective-permute-done((bf16[192,768]{1,0:T(8,128)(2,1)S(1)}, bf16[192,768]{1,0:T(8,128)(2,1)S(1)}, u32[]{:S(2)}, u32[]{:S(2)}) %collective-permute-start.2) | collective-permute-done | bytes 294944 | tf_op jit(solution)/shard_map/ppermute | solution.py:682
  101.5 20.6 %collective-permute-done.13.refs_0_ = bf16[4,96,768]{2,1,0:T(8,128)(2,1)S(1)} collective-permute-done((bf16[4,96,768]{2,1,0:T(8,128)(2,1)}, bf16[4,96,768]{2,1,0:T(8,128)(2,1)S(1)}, u32[]{:S(2)}, u32[]{:S(2)}) %collective-permute-start.13) | collective-permute-done | bytes 589856 | tf_op jit(solution)/shard_map/ppermute | solution.py:682
  123.0 2.3 pad_maximum_fusion.7.refs_1_
  127.8 4.4 collective-permute-start.8
  135.8 21.3 %collective-permute-done.8.refs_0_ = bf16[512,768]{1,0:T(8,128)(2,1)} collective-permute-done((bf16[512,768]{1,0:T(8,128)(2,1)S(1)}, bf16[512,768]{1,0:T(8,128)(2,1)}, u32[]{:S(2)}, u32[]{:S(2)}) %collective-permute-start.8) | collective-permute-done | bytes 786464 | tf_op jit(solution)/shard_map/ppermute | solution.py:888
  157.1 14.8 %attn_fwd.2 = (bf16[512,768]{1,0:T(8,128)(2,1)}, bf16[512,768]{1,0:T(8,128)(2,1)}, bf16[512,768]{1,0:T(8,128)(2,1)}, bf16[1024,768]{1,0:T(8,128)(2,1)}, bf16[102...) custom-call(s32[6]{0:T(128)} %stack.207.refs_0_, ...), custom_call_target="tpu_custom_call", output_to_operand_aliasing={{10}: (13, {})} | custom-call | tf_op jit(solution)/shard_map/attn_fwd/pallas_call | solution.py:74
  173.2 3.0 pad_maximum_fusion.1.refs_1_
  176.2 2.9 pad_maximum_fusion.refs_0_
  179.1 5.0 collective-permute-start.17
  184.1 7.7 %collective-permute-done.17.refs_0_ = bf16[2,2,4,96,768]{4,3,2,1,0:T(8,128)(2,1)S(1)} collective-permute-done((bf16[2,2,4,96,768]{4,3,2,1,0:T(8,128)(2,1)}, bf16[2,2,4,96,768]{4,3,2,1,0:T(8,128)(2,1)S(1)}, u32[]{:S(2)}, u32[]{:S(2)}) %collective-permute-start.17) | collective-permute-done | bytes 2359328 | tf_op jit(solution)/shard_map/ppermute | solution.py:682
  193.2 13.6 %ff_fwd.1 = (bf16[512,3072]{1,0:T(8,128)(2,1)}, bf16[512,3072]{1,0:T(8,128)(2,1)}, f32[512,768]{1,0:T(8,128)}, bf16[512,768]{1,0:T(8,128)(2,1)}, s32[8,128]{1,0:T(8,128)}) custom-call(f32[512,768]{1,0:T(8,128)} %get-tuple-element.308.refs_0_.refs_1_, bf16[512,768]{1,0:T(8,128)(2,1)} %get-tuple-element.309.refs_1_.refs_2_, ...), custom_call_target="tpu_custom_call", output_to_operand_aliasing={{4}: (8, {})} | custom-call | tf_op jit(solution)/shard_map/ff_fwd/pallas_call | solution.py:74
  206.9 4.7 collective-permute-start.19
  211.6 16.3 %collective-permute-done.19.refs_0_ = bf16[512,768]{1,0:T(8,128)(2,1)S(1)} collective-permute-done((bf16[512,768]{1,0:T(8,128)(2,1)}, bf16[512,768]{1,0:T(8,128)(2,1)S(1)}, u32[]{:S(2)}, u32[]{:S(2)}) %collective-permute-start.19) | collective-permute-done | bytes 786464 | tf_op jit(solution)/shard_map/ppermute | solution.py:888
  228.8 14.2 %attn_fwd.3 = (bf16[512,768]{1,0:T(8,128)(2,1)}, bf16[512,768]{1,0:T(8,128)(2,1)}, bf16[512,768]{1,0:T(8,128)(2,1)}, bf16[1024,768]{1,0:T(8,128)(2,1)}, bf16[102...) custom-call(s32[6]{0:T(128)} %stack.207.refs_0_, ...), custom_call_target="tpu_custom_call", output_to_operand_aliasing={{10}: (10, {})} | custom-call | tf_op jit(solution)/shard_map/attn_fwd/pallas_call | solution.py:74
  243.0 24.4 %ff_bwd.2 = (bf16[4,2,2,384,768]{4,3,2,1,0:T(8,128)(2,1)}, f32[512,768]{1,0:T(8,128)}, bf16[512,768]{1,0:T(8,128)(2,1)}, f32[1,768]{1,0:T(1,128)}, f32[1,768]{1,...) custom-call(s32[6]{0:T(128)} %stack.207.refs_0_, ...), custom_call_target="tpu_custom_call", output_to_operand_aliasing={{6}: (7, {})} | custom-call | tf_op jit(solution)/shard_map/ff_bwd/pallas_call | solution.py:74
  267.5 16.2 %attn_bwd.2 = (bf16[512,768]{1,0:T(8,128)(2,1)}, bf16[1024,768]{1,0:T(8,128)(2,1)}, bf16[1024,768]{1,0:T(8,128)(2,1)}, f32[256,256]{1,0:T(8,128)}, f32[512,768]{...) custom-call(s32[6]{0:T(128)} %stack.207.refs_0_, ...), custom_call_target="tpu_custom_call", output_to_operand_aliasing={{6}: (10, {})} | custom-call | tf_op jit(solution)/shard_map/attn_bwd/pallas_call | solution.py:74
  285.8 11.7 %attn_wgrad.2 = (bf16[4,192,768]{2,1,0:T(8,128)(2,1)}, bf16[4,192,768]{2,1,0:T(8,128)(2,1)}, bf16[4,192,768]{2,1,0:T(8,128)(2,1)}, bf16[4,192,768]{2,1,0:T(8,128)(2,1)}, s32[8,128]{1,0:T(8,128)}) custom-call(s32[6]{0:T(128)} %stack.207.refs_0_, bf16[512,768]{1,0:T(8,128)(2,1)} %get-tuple-element.352.refs_1_, ...), custom_call_target="tpu_custom_call", output_to_operand_aliasing={{4}: (8, {})} | custom-call | tf_op jit(solution)/shard_map/attn_wgrad/pallas_call | solution.py:74
  297.5 7.5 %collective-permute-done.20.refs_0_ = bf16[512,768]{1,0:T(8,128)(2,1)S(1)} collective-permute-done((bf16[512,768]{1,0:T(8,128)(2,1)}, bf16[512,768]{1,0:T(8,128)(2,1)S(1)}, u32[]{:S(2)}, u32[]{:S(2)}) %collective-permute-start.20) | collective-permute-done | bytes 786464 | tf_op jit(solution)/shard_map/ppermute | solution.py:891
  307.2 4.9 leave.2
  319.7 20.0 %ff_bwd.3 = (bf16[4,2,2,384,768]{4,3,2,1,0:T(8,128)(2,1)}, f32[512,768]{1,0:T(8,128)}, bf16[512,768]{1,0:T(8,128)(2,1)}, f32[1,768]{1,0:T(1,128)}, f32[1,768]{1,0:T(1,128)}, /*index=5*/s32[8,128]{1,0:T(8,128)}) custom-call(s32[6]{0:T(128)} %stack.207.refs_0_, f32[512,768]{1,0:T(8,128)} %get-tuple-element.308.refs_0_.refs_1_, ...), custom_call_target="tpu_custom_call", output_to_operand_aliasing={{5}: (11, {})} | custom-call | tf_op jit(solution)/shard_map/ff_bwd/pallas_call | solution.py:74
  345.3 3.8 reduce-scatter.3.cloned.1.call-done.refs_0_
  349.1 3.6 collective-permute-done.25.refs_0_
  359.7 17.8 %attn_bwd.3 = (bf16[512,768]{1,0:T(8,128)(2,1)}, bf16[1024,768]{1,0:T(8,128)(2,1)}, bf16[1024,768]{1,0:T(8,128)(2,1)}, f32[256,256]{1,0:T(8,128)}, f32[512,768]{...) custom-call(s32[6]{0:T(128)} %stack.207.refs_0_, ...), custom_call_target="tpu_custom_call", output_to_operand_aliasing={{6}: (13, {})} | custom-call | tf_op jit(solution)/shard_map/attn_bwd/pallas_call | solution.py:74
  377.5 12.4 %attn_wgrad.3 = (bf16[4,192,768]{2,1,0:T(8,128)(2,1)}, bf16[4,192,768]{2,1,0:T(8,128)(2,1)}, bf16[4,192,768]{2,1,0:T(8,128)(2,1)}, bf16[4,192,768]{2,1,0:T(8,128)(2,1)}, s32[8,128]{1,0:T(8,128)}) custom-call(s32[6]{0:T(128)} %stack.207.refs_0_, bf16[512,768]{1,0:T(8,128)(2,1)} %get-tuple-element.404.refs_1_, ...), custom_call_target="tpu_custom_call", output_to_operand_aliasing={{4}: (8, {})} | custom-call | tf_op jit(solution)/shard_map/attn_wgrad/pallas_call | solution.py:74
  390.0 7.3 %collective-permute-done.29.refs_2_ = bf16[288,768]{1,0:T(8,128)(2,1)S(1)} collective-permute-done((bf16[288,768]{1,0:T(8,128)(2,1)}, bf16[288,768]{1,0:T(8,128)(2,1)S(1)}, u32[]{:S(2)}, u32[]{:S(2)}) %collective-permute-start.29) | collective-permute-done | bytes 442400 | tf_op jit(solution)/shard_map/ppermute | solution.py:682
  398.0 2.3 collective-permute-start.31
  415.4 7.3 %collective-permute-done.30.refs_0_ = bf16[512,768]{1,0:T(8,128)(2,1)S(1)} collective-permute-done((bf16[512,768]{1,0:T(8,128)(2,1)}, bf16[512,768]{1,0:T(8,128)(2,1)S(1)}, u32[]{:S(2)}, u32[]{:S(2)}) %collective-permute-start.30) | collective-permute-done | bytes 786464 | tf_op jit(solution)/shard_map/ppermute | solution.py:891
  423.6 4.9 leave.3
  430.0 7.1 %collective-permute-done.33.refs_0_ = bf16[2,4,48,768]{3,2,1,0:T(8,128)(2,1)S(1)} collective-permute-done((bf16[2,4,48,768]{3,2,1,0:T(8,128)(2,1)}, bf16[2,4,48,768]{3,2,1,0:T(8,128)(2,1)S(1)}, u32[]{:S(2)}, u32[]{:S(2)}) %collective-permute-start.33) | collective-permute-done | bytes 589856 | tf_op jit(solution)/shard_map/ppermute | solution.py:682
  437.1 2.6 collective-permute-done.34.refs_1_
  445.1 2.3 collective-permute-start.37
  447.4 3.4 collective-permute-done.35.refs_0_
  459.3 5.8 %collective-permute-done.41.refs_0_ = bf16[536,256]{1,0:T(8,128)(2,1)S(1)} collective-permute-done((bf16[536,256]{1,0:T(8,128)(2,1)}, bf16[536,256]{1,0:T(8,128)(2,1)S(1)}, u32[]{:S(2)}, u32[]{:S(2)}) %collective-permute-start.41) | collective-permute-done | bytes 274464 | tf_op jit(solution)/shard_map/ppermute | solution.py:682
  467.7 2.4 collective-permute-start.39
  470.3 9.7 %collective-permute-done.42.refs_0_ = bf16[536,256]{1,0:T(8,128)(2,1)S(1)} collective-permute-done((bf16[536,256]{1,0:T(8,128)(2,1)}, bf16[536,256]{1,0:T(8,128)(2,1)S(1)}, u32[]{:S(2)}, u32[]{:S(2)}) %collective-permute-start.42) | collective-permute-done | bytes 274464 | tf_op jit(solution)/shard_map/ppermute | solution.py:682
  482.5 2.3 collective-permute-start.46
  484.8 6.1 %finish.2 = (f32[2,3,192,768]{3,2,1,0:T(8,128)}, f32[2,192,768]{2,1,0:T(8,128)}, f32[2,768,768]{2,1,0:T(8,128)}, f32[2,768,768]{2,1,0:T(8,128)}, s32[8,128]{1,0:T(8,128)}) custom-call(s32[6]{0:T(128)} %stack.207.refs_0_, bf16[8,288,768]{2,1,0:T(8,128)(2,1)} %get-tuple-element.479.refs_1_, ...), custom_call_target="tpu_custom_call", output_to_operand_aliasing={{4}: (2, {})} | custom-call | tf_op jit(solution)/shard_map/finish/pallas_call | solution.py:640
  491.3 18.6 %collective-permute-done.40.refs_2_ = bf16[288,768]{1,0:T(8,128)(2,1)} collective-permute-done((bf16[288,768]{1,0:T(8,128)(2,1)S(1)}, bf16[288,768]{1,0:T(8,128)(2,1)}, u32[]{:S(2)}, u32[]{:S(2)}) %collective-permute-start.40) | collective-permute-done | bytes 442400 | tf_op jit(solution)/shard_map/ppermute | solution.py:682
  512.9 7.2 %collective-permute-start.43 = (bf16[144,768]{1,0:T(8,128)(2,1)}, bf16[144,768]{1,0:T(8,128)(2,1)S(1)}, u32[]{:S(2)}, u32[]{:S(2)}) collective-permute-start(bf16[144,768]{1,0:T(8,128)(2,1)} %get-tuple-element.486), channel_id=1, source_target_pairs={{0,8},{4,12},{8,0},{12,4},{16,24},{20,28},{24,16},{28,20},{1,9},{5... | collective-permute-start | bytes 663560 | tf_op jit(solution)/shard_map/ppermute | solution.py:682
  521.8 6.1 %collective-permute-done.47.refs_2_ = bf16[536,256]{1,0:T(8,128)(2,1)S(1)} collective-permute-done((bf16[536,256]{1,0:T(8,128)(2,1)S(1)}, bf16[536,256]{1,0:T(8,128)(2,1)S(1)}, u32[]{:S(2)}, u32[]{:S(2)}) %collective-permute-start.47) | collective-permute-done | bytes 274464 | tf_op jit(solution)/shard_map/ppermute | solution.py:682
  536.6 2.3 gather_fusion
  546.3 9.0 %collective-permute-start.50 = (bf16[2,2,144,768]{3,2,1,0:T(8,128)(2,1)}, bf16[2,2,144,768]{3,2,1,0:T(8,128)(2,1)S(1)}, u32[]{:S(2)}, u32[]{:S(2)}) collective-permute-start(bf16[2,2,144,768]{3,2,1,0:T(8,128)(2,1)} %get-tuple-element.500), channel_id=1, source_target_pairs={{0,4},{4,0},{8,12},{12,8},{16,20},{20,16},{24,28},{28,24},{1,5},{5... | collective-permute-start | bytes 2654216 | tf_op jit(solution)/shard_map/ppermute | solution.py:682
  559.7 6.3 %finish.3 = (f32[2,3,192,768]{3,2,1,0:T(8,128)}, f32[2,192,768]{2,1,0:T(8,128)}, f32[2,768,768]{2,1,0:T(8,128)}, f32[2,768,768]{2,1,0:T(8,128)}, s32[8,128]{1,0:T(8,128)}) custom-call(s32[6]{0:T(128)} %stack.207.refs_0_, bf16[4,144,768]{2,1,0:T(8,128)(2,1)} %bitcast.251, ...), custom_call_target="tpu_custom_call", output_to_operand_aliasing={{0}: (5, {}), {1}: (6, {}), {2}: (7, {}), {3}: (8, {}), {4}... | custom-call | tf_op jit(solution)/shard_map/finish/pallas_call | solution.py:640
  (427 shorter events, 133.7 us)
Async XLA Ops:
  7.2 204.4 %all-gather.5.cloned.1.call-start = ((), (), s32[]{:S(2)}) async-start(), calls=%async_computation.4 | async-start | bytes 14598144 | tf_op jit(solution)/shard_map/all_gather | solution.py:902
  13.4 335.7 %reduce-scatter.3.cloned.1.call-start = ((), (), s32[]{:S(2)}) async-start(), calls=%async_computation.2 | async-start | bytes 10616832 | tf_op jit(solution)/shard_map/reduce_scatter | solution.py:791
  13.6 8.9 %collective-permute-start.3 = (bf16[96,768]{1,0:T(8,128)(2,1)S(1)}, bf16[96,768]{1,0:T(8,128)(2,1)S(1)}, u32[]{:S(2)}, u32[]{:S(2)}) collective-permute-start(bf16[96,768]{1,0:T(8,128)(2,1)S(1)} %copy-done.57), channel_id=1, source_target_pairs={{0,1},{1,0},{2,3},{3,2},{4,5},{5,4},{6,7},{7,6},{8,9},{9,8},{10,11... | collective-permute-start | bytes 442376 | tf_op jit(solution)/shard_map/ppermute | solution.py:682
  13.6 8.9 %collective-permute-start.4 = (bf16[96,768]{1,0:T(8,128)(2,1)S(1)}, bf16[96,768]{1,0:T(8,128)(2,1)S(1)}, u32[]{:S(2)}, u32[]{:S(2)}) collective-permute-start(bf16[96,768]{1,0:T(8,128)(2,1)S(1)} %copy-done.57), channel_id=1, source_target_pairs={{0,2},{1,3},{2,0},{3,1},{4,6},{5,7},{6,4},{7,5},{8,10},{9,11},{10,... | collective-permute-start | bytes 442376 | tf_op jit(solution)/shard_map/ppermute | solution.py:682
  16.0 17.6 %collective-permute-start.5 = (bf16[96,768]{1,0:T(8,128)(2,1)S(1)}, bf16[96,768]{1,0:T(8,128)(2,1)S(1)}, u32[]{:S(2)}, u32[]{:S(2)}) collective-permute-start(bf16[96,768]{1,0:T(8,128)(2,1)S(1)} %copy-done.57), channel_id=1, source_target_pairs={{0,3},{1,2},{2,1},{3,0},{4,7},{5,6},{6,5},{7,4},{8,11},{9,10},{10,... | collective-permute-start | bytes 442376 | tf_op jit(solution)/shard_map/ppermute | solution.py:682
  41.0 10.6 %collective-permute-start = (bf16[192,768]{1,0:T(8,128)(2,1)S(1)}, bf16[192,768]{1,0:T(8,128)(2,1)S(1)}, u32[]{:S(2)}, u32[]{:S(2)}) collective-permute-start(bf16[192,768]{1,0:T(8,128)(2,1)S(1)} %copy-done.26), channel_id=1, source_target_pairs={{0,1},{1,0},{2,3},{3,2},{4,5},{5,4},{6,7},{7,6},{8,9},{9,8},{10,11... | collective-permute-start | bytes 884744 | tf_op jit(solution)/shard_map/ppermute | solution.py:682
  41.0 32.7 %collective-permute-start.1 = (bf16[192,768]{1,0:T(8,128)(2,1)S(1)}, bf16[192,768]{1,0:T(8,128)(2,1)S(1)}, u32[]{:S(2)}, u32[]{:S(2)}) collective-permute-start(bf16[192,768]{1,0:T(8,128)(2,1)S(1)} %copy-done.26), channel_id=1, source_target_pairs={{0,2},{1,3},{2,0},{3,1},{4,6},{5,7},{6,4},{7,5},{8,10},{9,11},{10,... | collective-permute-start | bytes 884744 | tf_op jit(solution)/shard_map/ppermute | solution.py:682
  45.1 43.8 %collective-permute-start.2 = (bf16[192,768]{1,0:T(8,128)(2,1)S(1)}, bf16[192,768]{1,0:T(8,128)(2,1)S(1)}, u32[]{:S(2)}, u32[]{:S(2)}) collective-permute-start(bf16[192,768]{1,0:T(8,128)(2,1)S(1)} %copy-done.26), channel_id=1, source_target_pairs={{0,3},{1,2},{2,1},{3,0},{4,7},{5,6},{6,5},{7,4},{8,11},{9,10},{10,... | collective-permute-start | bytes 884744 | tf_op jit(solution)/shard_map/ppermute | solution.py:682
  50.1 45.4 %collective-permute-start.10 = (bf16[2,4,48,768]{3,2,1,0:T(8,128)(2,1)}, bf16[2,4,48,768]{3,2,1,0:T(8,128)(2,1)S(1)}, u32[]{:S(2)}, u32[]{:S(2)}) collective-permute-start(bf16[2,4,48,768]{3,2,1,0:T(8,128)(2,1)} %get-tuple-element.289), channel_id=1, source_target_pairs={{0,8},{4,12},{8,0},{12,4},{16,24},{20,28},{24,16},{28,20},{1,9},{5... | collective-permute-start | bytes 1769480 | tf_op jit(solution)/shard_map/ppermute | solution.py:682
  50.3 45.2 %collective-permute-start.9 = (bf16[2,4,48,768]{3,2,1,0:T(8,128)(2,1)}, bf16[2,4,48,768]{3,2,1,0:T(8,128)(2,1)S(1)}, u32[]{:S(2)}, u32[]{:S(2)}) collective-permute-start(bf16[2,4,48,768]{3,2,1,0:T(8,128)(2,1)} %get-tuple-element.288), channel_id=1, source_target_pairs={{0,16},{4,20},{8,24},{12,28},{16,0},{20,4},{24,8},{28,12},{1,17},{... | collective-permute-start | bytes 1769480 | tf_op jit(solution)/shard_map/ppermute | solution.py:682
  94.5 27.6 %collective-permute-start.13 = (bf16[4,96,768]{2,1,0:T(8,128)(2,1)}, bf16[4,96,768]{2,1,0:T(8,128)(2,1)S(1)}, u32[]{:S(2)}, u32[]{:S(2)}) collective-permute-start(bf16[4,96,768]{2,1,0:T(8,128)(2,1)} %get-tuple-element.296), channel_id=1, source_target_pairs={{0,8},{4,12},{8,0},{12,4},{16,24},{20,28},{24,16},{28,20},{1,9},{5... | collective-permute-start | bytes 1769480 | tf_op jit(solution)/shard_map/ppermute | solution.py:682
  95.2 27.7 %collective-permute-start.14 = (bf16[4,96,768]{2,1,0:T(8,128)(2,1)}, bf16[4,96,768]{2,1,0:T(8,128)(2,1)}, u32[]{:S(2)}, u32[]{:S(2)}) collective-permute-start(bf16[4,96,768]{2,1,0:T(8,128)(2,1)} %get-tuple-element.297), channel_id=1, source_target_pairs={{0,16},{4,20},{8,24},{12,28},{16,0},{20,4},{24,8},{28,12},{1,17},{... | collective-permute-start | bytes 1769480 | tf_op jit(solution)/shard_map/ppermute | solution.py:682
  100.0 34.4 %collective-permute-start.11 = (bf16[2,2,4,48,768]{4,3,2,1,0:T(8,128)(2,1)}, bf16[2,2,4,48,768]{4,3,2,1,0:T(8,128)(2,1)S(1)}, u32[]{:S(2)}, u32[]{:S(2)}) collective-permute-start(bf16[2,2,4,48,768]{4,3,2,1,0:T(8,128)(2,1)} %get-tuple-element.294), channel_id=1, source_target_pairs={{0,4},{4,0},{8,12},{12,8},{16,20},{20,16},{24,28},{28,24},{1,5},{5... | collective-permute-start | bytes 3538952 | tf_op jit(solution)/shard_map/ppermute | solution.py:682
  101.5 32.8 %collective-permute-start.12 = (bf16[2,2,4,48,768]{4,3,2,1,0:T(8,128)(2,1)}, bf16[2,2,4,48,768]{4,3,2,1,0:T(8,128)(2,1)S(1)}, u32[]{:S(2)}, u32[]{:S(2)}) collective-permute-start(bf16[2,2,4,48,768]{4,3,2,1,0:T(8,128)(2,1)} %get-tuple-element.295), channel_id=1, source_target_pairs={{0,4},{4,0},{8,12},{12,8},{16,20},{20,16},{24,28},{28,24},{1,5},{5... | collective-permute-start | bytes 3538952 | tf_op jit(solution)/shard_map/ppermute | solution.py:682
  126.4 45.5 %collective-permute-start.15 = (bf16[2,4,96,768]{3,2,1,0:T(8,128)(2,1)}, bf16[2,4,96,768]{3,2,1,0:T(8,128)(2,1)}, u32[]{:S(2)}, u32[]{:S(2)}) collective-permute-start(bf16[2,4,96,768]{3,2,1,0:T(8,128)(2,1)} %get-tuple-element.310), channel_id=1, source_target_pairs={{0,16},{4,20},{8,24},{12,28},{16,0},{20,4},{24,8},{28,12},{1,17},{... | collective-permute-start | bytes 3538952 | tf_op jit(solution)/shard_map/ppermute | solution.py:682
  127.2 44.7 %collective-permute-start.16 = (bf16[2,4,96,768]{3,2,1,0:T(8,128)(2,1)}, bf16[2,4,96,768]{3,2,1,0:T(8,128)(2,1)}, u32[]{:S(2)}, u32[]{:S(2)}) collective-permute-start(bf16[2,4,96,768]{3,2,1,0:T(8,128)(2,1)} %get-tuple-element.311), channel_id=1, source_target_pairs={{0,8},{4,12},{8,0},{12,4},{16,24},{20,28},{24,16},{28,20},{1,9},{5... | collective-permute-start | bytes 3538952 | tf_op jit(solution)/shard_map/ppermute | solution.py:682
  127.8 29.3 %collective-permute-start.8 = (bf16[512,768]{1,0:T(8,128)(2,1)S(1)}, bf16[512,768]{1,0:T(8,128)(2,1)}, u32[]{:S(2)}, u32[]{:S(2)}) collective-permute-start(bf16[512,768]{1,0:T(8,128)(2,1)S(1)} %copy-done.6), channel_id=1, source_target_pairs={{0,1},{1,2},{2,3},{4,5},{5,6},{6,7},{8,9},{9,10},{10,11},{12,13},{... | collective-permute-start | bytes 2359304 | tf_op jit(solution)/shard_map/ppermute | solution.py:888
  179.1 12.7 %collective-permute-start.17 = (bf16[2,2,4,96,768]{4,3,2,1,0:T(8,128)(2,1)}, bf16[2,2,4,96,768]{4,3,2,1,0:T(8,128)(2,1)S(1)}, u32[]{:S(2)}, u32[]{:S(2)}) collective-permute-start(bf16[2,2,4,96,768]{4,3,2,1,0:T(8,128)(2,1)} %get-tuple-element.316), channel_id=1, source_target_pairs={{0,4},{4,0},{8,12},{12,8},{16,20},{20,16},{24,28},{28,24},{1,5},{5... | collective-permute-start | bytes 7077896 | tf_op jit(solution)/shard_map/ppermute | solution.py:682
  184.1 7.9 %collective-permute-start.18 = (bf16[2,2,4,96,768]{4,3,2,1,0:T(8,128)(2,1)}, bf16[2,2,4,96,768]{4,3,2,1,0:T(8,128)(2,1)}, u32[]{:S(2)}, u32[]{:S(2)}) collective-permute-start(bf16[2,2,4,96,768]{4,3,2,1,0:T(8,128)(2,1)} %get-tuple-element.317), channel_id=1, source_target_pairs={{0,4},{4,0},{8,12},{12,8},{16,20},{20,16},{24,28},{28,24},{1,5},{5... | collective-permute-start | bytes 7077896 | tf_op jit(solution)/shard_map/ppermute | solution.py:682
  206.9 21.1 %collective-permute-start.19 = (bf16[512,768]{1,0:T(8,128)(2,1)}, bf16[512,768]{1,0:T(8,128)(2,1)S(1)}, u32[]{:S(2)}, u32[]{:S(2)}) collective-permute-start(bf16[512,768]{1,0:T(8,128)(2,1)} %get-tuple-element.325.refs_2_.refs_5_), channel_id=1, source_target_pairs={{0,1},{1,2},{2,3},{4,5},{5,6},{6,7},{8,9},{9,10},{10,11},{12,13},{... | collective-permute-start | bytes 2359304 | tf_op jit(solution)/shard_map/ppermute | solution.py:888
  267.4 188.7 %reduce-scatter.5.cloned.1.call-start = ((), (), s32[]{:S(2)}) async-start(), calls=%async_computation.3 | async-start | bytes 10616832 | tf_op jit(solution)/shard_map/reduce_scatter | solution.py:791
  283.7 21.3 %collective-permute-start.20 = (bf16[512,768]{1,0:T(8,128)(2,1)}, bf16[512,768]{1,0:T(8,128)(2,1)S(1)}, u32[]{:S(2)}, u32[]{:S(2)}) collective-permute-start(bf16[512,768]{1,0:T(8,128)(2,1)} %get-tuple-element.351), channel_id=1, source_target_pairs={{1,0},{2,1},{3,2},{5,4},{6,5},{7,6},{9,8},{10,9},{11,10},{13,12},{... | collective-permute-start | bytes 2359304 | tf_op jit(solution)/shard_map/ppermute | solution.py:891
  318.0 21.6 %collective-permute-start.23 = (bf16[2,4,48,768]{3,2,1,0:T(8,128)(2,1)}, bf16[2,4,48,768]{3,2,1,0:T(8,128)(2,1)S(1)}, u32[]{:S(2)}, u32[]{:S(2)}) collective-permute-start(bf16[2,4,48,768]{3,2,1,0:T(8,128)(2,1)} %get-tuple-element.384), channel_id=1, source_target_pairs={{0,16},{4,20},{8,24},{12,28},{16,0},{20,4},{24,8},{28,12},{1,17},{... | collective-permute-start | bytes 1769480 | tf_op jit(solution)/shard_map/ppermute | solution.py:682
  319.0 20.6 %collective-permute-start.24 = (bf16[2,4,48,768]{3,2,1,0:T(8,128)(2,1)}, bf16[2,4,48,768]{3,2,1,0:T(8,128)(2,1)S(1)}, u32[]{:S(2)}, u32[]{:S(2)}) collective-permute-start(bf16[2,4,48,768]{3,2,1,0:T(8,128)(2,1)} %get-tuple-element.385), channel_id=1, source_target_pairs={{0,8},{4,12},{8,0},{12,4},{16,24},{20,28},{24,16},{28,20},{1,9},{5... | collective-permute-start | bytes 1769480 | tf_op jit(solution)/shard_map/ppermute | solution.py:682
  340.7 144.1 %all-gather.7.cloned.1.call-start = ((), (), s32[]{:S(2)}) async-start(), calls=%async_computation.5 | async-start | bytes 3981312 | tf_op jit(solution)/shard_map/all_gather | solution.py:995
  343.5 9.3 %collective-permute-start.25 = (bf16[4,48,768]{2,1,0:T(8,128)(2,1)}, bf16[4,48,768]{2,1,0:T(8,128)(2,1)S(1)}, u32[]{:S(2)}, u32[]{:S(2)}) collective-permute-start(bf16[4,48,768]{2,1,0:T(8,128)(2,1)} %get-tuple-element.392), channel_id=1, source_target_pairs={{0,8},{4,12},{8,0},{12,4},{16,24},{20,28},{24,16},{28,20},{1,9},{5... | collective-permute-start | bytes 884744 | tf_op jit(solution)/shard_map/ppermute | solution.py:682
  344.5 8.3 %collective-permute-start.26 = (bf16[4,48,768]{2,1,0:T(8,128)(2,1)}, bf16[4,48,768]{2,1,0:T(8,128)(2,1)S(1)}, u32[]{:S(2)}, u32[]{:S(2)}) collective-permute-start(bf16[4,48,768]{2,1,0:T(8,128)(2,1)} %get-tuple-element.393), channel_id=1, source_target_pairs={{0,16},{4,20},{8,24},{12,28},{16,0},{20,4},{24,8},{28,12},{1,17},{... | collective-permute-start | bytes 884744 | tf_op jit(solution)/shard_map/ppermute | solution.py:682
  357.1 32.9 %collective-permute-start.27 = (bf16[288,768]{1,0:T(8,128)(2,1)}, bf16[288,768]{1,0:T(8,128)(2,1)S(1)}, u32[]{:S(2)}, u32[]{:S(2)}) collective-permute-start(bf16[288,768]{1,0:T(8,128)(2,1)} %get-tuple-element.411), channel_id=1, source_target_pairs={{0,1},{1,0},{2,3},{3,2},{4,5},{5,4},{6,7},{7,6},{8,9},{9,8},{10,11... | collective-permute-start | bytes 1327112 | tf_op jit(solution)/shard_map/ppermute | solution.py:682
  357.4 32.5 %collective-permute-start.28 = (bf16[288,768]{1,0:T(8,128)(2,1)}, bf16[288,768]{1,0:T(8,128)(2,1)}, u32[]{:S(2)}, u32[]{:S(2)}) collective-permute-start(bf16[288,768]{1,0:T(8,128)(2,1)} %get-tuple-element.412), channel_id=1, source_target_pairs={{0,2},{1,3},{2,0},{3,1},{4,6},{5,7},{6,4},{7,5},{8,10},{9,11},{10,... | collective-permute-start | bytes 1327112 | tf_op jit(solution)/shard_map/ppermute | solution.py:682
  359.7 37.6 %collective-permute-start.29 = (bf16[288,768]{1,0:T(8,128)(2,1)}, bf16[288,768]{1,0:T(8,128)(2,1)S(1)}, u32[]{:S(2)}, u32[]{:S(2)}) collective-permute-start(bf16[288,768]{1,0:T(8,128)(2,1)} %get-tuple-element.413), channel_id=1, source_target_pairs={{0,3},{1,2},{2,1},{3,0},{4,7},{5,6},{6,5},{7,4},{8,11},{9,10},{10,... | collective-permute-start | bytes 1327112 | tf_op jit(solution)/shard_map/ppermute | solution.py:682
  402.6 20.2 %collective-permute-start.30 = (bf16[512,768]{1,0:T(8,128)(2,1)}, bf16[512,768]{1,0:T(8,128)(2,1)S(1)}, u32[]{:S(2)}, u32[]{:S(2)}) collective-permute-start(bf16[512,768]{1,0:T(8,128)(2,1)} %get-tuple-element.417), channel_id=1, source_target_pairs={{1,0},{2,1},{3,2},{5,4},{6,5},{7,6},{9,8},{10,9},{11,10},{13,12},{... | collective-permute-start | bytes 2359304 | tf_op jit(solution)/shard_map/ppermute | solution.py:891
  411.4 25.7 %collective-permute-start.33 = (bf16[2,4,48,768]{3,2,1,0:T(8,128)(2,1)}, bf16[2,4,48,768]{3,2,1,0:T(8,128)(2,1)S(1)}, u32[]{:S(2)}, u32[]{:S(2)}) collective-permute-start(bf16[2,4,48,768]{3,2,1,0:T(8,128)(2,1)} %get-tuple-element.435), channel_id=1, source_target_pairs={{0,16},{4,20},{8,24},{12,28},{16,0},{20,4},{24,8},{28,12},{1,17},{... | collective-permute-start | bytes 1769480 | tf_op jit(solution)/shard_map/ppermute | solution.py:682
  412.4 27.2 %collective-permute-start.34 = (bf16[2,4,48,768]{3,2,1,0:T(8,128)(2,1)}, bf16[2,4,48,768]{3,2,1,0:T(8,128)(2,1)S(1)}, u32[]{:S(2)}, u32[]{:S(2)}) collective-permute-start(bf16[2,4,48,768]{3,2,1,0:T(8,128)(2,1)} %get-tuple-element.436), channel_id=1, source_target_pairs={{0,8},{4,12},{8,0},{12,4},{16,24},{20,28},{24,16},{28,20},{1,9},{5... | collective-permute-start | bytes 1769480 | tf_op jit(solution)/shard_map/ppermute | solution.py:682
  443.4 7.4 %collective-permute-start.35 = (bf16[4,48,768]{2,1,0:T(8,128)(2,1)}, bf16[4,48,768]{2,1,0:T(8,128)(2,1)S(1)}, u32[]{:S(2)}, u32[]{:S(2)}) collective-permute-start(bf16[4,48,768]{2,1,0:T(8,128)(2,1)} %get-tuple-element.441), channel_id=1, source_target_pairs={{0,8},{4,12},{8,0},{12,4},{16,24},{20,28},{24,16},{28,20},{1,9},{5... | collective-permute-start | bytes 884744 | tf_op jit(solution)/shard_map/ppermute | solution.py:682
  444.3 7.5 %collective-permute-start.36 = (bf16[4,48,768]{2,1,0:T(8,128)(2,1)}, bf16[4,48,768]{2,1,0:T(8,128)(2,1)S(1)}, u32[]{:S(2)}, u32[]{:S(2)}) collective-permute-start(bf16[4,48,768]{2,1,0:T(8,128)(2,1)} %get-tuple-element.442), channel_id=1, source_target_pairs={{0,16},{4,20},{8,24},{12,28},{16,0},{20,4},{24,8},{28,12},{1,17},{... | collective-permute-start | bytes 884744 | tf_op jit(solution)/shard_map/ppermute | solution.py:682
  445.1 7.4 %collective-permute-start.37 = (bf16[536,256]{1,0:T(8,128)(2,1)}, bf16[536,256]{1,0:T(8,128)(2,1)S(1)}, u32[]{:S(2)}, u32[]{:S(2)}) collective-permute-start(bf16[536,256]{1,0:T(8,128)(2,1)} %get-tuple-element.458), channel_id=1, source_target_pairs={{0,4},{4,0},{8,12},{12,8},{16,20},{20,16},{24,28},{28,24},{1,5},{5... | collective-permute-start | bytes 823304 | tf_op jit(solution)/shard_map/ppermute | solution.py:682
  467.6 12.4 %collective-permute-start.42 = (bf16[536,256]{1,0:T(8,128)(2,1)}, bf16[536,256]{1,0:T(8,128)(2,1)S(1)}, u32[]{:S(2)}, u32[]{:S(2)}) collective-permute-start(bf16[536,256]{1,0:T(8,128)(2,1)} %get-tuple-element.474), channel_id=1, source_target_pairs={{0,16},{4,20},{8,24},{12,28},{16,0},{20,4},{24,8},{28,12},{1,17},{... | collective-permute-start | bytes 823304 | tf_op jit(solution)/shard_map/ppermute | solution.py:682
  467.6 23.3 %collective-permute-start.38 = (bf16[288,768]{1,0:T(8,128)(2,1)S(1)}, bf16[288,768]{1,0:T(8,128)(2,1)S(1)}, u32[]{:S(2)}, u32[]{:S(2)}) collective-permute-start(bf16[288,768]{1,0:T(8,128)(2,1)S(1)} %copy-done.52), channel_id=1, source_target_pairs={{0,1},{1,0},{2,3},{3,2},{4,5},{5,4},{6,7},{7,6},{8,9},{9,8},{10,11... | collective-permute-start | bytes 1327112 | tf_op jit(solution)/shard_map/ppermute | solution.py:682
  467.7 23.7 %collective-permute-start.39 = (bf16[288,768]{1,0:T(8,128)(2,1)S(1)}, bf16[288,768]{1,0:T(8,128)(2,1)}, u32[]{:S(2)}, u32[]{:S(2)}) collective-permute-start(bf16[288,768]{1,0:T(8,128)(2,1)S(1)} %copy-done.51), channel_id=1, source_target_pairs={{0,2},{1,3},{2,0},{3,1},{4,6},{5,7},{6,4},{7,5},{8,10},{9,11},{10,... | collective-permute-start | bytes 1327112 | tf_op jit(solution)/shard_map/ppermute | solution.py:682
  470.1 39.9 %collective-permute-start.40 = (bf16[288,768]{1,0:T(8,128)(2,1)S(1)}, bf16[288,768]{1,0:T(8,128)(2,1)}, u32[]{:S(2)}, u32[]{:S(2)}) collective-permute-start(bf16[288,768]{1,0:T(8,128)(2,1)S(1)} %copy-done.50), channel_id=1, source_target_pairs={{0,3},{1,2},{2,1},{3,0},{4,7},{5,6},{6,5},{7,4},{8,11},{9,10},{10,... | collective-permute-start | bytes 1327112 | tf_op jit(solution)/shard_map/ppermute | solution.py:682
  482.5 38.5 %collective-permute-start.45 = (bf16[536,256]{1,0:T(8,128)(2,1)}, bf16[536,256]{1,0:T(8,128)(2,1)S(1)}, u32[]{:S(2)}, u32[]{:S(2)}) collective-permute-start(bf16[536,256]{1,0:T(8,128)(2,1)} %get-tuple-element.488), channel_id=1, source_target_pairs={{0,1},{1,0},{2,3},{3,2},{4,5},{5,4},{6,7},{7,6},{8,9},{9,8},{10,11... | collective-permute-start | bytes 823304 | tf_op jit(solution)/shard_map/ppermute | solution.py:682
  482.5 39.3 %collective-permute-start.46 = (bf16[536,256]{1,0:T(8,128)(2,1)}, bf16[536,256]{1,0:T(8,128)(2,1)S(1)}, u32[]{:S(2)}, u32[]{:S(2)}) collective-permute-start(bf16[536,256]{1,0:T(8,128)(2,1)} %get-tuple-element.488), channel_id=1, source_target_pairs={{0,2},{1,3},{2,0},{3,1},{4,6},{5,7},{6,4},{7,5},{8,10},{9,11},{10,... | collective-permute-start | bytes 823304 | tf_op jit(solution)/shard_map/ppermute | solution.py:682
  490.9 37.0 %collective-permute-start.47 = (bf16[536,256]{1,0:T(8,128)(2,1)S(1)}, bf16[536,256]{1,0:T(8,128)(2,1)S(1)}, u32[]{:S(2)}, u32[]{:S(2)}) collective-permute-start(bf16[536,256]{1,0:T(8,128)(2,1)S(1)} %copy-done.18), channel_id=1, source_target_pairs={{0,3},{1,2},{2,1},{3,0},{4,7},{5,6},{6,5},{7,4},{8,11},{9,10},{10,... | collective-permute-start | bytes 823304 | tf_op jit(solution)/shard_map/ppermute | solution.py:682
  512.9 15.7 %collective-permute-start.43 = (bf16[144,768]{1,0:T(8,128)(2,1)}, bf16[144,768]{1,0:T(8,128)(2,1)S(1)}, u32[]{:S(2)}, u32[]{:S(2)}) collective-permute-start(bf16[144,768]{1,0:T(8,128)(2,1)} %get-tuple-element.486), channel_id=1, source_target_pairs={{0,8},{4,12},{8,0},{12,4},{16,24},{20,28},{24,16},{28,20},{1,9},{5... | collective-permute-start | bytes 663560 | tf_op jit(solution)/shard_map/ppermute | solution.py:682
  520.1 8.5 %collective-permute-start.44 = (bf16[144,768]{1,0:T(8,128)(2,1)}, bf16[144,768]{1,0:T(8,128)(2,1)S(1)}, u32[]{:S(2)}, u32[]{:S(2)}) collective-permute-start(bf16[144,768]{1,0:T(8,128)(2,1)} %get-tuple-element.487), channel_id=1, source_target_pairs={{0,16},{4,20},{8,24},{12,28},{16,0},{20,4},{24,8},{28,12},{1,17},{... | collective-permute-start | bytes 663560 | tf_op jit(solution)/shard_map/ppermute | solution.py:682
  533.0 8.0 %collective-permute-start.48 = (bf16[2,144,768]{2,1,0:T(8,128)(2,1)}, bf16[2,144,768]{2,1,0:T(8,128)(2,1)}, u32[]{:S(2)}, u32[]{:S(2)}) collective-permute-start(bf16[2,144,768]{2,1,0:T(8,128)(2,1)} %get-tuple-element.494), channel_id=1, source_target_pairs={{0,16},{4,20},{8,24},{12,28},{16,0},{20,4},{24,8},{28,12},{1,17},{... | collective-permute-start | bytes 1327112 | tf_op jit(solution)/shard_map/ppermute | solution.py:682
  534.8 7.5 %collective-permute-start.49 = (bf16[2,144,768]{2,1,0:T(8,128)(2,1)}, bf16[2,144,768]{2,1,0:T(8,128)(2,1)}, u32[]{:S(2)}, u32[]{:S(2)}) collective-permute-start(bf16[2,144,768]{2,1,0:T(8,128)(2,1)} %get-tuple-element.495), channel_id=1, source_target_pairs={{0,8},{4,12},{8,0},{12,4},{16,24},{20,28},{24,16},{28,20},{1,9},{5... | collective-permute-start | bytes 1327112 | tf_op jit(solution)/shard_map/ppermute | solution.py:682
  546.3 12.5 %collective-permute-start.50 = (bf16[2,2,144,768]{3,2,1,0:T(8,128)(2,1)}, bf16[2,2,144,768]{3,2,1,0:T(8,128)(2,1)S(1)}, u32[]{:S(2)}, u32[]{:S(2)}) collective-permute-start(bf16[2,2,144,768]{3,2,1,0:T(8,128)(2,1)} %get-tuple-element.500), channel_id=1, source_target_pairs={{0,4},{4,0},{8,12},{12,8},{16,20},{20,16},{24,28},{28,24},{1,5},{5... | collective-permute-start | bytes 2654216 | tf_op jit(solution)/shard_map/ppermute | solution.py:682
  (99 other events, 435.6 us)
Sparse Core Ops, SparseCore 0:
  13.5 150.8 all-gather.4
  267.5 81.5 reduce-scatter.2
  352.6 88.8 reduce-scatter.4
  443.3 38.2 all-gather.6

commit v6 on v5

--- a/solution.py
+++ b/solution.py
@@ -898,10 +898,9 @@
         piece = attn_piece(0)
         attn0 = Gather(links, piece[:middle], piece[middle:])
         attn0.start_mp()
-        (later,) = order.pin(jnp.concatenate((attn_piece(1),) + ff_pieces(1), axis=0))
-        later = lax.all_gather(later, ("g", "c", "mp"), axis=0, tiled=False)
         ff0 = Gather(links, *ff_pieces(0))
         ff0.start_mp()
+        later = jnp.concatenate((attn_piece(1),) + ff_pieces(1), axis=0)
         x, normed = enter_kernel(order, tokens.reshape(rows, width), gains[0, 0], shifts[0, 0])
 
         seg_pad = jnp.concatenate([jnp.full((seqs, window), -1, segments.dtype), segments], axis=1)
@@ -915,6 +914,8 @@
         attn0.start()
         ff0.wait_mp()
         ff0.start()
+        (later,) = order.pin(later)
+        later = lax.all_gather(later, ("g", "c", "mp"), axis=0, tiled=False)
         (normed,) = order.pin(normed)
         halo = forward_halo(normed)
         attn0.wait_all()
@@ -1011,15 +1012,18 @@
             return (pair[0].astype(F32) + coming.astype(F32)).astype(BF)
 
         bits = [1 << k for k in range(dp.bit_length() - 1)]
+        pair = small_start(bits[0])
         r_attn0.wait()
+        small = small_wait(pair)
         r_attn0.start()
-        pair = small_start(bits[0])
+        for bit in bits[1:-1]:
+            pair = small_start(bit)
+            small = small_wait(pair)
         attn0_sum = r_attn0.wait_all()
+        pair = small_start(bits[-1])
         small = small_wait(pair)
         up0, down0 = wide0.wait()
         mp0 = ReduceMp(links, attn0_sum + [up0, down0], None)
-        for bit in bits[1:]:
-            small = small_wait(small_start(bit))
         (small,) = order.pin(small)
         small_parts = [links.swap(small, "mp", p) for p in range(1, mp)]
         (full1,) = order.pin(full1)

time: 579 us -> 541 us (0.934)
  waiting for transfers between devices: 205 us -> 164 us
    ppermute x48, waiting for transfers between devices: 149 us -> 97.3 us  [swap(): return lax.ppermute(value, axis, [(i, i ^ bit) for i in range(size)])]
    all_gather x1, waiting for transfers between devices: 0.01 us -> 7.77 us  [shards(): full1 = lax.all_gather(sum1, DP, axis=0, tiled=False)]
    unnamed x182 -> x184, local copies, waits for them, and re-layouts: 24.9 us -> 23.6 us
  transfers between devices with their start and end apart: 56 -> 56, of which waited for: 28 -> 30; matrix products, arithmetic and copies ran while one was open for 13% -> 13% of each run, Pallas kernels for 22% -> 23%
where the time goes in v6:
time: 541 us; the launch traced here: 535 us
  Pallas kernels  169 us (31%)
  waiting for transfers between devices  164 us (30%)
  starting transfers between devices  75.7 us (14%)
  other arithmetic  54.8 us (10%)
  local copies, waits for them, and re-layouts  49.5 us (9%)
  between operations  15.2 us (3%)
  matrix products  6.89 us (1%)
    pallas_call x12, Pallas kernels, run(): *results, order.token = kernel(*operands, order.token)  156 us
    ppermute x48, waiting for transfers between devices, swap(): return lax.ppermute(value, axis, [(i, i ^ bit) for i in range(size)])  97.3 us
    ppermute x48, starting transfers between devices, swap(): return lax.ppermute(value, axis, [(i, i ^ bit) for i in range(size)])  62.4 us
    ppermute x2, waiting for transfers between devices, forward_halo(): return lax.ppermute(value, 'mp', [(i, i + 1) for i in range(mp - 1)])  36.3 us
    another operation x12, other arithmetic, wait(): self.values[k] = jnp.stack([self.values[k], coming[k]], axis=place)  23.9 us
    unnamed x184, local copies, waits for them, and re-layouts  23.6 us
    ppermute x2, waiting for transfers between devices, backward_halo(): return lax.ppermute(value, 'mp', [(i + 1, i) for i in range(mp - 1)])  14.9 us
    pallas_call x2, Pallas kernels, finish_layer(): pl.pallas_call(with_token, grid_spec=pltpu.PrefetchScalarGridSpec(num_sca...  12.4 us
  transfers between devices with their start and end apart: 56, of which 30 were waited for; matrix products, arithmetic and copies ran while one was open for 13% of the time, Pallas kernels for 23%

profile of v6, /device:TPU:9, one launch (start us, length us, event | category | flops | bytes accessed | tf_op | source)
XLA Modules:
  0.0 535.0 jit_solution(16657174889504664271)
XLA Ops:
  10.3 2.5 collective-permute-start.4
  24.6 2.6 enter.1
  35.9 3.3 collective-permute-done.6.refs_0_
  44.6 6.5 %collective-permute-done.2.refs_2_ = bf16[192,768]{1,0:T(8,128)(2,1)S(1)} collective-permute-done((bf16[192,768]{1,0:T(8,128)(2,1)S(1)}, bf16[192,768]{1,0:T(8,128)(2,1)S(1)}, u32[]{:S(2)}, u32[]{:S(2)}) %collective-permute-start.2) | collective-permute-done | bytes 294944 | tf_op jit(solution)/shard_map/ppermute | solution.py:682
  59.8 10.5 %collective-permute-done.10.refs_1_ = bf16[2,4,48,768]{3,2,1,0:T(8,128)(2,1)S(1)} collective-permute-done((bf16[2,4,48,768]{3,2,1,0:T(8,128)(2,1)S(1)}, bf16[2,4,48,768]{3,2,1,0:T(8,128)(2,1)S(1)}, u32[]{:S(2)}, u32[]{:S(2)}) %collective-permute-start.10) | collective-permute-done | bytes 589856 | tf_op jit(solution)/shard_map/ppermute | solution.py:682
  72.8 2.2 pad_maximum_fusion.5.refs_1_
  76.2 7.6 %collective-permute-start.11 = (bf16[2,2,4,48,768]{4,3,2,1,0:T(8,128)(2,1)}, bf16[2,2,4,48,768]{4,3,2,1,0:T(8,128)(2,1)S(1)}, u32[]{:S(2)}, u32[]{:S(2)}) collective-permute-start(bf16[2,2,4,48,768]{4,3,2,1,0:T(8,128)(2,1)} %get-tuple-element.294), channel_id=1, source_target_pairs={{0,4},{4,0},{8,12},{12,8},{16,20},{20,16},{24,28},{28,24},{1,5},{5... | collective-permute-start | bytes 3538952 | tf_op jit(solution)/shard_map/ppermute | solution.py:682
  86.8 2.3 pad_maximum_fusion.7.refs_1_
  92.5 3.7 collective-permute-start.8
  99.9 21.8 %collective-permute-done.8.refs_0_ = bf16[512,768]{1,0:T(8,128)(2,1)} collective-permute-done((bf16[512,768]{1,0:T(8,128)(2,1)S(1)}, bf16[512,768]{1,0:T(8,128)(2,1)}, u32[]{:S(2)}, u32[]{:S(2)}) %collective-permute-start.8) | collective-permute-done | bytes 786464 | tf_op jit(solution)/shard_map/ppermute | solution.py:888
  121.7 14.6 %attn_fwd.2 = (bf16[512,768]{1,0:T(8,128)(2,1)}, bf16[512,768]{1,0:T(8,128)(2,1)}, bf16[512,768]{1,0:T(8,128)(2,1)}, bf16[1024,768]{1,0:T(8,128)(2,1)}, bf16[102...) custom-call(s32[6]{0:T(128)} %stack.207.refs_0_, ...), custom_call_target="tpu_custom_call", output_to_operand_aliasing={{10}: (13, {})} | custom-call | tf_op jit(solution)/shard_map/attn_fwd/pallas_call | solution.py:74
  137.6 3.0 pad_maximum_fusion.1.refs_1_
  140.6 2.9 pad_maximum_fusion.refs_0_
  143.5 3.5 collective-permute-start.17
  147.1 7.7 %collective-permute-done.17.refs_0_ = bf16[2,2,4,96,768]{4,3,2,1,0:T(8,128)(2,1)S(1)} collective-permute-done((bf16[2,2,4,96,768]{4,3,2,1,0:T(8,128)(2,1)}, bf16[2,2,4,96,768]{4,3,2,1,0:T(8,128)(2,1)S(1)}, u32[]{:S(2)}, u32[]{:S(2)}) %collective-permute-start.17) | collective-permute-done | bytes 2359328 | tf_op jit(solution)/shard_map/ppermute | solution.py:682
  156.1 13.7 %ff_fwd.1 = (bf16[512,3072]{1,0:T(8,128)(2,1)}, bf16[512,3072]{1,0:T(8,128)(2,1)}, f32[512,768]{1,0:T(8,128)}, bf16[512,768]{1,0:T(8,128)(2,1)}, s32[8,128]{1,0:T(8,128)}) custom-call(f32[512,768]{1,0:T(8,128)} %get-tuple-element.308.refs_0_.refs_1_, bf16[512,768]{1,0:T(8,128)(2,1)} %get-tuple-element.309.refs_1_.refs_2_, ...), custom_call_target="tpu_custom_call", output_to_operand_aliasing={{4}: (8, {})} | custom-call | tf_op jit(solution)/shard_map/ff_fwd/pallas_call | solution.py:74
  169.8 4.9 collective-permute-start.19
  176.7 14.5 %collective-permute-done.19.refs_0_ = bf16[512,768]{1,0:T(8,128)(2,1)S(1)} collective-permute-done((bf16[512,768]{1,0:T(8,128)(2,1)}, bf16[512,768]{1,0:T(8,128)(2,1)S(1)}, u32[]{:S(2)}, u32[]{:S(2)}) %collective-permute-start.19) | collective-permute-done | bytes 786464 | tf_op jit(solution)/shard_map/ppermute | solution.py:888
  192.1 14.1 %attn_fwd.3 = (bf16[512,768]{1,0:T(8,128)(2,1)}, bf16[512,768]{1,0:T(8,128)(2,1)}, bf16[512,768]{1,0:T(8,128)(2,1)}, bf16[1024,768]{1,0:T(8,128)(2,1)}, bf16[102...) custom-call(s32[6]{0:T(128)} %stack.207.refs_0_, ...), custom_call_target="tpu_custom_call", output_to_operand_aliasing={{10}: (10, {})} | custom-call | tf_op jit(solution)/shard_map/attn_fwd/pallas_call | solution.py:74
  206.2 24.4 %ff_bwd.2 = (bf16[4,2,2,384,768]{4,3,2,1,0:T(8,128)(2,1)}, f32[512,768]{1,0:T(8,128)}, bf16[512,768]{1,0:T(8,128)(2,1)}, f32[1,768]{1,0:T(1,128)}, f32[1,768]{1,...) custom-call(s32[6]{0:T(128)} %stack.207.refs_0_, ...), custom_call_target="tpu_custom_call", output_to_operand_aliasing={{6}: (7, {})} | custom-call | tf_op jit(solution)/shard_map/ff_bwd/pallas_call | solution.py:74
  230.7 16.1 %attn_bwd.2 = (bf16[512,768]{1,0:T(8,128)(2,1)}, bf16[1024,768]{1,0:T(8,128)(2,1)}, bf16[1024,768]{1,0:T(8,128)(2,1)}, f32[256,256]{1,0:T(8,128)}, f32[512,768]{...) custom-call(s32[6]{0:T(128)} %stack.207.refs_0_, ...), custom_call_target="tpu_custom_call", output_to_operand_aliasing={{6}: (10, {})} | custom-call | tf_op jit(solution)/shard_map/attn_bwd/pallas_call | solution.py:74
  248.9 11.9 %attn_wgrad.2 = (bf16[4,192,768]{2,1,0:T(8,128)(2,1)}, bf16[4,192,768]{2,1,0:T(8,128)(2,1)}, bf16[4,192,768]{2,1,0:T(8,128)(2,1)}, bf16[4,192,768]{2,1,0:T(8,128)(2,1)}, s32[8,128]{1,0:T(8,128)}) custom-call(s32[6]{0:T(128)} %stack.207.refs_0_, bf16[512,768]{1,0:T(8,128)(2,1)} %get-tuple-element.352.refs_1_, ...), custom_call_target="tpu_custom_call", output_to_operand_aliasing={{4}: (8, {})} | custom-call | tf_op jit(solution)/shard_map/attn_wgrad/pallas_call | solution.py:74
  260.9 6.9 %collective-permute-done.20.refs_0_ = bf16[512,768]{1,0:T(8,128)(2,1)S(1)} collective-permute-done((bf16[512,768]{1,0:T(8,128)(2,1)}, bf16[512,768]{1,0:T(8,128)(2,1)S(1)}, u32[]{:S(2)}, u32[]{:S(2)}) %collective-permute-start.20) | collective-permute-done | bytes 786464 | tf_op jit(solution)/shard_map/ppermute | solution.py:891
  270.4 5.2 leave.2
  284.2 19.8 %ff_bwd.3 = (bf16[4,2,2,384,768]{4,3,2,1,0:T(8,128)(2,1)}, f32[512,768]{1,0:T(8,128)}, bf16[512,768]{1,0:T(8,128)(2,1)}, f32[1,768]{1,0:T(1,128)}, f32[1,768]{1,0:T(1,128)}, /*index=5*/s32[8,128]{1,0:T(8,128)}) custom-call(s32[6]{0:T(128)} %stack.207.refs_0_, f32[512,768]{1,0:T(8,128)} %get-tuple-element.308.refs_0_.refs_1_, ...), custom_call_target="tpu_custom_call", output_to_operand_aliasing={{5}: (11, {})} | custom-call | tf_op jit(solution)/shard_map/ff_bwd/pallas_call | solution.py:74
  308.2 6.0 %reduce-scatter.3.cloned.1.call-done.refs_0_ = bf16[1,2,384,768]{3,2,1,0:T(8,128)(2,1)} async-done(((bf16[8,2,384,768]{3,2,1,0:T(8,128)(2,1)}), bf16[1,2,384,768]{3,2,1,0:T(8,128)(2,1)}) %reduce-scatter.3.cloned.1.call-update) | async-done | bytes 1179664 | tf_op jit(solution)/shard_map/reduce_scatter | solution.py:791
  314.2 3.7 collective-permute-done.25.refs_0_
  325.0 17.0 %attn_bwd.3 = (bf16[512,768]{1,0:T(8,128)(2,1)}, bf16[1024,768]{1,0:T(8,128)(2,1)}, bf16[1024,768]{1,0:T(8,128)(2,1)}, f32[256,256]{1,0:T(8,128)}, f32[512,768]{...) custom-call(s32[6]{0:T(128)} %stack.207.refs_0_, ...), custom_call_target="tpu_custom_call", output_to_operand_aliasing={{6}: (13, {})} | custom-call | tf_op jit(solution)/shard_map/attn_bwd/pallas_call | solution.py:74
  342.0 11.8 %attn_wgrad.3 = (bf16[4,192,768]{2,1,0:T(8,128)(2,1)}, bf16[4,192,768]{2,1,0:T(8,128)(2,1)}, bf16[4,192,768]{2,1,0:T(8,128)(2,1)}, bf16[4,192,768]{2,1,0:T(8,128)(2,1)}, s32[8,128]{1,0:T(8,128)}) custom-call(s32[6]{0:T(128)} %stack.207.refs_0_, bf16[512,768]{1,0:T(8,128)(2,1)} %get-tuple-element.404.refs_1_, ...), custom_call_target="tpu_custom_call", output_to_operand_aliasing={{4}: (8, {})} | custom-call | tf_op jit(solution)/shard_map/attn_wgrad/pallas_call | solution.py:74
  353.8 8.8 %collective-permute-done.29.refs_2_ = bf16[288,768]{1,0:T(8,128)(2,1)S(1)} collective-permute-done((bf16[288,768]{1,0:T(8,128)(2,1)}, bf16[288,768]{1,0:T(8,128)(2,1)S(1)}, u32[]{:S(2)}, u32[]{:S(2)}) %collective-permute-start.29) | collective-permute-done | bytes 442400 | tf_op jit(solution)/shard_map/ppermute | solution.py:682
  367.8 2.2 collective-permute-start.30
  380.0 8.0 %collective-permute-done.30.refs_0_ = bf16[512,768]{1,0:T(8,128)(2,1)S(1)} collective-permute-done((bf16[512,768]{1,0:T(8,128)(2,1)}, bf16[512,768]{1,0:T(8,128)(2,1)S(1)}, u32[]{:S(2)}, u32[]{:S(2)}) %collective-permute-start.30) | collective-permute-done | bytes 786464 | tf_op jit(solution)/shard_map/ppermute | solution.py:891
  388.9 4.9 leave.3
  406.7 2.8 collective-permute-done.38.refs_0_
  413.4 3.2 collective-permute-start.39
  418.7 7.1 %collective-permute-done.39.refs_0_ = bf16[536,256]{1,0:T(8,128)(2,1)S(1)} collective-permute-done((bf16[536,256]{1,0:T(8,128)(2,1)}, bf16[536,256]{1,0:T(8,128)(2,1)S(1)}, u32[]{:S(2)}, u32[]{:S(2)}) %collective-permute-start.39) | collective-permute-done | bytes 274464 | tf_op jit(solution)/shard_map/ppermute | solution.py:682
  429.2 3.4 collective-permute-start.40
  434.7 2.3 collective-permute-start.45
  437.0 7.8 %all-gather.7.cloned.1.call-done = bf16[2304,768]{1,0:T(8,128)(2,1)} async-done(((bf16[288,768]{1,0:T(8,128)(2,1)}), bf16[2304,768]{1,0:T(8,128)(2,1)}) %all-gather.7.cloned.1.call-update) | async-done | bytes 3538960 | tf_op jit(solution)/shard_map/all_gather | solution.py:996
  444.7 6.1 %finish.2 = (f32[2,3,192,768]{3,2,1,0:T(8,128)}, f32[2,192,768]{2,1,0:T(8,128)}, f32[2,768,768]{2,1,0:T(8,128)}, f32[2,768,768]{2,1,0:T(8,128)}, s32[8,128]{1,0:T(8,128)}) custom-call(s32[6]{0:T(128)} %stack.207.refs_0_, bf16[8,288,768]{2,1,0:T(8,128)(2,1)} %get-tuple-element.479.refs_1_, ...), custom_call_target="tpu_custom_call", output_to_operand_aliasing={{4}: (2, {})} | custom-call | tf_op jit(solution)/shard_map/finish/pallas_call | solution.py:640
  452.1 30.0 %collective-permute-done.42.refs_2_ = bf16[288,768]{1,0:T(8,128)(2,1)S(1)} collective-permute-done((bf16[288,768]{1,0:T(8,128)(2,1)}, bf16[288,768]{1,0:T(8,128)(2,1)S(1)}, u32[]{:S(2)}, u32[]{:S(2)}) %collective-permute-start.42) | collective-permute-done | bytes 442400 | tf_op jit(solution)/shard_map/ppermute | solution.py:682
  485.8 2.4 collective-permute-start.43
  488.6 4.9 collective-permute-done.47.refs_2_
  498.7 3.1 collective-permute-start.49
  503.3 2.3 gather_fusion
  506.1 2.7 collective-permute-done.49.refs_1_
  512.8 4.4 collective-permute-start.50
  521.7 6.3 %finish.3 = (f32[2,3,192,768]{3,2,1,0:T(8,128)}, f32[2,192,768]{2,1,0:T(8,128)}, f32[2,768,768]{2,1,0:T(8,128)}, f32[2,768,768]{2,1,0:T(8,128)}, s32[8,128]{1,0:T(8,128)}) custom-call(s32[6]{0:T(128)} %stack.207.refs_0_, bf16[4,144,768]{2,1,0:T(8,128)(2,1)} %bitcast.251, ...), custom_call_target="tpu_custom_call", output_to_operand_aliasing={{0}: (5, {}), {1}: (6, {}), {2}: (7, {}), {3}: (8, {}), {4}... | custom-call | tf_op jit(solution)/shard_map/finish/pallas_call | solution.py:640
  (429 shorter events, 142.2 us)
Async XLA Ops:
  7.2 169.6 %all-gather.5.cloned.1.call-start = ((), (), s32[]{:S(2)}) async-start(), calls=%async_computation.4 | async-start | bytes 14598144 | tf_op jit(solution)/shard_map/all_gather | solution.py:918
  10.3 16.9 %collective-permute-start.3 = (bf16[96,768]{1,0:T(8,128)(2,1)}, bf16[96,768]{1,0:T(8,128)(2,1)S(1)}, u32[]{:S(2)}, u32[]{:S(2)}) collective-permute-start(bf16[96,768]{1,0:T(8,128)(2,1)} %get-tuple-element.268), channel_id=1, source_target_pairs={{0,1},{1,0},{2,3},{3,2},{4,5},{5,4},{6,7},{7,6},{8,9},{9,8},{10,11... | collective-permute-start | bytes 442376 | tf_op jit(solution)/shard_map/ppermute | solution.py:682
  10.3 17.2 %collective-permute-start.4 = (bf16[96,768]{1,0:T(8,128)(2,1)}, bf16[96,768]{1,0:T(8,128)(2,1)S(1)}, u32[]{:S(2)}, u32[]{:S(2)}) collective-permute-start(bf16[96,768]{1,0:T(8,128)(2,1)} %get-tuple-element.268), channel_id=1, source_target_pairs={{0,2},{1,3},{2,0},{3,1},{4,6},{5,7},{6,4},{7,5},{8,10},{9,11},{10,... | collective-permute-start | bytes 442376 | tf_op jit(solution)/shard_map/ppermute | solution.py:682
  12.8 14.8 %collective-permute-start.5 = (bf16[96,768]{1,0:T(8,128)(2,1)}, bf16[96,768]{1,0:T(8,128)(2,1)S(1)}, u32[]{:S(2)}, u32[]{:S(2)}) collective-permute-start(bf16[96,768]{1,0:T(8,128)(2,1)} %get-tuple-element.268), channel_id=1, source_target_pairs={{0,3},{1,2},{2,1},{3,0},{4,7},{5,6},{6,5},{7,4},{8,11},{9,10},{10,... | collective-permute-start | bytes 442376 | tf_op jit(solution)/shard_map/ppermute | solution.py:682
  17.2 27.4 %collective-permute-start = (bf16[192,768]{1,0:T(8,128)(2,1)}, bf16[192,768]{1,0:T(8,128)(2,1)S(1)}, u32[]{:S(2)}, u32[]{:S(2)}) collective-permute-start(bf16[192,768]{1,0:T(8,128)(2,1)} %get-tuple-element.267), channel_id=1, source_target_pairs={{0,1},{1,0},{2,3},{3,2},{4,5},{5,4},{6,7},{7,6},{8,9},{9,8},{10,11... | collective-permute-start | bytes 884744 | tf_op jit(solution)/shard_map/ppermute | solution.py:682
  18.3 26.3 %collective-permute-start.1 = (bf16[192,768]{1,0:T(8,128)(2,1)}, bf16[192,768]{1,0:T(8,128)(2,1)S(1)}, u32[]{:S(2)}, u32[]{:S(2)}) collective-permute-start(bf16[192,768]{1,0:T(8,128)(2,1)} %get-tuple-element.267), channel_id=1, source_target_pairs={{0,2},{1,3},{2,0},{3,1},{4,6},{5,7},{6,4},{7,5},{8,10},{9,11},{10,... | collective-permute-start | bytes 884744 | tf_op jit(solution)/shard_map/ppermute | solution.py:682
  27.3 23.7 %collective-permute-start.2 = (bf16[192,768]{1,0:T(8,128)(2,1)S(1)}, bf16[192,768]{1,0:T(8,128)(2,1)S(1)}, u32[]{:S(2)}, u32[]{:S(2)}) collective-permute-start(bf16[192,768]{1,0:T(8,128)(2,1)S(1)} %copy-done.26), channel_id=1, source_target_pairs={{0,3},{1,2},{2,1},{3,0},{4,7},{5,6},{6,5},{7,4},{8,11},{9,10},{10,... | collective-permute-start | bytes 884744 | tf_op jit(solution)/shard_map/ppermute | solution.py:682
  32.6 6.6 %collective-permute-start.6 = (bf16[4,48,768]{2,1,0:T(8,128)(2,1)}, bf16[4,48,768]{2,1,0:T(8,128)(2,1)S(1)}, u32[]{:S(2)}, u32[]{:S(2)}) collective-permute-start(bf16[4,48,768]{2,1,0:T(8,128)(2,1)} %get-tuple-element.274), channel_id=1, source_target_pairs={{0,8},{4,12},{8,0},{12,4},{16,24},{20,28},{24,16},{28,20},{1,9},{5... | collective-permute-start | bytes 884744 | tf_op jit(solution)/shard_map/ppermute | solution.py:682
  56.6 257.7 %reduce-scatter.3.cloned.1.call-start = ((), (), s32[]{:S(2)}) async-start(), calls=%async_computation.2 | async-start | bytes 10616832 | tf_op jit(solution)/shard_map/reduce_scatter | solution.py:791
  56.9 13.4 %collective-permute-start.10 = (bf16[2,4,48,768]{3,2,1,0:T(8,128)(2,1)S(1)}, bf16[2,4,48,768]{3,2,1,0:T(8,128)(2,1)S(1)}, u32[]{:S(2)}, u32[]{:S(2)}) collective-permute-start(bf16[2,4,48,768]{3,2,1,0:T(8,128)(2,1)S(1)} %copy-done.8), channel_id=1, source_target_pairs={{0,8},{4,12},{8,0},{12,4},{16,24},{20,28},{24,16},{28,20},{1,9},{5... | collective-permute-start | bytes 1769480 | tf_op jit(solution)/shard_map/ppermute | solution.py:682
  58.1 13.9 %collective-permute-start.9 = (bf16[2,4,48,768]{3,2,1,0:T(8,128)(2,1)S(1)}, bf16[2,4,48,768]{3,2,1,0:T(8,128)(2,1)S(1)}, u32[]{:S(2)}, u32[]{:S(2)}) collective-permute-start(bf16[2,4,48,768]{3,2,1,0:T(8,128)(2,1)S(1)} %copy-done.10), channel_id=1, source_target_pairs={{0,16},{4,20},{8,24},{12,28},{16,0},{20,4},{24,8},{28,12},{1,17},{... | collective-permute-start | bytes 1769480 | tf_op jit(solution)/shard_map/ppermute | solution.py:682
  59.4 26.5 %collective-permute-start.13 = (bf16[4,96,768]{2,1,0:T(8,128)(2,1)}, bf16[4,96,768]{2,1,0:T(8,128)(2,1)S(1)}, u32[]{:S(2)}, u32[]{:S(2)}) collective-permute-start(bf16[4,96,768]{2,1,0:T(8,128)(2,1)} %get-tuple-element.296), channel_id=1, source_target_pairs={{0,8},{4,12},{8,0},{12,4},{16,24},{20,28},{24,16},{28,20},{1,9},{5... | collective-permute-start | bytes 1769480 | tf_op jit(solution)/shard_map/ppermute | solution.py:682
  59.6 27.1 %collective-permute-start.14 = (bf16[4,96,768]{2,1,0:T(8,128)(2,1)}, bf16[4,96,768]{2,1,0:T(8,128)(2,1)}, u32[]{:S(2)}, u32[]{:S(2)}) collective-permute-start(bf16[4,96,768]{2,1,0:T(8,128)(2,1)} %get-tuple-element.297), channel_id=1, source_target_pairs={{0,16},{4,20},{8,24},{12,28},{16,0},{20,4},{24,8},{28,12},{1,17},{... | collective-permute-start | bytes 1769480 | tf_op jit(solution)/shard_map/ppermute | solution.py:682
  76.2 22.2 %collective-permute-start.11 = (bf16[2,2,4,48,768]{4,3,2,1,0:T(8,128)(2,1)}, bf16[2,2,4,48,768]{4,3,2,1,0:T(8,128)(2,1)S(1)}, u32[]{:S(2)}, u32[]{:S(2)}) collective-permute-start(bf16[2,2,4,48,768]{4,3,2,1,0:T(8,128)(2,1)} %get-tuple-element.294), channel_id=1, source_target_pairs={{0,4},{4,0},{8,12},{12,8},{16,20},{20,16},{24,28},{28,24},{1,5},{5... | collective-permute-start | bytes 3538952 | tf_op jit(solution)/shard_map/ppermute | solution.py:682
  83.8 14.6 %collective-permute-start.12 = (bf16[2,2,4,48,768]{4,3,2,1,0:T(8,128)(2,1)}, bf16[2,2,4,48,768]{4,3,2,1,0:T(8,128)(2,1)S(1)}, u32[]{:S(2)}, u32[]{:S(2)}) collective-permute-start(bf16[2,2,4,48,768]{4,3,2,1,0:T(8,128)(2,1)} %get-tuple-element.295), channel_id=1, source_target_pairs={{0,4},{4,0},{8,12},{12,8},{16,20},{20,16},{24,28},{28,24},{1,5},{5... | collective-permute-start | bytes 3538952 | tf_op jit(solution)/shard_map/ppermute | solution.py:682
  90.2 46.1 %collective-permute-start.15 = (bf16[2,4,96,768]{3,2,1,0:T(8,128)(2,1)}, bf16[2,4,96,768]{3,2,1,0:T(8,128)(2,1)}, u32[]{:S(2)}, u32[]{:S(2)}) collective-permute-start(bf16[2,4,96,768]{3,2,1,0:T(8,128)(2,1)} %get-tuple-element.310), channel_id=1, source_target_pairs={{0,16},{4,20},{8,24},{12,28},{16,0},{20,4},{24,8},{28,12},{1,17},{... | collective-permute-start | bytes 3538952 | tf_op jit(solution)/shard_map/ppermute | solution.py:682
  91.4 44.9 %collective-permute-start.16 = (bf16[2,4,96,768]{3,2,1,0:T(8,128)(2,1)}, bf16[2,4,96,768]{3,2,1,0:T(8,128)(2,1)}, u32[]{:S(2)}, u32[]{:S(2)}) collective-permute-start(bf16[2,4,96,768]{3,2,1,0:T(8,128)(2,1)} %get-tuple-element.311), channel_id=1, source_target_pairs={{0,8},{4,12},{8,0},{12,4},{16,24},{20,28},{24,16},{28,20},{1,9},{5... | collective-permute-start | bytes 3538952 | tf_op jit(solution)/shard_map/ppermute | solution.py:682
  92.5 29.2 %collective-permute-start.8 = (bf16[512,768]{1,0:T(8,128)(2,1)S(1)}, bf16[512,768]{1,0:T(8,128)(2,1)}, u32[]{:S(2)}, u32[]{:S(2)}) collective-permute-start(bf16[512,768]{1,0:T(8,128)(2,1)S(1)} %copy-done.6), channel_id=1, source_target_pairs={{0,1},{1,2},{2,3},{4,5},{5,6},{6,7},{8,9},{9,10},{10,11},{12,13},{... | collective-permute-start | bytes 2359304 | tf_op jit(solution)/shard_map/ppermute | solution.py:888
  143.5 11.3 %collective-permute-start.17 = (bf16[2,2,4,96,768]{4,3,2,1,0:T(8,128)(2,1)}, bf16[2,2,4,96,768]{4,3,2,1,0:T(8,128)(2,1)S(1)}, u32[]{:S(2)}, u32[]{:S(2)}) collective-permute-start(bf16[2,2,4,96,768]{4,3,2,1,0:T(8,128)(2,1)} %get-tuple-element.316), channel_id=1, source_target_pairs={{0,4},{4,0},{8,12},{12,8},{16,20},{20,16},{24,28},{28,24},{1,5},{5... | collective-permute-start | bytes 7077896 | tf_op jit(solution)/shard_map/ppermute | solution.py:682
  147.0 8.0 %collective-permute-start.18 = (bf16[2,2,4,96,768]{4,3,2,1,0:T(8,128)(2,1)}, bf16[2,2,4,96,768]{4,3,2,1,0:T(8,128)(2,1)}, u32[]{:S(2)}, u32[]{:S(2)}) collective-permute-start(bf16[2,2,4,96,768]{4,3,2,1,0:T(8,128)(2,1)} %get-tuple-element.317), channel_id=1, source_target_pairs={{0,4},{4,0},{8,12},{12,8},{16,20},{20,16},{24,28},{28,24},{1,5},{5... | collective-permute-start | bytes 7077896 | tf_op jit(solution)/shard_map/ppermute | solution.py:682
  169.8 21.4 %collective-permute-start.19 = (bf16[512,768]{1,0:T(8,128)(2,1)}, bf16[512,768]{1,0:T(8,128)(2,1)S(1)}, u32[]{:S(2)}, u32[]{:S(2)}) collective-permute-start(bf16[512,768]{1,0:T(8,128)(2,1)} %get-tuple-element.325.refs_2_.refs_5_), channel_id=1, source_target_pairs={{0,1},{1,2},{2,3},{4,5},{5,6},{6,7},{8,9},{9,10},{10,11},{12,13},{... | collective-permute-start | bytes 2359304 | tf_op jit(solution)/shard_map/ppermute | solution.py:888
  230.6 195.9 %reduce-scatter.5.cloned.1.call-start = ((), (), s32[]{:S(2)}) async-start(), calls=%async_computation.3 | async-start | bytes 10616832 | tf_op jit(solution)/shard_map/reduce_scatter | solution.py:791
  246.8 20.9 %collective-permute-start.20 = (bf16[512,768]{1,0:T(8,128)(2,1)}, bf16[512,768]{1,0:T(8,128)(2,1)S(1)}, u32[]{:S(2)}, u32[]{:S(2)}) collective-permute-start(bf16[512,768]{1,0:T(8,128)(2,1)} %get-tuple-element.351), channel_id=1, source_target_pairs={{1,0},{2,1},{3,2},{5,4},{6,5},{7,6},{9,8},{10,9},{11,10},{13,12},{... | collective-permute-start | bytes 2359304 | tf_op jit(solution)/shard_map/ppermute | solution.py:891
  268.7 6.9 %collective-permute-start.21 = (bf16[4,192,768]{2,1,0:T(8,128)(2,1)}, bf16[4,192,768]{2,1,0:T(8,128)(2,1)S(1)}, u32[]{:S(2)}, u32[]{:S(2)}) collective-permute-start(bf16[4,192,768]{2,1,0:T(8,128)(2,1)} %get-tuple-element.367), channel_id=1, source_target_pairs={{0,4},{4,0},{8,12},{12,8},{16,20},{20,16},{24,28},{28,24},{1,5},{5... | collective-permute-start | bytes 3538952 | tf_op jit(solution)/shard_map/ppermute | solution.py:682
  281.5 22.5 %collective-permute-start.23 = (bf16[2,4,48,768]{3,2,1,0:T(8,128)(2,1)}, bf16[2,4,48,768]{3,2,1,0:T(8,128)(2,1)S(1)}, u32[]{:S(2)}, u32[]{:S(2)}) collective-permute-start(bf16[2,4,48,768]{3,2,1,0:T(8,128)(2,1)} %get-tuple-element.384), channel_id=1, source_target_pairs={{0,16},{4,20},{8,24},{12,28},{16,0},{20,4},{24,8},{28,12},{1,17},{... | collective-permute-start | bytes 1769480 | tf_op jit(solution)/shard_map/ppermute | solution.py:682
  282.9 21.1 %collective-permute-start.24 = (bf16[2,4,48,768]{3,2,1,0:T(8,128)(2,1)}, bf16[2,4,48,768]{3,2,1,0:T(8,128)(2,1)S(1)}, u32[]{:S(2)}, u32[]{:S(2)}) collective-permute-start(bf16[2,4,48,768]{3,2,1,0:T(8,128)(2,1)} %get-tuple-element.385), channel_id=1, source_target_pairs={{0,8},{4,12},{8,0},{12,4},{16,24},{20,28},{24,16},{28,20},{1,9},{5... | collective-permute-start | bytes 1769480 | tf_op jit(solution)/shard_map/ppermute | solution.py:682
  305.1 139.7 %all-gather.7.cloned.1.call-start = ((), (), s32[]{:S(2)}) async-start(), calls=%async_computation.5 | async-start | bytes 3981312 | tf_op jit(solution)/shard_map/all_gather | solution.py:996
  307.9 10.1 %collective-permute-start.25 = (bf16[4,48,768]{2,1,0:T(8,128)(2,1)}, bf16[4,48,768]{2,1,0:T(8,128)(2,1)S(1)}, u32[]{:S(2)}, u32[]{:S(2)}) collective-permute-start(bf16[4,48,768]{2,1,0:T(8,128)(2,1)} %get-tuple-element.392), channel_id=1, source_target_pairs={{0,8},{4,12},{8,0},{12,4},{16,24},{20,28},{24,16},{28,20},{1,9},{5... | collective-permute-start | bytes 884744 | tf_op jit(solution)/shard_map/ppermute | solution.py:682
  308.1 9.8 %collective-permute-start.26 = (bf16[4,48,768]{2,1,0:T(8,128)(2,1)}, bf16[4,48,768]{2,1,0:T(8,128)(2,1)S(1)}, u32[]{:S(2)}, u32[]{:S(2)}) collective-permute-start(bf16[4,48,768]{2,1,0:T(8,128)(2,1)} %get-tuple-element.393), channel_id=1, source_target_pairs={{0,16},{4,20},{8,24},{12,28},{16,0},{20,4},{24,8},{28,12},{1,17},{... | collective-permute-start | bytes 884744 | tf_op jit(solution)/shard_map/ppermute | solution.py:682
  322.3 31.5 %collective-permute-start.27 = (bf16[288,768]{1,0:T(8,128)(2,1)}, bf16[288,768]{1,0:T(8,128)(2,1)S(1)}, u32[]{:S(2)}, u32[]{:S(2)}) collective-permute-start(bf16[288,768]{1,0:T(8,128)(2,1)} %get-tuple-element.411), channel_id=1, source_target_pairs={{0,1},{1,0},{2,3},{3,2},{4,5},{5,4},{6,7},{7,6},{8,9},{9,8},{10,11... | collective-permute-start | bytes 1327112 | tf_op jit(solution)/shard_map/ppermute | solution.py:682
  322.7 31.1 %collective-permute-start.28 = (bf16[288,768]{1,0:T(8,128)(2,1)}, bf16[288,768]{1,0:T(8,128)(2,1)S(1)}, u32[]{:S(2)}, u32[]{:S(2)}) collective-permute-start(bf16[288,768]{1,0:T(8,128)(2,1)} %get-tuple-element.412), channel_id=1, source_target_pairs={{0,2},{1,3},{2,0},{3,1},{4,6},{5,7},{6,4},{7,5},{8,10},{9,11},{10,... | collective-permute-start | bytes 1327112 | tf_op jit(solution)/shard_map/ppermute | solution.py:682
  324.6 38.0 %collective-permute-start.29 = (bf16[288,768]{1,0:T(8,128)(2,1)}, bf16[288,768]{1,0:T(8,128)(2,1)S(1)}, u32[]{:S(2)}, u32[]{:S(2)}) collective-permute-start(bf16[288,768]{1,0:T(8,128)(2,1)} %get-tuple-element.413), channel_id=1, source_target_pairs={{0,3},{1,2},{2,1},{3,0},{4,7},{5,6},{6,5},{7,4},{8,11},{9,10},{10,... | collective-permute-start | bytes 1327112 | tf_op jit(solution)/shard_map/ppermute | solution.py:682
  367.8 20.2 %collective-permute-start.30 = (bf16[512,768]{1,0:T(8,128)(2,1)}, bf16[512,768]{1,0:T(8,128)(2,1)S(1)}, u32[]{:S(2)}, u32[]{:S(2)}) collective-permute-start(bf16[512,768]{1,0:T(8,128)(2,1)} %get-tuple-element.417), channel_id=1, source_target_pairs={{1,0},{2,1},{3,2},{5,4},{6,5},{7,6},{9,8},{10,9},{11,10},{13,12},{... | collective-permute-start | bytes 2359304 | tf_op jit(solution)/shard_map/ppermute | solution.py:891
  375.9 22.1 %collective-permute-start.33 = (bf16[2,4,48,768]{3,2,1,0:T(8,128)(2,1)}, bf16[2,4,48,768]{3,2,1,0:T(8,128)(2,1)S(1)}, u32[]{:S(2)}, u32[]{:S(2)}) collective-permute-start(bf16[2,4,48,768]{3,2,1,0:T(8,128)(2,1)} %get-tuple-element.435), channel_id=1, source_target_pairs={{0,16},{4,20},{8,24},{12,28},{16,0},{20,4},{24,8},{28,12},{1,17},{... | collective-permute-start | bytes 1769480 | tf_op jit(solution)/shard_map/ppermute | solution.py:682
  377.3 21.1 %collective-permute-start.34 = (bf16[2,4,48,768]{3,2,1,0:T(8,128)(2,1)}, bf16[2,4,48,768]{3,2,1,0:T(8,128)(2,1)S(1)}, u32[]{:S(2)}, u32[]{:S(2)}) collective-permute-start(bf16[2,4,48,768]{3,2,1,0:T(8,128)(2,1)} %get-tuple-element.436), channel_id=1, source_target_pairs={{0,8},{4,12},{8,0},{12,4},{16,24},{20,28},{24,16},{28,20},{1,9},{5... | collective-permute-start | bytes 1769480 | tf_op jit(solution)/shard_map/ppermute | solution.py:682
  404.8 7.8 %collective-permute-start.36 = (bf16[4,48,768]{2,1,0:T(8,128)(2,1)}, bf16[4,48,768]{2,1,0:T(8,128)(2,1)S(1)}, u32[]{:S(2)}, u32[]{:S(2)}) collective-permute-start(bf16[4,48,768]{2,1,0:T(8,128)(2,1)} %get-tuple-element.454), channel_id=1, source_target_pairs={{0,8},{4,12},{8,0},{12,4},{16,24},{20,28},{24,16},{28,20},{1,9},{5... | collective-permute-start | bytes 884744 | tf_op jit(solution)/shard_map/ppermute | solution.py:682
  405.3 7.3 %collective-permute-start.37 = (bf16[4,48,768]{2,1,0:T(8,128)(2,1)}, bf16[4,48,768]{2,1,0:T(8,128)(2,1)S(1)}, u32[]{:S(2)}, u32[]{:S(2)}) collective-permute-start(bf16[4,48,768]{2,1,0:T(8,128)(2,1)} %get-tuple-element.455), channel_id=1, source_target_pairs={{0,16},{4,20},{8,24},{12,28},{16,0},{20,4},{24,8},{28,12},{1,17},{... | collective-permute-start | bytes 884744 | tf_op jit(solution)/shard_map/ppermute | solution.py:682
  413.4 12.4 %collective-permute-start.39 = (bf16[536,256]{1,0:T(8,128)(2,1)}, bf16[536,256]{1,0:T(8,128)(2,1)S(1)}, u32[]{:S(2)}, u32[]{:S(2)}) collective-permute-start(bf16[536,256]{1,0:T(8,128)(2,1)} %get-tuple-element.466), channel_id=1, source_target_pairs={{0,16},{4,20},{8,24},{12,28},{16,0},{20,4},{24,8},{28,12},{1,17},{... | collective-permute-start | bytes 823304 | tf_op jit(solution)/shard_map/ppermute | solution.py:682
  429.2 22.2 %collective-permute-start.40 = (bf16[288,768]{1,0:T(8,128)(2,1)}, bf16[288,768]{1,0:T(8,128)(2,1)S(1)}, u32[]{:S(2)}, u32[]{:S(2)}) collective-permute-start(bf16[288,768]{1,0:T(8,128)(2,1)} %get-tuple-element.472), channel_id=1, source_target_pairs={{0,1},{1,0},{2,3},{3,2},{4,5},{5,4},{6,7},{7,6},{8,9},{9,8},{10,11... | collective-permute-start | bytes 1327112 | tf_op jit(solution)/shard_map/ppermute | solution.py:682
  432.6 19.5 %collective-permute-start.41 = (bf16[288,768]{1,0:T(8,128)(2,1)}, bf16[288,768]{1,0:T(8,128)(2,1)S(1)}, u32[]{:S(2)}, u32[]{:S(2)}) collective-permute-start(bf16[288,768]{1,0:T(8,128)(2,1)} %get-tuple-element.473), channel_id=1, source_target_pairs={{0,2},{1,3},{2,0},{3,1},{4,6},{5,7},{6,4},{7,5},{8,10},{9,11},{10,... | collective-permute-start | bytes 1327112 | tf_op jit(solution)/shard_map/ppermute | solution.py:682
  432.6 49.5 %collective-permute-start.42 = (bf16[288,768]{1,0:T(8,128)(2,1)}, bf16[288,768]{1,0:T(8,128)(2,1)S(1)}, u32[]{:S(2)}, u32[]{:S(2)}) collective-permute-start(bf16[288,768]{1,0:T(8,128)(2,1)} %get-tuple-element.474), channel_id=1, source_target_pairs={{0,3},{1,2},{2,1},{3,0},{4,7},{5,6},{6,5},{7,4},{8,11},{9,10},{10,... | collective-permute-start | bytes 1327112 | tf_op jit(solution)/shard_map/ppermute | solution.py:682
  434.7 54.0 %collective-permute-start.45 = (bf16[536,256]{1,0:T(8,128)(2,1)}, bf16[536,256]{1,0:T(8,128)(2,1)S(1)}, u32[]{:S(2)}, u32[]{:S(2)}) collective-permute-start(bf16[536,256]{1,0:T(8,128)(2,1)} %get-tuple-element.488), channel_id=1, source_target_pairs={{0,1},{1,0},{2,3},{3,2},{4,5},{5,4},{6,7},{7,6},{8,9},{9,8},{10,11... | collective-permute-start | bytes 823304 | tf_op jit(solution)/shard_map/ppermute | solution.py:682
  437.0 51.7 %collective-permute-start.46 = (bf16[536,256]{1,0:T(8,128)(2,1)}, bf16[536,256]{1,0:T(8,128)(2,1)S(1)}, u32[]{:S(2)}, u32[]{:S(2)}) collective-permute-start(bf16[536,256]{1,0:T(8,128)(2,1)} %get-tuple-element.488), channel_id=1, source_target_pairs={{0,2},{1,3},{2,0},{3,1},{4,6},{5,7},{6,4},{7,5},{8,10},{9,11},{10,... | collective-permute-start | bytes 823304 | tf_op jit(solution)/shard_map/ppermute | solution.py:682
  451.4 42.1 %collective-permute-start.47 = (bf16[536,256]{1,0:T(8,128)(2,1)S(1)}, bf16[536,256]{1,0:T(8,128)(2,1)S(1)}, u32[]{:S(2)}, u32[]{:S(2)}) collective-permute-start(bf16[536,256]{1,0:T(8,128)(2,1)S(1)} %copy-done.18), channel_id=1, source_target_pairs={{0,3},{1,2},{2,1},{3,0},{4,7},{5,6},{6,5},{7,4},{8,11},{9,10},{10,... | collective-permute-start | bytes 823304 | tf_op jit(solution)/shard_map/ppermute | solution.py:682
  485.8 8.5 %collective-permute-start.43 = (bf16[144,768]{1,0:T(8,128)(2,1)}, bf16[144,768]{1,0:T(8,128)(2,1)S(1)}, u32[]{:S(2)}, u32[]{:S(2)}) collective-permute-start(bf16[144,768]{1,0:T(8,128)(2,1)} %get-tuple-element.486), channel_id=1, source_target_pairs={{0,8},{4,12},{8,0},{12,4},{16,24},{20,28},{24,16},{28,20},{1,9},{5... | collective-permute-start | bytes 663560 | tf_op jit(solution)/shard_map/ppermute | solution.py:682
  498.7 7.5 %collective-permute-start.48 = (bf16[2,144,768]{2,1,0:T(8,128)(2,1)}, bf16[2,144,768]{2,1,0:T(8,128)(2,1)}, u32[]{:S(2)}, u32[]{:S(2)}) collective-permute-start(bf16[2,144,768]{2,1,0:T(8,128)(2,1)} %get-tuple-element.494), channel_id=1, source_target_pairs={{0,16},{4,20},{8,24},{12,28},{16,0},{20,4},{24,8},{28,12},{1,17},{... | collective-permute-start | bytes 1327112 | tf_op jit(solution)/shard_map/ppermute | solution.py:682
  498.7 10.1 %collective-permute-start.49 = (bf16[2,144,768]{2,1,0:T(8,128)(2,1)}, bf16[2,144,768]{2,1,0:T(8,128)(2,1)}, u32[]{:S(2)}, u32[]{:S(2)}) collective-permute-start(bf16[2,144,768]{2,1,0:T(8,128)(2,1)} %get-tuple-element.495), channel_id=1, source_target_pairs={{0,8},{4,12},{8,0},{12,4},{16,24},{20,28},{24,16},{28,20},{1,9},{5... | collective-permute-start | bytes 1327112 | tf_op jit(solution)/shard_map/ppermute | solution.py:682
  512.8 7.9 %collective-permute-start.50 = (bf16[2,2,144,768]{3,2,1,0:T(8,128)(2,1)}, bf16[2,2,144,768]{3,2,1,0:T(8,128)(2,1)S(1)}, u32[]{:S(2)}, u32[]{:S(2)}) collective-permute-start(bf16[2,2,144,768]{3,2,1,0:T(8,128)(2,1)} %get-tuple-element.500), channel_id=1, source_target_pairs={{0,4},{4,0},{8,12},{12,8},{16,20},{20,16},{24,28},{28,24},{1,5},{5... | collective-permute-start | bytes 2654216 | tf_op jit(solution)/shard_map/ppermute | solution.py:682
  (100 other events, 402.2 us)
Sparse Core Ops, SparseCore 0:
  56.7 120.0 all-gather.4
  230.8 83.4 reduce-scatter.2
  317.7 89.1 reduce-scatter.4
  408.7 35.9 all-gather.6

commit v7 on v6

--- a/solution.py
+++ b/solution.py
@@ -11,6 +11,8 @@
 F32 = jnp.float32
 VMEM_LIMIT = 58 * 1024 * 1024
 TOKEN = (8, 128)
+SUB = 256
+RIDERS = 16
 GELU_A = 0.7978845608028654
 GELU_B = 0.044715
 
@@ -44,7 +46,7 @@
     return pl.BlockSpec(shape, lambda *_: (0,) * len(shape))
 
 
-def call(order, body, grid, in_specs, out_specs, out_shape, scratch=(), prefetch=0, name=None):
+def call(order, body, grid, in_specs, out_specs, out_shape, scratch=(), prefetch=0, name=None, aliases=None):
     first = prefetch + len(in_specs)
     second = first + 1 + len(out_specs)
     anywhere = pl.BlockSpec(memory_space=pl.ANY)
@@ -62,7 +64,7 @@
             scratch_shapes=list(scratch),
         ),
         out_shape=list(out_shape) + [shape_of(TOKEN, jnp.int32)],
-        input_output_aliases={first: len(out_specs)},
+        input_output_aliases={**(aliases or {}), first: len(out_specs)},
         compiler_params=pltpu.CompilerParams(
             dimension_semantics=("arbitrary",) * len(grid), vmem_limit_bytes=VMEM_LIMIT
         ),
@@ -249,51 +251,50 @@
     return own, other
 
 
-def ff_forward(order, x1, normed, ups, downs, gain, shift):
+def ff_forward(order, x1, normed, up, down, gain, shift):
     rows, width = x1.shape
-    half = ups[0].shape[0]
-    per_half = 2
-    chunk = half // per_half
-    steps = 2 * per_half
-
-    def body(x_ref, n_ref, u0, u1, d0, d1, g_ref, s_ref, act_ref, slope_ref, x2_ref, next_ref):
+    half = up.shape[0]
+    chunk = width
+    steps = half // chunk
+    last = gain is not None
+
+    def body(x_ref, n_ref, u, d, *rest):
+        if last:
+            g_ref, s_ref, act_ref, slope_ref, x2_ref, next_ref = rest
+        else:
+            act_ref, slope_ref, x2_ref = rest
         step = pl.program_id(0)
 
         @pl.when(step == 0)
         def _():
             x2_ref[...] = x_ref[...]
 
-        def part(u, d):
-            act, slope = gelu_both(dot_nt(n_ref[...], u[...]))
-            act = act.astype(BF)
-            act_ref[...] = act
-            slope_ref[...] = slope.astype(BF)
-            x2_ref[...] += dot_nn(act, d[...])
-
-        pl.when(step < per_half)(lambda: part(u0, d0))
-        pl.when(step >= per_half)(lambda: part(u1, d1))
-
-        @pl.when(step == steps - 1)
-        def _():
-            normal, _ = normalize(x2_ref[...])
-            next_ref[...] = (normal * g_ref[...] + s_ref[...]).astype(BF)
-
-    own, other = chunk_specs(chunk, width, per_half)
+        for k in range(chunk // SUB):
+            here = slice(k * SUB, (k + 1) * SUB)
+            act, slope = gelu_both(dot_nt(n_ref[...], u[here]))
+            act_ref[:, here] = act.astype(BF)
+            slope_ref[:, here] = slope.astype(BF)
+        x2_ref[...] += dot_nn(act_ref[...], d[...])
+
+        if last:
+
+            @pl.when(step == steps - 1)
+            def _():
+                normal, _ = normalize(x2_ref[...])
+                next_ref[...] = (normal * g_ref[...] + s_ref[...]).astype(BF)
+
+    full = whole((rows, width))
+    weight = pl.BlockSpec((chunk, width), lambda i: (i, 0))
     col = pl.BlockSpec((rows, chunk), lambda i: (0, i))
     return call(
         order,
         body,
         (steps,),
-        [whole((rows, width))] * 2 + [own, other, own, other] + [whole((1, width))] * 2,
-        [col, col, whole((rows, width)), whole((rows, width))],
-        [
-            shape_of((rows, 2 * half), BF),
-            shape_of((rows, 2 * half), BF),
-            shape_of((rows, width), F32),
-            shape_of((rows, width), BF),
-        ],
+        [full, full, weight, weight] + [whole((1, width))] * (2 if last else 0),
+        [col, col, full] + ([full] if last else []),
+        [shape_of((rows, half), BF)] * 2 + [shape_of((rows, width), F32)] + ([shape_of((rows, width), BF)] if last else []),
         name="ff_fwd",
-    )(x1, normed, *ups, *downs, gain, shift)
+    )(x1, normed, up, down, *((gain, shift) if last else ()))
 
 
 def ff_specs(weights, chunk):
@@ -330,9 +331,12 @@
         rest = list(rest)
         w_refs = [rest.pop(0) for _ in operands]
         grad_ref, g_ref = rest.pop(0), rest.pop(0)
-        act_ref, slope_ref = (None, None) if fresh else (rest.pop(0), rest.pop(0))
-        wg_ref, g1_ref, ga_ref, gg_ref, gs_ref = rest[:5]
-        out_ref, (low, dn, x2) = (rest[5], rest[6:]) if fresh else (None, (rest[5], rest[6], None))
+        kept = [] if fresh else [rest.pop(0) for _ in range(4)]
+        wg_ref = rest.pop(0)
+        g1_ref, ga_ref, gg_ref, gs_ref = rest[:4]
+        out_ref = rest[4] if fresh else None
+        low, dn, pre_grads = rest[5:8] if fresh else rest[4:7]
+        acts, x2 = rest[8:] if fresh else (None, None)
         step = pl.program_id(0)
 
         @pl.when(step == 0)
@@ -342,16 +346,21 @@
             if fresh:
                 x2[...] = x_ref[...]
 
-        def part(u_ref, d_ref):
+        def part(u_ref, d_ref, act_ref, slope_ref):
             u = u_ref[...].reshape(chunk, width)
             d = d_ref[...].reshape(chunk, width)
+            for k in range(chunk // SUB):
+                here = slice(k * SUB, (k + 1) * SUB)
+                if fresh:
+                    act, slope = gelu_both(dot_nt(n_ref[...], u[here]))
+                    acts[:, here] = act.astype(BF)
+                else:
+                    slope = slope_ref[:, here].astype(F32)
+                pre_grads[:, here] = (dot_nt(low[...], d[here]) * slope).astype(BF)
+            pre_grad = pre_grads[...]
+            act = acts[...] if fresh else act_ref[...]
             if fresh:
-                act, slope = gelu_both(dot_nt(n_ref[...], u))
-                act = act.astype(BF)
                 x2[...] += dot_nn(act, d)
-            else:
-                act, slope = act_ref[...], slope_ref[...].astype(F32)
-            pre_grad = (dot_nt(low[...], d) * slope).astype(BF)
             dn[...] += dot_nn(pre_grad, u)
             for which, value in ((0, dot_tn(pre_grad, n_ref[...])), (1, dot_tn(act, low[...]))):
                 value = value.astype(BF)
@@ -359,11 +368,13 @@
                     spot = (place_ref[5] ^ k) if relative else k
                     wg_ref[spot, 0, which] = value[k * group_rows : (k + 1) * group_rows]
 
-        if relative:
-            pl.when(step < per_half)(lambda: part(w_refs[0], w_refs[2]))
-            pl.when(step >= per_half)(lambda: part(w_refs[1], w_refs[3]))
+        own_w, other_w = (w_refs[::2], w_refs[1::2]) if relative else (w_refs, w_refs)
+        if fresh:
+            pl.when(step < per_half)(lambda: part(*own_w, None, None))
+            pl.when(step >= per_half)(lambda: part(*other_w, None, None))
         else:
-            part(*w_refs)
+            pl.when(step < per_half)(lambda: part(*own_w, *kept[:2]))
+            pl.when(step >= per_half)(lambda: part(*other_w, *kept[2:]))
 
         @pl.when(step == steps - 1)
         def _():
@@ -378,29 +389,41 @@
             gs_ref[...] = jnp.sum(total, axis=0, keepdims=True)
 
     full = whole((rows, width))
-    col = pl.BlockSpec((rows, chunk), lambda i, *_: (0, i))
-    wg = pl.BlockSpec(
-        (per, 1, 2, group_rows, width),
-        lambda i, place: (
-            (place[4] ^ (i % per_half)) if relative else i % per_half, place[3] ^ (i // per_half), 0, 0, 0,
-        ),
-    )
+    def own_index(i):
+        return jnp.minimum(i, per_half - 1)
+
+    def other_index(i):
+        return jnp.maximum(i - per_half, 0)
+
+    wg_specs = [
+        pl.BlockSpec(
+            (per, 1, 2, group_rows, width),
+            lambda i, place: (
+                (place[4] ^ (i % per_half)) if relative else i % per_half, place[3] ^ (i // per_half), 0, 0, 0,
+            ),
+        )
+    ]
+    wg_shapes = [shape_of((groups, 2, 2, group_rows, width), BF)]
+    kept_specs = [
+        pl.BlockSpec((rows, chunk), lambda i, *_, index=index: (0, index(i)))
+        for index in (() if fresh else (own_index, own_index, other_index, other_index))
+    ]
     return call(
         order,
         body,
         (steps,),
-        [full, full] + w_specs + [full, whole((1, width))] + ([] if fresh else [col, col]),
-        [wg, full, full, whole((1, width)), whole((1, width))] + ([full] if fresh else []),
-        [
-            shape_of((groups, 2, 2, group_rows, width), BF),
+        [full, full] + w_specs + [full, whole((1, width))] + kept_specs,
+        wg_specs + [full, full, whole((1, width)), whole((1, width))] + ([full] if fresh else []),
+        wg_shapes
+        + [
             shape_of((rows, width), F32),
             shape_of((rows, width), BF),
             shape_of((1, width), F32),
             shape_of((1, width), F32),
         ]
         + ([shape_of((rows, width), BF)] if fresh else []),
-        [pltpu.VMEM((rows, width), BF), pltpu.VMEM((rows, width), F32)]
-        + ([pltpu.VMEM((rows, width), F32)] if fresh else []),
+        [pltpu.VMEM((rows, width), BF), pltpu.VMEM((rows, width), F32), pltpu.VMEM((rows, chunk), BF)]
+        + ([pltpu.VMEM((rows, chunk), BF), pltpu.VMEM((rows, width), F32)] if fresh else []),
         prefetch=1,
         name="ff_bwd",
     )(place, x1, normed, *operands, grad, gain, *(() if fresh else saved))
@@ -498,54 +521,59 @@
     )(place, grad_low, *weights, sg, ratio, rden, v, wsum, carried, masked)
 
 
-def attn_weight_grads(order, place, gq, gk, gv, mixed, normed, halo, grad_low, mp, mixed_rows):
+def attn_weight_grads(order, place, gq, gk, gv, mixed, normed, halo, grad_low, band, mp, mixed_rows, riding):
     rows, width = gq.shape
     half = width // 2
     quarter = half // 2
-
-    def body(place_ref, gq_ref, gk_ref, gv_ref, mixed_ref, n_ref, h_ref, ga_ref, oa, ob, ta, tb):
-        step = pl.program_id(0)
-        mat = lax.rem(step, 4)
-
-        def store(value):
-            low = value.astype(BF)
-
-            def put(a_ref, b_ref):
+    piece = quarter // mp
+    window = band.shape[1]
+    share = 2 * RIDERS
+    def body(place_ref, gq_ref, gk_ref, gv_ref, mixed_ref, n_ref, h_ref, ga_ref, band_ref, *out_refs):
+        def part(outs, core):
+            if riding:
+                for p in range(4):
+                    owner = 2 * (place_ref[2] ^ p) + (place_ref[3] ^ core)
+                    start = pl.multiple_of(owner * share, share)
+                    rows_here = band_ref[pl.ds(start, share)].astype(BF)
+                    outs[0][p, quarter:] = jnp.concatenate(
+                        [rows_here[:RIDERS], rows_here[RIDERS:], jnp.zeros((RIDERS, width - 2 * window), BF)], axis=1
+                    )
+
+            def put(m, value):
+                low = value.astype(BF)
+                spot = place_ref[0] ^ m
                 if not mixed_rows:
-                    a_ref[0] = low[:quarter]
-                    b_ref[0] = low[quarter:]
+                    outs[0][spot, :quarter] = low[:quarter]
+                    outs[1][spot] = low[quarter:]
                     return
-                piece = quarter // mp
                 for z in range(mp):
-                    a_ref[0, z * piece : (z + 1) * piece] = low[2 * z * piece : (2 * z + 1) * piece]
-                    b_ref[0, z * piece : (z + 1) * piece] = low[(2 * z + 1) * piece : (2 * z + 2) * piece]
-
-            pl.when(step < 4)(lambda: put(oa, ob))
-            pl.when(step >= 4)(lambda: put(ta, tb))
-
-        def keys_grad(ref):
-            return dot_tn(ref[:rows], h_ref[...]) + dot_tn(ref[rows:], n_ref[...])
-
-        pl.when(mat == 0)(lambda: store(dot_tn(gq_ref[...], n_ref[...])))
-        pl.when(mat == 1)(lambda: store(keys_grad(gk_ref)))
-        pl.when(mat == 2)(lambda: store(keys_grad(gv_ref)))
-        pl.when(mat == 3)(lambda: store(dot_tn(mixed_ref[...], ga_ref[...])))
+                    for k in range(2):
+                        outs[k][spot, z * piece : (z + 1) * piece] = low[
+                            (2 * z + k) * piece : (2 * z + k + 1) * piece
+                        ]
+
+            put(0, dot_tn(gq_ref[...], n_ref[...]))
+            for m, ref in ((1, gk_ref), (2, gv_ref)):
+                put(m, dot_tn(ref[:rows], h_ref[...]) + dot_tn(ref[rows:], n_ref[...]))
+            put(3, dot_tn(mixed_ref[...], ga_ref[...]))
+
+        pl.when(pl.program_id(0) == 0)(lambda: part(out_refs[:2], 0))
+        pl.when(pl.program_id(0) == 1)(lambda: part(out_refs[2:], 1))
 
     def col(n):
-        return pl.BlockSpec((n, half), lambda i, *_: (0, i // 4))
-
-    own = pl.BlockSpec((1, quarter, width), lambda i, t: (jnp.minimum(i, 3) ^ t[0], 0, 0))
-    other = pl.BlockSpec((1, quarter, width), lambda i, t: (jnp.maximum(i - 4, 0) ^ t[0], 0, 0))
+        return pl.BlockSpec((n, half), lambda i, *_: (0, i))
+
+    shapes = [(4, quarter + (RIDERS if riding else 0), width), (4, quarter, width)] * 2
     return call(
         order,
         body,
-        (8,),
-        [col(rows), col(2 * rows), col(2 * rows), col(rows)] + [whole((rows, width))] * 3,
-        [own, own, other, other],
-        [shape_of((4, quarter, width), BF)] * 4,
+        (2,),
+        [col(rows), col(2 * rows), col(2 * rows), col(rows)] + [whole((rows, width))] * 3 + [whole(band.shape)],
+        [whole(shape) for shape in shapes],
+        [shape_of(shape, BF) for shape in shapes],
         prefetch=1,
         name="attn_wgrad",
-    )(place, gq, gk, gv, mixed, normed, halo, grad_low)
+    )(place, gq, gk, gv, mixed, normed, halo, grad_low, band)
 
 
 def leave_attn(order, x, grad, own, back, gain):
@@ -569,92 +597,90 @@
     )(x, grad, own, back, gain)
 
 
-def finish_layer(order, layer, layers, place, parts, channels, hidden, mp_rows, previous):
+def finish_layer(order, layer, layers, place, parts, channels, hidden, mp, window, norm_rows, previous):
     width = parts[0].shape[-1]
-    piece = mp_rows
-    small = piece // 2
     total = 4 * channels
+    single = len(parts) == 1
+    groups = len(parts) // 2
+    dp = parts[0].shape[0] if single else len(parts)
+    piece = total // dp
+    share = 2 * RIDERS
+    block = dp * share
 
     def body(place_ref, *rest):
-        p_refs, (qkv_ref, out_ref, up_ref, down_ref, up) = rest[: len(parts)], rest[len(parts) :]
-
-        def put(owner, count, shift, value):
-            start = owner * piece + shift
-            mat = start // channels
-            inner = pl.multiple_of(start - mat * channels, small)
+        p_refs, rest = rest[: len(parts)], rest[len(parts) :]
+        qkv_ref, out_ref, up_ref, down_ref, band_ref = rest[:5]
+        up = rest[-1]
+
+        def put(owner, rows_of):
+            start = pl.multiple_of(owner * piece, piece)
+            mat = owner * piece // channels
+            inner = pl.multiple_of(owner * piece - mat * channels, piece)
+            value = rows_of(0, piece).astype(F32)
 
             @pl.when(mat < 3)
             def _():
-                qkv_ref[0, jnp.minimum(mat, 2), pl.ds(inner, count)] = value
+                qkv_ref[0, jnp.minimum(mat, 2), pl.ds(inner, piece)] = value
 
             @pl.when(mat == 3)
             def _():
-                out_ref[0, pl.ds(inner, count)] = value
-
-        if len(parts) == 1:
-            for owner in range(total // piece):
-                here = slice(owner * piece, (owner + 1) * piece)
-                mat = owner * piece // channels
-                inner = slice(owner * piece - mat * channels, owner * piece - mat * channels + piece)
-                value = p_refs[0][owner, :piece].astype(F32)
-                if mat < 3:
-                    qkv_ref[0, mat, inner] = value
-                else:
-                    out_ref[0, inner] = value
-                up[here] = p_refs[0][owner, piece : 2 * piece].astype(F32)
-                down_ref[0, here] = p_refs[0][owner, 2 * piece :].astype(F32)
+                out_ref[0, pl.ds(inner, piece)] = value
+
+            up[pl.ds(start, piece)] = rows_of(piece, piece).astype(F32)
+            down_ref[0, pl.ds(start, piece)] = rows_of(2 * piece, piece).astype(F32)
+            for p in range(mp):
+                band = rows_of(3 * piece + norm_rows + p * RIDERS, RIDERS).astype(F32)
+                first = pl.multiple_of((place_ref[1] ^ p) * block + owner * share, share)
+                band_ref[0, pl.ds(first, RIDERS)] = band[:, :window]
+                band_ref[0, pl.ds(first + RIDERS, RIDERS)] = band[:, window : 2 * window]
+
+        if single:
+            for owner in range(dp):
+                put(jnp.int32(owner), lambda start, count, owner=owner: p_refs[0][owner, start : start + count])
         else:
             for core in range(2):
-                pa, pb = p_refs[2 * core], p_refs[2 * core + 1]
-                for p in range(pa.shape[0]):
+                for p in range(groups):
+                    ref = p_refs[core * groups + p]
                     owner = 2 * (place_ref[2] ^ p) + (place_ref[3] ^ core)
-                    start = pl.multiple_of(owner * piece, piece)
-                    up[pl.ds(start, piece)] = pa[p, :piece].astype(F32)
-                    down_ref[0, pl.ds(start, piece)] = pb[p, :piece].astype(F32)
-                    put(owner, small, 0, pa[p, piece:].astype(F32))
-                    put(owner, small, small, pb[p, piece:].astype(F32))
+                    put(owner, lambda start, count, ref=ref: ref[start : start + count])
         up_ref[0] = up[...].T
+        if norm_rows:
+            half = norm_rows // 2
+            sums = []
+            for p in range(groups):
+                for core in range(2):
+                    rows = p_refs[core * groups + p][3 * piece : 3 * piece + norm_rows].astype(F32)
+                    sums.append(rows[:half] + rows[half:])
+            while len(sums) > 1:
+                sums = [sums[k] + sums[k + 1] for k in range(0, len(sums), 2)]
+            rest[5][...] = sums[0]
 
     shapes = [
         (layers, 3, channels, width),
         (layers, channels, width),
         (layers, width, hidden),
         (layers, hidden, width),
+        (layers, mp * block, window),
     ]
 
     def here(shape):
         return pl.BlockSpec((1,) + shape[1:], lambda i, *_: (layer,) + (0,) * (len(shape) - 1))
 
-    first = len(parts) + 1
     extra = list(previous) if previous is not None else []
-    order_in = first + len(extra)
     anywhere = pl.BlockSpec(memory_space=pl.ANY)
-
-    def with_token(*refs):
-        ins = refs[: first + len(extra)]
-        outs = refs[order_in + 1 : order_in + 5]
-        return body(*ins[:first], *outs, *refs[order_in + 6 :])
-
-    aliases = {first + k: k for k in range(len(extra))}
-    aliases[order_in] = 4
-    *results, order.token = pl.pallas_call(
-        with_token,
-        grid_spec=pltpu.PrefetchScalarGridSpec(
-            num_scalar_prefetch=1,
-            grid=(1,),
-            in_specs=[whole(part.shape) for part in parts] + [anywhere] * (len(extra) + 1),
-            out_specs=[here(shape) for shape in shapes] + [anywhere],
-            scratch_shapes=[pltpu.VMEM((total, width), F32)],
-        ),
-        out_shape=[shape_of(shape, F32) for shape in shapes] + [shape_of(TOKEN, jnp.int32)],
-        input_output_aliases=aliases,
-        compiler_params=pltpu.CompilerParams(
-            dimension_semantics=("arbitrary",), vmem_limit_bytes=VMEM_LIMIT
-        ),
-        cost_estimate=pl.CostEstimate(flops=0, bytes_accessed=0, transcendentals=0),
+    return call(
+        order,
+        lambda *refs: body(*refs[: 1 + len(parts)], *refs[1 + len(parts) + len(extra) :]),
+        (1,),
+        [whole(part.shape) for part in parts] + [anywhere] * len(extra),
+        [here(shape) for shape in shapes] + ([whole((norm_rows // 2, width))] if norm_rows else []),
+        [shape_of(shape, F32) for shape in shapes]
+        + ([shape_of((norm_rows // 2, width), F32)] if norm_rows else []),
+        [pltpu.VMEM((total, width), F32)],
+        prefetch=1,
         name="finish",
-    )(place, *parts, *extra, order.token)
-    return results
+        aliases={1 + len(parts) + k: k for k in range(len(extra))},
+    )(place, *parts, *extra)
 
 
 DP = ("g", "c")
@@ -751,19 +777,20 @@
         coming = self.links.order.pin(*self.coming)
         mp = self.links.mp
         self.have = [sorted(route, reverse=True) for route in self.links.routes]
-        self.values = []
+        lead = (2,) * len(self.have[0])
+        self.terms = []
         for own, other in zip(self.halves[:2], coming):
-            total = (own.astype(F32) + other.astype(F32)).astype(BF)
-            groups = self.links.dp // 2
-            rows = total.size // total.shape[-1] // groups // mp
-            self.values.append(total.reshape((2,) * len(self.have[0]) + (mp, rows, total.shape[-1])))
+            shape = lead + (-1, own.shape[-1])
+            self.terms.append([own.reshape(shape), other.reshape(shape)])
 
     def start(self):
-        sends, self.keeps = [], []
+        sends = []
         for k in range(2):
             place = self.have[k].index(self.links.routes[1 - k][self.phase])
-            self.keeps.append(lax.index_in_dim(self.values[k], 0, place, keepdims=False))
-            sends.append(lax.index_in_dim(self.values[k], 1, place, keepdims=False))
+            sends.append(
+                sum(lax.index_in_dim(term, 1, place, keepdims=False).astype(F32) for term in self.terms[k]).astype(BF)
+            )
+            self.terms[k] = [lax.index_in_dim(term, 0, place, keepdims=False) for term in self.terms[k]]
         sends = self.links.order.pin(*sends)
         self.coming = [
             self.links.swap(sends[k], DP, self.links.routes[1 - k][self.phase]) for k in range(2)
@@ -772,7 +799,7 @@
     def wait(self):
         coming = self.links.order.pin(*self.coming)
         for k in range(2):
-            self.values[k] = (self.keeps[k].astype(F32) + coming[k].astype(F32)).astype(BF)
+            self.terms[k].append(coming[k])
             self.have[k].remove(self.links.routes[1 - k][self.phase])
         self.phase += 1
 
@@ -781,7 +808,11 @@
         while self.phase < len(self.links.routes[0]):
             self.start()
             self.wait()
-        return self.values
+        sums = [sum(term.astype(F32) for term in terms).astype(BF) for terms in self.terms]
+        count = sums[1].shape[0]
+        mp = self.links.mp
+        riders = sums[0][count:]
+        return [value[:count].reshape(mp, count // mp, -1) for value in sums], riders
 
 
 class ReduceWide:
@@ -792,13 +823,15 @@
 
     def wait(self):
         (sums,) = self.links.order.pin(self.sums)
-        return sums.reshape(2, self.links.mp, -1, sums.shape[-1])
+        sums = sums.reshape(2, self.links.mp, -1, sums.shape[-1])
+        return [sums[0], sums[1]]
 
 
 class ReduceMp:
-    def __init__(self, links, arrays, index):
+    def __init__(self, links, arrays, index, riders):
         self.links = links
         joined = jnp.concatenate(arrays, axis=1)
+        self.count = joined.shape[1]
         if index is None:
             blocks = [joined[p] for p in range(links.mp)]
         else:
@@ -806,14 +839,15 @@
                 lax.dynamic_index_in_dim(joined, jnp.bitwise_xor(index, p), 0, keepdims=False)
                 for p in range(links.mp)
             ]
+        if riders is not None:
+            blocks = [jnp.concatenate([block, riders], axis=0) for block in blocks]
         self.kept, *sends = links.order.pin(*blocks)
         self.coming = [links.swap(send, "mp", p + 1) for p, send in enumerate(sends)]
 
     def wait(self):
-        total = self.kept.astype(F32)
-        for part in self.links.order.pin(*self.coming):
-            total = total + part.astype(F32)
-        return total.astype(BF)
+        parts = [self.kept] + self.links.order.pin(*self.coming)
+        total = sum(part[: self.count].astype(F32) for part in parts)
+        return total.astype(BF), [part[self.count :] for part in parts]
 
 
 def make_shards(dp, mp):
@@ -893,7 +927,9 @@
         gains = norm_gain.reshape(layers, 2, 1, width)
         shifts = norm_bias.reshape(layers, 2, 1, width)
         middle = attn_rows // 2
-        in_blocks = middle % 16 == 0
+        in_blocks = (
+            middle % 16 == 0 and groups == 4 and block == 2 * RIDERS * dp and width == 3 * window
+        )
 
         piece = attn_piece(0)
         attn0 = Gather(links, piece[:middle], piece[middle:])
@@ -902,6 +938,8 @@
         ff0.start_mp()
         later = jnp.concatenate((attn_piece(1),) + ff_pieces(1), axis=0)
         x, normed = enter_kernel(order, tokens.reshape(rows, width), gains[0, 0], shifts[0, 0])
+        (normed,) = order.pin(normed)
+        halo = forward_halo(normed)
 
         seg_pad = jnp.concatenate([jnp.full((seqs, window), -1, segments.dtype), segments], axis=1)
         seg_keys = lax.dynamic_slice_in_dim(seg_pad, mp_index * block, block + window, axis=1)
@@ -916,14 +954,12 @@
         ff0.start()
         (later,) = order.pin(later)
         later = lax.all_gather(later, ("g", "c", "mp"), axis=0, tiled=False)
-        (normed,) = order.pin(normed)
-        halo = forward_halo(normed)
+        (halo,) = order.pin(halo)
         attn0.wait_all()
-        attn0.start_cores()
         ff0.wait()
         ff0.start()
+        attn0.start_cores()
         w_attn0 = attn_mats(attn0.wait_cores())
-        (halo,) = order.pin(halo)
 
         def attn(layer, x, normed, halo, w_attn):
             sg, ratio, rden, v, wsum, carried, mixed, masked, x1, normed_b = attn_forward(
@@ -935,9 +971,11 @@
         x1_0, normed_b0, saved0, rows0 = attn(0, x, normed, halo, w_attn0)
         ff0.wait_all()
         ff0.start_cores()
+        own_up, own_down = [value.reshape(-1, width) for value in ff0.values]
+        act0, slope0, x_half = ff_forward(order, x1_0, normed_b0, own_up, own_down, None, None)
         ups0, downs0 = ff_mats(ff0.wait_cores())
-        act0, slope0, x2, normed2 = ff_forward(
-            order, x1_0, normed_b0, ups0, downs0, gains[1, 0], shifts[1, 0]
+        act0o, slope0o, x2, normed2 = ff_forward(
+            order, x_half, normed_b0, ups0[1], downs0[1], gains[1, 0], shifts[1, 0]
         )
         (normed2,) = order.pin(normed2)
         halo2 = forward_halo(normed2)
@@ -954,93 +992,84 @@
         (halo2,) = order.pin(halo2)
         x1_1, normed_b1, saved1, rows1 = attn(1, x2, normed2, halo2, w_attn1)
 
-        def ff_back(layer, x1, normed_b, weights, grad, saved):
-            grads, *rest = ff_backward(
-                order, place, x1, normed_b, weights, groups, grad, gains[layer, 1], saved
-            )
-            return grads, rest
-
-        ff_grads1, (grad1, grad1_low, gain_b1, shift_b1, output) = ff_back(
-            1, x1_1, normed_b1, w_ff1, cotangent.reshape(rows, width), None
+        wide1, grad1, grad1_low, gain_b1, shift_b1, output = ff_backward(
+            order, place, x1_1, normed_b1, w_ff1, groups, cotangent.reshape(rows, width), gains[1, 1], None
         )
-        wide1 = ReduceWide(links, ff_grads1)
+        wide1 = ReduceWide(links, wide1)
         gq, gk, gv, band1, dn_own1, back1 = attn_backward(order, place, grad1_low, w_attn1, *saved1)
         (back1,) = order.pin(back1)
         back1 = backward_halo(back1)
         r_attn1 = Reduce(
-            links, attn_weight_grads(order, place, gq, gk, gv, *rows1, grad1_low, mp, in_blocks)
+            links, attn_weight_grads(order, place, gq, gk, gv, *rows1, grad1_low, band1, mp, in_blocks, in_blocks)
         )
         (back1,) = order.pin(back1)
         r_attn1.start_cores()
         grad2, gain_a1, shift_a1 = leave_attn(order, x2, grad1, dn_own1, back1, gains[1, 0])
         r_attn1.wait_cores()
         r_attn1.start()
-        ff_grads0, (grad3, grad3_low, gain_b0, shift_b0) = ff_back(
-            0, x1_0, normed_b0, ups0 + downs0, grad2, (act0, slope0)
+        wide0, grad3, grad3_low, gain_b0, shift_b0 = ff_backward(
+            order, place, x1_0, normed_b0, ups0 + downs0, groups, grad2, gains[0, 1],
+            (act0, slope0, act0o, slope0o),
         )
         r_attn1.wait()
-        wide0 = ReduceWide(links, ff_grads0)
+        wide0 = ReduceWide(links, wide0)
         r_attn1.start()
-        up1, down1 = wide1.wait()
-        attn1_sum = r_attn1.wait_all()
-        mp1 = ReduceMp(links, attn1_sum + [up1, down1], mp_index if in_blocks else None)
+        z_of_1 = mp_index if in_blocks else None
+        attn1_sum, riders1 = r_attn1.wait_all()
+        z_ff1 = ReduceMp(links, wide1.wait(), z_of_1, None)
         gq, gk, gv, band0, dn_own0, back0 = attn_backward(order, place, grad3_low, w_attn0, *saved0)
         r_attn0 = Reduce(
-            links, attn_weight_grads(order, place, gq, gk, gv, *rows0, grad3_low, mp, False)
+            links, attn_weight_grads(order, place, gq, gk, gv, *rows0, grad3_low, band0, mp, False, in_blocks)
         )
-        sum1 = mp1.wait()
+        sum1_ff, _ = z_ff1.wait()
         r_attn0.start_cores()
-        (back0,) = order.pin(back0)
-        back0 = backward_halo(back0)
-        (sum1,) = order.pin(sum1)
-        full1 = lax.all_gather(sum1, DP, axis=0, tiled=False)
         r_attn0.wait_cores()
         r_attn0.start()
         (back0,) = order.pin(back0)
+        back0 = backward_halo(back0)
+        r_attn0.wait()
+        (back0,) = order.pin(back0)
+        r_attn0.start()
+        z_attn1 = ReduceMp(links, attn1_sum, z_of_1, riders1)
         grad4, gain_a0, shift_a0 = leave_attn(order, x, grad3, dn_own0, back0, gains[0, 0])
         norms = jnp.concatenate(
             [gain_a0, gain_b0, shift_a0, shift_b0, gain_a1, gain_b1, shift_a1, shift_b1], axis=0
-        ).reshape(-1, window)
-        small = jnp.concatenate([band0, band1, norms], axis=0).astype(BF)
-
-        def small_start(bit):
-            (here,) = order.pin(small)
-            return here, links.swap(here, DP, bit)
-
-        def small_wait(pair):
-            (coming,) = order.pin(pair[1])
-            return (pair[0].astype(F32) + coming.astype(F32)).astype(BF)
-
-        bits = [1 << k for k in range(dp.bit_length() - 1)]
-        pair = small_start(bits[0])
-        r_attn0.wait()
-        small = small_wait(pair)
-        r_attn0.start()
-        for bit in bits[1:-1]:
-            pair = small_start(bit)
-            small = small_wait(pair)
-        attn0_sum = r_attn0.wait_all()
-        pair = small_start(bits[-1])
-        small = small_wait(pair)
-        up0, down0 = wide0.wait()
-        mp0 = ReduceMp(links, attn0_sum + [up0, down0], None)
-        (small,) = order.pin(small)
-        small_parts = [links.swap(small, "mp", p) for p in range(1, mp)]
+        )
+
+        def two_parts(value):
+            high = value.astype(BF)
+            return jnp.concatenate([high, (value - high.astype(F32)).astype(BF)], axis=0)
+
+        def one_part(value):
+            count = value.shape[0] // 2
+            return value[:count].astype(F32) + value[count:].astype(F32)
+
+        attn0_sum, riders0 = r_attn0.wait_all()
+        sum1_attn, riders1 = z_attn1.wait()
+        (full1,) = order.pin(jnp.concatenate([sum1_attn, sum1_ff] + riders1, axis=0))
+        full1 = lax.all_gather(full1, DP, axis=0, tiled=False)
+        z_0 = ReduceMp(
+            links, attn0_sum + wide0.wait(), None, jnp.concatenate([two_parts(norms), riders0], axis=0)
+        )
         (full1,) = order.pin(full1)
+
+        cut = 2 * norms.shape[0]
 
         def finish(layer, full, previous):
             if in_blocks:
-                return finish_layer(order, layer, layers, place, full, channels, hidden, attn_rows, previous)
+                norm_rows = 0 if len(full) == 1 else cut
+                return finish_layer(
+                    order, layer, layers, place, full, channels, hidden, mp, window, norm_rows, previous
+                )
             if len(full) == 1:
                 owner = jnp.arange(dp)
-                attn_part, up_part, down_part = jnp.split(full[0], [attn_rows, attn_rows + ff_rows], axis=1)
+                joined = full[0]
             else:
                 owner = jnp.bitwise_xor(jnp.arange(dp), dp_index)
-                part_a, part_b = [
-                    jnp.stack([full[k], full[2 + k]], axis=1).reshape(dp, -1, width) for k in range(2)
-                ]
-                attn_part = jnp.concatenate([part_a[:, ff_rows:], part_b[:, ff_rows:]], axis=1)
-                up_part, down_part = part_a[:, :ff_rows], part_b[:, :ff_rows]
+                joined = jnp.stack(full).reshape(2, groups, -1, width)
+                joined = jnp.swapaxes(joined, 0, 1).reshape(dp, -1, width)
+            joined = joined[:, : attn_rows + 2 * ff_rows]
+            attn_part, up_part, down_part = jnp.split(joined, [attn_rows, attn_rows + ff_rows], axis=1)
 
             def rows_of(value):
                 return value.reshape(-1, width)
@@ -1065,31 +1094,32 @@
             ]
 
         big = finish(1, [full1], None)
-        sum0 = mp0.wait()
-        spread0 = Spread(
-            links,
-            [
-                jnp.concatenate([sum0[attn_rows : attn_rows + ff_rows], sum0[:middle]], axis=0),
-                jnp.concatenate([sum0[attn_rows + ff_rows :], sum0[middle:attn_rows]], axis=0),
-            ],
+        sum0, riders0 = z_0.wait()
+        norms = [one_part(part[:cut]) for part in riders0]
+        while len(norms) > 1:
+            norms = [norms[k] + norms[k + 1] for k in range(0, len(norms), 2)]
+        (sum0,) = order.pin(
+            jnp.concatenate([sum0, two_parts(norms[0])] + [part[cut:] for part in riders0], axis=0)
         )
-        spread0.start()
-        small_parts = [small] + order.pin(*small_parts)
-        spread0.wait()
-        spread0.start()
-        small_all = jnp.stack(small_parts)
-        pairs = small_all[:, 2 * block :].astype(F32)
-        while pairs.shape[0] > 1:
-            pairs = pairs[0::2] + pairs[1::2]
-        norm_sum = pairs[0].reshape(layers, 4, width)
-        bands = jnp.take(
-            small_all[:, : 2 * block].astype(F32), jnp.bitwise_xor(jnp.arange(mp), mp_index), axis=0
-        ).reshape(mp, layers, block, window)
-        band_sum = jnp.transpose(bands, (1, 0, 2, 3)).reshape(layers, mp * block, window)
-        spread0.wait_all()
-        spread0.start_cores()
-        full0 = [part.reshape(groups, -1, width) for part in spread0.wait_cores()]
-        qkv_out, out_out, up_out, down_out = finish(0, full0, big)
+        full0 = [sum0] + [links.swap(sum0, DP, 2 * p) for p in range(1, groups)]
+        others = [links.swap(sum0, DP, 1)]
+        others[0], *full0[1:] = order.pin(others[0], *full0[1:])
+        full0[1:] = order.pin(*full0[1:])
+        others += [links.swap(part, DP, 1) for part in full0[1:]]
+        others[1:] = order.pin(*others[1:])
+        qkv_out, out_out, up_out, down_out, *small = finish(0, full0 + others, big)
+        if in_blocks:
+            band_sum, norm_sum = small
+        else:
+            count = attn_rows + 2 * ff_rows
+            sums = [one_part(part[count : count + cut]) for pair in zip(full0, others) for part in pair]
+            while len(sums) > 1:
+                sums = [sums[k] + sums[k + 1] for k in range(0, len(sums), 2)]
+            norm_sum = sums[0]
+            band_sum = lax.all_gather(
+                lax.psum(jnp.stack([band0, band1]), DP), "mp", axis=1, tiled=True
+            )
+        norm_sum = norm_sum.reshape(layers, 4, width)
         return (
             output.reshape(tokens.shape),
             grad4.reshape(tokens.shape),

time: 541 us -> 529 us (0.978)
  starting transfers between devices: 75.7 us -> 55.1 us
  waiting for transfers between devices: 164 us -> 178 us
  local copies, waits for them, and re-layouts: 49.5 us -> 42.2 us
    all_gather x1, waiting for transfers between devices: 7.77 us -> 29.3 us  [shards(): full1 = lax.all_gather(full1, DP, axis=0, tiled=False)]
    ppermute x48 -> x46, starting transfers between devices: 62.4 us -> 43.3 us  [swap(): return lax.ppermute(value, axis, [(i, i ^ bit) for i in range(size)])]
    pallas_call x12 -> x15, Pallas kernels: 156 us -> 172 us  [run(): *results, order.token = kernel(*operands, order.token)]
    all_gather x1, waiting for transfers between devices: 1.99 us -> 17.1 us  [shards(): later = lax.all_gather(later, ('g', 'c', 'mp'), axis=0, tiled=False)]
    pallas_call x2 -> x0, Pallas kernels: 12.4 us -> none  [finish_layer(): pl.pallas_call(with_token, grid_spec=pltpu.PrefetchScalarGridSpec(num_sca...]
    ppermute x2, waiting for transfers between devices: 36.3 us -> 28.8 us  [forward_halo(): return lax.ppermute(value, 'mp', [(i, i + 1) for i in range(mp - 1)])]
    another operation x12 -> x8, other arithmetic: 23.9 us -> 16.4 us  [wait(): self.values[k] = jnp.stack([self.values[k], coming[k]], axis=place)]
    ppermute x2, waiting for transfers between devices: 14.9 us -> 8.77 us  [backward_halo(): return lax.ppermute(value, 'mp', [(i + 1, i) for i in range(mp - 1)])]
  transfers between devices with their start and end apart: 56 -> 54, of which waited for: 30 -> 25; matrix products, arithmetic and copies ran while one was open for 13% -> 13% of each run, Pallas kernels for 23% -> 24%
where the time goes in v7:
time: 529 us; the launch traced here: 522 us
  waiting for transfers between devices  178 us (34%)
  Pallas kernels  172 us (33%)
  starting transfers between devices  55.1 us (10%)
  other arithmetic  53.8 us (10%)
  local copies, waits for them, and re-layouts  42.2 us (8%)
  between operations  15.1 us (3%)
  matrix products  6.88 us (1%)
    pallas_call x15, Pallas kernels, run(): *results, order.token = kernel(*operands, order.token)  172 us
    ppermute x46, waiting for transfers between devices, swap(): return lax.ppermute(value, axis, [(i, i ^ bit) for i in range(size)])  93.6 us
    ppermute x46, starting transfers between devices, swap(): return lax.ppermute(value, axis, [(i, i ^ bit) for i in range(size)])  43.3 us
    all_gather x1, waiting for transfers between devices, shards(): full1 = lax.all_gather(full1, DP, axis=0, tiled=False)  29.3 us
    ppermute x2, waiting for transfers between devices, forward_halo(): return lax.ppermute(value, 'mp', [(i, i + 1) for i in range(mp - 1)])  28.8 us
    unnamed x164, local copies, waits for them, and re-layouts  25.2 us
    all_gather x1, waiting for transfers between devices, shards(): later = lax.all_gather(later, ('g', 'c', 'mp'), axis=0, tiled=False)  17.1 us
    another operation x8, other arithmetic, wait(): self.values[k] = jnp.stack([self.values[k], coming[k]], axis=place)  16.4 us
  transfers between devices with their start and end apart: 54, of which 25 were waited for; matrix products, arithmetic and copies ran while one was open for 13% of the time, Pallas kernels for 24%

profile of v7, /device:TPU:9, one launch (start us, length us, event | category | flops | bytes accessed | tf_op | source)
XLA Modules:
  0.0 522.4 jit_solution(7791419924892775187)
XLA Ops:
  10.3 2.5 collective-permute-start.5
  24.6 2.6 enter.1
  35.9 3.3 collective-permute-done.7.refs_0_
  44.1 7.0 %collective-permute-done.3.refs_2_ = bf16[192,768]{1,0:T(8,128)(2,1)S(1)} collective-permute-done((bf16[192,768]{1,0:T(8,128)(2,1)S(1)}, bf16[192,768]{1,0:T(8,128)(2,1)S(1)}, u32[]{:S(2)}, u32[]{:S(2)}) %collective-permute-start.3) | collective-permute-done | bytes 294944 | tf_op jit(solution)/shard_map/ppermute | solution.py:708
  56.8 3.3 collective-permute-start
  63.1 21.3 %collective-permute-done.refs_0_ = bf16[512,768]{1,0:T(8,128)(2,1)S(1)} collective-permute-done((bf16[512,768]{1,0:T(8,128)(2,1)S(1)}, bf16[512,768]{1,0:T(8,128)(2,1)S(1)}, u32[]{:S(2)}, u32[]{:S(2)}) %collective-permute-start) | collective-permute-done | bytes 786464 | tf_op jit(solution)/shard_map/ppermute | solution.py:922
  85.3 3.7 collective-permute-done.11.refs_0_
  90.0 2.3 pad_maximum_fusion.6.refs_1_
  95.5 2.2 pad_maximum_fusion.3.refs_0_
  97.7 3.1 collective-permute-start.13
  106.4 14.9 %attn_fwd.2 = (bf16[512,768]{1,0:T(8,128)(2,1)}, bf16[512,768]{1,0:T(8,128)(2,1)}, bf16[512,768]{1,0:T(8,128)(2,1)}, bf16[1024,768]{1,0:T(8,128)(2,1)}, bf16[102...) custom-call(s32[6]{0:T(128)} %stack.156.refs_0_, ...), custom_call_target="tpu_custom_call", output_to_operand_aliasing={{10}: (13, {})} | custom-call | tf_op jit(solution)/shard_map/attn_fwd/pallas_call | solution.py:76
  121.3 7.3 %collective-permute-done.15.refs_0_ = bf16[2,4,96,768]{3,2,1,0:T(8,128)(2,1)} collective-permute-done((bf16[2,4,96,768]{3,2,1,0:T(8,128)(2,1)}, bf16[2,4,96,768]{3,2,1,0:T(8,128)(2,1)}, u32[]{:S(2)}, u32[]{:S(2)}) %collective-permute-start.15) | collective-permute-done | bytes 1179680 | tf_op jit(solution)/shard_map/ppermute | solution.py:708
  128.5 5.9 %collective-permute-done.16.refs_1_ = bf16[2,4,96,768]{3,2,1,0:T(8,128)(2,1)} collective-permute-done((bf16[2,4,96,768]{3,2,1,0:T(8,128)(2,1)S(1)}, bf16[2,4,96,768]{3,2,1,0:T(8,128)(2,1)}, u32[]{:S(2)}, u32[]{:S(2)}) %collective-permute-start.16) | collective-permute-done | bytes 1179680 | tf_op jit(solution)/shard_map/ppermute | solution.py:708
  134.4 3.0 pad_maximum_fusion.1.refs_1_
  137.4 2.9 pad_maximum_fusion.refs_0_
  141.9 7.9 %ff_fwd.2 = (bf16[512,1536]{1,0:T(8,128)(2,1)}, bf16[512,1536]{1,0:T(8,128)(2,1)}, f32[512,768]{1,0:T(8,128)}, s32[8,128]{1,0:T(8,128)}) custom-call(f32[512,768]{1,0:T(8,128)} %get-tuple-element.303.refs_0_.refs_1_, bf16[512,768]{1,0:T(8,128)(2,1)} %get-tuple-element.304.refs_1_.refs_2_, ...), custom_call_target="tpu_custom_call", output_to_operand_aliasing={{3}: (4, {})} | custom-call | tf_op jit(solution)/shard_map/ff_fwd/pallas_call | solution.py:76
  151.2 9.1 %ff_fwd.3 = (bf16[512,1536]{1,0:T(8,128)(2,1)}, bf16[512,1536]{1,0:T(8,128)(2,1)}, f32[512,768]{1,0:T(8,128)}, bf16[512,768]{1,0:T(8,128)(2,1)}, s32[8,128]{1,0:T(8,128)}) custom-call(f32[512,768]{1,0:T(8,128)} %get-tuple-element.314.refs_0_, bf16[512,768]{1,0:T(8,128)(2,1)} %get-tuple-element.304.refs_1_.refs_2_, ...), custom_call_target="tpu_custom_call", output_to_operand_aliasing={{4}: (6, {})} | custom-call | tf_op jit(solution)/shard_map/ff_fwd/pallas_call | solution.py:76
  160.3 3.1 collective-permute-start.19
  163.4 17.1 %all-gather.5.cloned.1.call-done = bf16[9216,768]{1,0:T(8,128)(2,1)} async-done(((bf16[288,768]{1,0:T(8,128)(2,1)}), bf16[9216,768]{1,0:T(8,128)(2,1)}) %all-gather.5.cloned.1.call-update) | async-done | bytes 14155792 | tf_op jit(solution)/shard_map/all_gather | solution.py:956
  180.5 7.5 %collective-permute-done.19.refs_0_ = bf16[512,768]{1,0:T(8,128)(2,1)S(1)} collective-permute-done((bf16[512,768]{1,0:T(8,128)(2,1)}, bf16[512,768]{1,0:T(8,128)(2,1)S(1)}, u32[]{:S(2)}, u32[]{:S(2)}) %collective-permute-start.19) | collective-permute-done | bytes 786464 | tf_op jit(solution)/shard_map/ppermute | solution.py:922
  188.9 14.7 %attn_fwd.3 = (bf16[512,768]{1,0:T(8,128)(2,1)}, bf16[512,768]{1,0:T(8,128)(2,1)}, bf16[512,768]{1,0:T(8,128)(2,1)}, bf16[1024,768]{1,0:T(8,128)(2,1)}, bf16[102...) custom-call(s32[6]{0:T(128)} %stack.156.refs_0_, ...), custom_call_target="tpu_custom_call", output_to_operand_aliasing={{10}: (10, {})} | custom-call | tf_op jit(solution)/shard_map/attn_fwd/pallas_call | solution.py:76
  203.6 24.2 %ff_bwd.2 = (bf16[4,2,2,384,768]{4,3,2,1,0:T(8,128)(2,1)}, f32[512,768]{1,0:T(8,128)}, bf16[512,768]{1,0:T(8,128)(2,1)}, f32[1,768]{1,0:T(1,128)}, f32[1,768]{1,...) custom-call(s32[6]{0:T(128)} %stack.156.refs_0_, ...), custom_call_target="tpu_custom_call", output_to_operand_aliasing={{6}: (7, {})} | custom-call | tf_op jit(solution)/shard_map/ff_bwd/pallas_call | solution.py:76
  227.9 16.2 %attn_bwd.2 = (bf16[512,768]{1,0:T(8,128)(2,1)}, bf16[1024,768]{1,0:T(8,128)(2,1)}, bf16[1024,768]{1,0:T(8,128)(2,1)}, f32[256,256]{1,0:T(8,128)}, f32[512,768]{...) custom-call(s32[6]{0:T(128)} %stack.156.refs_0_, ...), custom_call_target="tpu_custom_call", output_to_operand_aliasing={{6}: (10, {})} | custom-call | tf_op jit(solution)/shard_map/attn_bwd/pallas_call | solution.py:76
  246.0 10.0 %attn_wgrad.2 = (bf16[4,208,768]{2,1,0:T(8,128)(2,1)}, bf16[4,192,768]{2,1,0:T(8,128)(2,1)}, bf16[4,208,768]{2,1,0:T(8,128)(2,1)}, bf16[4,192,768]{2,1,0:T(8,128)(2,1)}, s32[8,128]{1,0:T(8,128)}) custom-call(s32[6]{0:T(128)} %stack.156.refs_0_, bf16[512,768]{1,0:T(8,128)(2,1)} %get-tuple-element.349.refs_1_, ...), custom_call_target="tpu_custom_call", output_to_operand_aliasing={{4}: (9, {})} | custom-call | tf_op jit(solution)/shard_map/attn_wgrad/pallas_call | solution.py:76
  256.0 8.8 %collective-permute-done.20.refs_0_ = bf16[512,768]{1,0:T(8,128)(2,1)S(1)} collective-permute-done((bf16[512,768]{1,0:T(8,128)(2,1)}, bf16[512,768]{1,0:T(8,128)(2,1)S(1)}, u32[]{:S(2)}, u32[]{:S(2)}) %collective-permute-start.20) | collective-permute-done | bytes 786464 | tf_op jit(solution)/shard_map/ppermute | solution.py:925
  267.0 4.9 leave.2
  273.5 2.3 fusion.26.refs_1_
  279.3 21.0 %ff_bwd.3 = (bf16[4,2,2,384,768]{4,3,2,1,0:T(8,128)(2,1)}, f32[512,768]{1,0:T(8,128)}, bf16[512,768]{1,0:T(8,128)(2,1)}, f32[1,768]{1,0:T(1,128)}, f32[1,768]{1,0:T(1,128)}, /*index=5*/s32[8,128]{1,0:T(8,128)}) custom-call(s32[6]{0:T(128)} %stack.156.refs_0_, f32[512,768]{1,0:T(8,128)} %get-tuple-element.303.refs_0_.refs_1_, ...), custom_call_target="tpu_custom_call", output_to_operand_aliasing={{5}: (13, {})} | custom-call | tf_op jit(solution)/shard_map/ff_bwd/pallas_call | solution.py:76
  307.9 7.0 %collective-permute-done.26.refs_1_ = bf16[192,768]{1,0:T(8,128)(2,1)S(1)} collective-permute-done((bf16[192,768]{1,0:T(8,128)(2,1)}, bf16[192,768]{1,0:T(8,128)(2,1)S(1)}, u32[]{:S(2)}, u32[]{:S(2)}) %collective-permute-start.26) | collective-permute-done | bytes 294944 | tf_op jit(solution)/shard_map/ppermute | solution.py:708
  320.8 18.0 %attn_bwd.3 = (bf16[512,768]{1,0:T(8,128)(2,1)}, bf16[1024,768]{1,0:T(8,128)(2,1)}, bf16[1024,768]{1,0:T(8,128)(2,1)}, f32[256,256]{1,0:T(8,128)}, f32[512,768]{...) custom-call(s32[6]{0:T(128)} %stack.156.refs_0_, ...), custom_call_target="tpu_custom_call", output_to_operand_aliasing={{6}: (13, {})} | custom-call | tf_op jit(solution)/shard_map/attn_bwd/pallas_call | solution.py:76
  338.8 9.8 %attn_wgrad.3 = (bf16[4,208,768]{2,1,0:T(8,128)(2,1)}, bf16[4,192,768]{2,1,0:T(8,128)(2,1)}, bf16[4,208,768]{2,1,0:T(8,128)(2,1)}, bf16[4,192,768]{2,1,0:T(8,128)(2,1)}, s32[8,128]{1,0:T(8,128)}) custom-call(s32[6]{0:T(128)} %stack.156.refs_0_, bf16[512,768]{1,0:T(8,128)(2,1)} %get-tuple-element.402.refs_1_, ...), custom_call_target="tpu_custom_call", output_to_operand_aliasing={{4}: (9, {})} | custom-call | tf_op jit(solution)/shard_map/attn_wgrad/pallas_call | solution.py:76
  349.6 2.4 collective-permute-start.30
  352.0 4.5 collective-permute-done.31.refs_1_
  358.6 2.3 fusion.27.refs_1_
  364.2 3.3 collective-permute-start.32
  371.7 8.2 %collective-permute-done.34.refs_1_ = bf16[2,192,768]{2,1,0:T(8,128)(2,1)} collective-permute-done((bf16[2,192,768]{2,1,0:T(8,128)(2,1)}, bf16[2,192,768]{2,1,0:T(8,128)(2,1)}, u32[]{:S(2)}, u32[]{:S(2)}) %collective-permute-start.34) | collective-permute-done | bytes 589856 | tf_op jit(solution)/shard_map/ppermute | solution.py:708
  379.8 3.0 collective-permute-done.33.refs_0_
  391.2 2.3 collective-permute-start.38
  393.9 5.0 leave.3
  399.7 8.8 %collective-permute-done.39.refs_2_ = bf16[112,768]{1,0:T(8,128)(2,1)} collective-permute-done((bf16[112,768]{1,0:T(8,128)(2,1)}, bf16[112,768]{1,0:T(8,128)(2,1)}, u32[]{:S(2)}, u32[]{:S(2)}) %collective-permute-start.39) | collective-permute-done | bytes 172064 | tf_op jit(solution)/shard_map/ppermute | solution.py:708
  421.3 2.2 collective-permute-start.41
  424.0 29.3 %all-gather.7.cloned.1.call-done = bf16[2816,768]{1,0:T(8,128)(2,1)} async-done(((bf16[352,768]{1,0:T(8,128)(2,1)}), bf16[2816,768]{1,0:T(8,128)(2,1)}) %all-gather.7.cloned.1.call-update) | async-done | bytes 4325392 | tf_op jit(solution)/shard_map/all_gather | solution.py:1050
  453.2 6.5 %finish.2 = (f32[2,3,192,768]{3,2,1,0:T(8,128)}, f32[2,192,768]{2,1,0:T(8,128)}, f32[2,768,768]{2,1,0:T(8,128)}, f32[2,768,768]{2,1,0:T(8,128)}, f32[2,1024,256]{2,1,0:T(8,128)}, /*index=5*/s32[8,128]{1,0:T(8,128)}) custom-call(s32[6]{0:T(128)} %stack.156.refs_0_, bf16[8,352,768]{2,1,0:T(8,128)(2,1)} %get-tuple-element.474.refs_1_, ...), custom_call_target="tpu_custom_call", output_to_operand_aliasing={{5}: (2, {})} | custom-call | tf_op jit(solution)/shard_map/finish/pallas_call | solution.py:76
  459.7 4.9 collective-permute-done.42.refs_2_
  470.9 3.3 collective-permute-start.43
  476.8 12.0 %collective-permute-done.44.refs_1_ = bf16[368,768]{1,0:T(8,128)(2,1)S(1)} collective-permute-done((bf16[368,768]{1,0:T(8,128)(2,1)}, bf16[368,768]{1,0:T(8,128)(2,1)S(1)}, u32[]{:S(2)}, u32[]{:S(2)}) %collective-permute-start.44) | collective-permute-done | bytes 565280 | tf_op jit(solution)/shard_map/ppermute | solution.py:708
  488.8 12.6 %collective-permute-done.46.refs_3_ = bf16[368,768]{1,0:T(8,128)(2,1)S(1)} collective-permute-done((bf16[368,768]{1,0:T(8,128)(2,1)}, bf16[368,768]{1,0:T(8,128)(2,1)S(1)}, u32[]{:S(2)}, u32[]{:S(2)}) %collective-permute-start.46) | collective-permute-done | bytes 565280 | tf_op jit(solution)/shard_map/ppermute | solution.py:708
  507.2 6.8 %finish.3 = (f32[2,3,192,768]{3,2,1,0:T(8,128)}, f32[2,192,768]{2,1,0:T(8,128)}, f32[2,768,768]{2,1,0:T(8,128)}, f32[2,768,768]{2,1,0:T(8,128)}, f32[2,1024,256]...) custom-call(s32[6]{0:T(128)} %stack.156.refs_0_, ...), custom_call_target="tpu_custom_call", output_to_operand_aliasing={{0}: (9, {}), {1}: (10, {}), {2}: (11, {}), {3}: (12, {}), ... | custom-call | tf_op jit(solution)/shard_map/finish/pallas_call | solution.py:76
  (372 shorter events, 123.0 us)
Async XLA Ops:
  7.2 173.3 %all-gather.5.cloned.1.call-start = ((), (), s32[]{:S(2)}) async-start(), calls=%async_computation.4 | async-start | bytes 14598144 | tf_op jit(solution)/shard_map/all_gather | solution.py:956
  10.3 16.9 %collective-permute-start.4 = (bf16[96,768]{1,0:T(8,128)(2,1)}, bf16[96,768]{1,0:T(8,128)(2,1)S(1)}, u32[]{:S(2)}, u32[]{:S(2)}) collective-permute-start(bf16[96,768]{1,0:T(8,128)(2,1)} %get-tuple-element.265), channel_id=1, source_target_pairs={{0,1},{1,0},{2,3},{3,2},{4,5},{5,4},{6,7},{7,6},{8,9},{9,8},{10,11... | collective-permute-start | bytes 442376 | tf_op jit(solution)/shard_map/ppermute | solution.py:708
  10.3 17.2 %collective-permute-start.5 = (bf16[96,768]{1,0:T(8,128)(2,1)}, bf16[96,768]{1,0:T(8,128)(2,1)S(1)}, u32[]{:S(2)}, u32[]{:S(2)}) collective-permute-start(bf16[96,768]{1,0:T(8,128)(2,1)} %get-tuple-element.265), channel_id=1, source_target_pairs={{0,2},{1,3},{2,0},{3,1},{4,6},{5,7},{6,4},{7,5},{8,10},{9,11},{10,... | collective-permute-start | bytes 442376 | tf_op jit(solution)/shard_map/ppermute | solution.py:708
  12.8 14.8 %collective-permute-start.6 = (bf16[96,768]{1,0:T(8,128)(2,1)}, bf16[96,768]{1,0:T(8,128)(2,1)S(1)}, u32[]{:S(2)}, u32[]{:S(2)}) collective-permute-start(bf16[96,768]{1,0:T(8,128)(2,1)} %get-tuple-element.265), channel_id=1, source_target_pairs={{0,3},{1,2},{2,1},{3,0},{4,7},{5,6},{6,5},{7,4},{8,11},{9,10},{10,... | collective-permute-start | bytes 442376 | tf_op jit(solution)/shard_map/ppermute | solution.py:708
  17.2 26.5 %collective-permute-start.1 = (bf16[192,768]{1,0:T(8,128)(2,1)}, bf16[192,768]{1,0:T(8,128)(2,1)S(1)}, u32[]{:S(2)}, u32[]{:S(2)}) collective-permute-start(bf16[192,768]{1,0:T(8,128)(2,1)} %get-tuple-element.264), channel_id=1, source_target_pairs={{0,1},{1,0},{2,3},{3,2},{4,5},{5,4},{6,7},{7,6},{8,9},{9,8},{10,11... | collective-permute-start | bytes 884744 | tf_op jit(solution)/shard_map/ppermute | solution.py:708
  18.3 25.8 %collective-permute-start.2 = (bf16[192,768]{1,0:T(8,128)(2,1)}, bf16[192,768]{1,0:T(8,128)(2,1)S(1)}, u32[]{:S(2)}, u32[]{:S(2)}) collective-permute-start(bf16[192,768]{1,0:T(8,128)(2,1)} %get-tuple-element.264), channel_id=1, source_target_pairs={{0,2},{1,3},{2,0},{3,1},{4,6},{5,7},{6,4},{7,5},{8,10},{9,11},{10,... | collective-permute-start | bytes 884744 | tf_op jit(solution)/shard_map/ppermute | solution.py:708
  27.3 23.7 %collective-permute-start.3 = (bf16[192,768]{1,0:T(8,128)(2,1)S(1)}, bf16[192,768]{1,0:T(8,128)(2,1)S(1)}, u32[]{:S(2)}, u32[]{:S(2)}) collective-permute-start(bf16[192,768]{1,0:T(8,128)(2,1)S(1)} %copy-done.27), channel_id=1, source_target_pairs={{0,3},{1,2},{2,1},{3,0},{4,7},{5,6},{6,5},{7,4},{8,11},{9,10},{10,... | collective-permute-start | bytes 884744 | tf_op jit(solution)/shard_map/ppermute | solution.py:708
  32.6 6.6 %collective-permute-start.7 = (bf16[4,48,768]{2,1,0:T(8,128)(2,1)}, bf16[4,48,768]{2,1,0:T(8,128)(2,1)S(1)}, u32[]{:S(2)}, u32[]{:S(2)}) collective-permute-start(bf16[4,48,768]{2,1,0:T(8,128)(2,1)} %get-tuple-element.271), channel_id=1, source_target_pairs={{0,8},{4,12},{8,0},{12,4},{16,24},{20,28},{24,16},{28,20},{1,9},{5... | collective-permute-start | bytes 884744 | tf_op jit(solution)/shard_map/ppermute | solution.py:708
  33.8 6.4 %collective-permute-start.8 = (bf16[4,48,768]{2,1,0:T(8,128)(2,1)}, bf16[4,48,768]{2,1,0:T(8,128)(2,1)S(1)}, u32[]{:S(2)}, u32[]{:S(2)}) collective-permute-start(bf16[4,48,768]{2,1,0:T(8,128)(2,1)} %get-tuple-element.272), channel_id=1, source_target_pairs={{0,16},{4,20},{8,24},{12,28},{16,0},{20,4},{24,8},{28,12},{1,17},{... | collective-permute-start | bytes 884744 | tf_op jit(solution)/shard_map/ppermute | solution.py:708
  55.7 260.1 %reduce-scatter.3.cloned.1.call-start = ((), (), s32[]{:S(2)}) async-start(), calls=%async_computation.2 | async-start | bytes 10616832 | tf_op jit(solution)/shard_map/reduce_scatter | solution.py:822
  56.8 27.6 %collective-permute-start = (bf16[512,768]{1,0:T(8,128)(2,1)S(1)}, bf16[512,768]{1,0:T(8,128)(2,1)S(1)}, u32[]{:S(2)}, u32[]{:S(2)}) collective-permute-start(bf16[512,768]{1,0:T(8,128)(2,1)S(1)} %copy-done.7), channel_id=1, source_target_pairs={{0,1},{1,2},{2,3},{4,5},{5,6},{6,7},{8,9},{9,10},{10,11},{12,13},{... | collective-permute-start | bytes 2359304 | tf_op jit(solution)/shard_map/ppermute | solution.py:922
  60.1 25.2 %collective-permute-start.10 = (bf16[2,4,48,768]{3,2,1,0:T(8,128)(2,1)S(1)}, bf16[2,4,48,768]{3,2,1,0:T(8,128)(2,1)}, u32[]{:S(2)}, u32[]{:S(2)}) collective-permute-start(bf16[2,4,48,768]{3,2,1,0:T(8,128)(2,1)S(1)} %copy-done.9), channel_id=1, source_target_pairs={{0,8},{4,12},{8,0},{12,4},{16,24},{20,28},{24,16},{28,20},{1,9},{5... | collective-permute-start | bytes 1769480 | tf_op jit(solution)/shard_map/ppermute | solution.py:708
  61.4 23.9 %collective-permute-start.9 = (bf16[2,4,48,768]{3,2,1,0:T(8,128)(2,1)S(1)}, bf16[2,4,48,768]{3,2,1,0:T(8,128)(2,1)}, u32[]{:S(2)}, u32[]{:S(2)}) collective-permute-start(bf16[2,4,48,768]{3,2,1,0:T(8,128)(2,1)S(1)} %copy-done.11), channel_id=1, source_target_pairs={{0,16},{4,20},{8,24},{12,28},{16,0},{20,4},{24,8},{28,12},{1,17},{... | collective-permute-start | bytes 1769480 | tf_op jit(solution)/shard_map/ppermute | solution.py:708
  62.6 26.4 %collective-permute-start.11 = (bf16[4,96,768]{2,1,0:T(8,128)(2,1)}, bf16[4,96,768]{2,1,0:T(8,128)(2,1)S(1)}, u32[]{:S(2)}, u32[]{:S(2)}) collective-permute-start(bf16[4,96,768]{2,1,0:T(8,128)(2,1)} %get-tuple-element.290), channel_id=1, source_target_pairs={{0,8},{4,12},{8,0},{12,4},{16,24},{20,28},{24,16},{28,20},{1,9},{5... | collective-permute-start | bytes 1769480 | tf_op jit(solution)/shard_map/ppermute | solution.py:708
  62.9 27.0 %collective-permute-start.12 = (bf16[4,96,768]{2,1,0:T(8,128)(2,1)}, bf16[4,96,768]{2,1,0:T(8,128)(2,1)}, u32[]{:S(2)}, u32[]{:S(2)}) collective-permute-start(bf16[4,96,768]{2,1,0:T(8,128)(2,1)} %get-tuple-element.291), channel_id=1, source_target_pairs={{0,16},{4,20},{8,24},{12,28},{16,0},{20,4},{24,8},{28,12},{1,17},{... | collective-permute-start | bytes 1769480 | tf_op jit(solution)/shard_map/ppermute | solution.py:708
  97.7 7.3 %collective-permute-start.13 = (bf16[2,2,4,48,768]{4,3,2,1,0:T(8,128)(2,1)}, bf16[2,2,4,48,768]{4,3,2,1,0:T(8,128)(2,1)S(1)}, u32[]{:S(2)}, u32[]{:S(2)}) collective-permute-start(bf16[2,2,4,48,768]{4,3,2,1,0:T(8,128)(2,1)} %get-tuple-element.297), channel_id=1, source_target_pairs={{0,4},{4,0},{8,12},{12,8},{16,20},{20,16},{24,28},{28,24},{1,5},{5... | collective-permute-start | bytes 3538952 | tf_op jit(solution)/shard_map/ppermute | solution.py:708
  100.9 27.6 %collective-permute-start.15 = (bf16[2,4,96,768]{3,2,1,0:T(8,128)(2,1)}, bf16[2,4,96,768]{3,2,1,0:T(8,128)(2,1)}, u32[]{:S(2)}, u32[]{:S(2)}) collective-permute-start(bf16[2,4,96,768]{3,2,1,0:T(8,128)(2,1)} %get-tuple-element.305), channel_id=1, source_target_pairs={{0,16},{4,20},{8,24},{12,28},{16,0},{20,4},{24,8},{28,12},{1,17},{... | collective-permute-start | bytes 3538952 | tf_op jit(solution)/shard_map/ppermute | solution.py:708
  102.2 32.2 %collective-permute-start.16 = (bf16[2,4,96,768]{3,2,1,0:T(8,128)(2,1)S(1)}, bf16[2,4,96,768]{3,2,1,0:T(8,128)(2,1)}, u32[]{:S(2)}, u32[]{:S(2)}) collective-permute-start(bf16[2,4,96,768]{3,2,1,0:T(8,128)(2,1)S(1)} %copy-done.3), channel_id=1, source_target_pairs={{0,8},{4,12},{8,0},{12,4},{16,24},{20,28},{24,16},{28,20},{1,9},{5... | collective-permute-start | bytes 3538952 | tf_op jit(solution)/shard_map/ppermute | solution.py:708
  140.3 9.5 %collective-permute-start.17 = (bf16[2,2,4,96,768]{4,3,2,1,0:T(8,128)(2,1)}, bf16[2,2,4,96,768]{4,3,2,1,0:T(8,128)(2,1)S(1)}, u32[]{:S(2)}, u32[]{:S(2)}) collective-permute-start(bf16[2,2,4,96,768]{4,3,2,1,0:T(8,128)(2,1)} %get-tuple-element.311), channel_id=1, source_target_pairs={{0,4},{4,0},{8,12},{12,8},{16,20},{20,16},{24,28},{28,24},{1,5},{5... | collective-permute-start | bytes 7077896 | tf_op jit(solution)/shard_map/ppermute | solution.py:708
  141.9 8.0 %collective-permute-start.18 = (bf16[2,2,4,96,768]{4,3,2,1,0:T(8,128)(2,1)}, bf16[2,2,4,96,768]{4,3,2,1,0:T(8,128)(2,1)}, u32[]{:S(2)}, u32[]{:S(2)}) collective-permute-start(bf16[2,2,4,96,768]{4,3,2,1,0:T(8,128)(2,1)} %get-tuple-element.312), channel_id=1, source_target_pairs={{0,4},{4,0},{8,12},{12,8},{16,20},{20,16},{24,28},{28,24},{1,5},{5... | collective-permute-start | bytes 7077896 | tf_op jit(solution)/shard_map/ppermute | solution.py:708
  160.3 27.7 %collective-permute-start.19 = (bf16[512,768]{1,0:T(8,128)(2,1)}, bf16[512,768]{1,0:T(8,128)(2,1)S(1)}, u32[]{:S(2)}, u32[]{:S(2)}) collective-permute-start(bf16[512,768]{1,0:T(8,128)(2,1)} %get-tuple-element.322.refs_2_.refs_5_), channel_id=1, source_target_pairs={{0,1},{1,2},{2,3},{4,5},{5,6},{6,7},{8,9},{9,10},{10,11},{12,13},{... | collective-permute-start | bytes 2359304 | tf_op jit(solution)/shard_map/ppermute | solution.py:922
  227.8 189.9 %reduce-scatter.5.cloned.1.call-start = ((), (), s32[]{:S(2)}) async-start(), calls=%async_computation.3 | async-start | bytes 10616832 | tf_op jit(solution)/shard_map/reduce_scatter | solution.py:822
  244.1 20.7 %collective-permute-start.20 = (bf16[512,768]{1,0:T(8,128)(2,1)}, bf16[512,768]{1,0:T(8,128)(2,1)S(1)}, u32[]{:S(2)}, u32[]{:S(2)}) collective-permute-start(bf16[512,768]{1,0:T(8,128)(2,1)} %get-tuple-element.348), channel_id=1, source_target_pairs={{1,0},{2,1},{3,2},{5,4},{6,5},{7,6},{9,8},{10,9},{11,10},{13,12},{... | collective-permute-start | bytes 2359304 | tf_op jit(solution)/shard_map/ppermute | solution.py:925
  265.7 6.3 %collective-permute-start.21 = (bf16[4,208,768]{2,1,0:T(8,128)(2,1)}, bf16[4,208,768]{2,1,0:T(8,128)(2,1)S(1)}, u32[]{:S(2)}, u32[]{:S(2)}) collective-permute-start(bf16[4,208,768]{2,1,0:T(8,128)(2,1)} %get-tuple-element.367), channel_id=1, source_target_pairs={{0,4},{4,0},{8,12},{12,8},{16,20},{20,16},{24,28},{28,24},{1,5},{5... | collective-permute-start | bytes 3833864 | tf_op jit(solution)/shard_map/ppermute | solution.py:708
  277.9 22.4 %collective-permute-start.23 = (bf16[2,208,768]{2,1,0:T(8,128)(2,1)}, bf16[2,208,768]{2,1,0:T(8,128)(2,1)S(1)}, u32[]{:S(2)}, u32[]{:S(2)}) collective-permute-start(bf16[2,208,768]{2,1,0:T(8,128)(2,1)} %get-tuple-element.385), channel_id=1, source_target_pairs={{0,16},{4,20},{8,24},{12,28},{16,0},{20,4},{24,8},{28,12},{1,17},{... | collective-permute-start | bytes 1916936 | tf_op jit(solution)/shard_map/ppermute | solution.py:708
  279.1 21.2 %collective-permute-start.24 = (bf16[2,192,768]{2,1,0:T(8,128)(2,1)}, bf16[2,192,768]{2,1,0:T(8,128)(2,1)S(1)}, u32[]{:S(2)}, u32[]{:S(2)}) collective-permute-start(bf16[2,192,768]{2,1,0:T(8,128)(2,1)} %get-tuple-element.386), channel_id=1, source_target_pairs={{0,8},{4,12},{8,0},{12,4},{16,24},{20,28},{24,16},{28,20},{1,9},{5... | collective-permute-start | bytes 1769480 | tf_op jit(solution)/shard_map/ppermute | solution.py:708
  301.4 151.8 %all-gather.7.cloned.1.call-start = ((), (), s32[]{:S(2)}) async-start(), calls=%async_computation.5 | async-start | bytes 4866048 | tf_op jit(solution)/shard_map/all_gather | solution.py:1050
  306.1 8.8 %collective-permute-start.25 = (bf16[208,768]{1,0:T(8,128)(2,1)}, bf16[208,768]{1,0:T(8,128)(2,1)S(1)}, u32[]{:S(2)}, u32[]{:S(2)}) collective-permute-start(bf16[208,768]{1,0:T(8,128)(2,1)} %get-tuple-element.393), channel_id=1, source_target_pairs={{0,8},{4,12},{8,0},{12,4},{16,24},{20,28},{24,16},{28,20},{1,9},{5... | collective-permute-start | bytes 958472 | tf_op jit(solution)/shard_map/ppermute | solution.py:708
  307.3 7.6 %collective-permute-start.26 = (bf16[192,768]{1,0:T(8,128)(2,1)}, bf16[192,768]{1,0:T(8,128)(2,1)S(1)}, u32[]{:S(2)}, u32[]{:S(2)}) collective-permute-start(bf16[192,768]{1,0:T(8,128)(2,1)} %get-tuple-element.394), channel_id=1, source_target_pairs={{0,16},{4,20},{8,24},{12,28},{16,0},{20,4},{24,8},{28,12},{1,17},{... | collective-permute-start | bytes 884744 | tf_op jit(solution)/shard_map/ppermute | solution.py:708
  318.2 30.5 %collective-permute-start.27 = (bf16[192,768]{1,0:T(8,128)(2,1)}, bf16[192,768]{1,0:T(8,128)(2,1)S(1)}, u32[]{:S(2)}, u32[]{:S(2)}) collective-permute-start(bf16[192,768]{1,0:T(8,128)(2,1)} %get-tuple-element.411), channel_id=1, source_target_pairs={{0,1},{1,0},{2,3},{3,2},{4,5},{5,4},{6,7},{7,6},{8,9},{9,8},{10,11... | collective-permute-start | bytes 884744 | tf_op jit(solution)/shard_map/ppermute | solution.py:708
  318.4 30.3 %collective-permute-start.28 = (bf16[192,768]{1,0:T(8,128)(2,1)}, bf16[192,768]{1,0:T(8,128)(2,1)S(1)}, u32[]{:S(2)}, u32[]{:S(2)}) collective-permute-start(bf16[192,768]{1,0:T(8,128)(2,1)} %get-tuple-element.412), channel_id=1, source_target_pairs={{0,2},{1,3},{2,0},{3,1},{4,6},{5,7},{6,4},{7,5},{8,10},{9,11},{10,... | collective-permute-start | bytes 884744 | tf_op jit(solution)/shard_map/ppermute | solution.py:708
  320.6 28.1 %collective-permute-start.29 = (bf16[192,768]{1,0:T(8,128)(2,1)}, bf16[192,768]{1,0:T(8,128)(2,1)S(1)}, u32[]{:S(2)}, u32[]{:S(2)}) collective-permute-start(bf16[192,768]{1,0:T(8,128)(2,1)} %get-tuple-element.413), channel_id=1, source_target_pairs={{0,3},{1,2},{2,1},{3,0},{4,7},{5,6},{6,5},{7,4},{8,11},{9,10},{10,... | collective-permute-start | bytes 884744 | tf_op jit(solution)/shard_map/ppermute | solution.py:708
  349.6 7.0 %collective-permute-start.30 = (bf16[4,208,768]{2,1,0:T(8,128)(2,1)}, bf16[4,208,768]{2,1,0:T(8,128)(2,1)S(1)}, u32[]{:S(2)}, u32[]{:S(2)}) collective-permute-start(bf16[4,208,768]{2,1,0:T(8,128)(2,1)} %get-tuple-element.416), channel_id=1, source_target_pairs={{0,4},{4,0},{8,12},{12,8},{16,20},{20,16},{24,28},{28,24},{1,5},{5... | collective-permute-start | bytes 3833864 | tf_op jit(solution)/shard_map/ppermute | solution.py:708
  363.0 19.9 %collective-permute-start.33 = (bf16[2,208,768]{2,1,0:T(8,128)(2,1)}, bf16[2,208,768]{2,1,0:T(8,128)(2,1)}, u32[]{:S(2)}, u32[]{:S(2)}) collective-permute-start(bf16[2,208,768]{2,1,0:T(8,128)(2,1)} %get-tuple-element.425), channel_id=1, source_target_pairs={{0,16},{4,20},{8,24},{12,28},{16,0},{20,4},{24,8},{28,12},{1,17},{... | collective-permute-start | bytes 1916936 | tf_op jit(solution)/shard_map/ppermute | solution.py:708
  363.9 16.0 %collective-permute-start.34 = (bf16[2,192,768]{2,1,0:T(8,128)(2,1)}, bf16[2,192,768]{2,1,0:T(8,128)(2,1)}, u32[]{:S(2)}, u32[]{:S(2)}) collective-permute-start(bf16[2,192,768]{2,1,0:T(8,128)(2,1)} %get-tuple-element.426), channel_id=1, source_target_pairs={{0,8},{4,12},{8,0},{12,4},{16,24},{20,28},{24,16},{28,20},{1,9},{5... | collective-permute-start | bytes 1769480 | tf_op jit(solution)/shard_map/ppermute | solution.py:708
  364.2 22.5 %collective-permute-start.32 = (bf16[512,768]{1,0:T(8,128)(2,1)}, bf16[512,768]{1,0:T(8,128)(2,1)S(1)}, u32[]{:S(2)}, u32[]{:S(2)}) collective-permute-start(bf16[512,768]{1,0:T(8,128)(2,1)} %get-tuple-element.424), channel_id=1, source_target_pairs={{1,0},{2,1},{3,2},{5,4},{6,5},{7,6},{9,8},{10,9},{11,10},{13,12},{... | collective-permute-start | bytes 2359304 | tf_op jit(solution)/shard_map/ppermute | solution.py:925
  387.5 11.3 %collective-permute-start.35 = (bf16[208,768]{1,0:T(8,128)(2,1)}, bf16[208,768]{1,0:T(8,128)(2,1)S(1)}, u32[]{:S(2)}, u32[]{:S(2)}) collective-permute-start(bf16[208,768]{1,0:T(8,128)(2,1)} %get-tuple-element.438), channel_id=1, source_target_pairs={{0,8},{4,12},{8,0},{12,4},{16,24},{20,28},{24,16},{28,20},{1,9},{5... | collective-permute-start | bytes 958472 | tf_op jit(solution)/shard_map/ppermute | solution.py:708
  390.0 8.8 %collective-permute-start.36 = (bf16[192,768]{1,0:T(8,128)(2,1)}, bf16[192,768]{1,0:T(8,128)(2,1)S(1)}, u32[]{:S(2)}, u32[]{:S(2)}) collective-permute-start(bf16[192,768]{1,0:T(8,128)(2,1)} %get-tuple-element.439), channel_id=1, source_target_pairs={{0,16},{4,20},{8,24},{12,28},{16,0},{20,4},{24,8},{28,12},{1,17},{... | collective-permute-start | bytes 884744 | tf_op jit(solution)/shard_map/ppermute | solution.py:708
  391.2 8.4 %collective-permute-start.37 = (bf16[112,768]{1,0:T(8,128)(2,1)}, bf16[112,768]{1,0:T(8,128)(2,1)}, u32[]{:S(2)}, u32[]{:S(2)}) collective-permute-start(bf16[112,768]{1,0:T(8,128)(2,1)} %get-tuple-element.445), channel_id=1, source_target_pairs={{0,1},{1,0},{2,3},{3,2},{4,5},{5,4},{6,7},{7,6},{8,9},{9,8},{10,11... | collective-permute-start | bytes 516104 | tf_op jit(solution)/shard_map/ppermute | solution.py:708
  391.2 8.4 %collective-permute-start.38 = (bf16[112,768]{1,0:T(8,128)(2,1)}, bf16[112,768]{1,0:T(8,128)(2,1)}, u32[]{:S(2)}, u32[]{:S(2)}) collective-permute-start(bf16[112,768]{1,0:T(8,128)(2,1)} %get-tuple-element.446), channel_id=1, source_target_pairs={{0,2},{1,3},{2,0},{3,1},{4,6},{5,7},{6,4},{7,5},{8,10},{9,11},{10,... | collective-permute-start | bytes 516104 | tf_op jit(solution)/shard_map/ppermute | solution.py:708
  393.5 14.9 %collective-permute-start.39 = (bf16[112,768]{1,0:T(8,128)(2,1)}, bf16[112,768]{1,0:T(8,128)(2,1)}, u32[]{:S(2)}, u32[]{:S(2)}) collective-permute-start(bf16[112,768]{1,0:T(8,128)(2,1)} %get-tuple-element.447), channel_id=1, source_target_pairs={{0,3},{1,2},{2,1},{3,0},{4,7},{5,6},{6,5},{7,4},{8,11},{9,10},{10,... | collective-permute-start | bytes 516104 | tf_op jit(solution)/shard_map/ppermute | solution.py:708
  421.3 38.4 %collective-permute-start.40 = (bf16[320,768]{1,0:T(8,128)(2,1)}, bf16[320,768]{1,0:T(8,128)(2,1)S(1)}, u32[]{:S(2)}, u32[]{:S(2)}) collective-permute-start(bf16[320,768]{1,0:T(8,128)(2,1)} %get-tuple-element.469), channel_id=1, source_target_pairs={{0,1},{1,0},{2,3},{3,2},{4,5},{5,4},{6,7},{7,6},{8,9},{9,8},{10,11... | collective-permute-start | bytes 1474568 | tf_op jit(solution)/shard_map/ppermute | solution.py:708
  421.3 38.4 %collective-permute-start.41 = (bf16[320,768]{1,0:T(8,128)(2,1)}, bf16[320,768]{1,0:T(8,128)(2,1)S(1)}, u32[]{:S(2)}, u32[]{:S(2)}) collective-permute-start(bf16[320,768]{1,0:T(8,128)(2,1)} %get-tuple-element.470), channel_id=1, source_target_pairs={{0,2},{1,3},{2,0},{3,1},{4,6},{5,7},{6,4},{7,5},{8,10},{9,11},{10,... | collective-permute-start | bytes 1474568 | tf_op jit(solution)/shard_map/ppermute | solution.py:708
  423.6 41.1 %collective-permute-start.42 = (bf16[320,768]{1,0:T(8,128)(2,1)}, bf16[320,768]{1,0:T(8,128)(2,1)S(1)}, u32[]{:S(2)}, u32[]{:S(2)}) collective-permute-start(bf16[320,768]{1,0:T(8,128)(2,1)} %get-tuple-element.471), channel_id=1, source_target_pairs={{0,3},{1,2},{2,1},{3,0},{4,7},{5,6},{6,5},{7,4},{8,11},{9,10},{10,... | collective-permute-start | bytes 1474568 | tf_op jit(solution)/shard_map/ppermute | solution.py:708
  470.9 6.0 %collective-permute-start.43 = (bf16[368,768]{1,0:T(8,128)(2,1)}, bf16[368,768]{1,0:T(8,128)(2,1)S(1)}, u32[]{:S(2)}, u32[]{:S(2)}) collective-permute-start(bf16[368,768]{1,0:T(8,128)(2,1)} %get-tuple-element.481.refs_1_), channel_id=1, source_target_pairs={{0,4},{4,0},{8,12},{12,8},{16,20},{20,16},{24,28},{28,24},{1,5},{5... | collective-permute-start | bytes 1695752 | tf_op jit(solution)/shard_map/ppermute | solution.py:708
  474.2 14.6 %collective-permute-start.44 = (bf16[368,768]{1,0:T(8,128)(2,1)}, bf16[368,768]{1,0:T(8,128)(2,1)S(1)}, u32[]{:S(2)}, u32[]{:S(2)}) collective-permute-start(bf16[368,768]{1,0:T(8,128)(2,1)} %get-tuple-element.481.refs_1_), channel_id=1, source_target_pairs={{0,8},{4,12},{8,0},{12,4},{16,24},{20,28},{24,16},{28,20},{1,9},{5... | collective-permute-start | bytes 1695752 | tf_op jit(solution)/shard_map/ppermute | solution.py:708
  474.2 14.6 %collective-permute-start.45 = (bf16[368,768]{1,0:T(8,128)(2,1)}, bf16[368,768]{1,0:T(8,128)(2,1)S(1)}, u32[]{:S(2)}, u32[]{:S(2)}) collective-permute-start(bf16[368,768]{1,0:T(8,128)(2,1)} %get-tuple-element.481.refs_1_), channel_id=1, source_target_pairs={{0,16},{4,20},{8,24},{12,28},{16,0},{20,4},{24,8},{28,12},{1,17},{... | collective-permute-start | bytes 1695752 | tf_op jit(solution)/shard_map/ppermute | solution.py:708
  475.1 26.2 %collective-permute-start.46 = (bf16[368,768]{1,0:T(8,128)(2,1)}, bf16[368,768]{1,0:T(8,128)(2,1)S(1)}, u32[]{:S(2)}, u32[]{:S(2)}) collective-permute-start(bf16[368,768]{1,0:T(8,128)(2,1)} %get-tuple-element.481.refs_1_), channel_id=1, source_target_pairs={{0,24},{4,28},{8,16},{12,20},{16,8},{20,12},{24,0},{28,4},{1,25},{... | collective-permute-start | bytes 1695752 | tf_op jit(solution)/shard_map/ppermute | solution.py:708
  (88 other events, 305.2 us)
Sparse Core Ops, SparseCore 0:
  55.8 124.6 all-gather.4
  227.9 81.3 reduce-scatter.2
  312.9 81.6 reduce-scatter.4
  414.9 38.2 all-gather.6

commit v8 on v7

--- a/solution.py
+++ b/solution.py
@@ -601,8 +601,8 @@
     width = parts[0].shape[-1]
     total = 4 * channels
     single = len(parts) == 1
-    groups = len(parts) // 2
-    dp = parts[0].shape[0] if single else len(parts)
+    groups = len(parts) // 4
+    dp = parts[0].shape[0] if single else 2 * groups
     piece = total // dp
     share = 2 * RIDERS
     block = dp * share
@@ -612,7 +612,7 @@
         qkv_ref, out_ref, up_ref, down_ref, band_ref = rest[:5]
         up = rest[-1]
 
-        def put(owner, rows_of):
+        def put(owner, rows_of, ff_rows_of, bands):
             start = pl.multiple_of(owner * piece, piece)
             mat = owner * piece // channels
             inner = pl.multiple_of(owner * piece - mat * channels, piece)
@@ -626,30 +626,40 @@
             def _():
                 out_ref[0, pl.ds(inner, piece)] = value
 
-            up[pl.ds(start, piece)] = rows_of(piece, piece).astype(F32)
-            down_ref[0, pl.ds(start, piece)] = rows_of(2 * piece, piece).astype(F32)
+            up[pl.ds(start, piece)] = ff_rows_of(0, piece).astype(F32)
+            down_ref[0, pl.ds(start, piece)] = ff_rows_of(piece, piece).astype(F32)
             for p in range(mp):
-                band = rows_of(3 * piece + norm_rows + p * RIDERS, RIDERS).astype(F32)
+                band = rows_of(bands + p * RIDERS, RIDERS).astype(F32)
                 first = pl.multiple_of((place_ref[1] ^ p) * block + owner * share, share)
                 band_ref[0, pl.ds(first, RIDERS)] = band[:, :window]
                 band_ref[0, pl.ds(first + RIDERS, RIDERS)] = band[:, window : 2 * window]
 
         if single:
             for owner in range(dp):
-                put(jnp.int32(owner), lambda start, count, owner=owner: p_refs[0][owner, start : start + count])
+                put(
+                    jnp.int32(owner),
+                    lambda start, count, owner=owner: p_refs[0][owner, start : start + count],
+                    lambda start, count, owner=owner: p_refs[0][owner, piece + start : piece + start + count],
+                    3 * piece,
+                )
         else:
             for core in range(2):
                 for p in range(groups):
-                    ref = p_refs[core * groups + p]
+                    ref, ff_ref = p_refs[core * groups + p], p_refs[(2 + core) * groups + p]
                     owner = 2 * (place_ref[2] ^ p) + (place_ref[3] ^ core)
-                    put(owner, lambda start, count, ref=ref: ref[start : start + count])
+                    put(
+                        owner,
+                        lambda start, count, ref=ref: ref[start : start + count],
+                        lambda start, count, ref=ff_ref: ref[start : start + count],
+                        piece + norm_rows,
+                    )
         up_ref[0] = up[...].T
         if norm_rows:
             half = norm_rows // 2
             sums = []
             for p in range(groups):
                 for core in range(2):
-                    rows = p_refs[core * groups + p][3 * piece : 3 * piece + norm_rows].astype(F32)
+                    rows = p_refs[core * groups + p][piece : piece + norm_rows].astype(F32)
                     sums.append(rows[:half] + rows[half:])
             while len(sums) > 1:
                 sums = [sums[k] + sums[k + 1] for k in range(0, len(sums), 2)]
@@ -1016,12 +1026,12 @@
         r_attn1.start()
         z_of_1 = mp_index if in_blocks else None
         attn1_sum, riders1 = r_attn1.wait_all()
-        z_ff1 = ReduceMp(links, wide1.wait(), z_of_1, None)
+        z_1 = ReduceMp(links, attn1_sum + wide1.wait(), z_of_1, riders1)
         gq, gk, gv, band0, dn_own0, back0 = attn_backward(order, place, grad3_low, w_attn0, *saved0)
         r_attn0 = Reduce(
             links, attn_weight_grads(order, place, gq, gk, gv, *rows0, grad3_low, band0, mp, False, in_blocks)
         )
-        sum1_ff, _ = z_ff1.wait()
+        sum1, riders1 = z_1.wait()
         r_attn0.start_cores()
         r_attn0.wait_cores()
         r_attn0.start()
@@ -1029,8 +1039,11 @@
         back0 = backward_halo(back0)
         r_attn0.wait()
         (back0,) = order.pin(back0)
+        ff0_sum = wide0.wait()
         r_attn0.start()
-        z_attn1 = ReduceMp(links, attn1_sum, z_of_1, riders1)
+        z_ff0 = ReduceMp(links, ff0_sum, None, None)
+        (full1,) = order.pin(jnp.concatenate([sum1] + riders1, axis=0))
+        full1 = lax.all_gather(full1, DP, axis=0, tiled=False)
         grad4, gain_a0, shift_a0 = leave_attn(order, x, grad3, dn_own0, back0, gains[0, 0])
         norms = jnp.concatenate(
             [gain_a0, gain_b0, shift_a0, shift_b0, gain_a1, gain_b1, shift_a1, shift_b1], axis=0
@@ -1045,19 +1058,31 @@
             return value[:count].astype(F32) + value[count:].astype(F32)
 
         attn0_sum, riders0 = r_attn0.wait_all()
-        sum1_attn, riders1 = z_attn1.wait()
-        (full1,) = order.pin(jnp.concatenate([sum1_attn, sum1_ff] + riders1, axis=0))
-        full1 = lax.all_gather(full1, DP, axis=0, tiled=False)
-        z_0 = ReduceMp(
-            links, attn0_sum + wide0.wait(), None, jnp.concatenate([two_parts(norms), riders0], axis=0)
-        )
+
+        def regather(value):
+            (value,) = order.pin(value)
+            return [value] + [links.swap(value, DP, 2 * p) for p in range(1, groups)], [links.swap(value, DP, 1)]
+
+        def regather_cores(parts):
+            same, other = parts
+            other[0], *same[1:] = order.pin(other[0], *same[1:])
+            same[1:] = order.pin(*same[1:])
+            return same, other + [links.swap(part, DP, 1) for part in same[1:]]
+
+        def regather_wait(parts):
+            same, other = parts
+            return same + other[:1] + order.pin(*other[1:])
+
+        ff0_sum, _ = z_ff0.wait()
+        z_attn0 = ReduceMp(links, attn0_sum, None, jnp.concatenate([two_parts(norms), riders0], axis=0))
+        ff0_parts = regather(ff0_sum)
         (full1,) = order.pin(full1)
 
         cut = 2 * norms.shape[0]
 
         def finish(layer, full, previous):
             if in_blocks:
-                norm_rows = 0 if len(full) == 1 else cut
+                norm_rows = 0 if layer else cut
                 return finish_layer(
                     order, layer, layers, place, full, channels, hidden, mp, window, norm_rows, previous
                 )
@@ -1066,7 +1091,9 @@
                 joined = full[0]
             else:
                 owner = jnp.bitwise_xor(jnp.arange(dp), dp_index)
-                joined = jnp.stack(full).reshape(2, groups, -1, width)
+                joined = jnp.concatenate(
+                    [jnp.stack(full[: 2 * groups])[:, :attn_rows], jnp.stack(full[2 * groups :])], axis=1
+                ).reshape(2, groups, -1, width)
                 joined = jnp.swapaxes(joined, 0, 1).reshape(dp, -1, width)
             joined = joined[:, : attn_rows + 2 * ff_rows]
             attn_part, up_part, down_part = jnp.split(joined, [attn_rows, attn_rows + ff_rows], axis=1)
@@ -1094,25 +1121,20 @@
             ]
 
         big = finish(1, [full1], None)
-        sum0, riders0 = z_0.wait()
+        sum0, riders0 = z_attn0.wait()
         norms = [one_part(part[:cut]) for part in riders0]
         while len(norms) > 1:
             norms = [norms[k] + norms[k + 1] for k in range(0, len(norms), 2)]
-        (sum0,) = order.pin(
-            jnp.concatenate([sum0, two_parts(norms[0])] + [part[cut:] for part in riders0], axis=0)
-        )
-        full0 = [sum0] + [links.swap(sum0, DP, 2 * p) for p in range(1, groups)]
-        others = [links.swap(sum0, DP, 1)]
-        others[0], *full0[1:] = order.pin(others[0], *full0[1:])
-        full0[1:] = order.pin(*full0[1:])
-        others += [links.swap(part, DP, 1) for part in full0[1:]]
-        others[1:] = order.pin(*others[1:])
-        qkv_out, out_out, up_out, down_out, *small = finish(0, full0 + others, big)
+        sum0 = jnp.concatenate([sum0, two_parts(norms[0])] + [part[cut:] for part in riders0], axis=0)
+        ff0_parts = regather_cores(ff0_parts)
+        attn0_parts = regather(sum0)
+        ff0_parts = regather_wait(ff0_parts)
+        attn0_parts = regather_wait(regather_cores(attn0_parts))
+        qkv_out, out_out, up_out, down_out, *small = finish(0, attn0_parts + ff0_parts, big)
         if in_blocks:
             band_sum, norm_sum = small
         else:
-            count = attn_rows + 2 * ff_rows
-            sums = [one_part(part[count : count + cut]) for pair in zip(full0, others) for part in pair]
+            sums = [one_part(attn0_parts[p + k][attn_rows : attn_rows + cut]) for p in range(groups) for k in (0, groups)]
             while len(sums) > 1:
                 sums = [sums[k] + sums[k + 1] for k in range(0, len(sums), 2)]
             norm_sum = sums[0]

time: 529 us -> 509 us (0.962)
  waiting for transfers between devices: 178 us -> 159 us
    all_gather x1, waiting for transfers between devices: 29.3 us -> 0.01 us  [shards(): full1 = lax.all_gather(full1, DP, axis=0, tiled=False)]
    ppermute x46 -> x53, waiting for transfers between devices: 93.6 us -> 104 us  [swap(): return lax.ppermute(value, axis, [(i, i ^ bit) for i in range(size)])]
    ppermute x46 -> x53, starting transfers between devices: 43.3 us -> 48.4 us  [swap(): return lax.ppermute(value, axis, [(i, i ^ bit) for i in range(size)])]
    unnamed x164 -> x178, local copies, waits for them, and re-layouts: 25.2 us -> 22.6 us
  transfers between devices with their start and end apart: 54 -> 61, of which waited for: 25 -> 29; matrix products, arithmetic and copies ran while one was open for 13% -> 13% of each run, Pallas kernels for 24% -> 25%
where the time goes in v8:
time: 509 us; the launch traced here: 501 us
  Pallas kernels  171 us (34%)
  waiting for transfers between devices  159 us (31%)
  starting transfers between devices  59.1 us (12%)
  other arithmetic  50.6 us (10%)
  local copies, waits for them, and re-layouts  38.9 us (8%)
  between operations  15.2 us (3%)
  matrix products  6.88 us (1%)
    pallas_call x15, Pallas kernels, run(): *results, order.token = kernel(*operands, order.token)  171 us
    ppermute x53, waiting for transfers between devices, swap(): return lax.ppermute(value, axis, [(i, i ^ bit) for i in range(size)])  104 us
    ppermute x53, starting transfers between devices, swap(): return lax.ppermute(value, axis, [(i, i ^ bit) for i in range(size)])  48.4 us
    ppermute x2, waiting for transfers between devices, forward_halo(): return lax.ppermute(value, 'mp', [(i, i + 1) for i in range(mp - 1)])  28.7 us
    unnamed x178, local copies, waits for them, and re-layouts  22.6 us
    all_gather x1, waiting for transfers between devices, shards(): later = lax.all_gather(later, ('g', 'c', 'mp'), axis=0, tiled=False)  17.3 us
    another operation x8, other arithmetic, wait(): self.values[k] = jnp.stack([self.values[k], coming[k]], axis=place)  16.4 us
    convert_element_type x8, other arithmetic, start(): sum((lax.index_in_dim(term, 1, place, keepdims=False).astype(F32) for ter...  16.3 us
  transfers between devices with their start and end apart: 61, of which 29 were waited for; matrix products, arithmetic and copies ran while one was open for 13% of the time, Pallas kernels for 25%

profile of v8, /device:TPU:9, one launch (start us, length us, event | category | flops | bytes accessed | tf_op | source)
XLA Modules:
  0.0 500.7 jit_solution(16669876840504643665)
XLA Ops:
  10.3 2.5 collective-permute-start.5
  24.6 2.7 enter.1
  35.9 3.3 collective-permute-done.7.refs_0_
  44.1 7.0 %collective-permute-done.3.refs_2_ = bf16[192,768]{1,0:T(8,128)(2,1)S(1)} collective-permute-done((bf16[192,768]{1,0:T(8,128)(2,1)S(1)}, bf16[192,768]{1,0:T(8,128)(2,1)S(1)}, u32[]{:S(2)}, u32[]{:S(2)}) %collective-permute-start.3) | collective-permute-done | bytes 294944 | tf_op jit(solution)/shard_map/ppermute | solution.py:718
  56.8 3.3 collective-permute-start
  63.1 21.3 %collective-permute-done.refs_0_ = bf16[512,768]{1,0:T(8,128)(2,1)S(1)} collective-permute-done((bf16[512,768]{1,0:T(8,128)(2,1)S(1)}, bf16[512,768]{1,0:T(8,128)(2,1)S(1)}, u32[]{:S(2)}, u32[]{:S(2)}) %collective-permute-start) | collective-permute-done | bytes 786464 | tf_op jit(solution)/shard_map/ppermute | solution.py:932
  85.3 3.7 collective-permute-done.11.refs_0_
  90.0 2.3 pad_maximum_fusion.6.refs_1_
  93.4 2.2 pad_maximum_fusion.4.refs_1_
  95.6 2.2 pad_maximum_fusion.3.refs_0_
  97.8 3.1 collective-permute-start.13
  106.4 14.9 %attn_fwd.2 = (bf16[512,768]{1,0:T(8,128)(2,1)}, bf16[512,768]{1,0:T(8,128)(2,1)}, bf16[512,768]{1,0:T(8,128)(2,1)}, bf16[1024,768]{1,0:T(8,128)(2,1)}, bf16[102...) custom-call(s32[6]{0:T(128)} %stack.156.refs_0_, ...), custom_call_target="tpu_custom_call", output_to_operand_aliasing={{10}: (13, {})} | custom-call | tf_op jit(solution)/shard_map/attn_fwd/pallas_call | solution.py:76
  121.3 7.4 %collective-permute-done.15.refs_0_ = bf16[2,4,96,768]{3,2,1,0:T(8,128)(2,1)} collective-permute-done((bf16[2,4,96,768]{3,2,1,0:T(8,128)(2,1)}, bf16[2,4,96,768]{3,2,1,0:T(8,128)(2,1)}, u32[]{:S(2)}, u32[]{:S(2)}) %collective-permute-start.15) | collective-permute-done | bytes 1179680 | tf_op jit(solution)/shard_map/ppermute | solution.py:718
  128.6 5.8 %collective-permute-done.16.refs_1_ = bf16[2,4,96,768]{3,2,1,0:T(8,128)(2,1)} collective-permute-done((bf16[2,4,96,768]{3,2,1,0:T(8,128)(2,1)S(1)}, bf16[2,4,96,768]{3,2,1,0:T(8,128)(2,1)}, u32[]{:S(2)}, u32[]{:S(2)}) %collective-permute-start.16) | collective-permute-done | bytes 1179680 | tf_op jit(solution)/shard_map/ppermute | solution.py:718
  134.4 3.0 pad_maximum_fusion.1.refs_1_
  137.4 2.9 pad_maximum_fusion.refs_0_
  141.9 7.7 %ff_fwd.2 = (bf16[512,1536]{1,0:T(8,128)(2,1)}, bf16[512,1536]{1,0:T(8,128)(2,1)}, f32[512,768]{1,0:T(8,128)}, s32[8,128]{1,0:T(8,128)}) custom-call(f32[512,768]{1,0:T(8,128)} %get-tuple-element.318.refs_0_.refs_1_, bf16[512,768]{1,0:T(8,128)(2,1)} %get-tuple-element.319.refs_1_.refs_2_, ...), custom_call_target="tpu_custom_call", output_to_operand_aliasing={{3}: (4, {})} | custom-call | tf_op jit(solution)/shard_map/ff_fwd/pallas_call | solution.py:76
  151.0 9.1 %ff_fwd.3 = (bf16[512,1536]{1,0:T(8,128)(2,1)}, bf16[512,1536]{1,0:T(8,128)(2,1)}, f32[512,768]{1,0:T(8,128)}, bf16[512,768]{1,0:T(8,128)(2,1)}, s32[8,128]{1,0:T(8,128)}) custom-call(f32[512,768]{1,0:T(8,128)} %get-tuple-element.329.refs_0_, bf16[512,768]{1,0:T(8,128)(2,1)} %get-tuple-element.319.refs_1_.refs_2_, ...), custom_call_target="tpu_custom_call", output_to_operand_aliasing={{4}: (6, {})} | custom-call | tf_op jit(solution)/shard_map/ff_fwd/pallas_call | solution.py:76
  160.2 3.1 collective-permute-start.19
  163.3 17.3 %all-gather.5.cloned.1.call-done = bf16[9216,768]{1,0:T(8,128)(2,1)} async-done(((bf16[288,768]{1,0:T(8,128)(2,1)}), bf16[9216,768]{1,0:T(8,128)(2,1)}) %all-gather.5.cloned.1.call-update) | async-done | bytes 14155792 | tf_op jit(solution)/shard_map/all_gather | solution.py:966
  180.6 7.4 %collective-permute-done.19.refs_0_ = bf16[512,768]{1,0:T(8,128)(2,1)S(1)} collective-permute-done((bf16[512,768]{1,0:T(8,128)(2,1)}, bf16[512,768]{1,0:T(8,128)(2,1)S(1)}, u32[]{:S(2)}, u32[]{:S(2)}) %collective-permute-start.19) | collective-permute-done | bytes 786464 | tf_op jit(solution)/shard_map/ppermute | solution.py:932
  188.9 14.7 %attn_fwd.3 = (bf16[512,768]{1,0:T(8,128)(2,1)}, bf16[512,768]{1,0:T(8,128)(2,1)}, bf16[512,768]{1,0:T(8,128)(2,1)}, bf16[1024,768]{1,0:T(8,128)(2,1)}, bf16[102...) custom-call(s32[6]{0:T(128)} %stack.156.refs_0_, ...), custom_call_target="tpu_custom_call", output_to_operand_aliasing={{10}: (10, {})} | custom-call | tf_op jit(solution)/shard_map/attn_fwd/pallas_call | solution.py:76
  203.6 24.2 %ff_bwd.2 = (bf16[4,2,2,384,768]{4,3,2,1,0:T(8,128)(2,1)}, f32[512,768]{1,0:T(8,128)}, bf16[512,768]{1,0:T(8,128)(2,1)}, f32[1,768]{1,0:T(1,128)}, f32[1,768]{1,...) custom-call(s32[6]{0:T(128)} %stack.156.refs_0_, ...), custom_call_target="tpu_custom_call", output_to_operand_aliasing={{6}: (7, {})} | custom-call | tf_op jit(solution)/shard_map/ff_bwd/pallas_call | solution.py:76
  227.9 16.2 %attn_bwd.2 = (bf16[512,768]{1,0:T(8,128)(2,1)}, bf16[1024,768]{1,0:T(8,128)(2,1)}, bf16[1024,768]{1,0:T(8,128)(2,1)}, f32[256,256]{1,0:T(8,128)}, f32[512,768]{...) custom-call(s32[6]{0:T(128)} %stack.156.refs_0_, ...), custom_call_target="tpu_custom_call", output_to_operand_aliasing={{6}: (10, {})} | custom-call | tf_op jit(solution)/shard_map/attn_bwd/pallas_call | solution.py:76
  246.1 10.0 %attn_wgrad.2 = (bf16[4,208,768]{2,1,0:T(8,128)(2,1)}, bf16[4,192,768]{2,1,0:T(8,128)(2,1)}, bf16[4,208,768]{2,1,0:T(8,128)(2,1)}, bf16[4,192,768]{2,1,0:T(8,128)(2,1)}, s32[8,128]{1,0:T(8,128)}) custom-call(s32[6]{0:T(128)} %stack.156.refs_0_, bf16[512,768]{1,0:T(8,128)(2,1)} %get-tuple-element.364.refs_1_, ...), custom_call_target="tpu_custom_call", output_to_operand_aliasing={{4}: (9, {})} | custom-call | tf_op jit(solution)/shard_map/attn_wgrad/pallas_call | solution.py:76
  256.1 8.8 %collective-permute-done.20.refs_0_ = bf16[512,768]{1,0:T(8,128)(2,1)S(1)} collective-permute-done((bf16[512,768]{1,0:T(8,128)(2,1)}, bf16[512,768]{1,0:T(8,128)(2,1)S(1)}, u32[]{:S(2)}, u32[]{:S(2)}) %collective-permute-start.20) | collective-permute-done | bytes 786464 | tf_op jit(solution)/shard_map/ppermute | solution.py:935
  267.1 4.9 leave.2
  273.5 2.3 fusion.26.refs_1_
  279.2 21.1 %ff_bwd.3 = (bf16[4,2,2,384,768]{4,3,2,1,0:T(8,128)(2,1)}, f32[512,768]{1,0:T(8,128)}, bf16[512,768]{1,0:T(8,128)(2,1)}, f32[1,768]{1,0:T(1,128)}, f32[1,768]{1,0:T(1,128)}, /*index=5*/s32[8,128]{1,0:T(8,128)}) custom-call(s32[6]{0:T(128)} %stack.156.refs_0_, f32[512,768]{1,0:T(8,128)} %get-tuple-element.318.refs_0_.refs_1_, ...), custom_call_target="tpu_custom_call", output_to_operand_aliasing={{5}: (13, {})} | custom-call | tf_op jit(solution)/shard_map/ff_bwd/pallas_call | solution.py:76
  307.9 7.3 %collective-permute-done.26.refs_1_ = bf16[192,768]{1,0:T(8,128)(2,1)} collective-permute-done((bf16[192,768]{1,0:T(8,128)(2,1)}, bf16[192,768]{1,0:T(8,128)(2,1)}, u32[]{:S(2)}, u32[]{:S(2)}) %collective-permute-start.26) | collective-permute-done | bytes 294944 | tf_op jit(solution)/shard_map/ppermute | solution.py:718
  325.0 17.2 %attn_bwd.3 = (bf16[512,768]{1,0:T(8,128)(2,1)}, bf16[1024,768]{1,0:T(8,128)(2,1)}, bf16[1024,768]{1,0:T(8,128)(2,1)}, f32[256,256]{1,0:T(8,128)}, f32[512,768]{...) custom-call(s32[6]{0:T(128)} %stack.156.refs_0_, ...), custom_call_target="tpu_custom_call", output_to_operand_aliasing={{6}: (13, {})} | custom-call | tf_op jit(solution)/shard_map/attn_bwd/pallas_call | solution.py:76
  342.2 9.7 %attn_wgrad.3 = (bf16[4,208,768]{2,1,0:T(8,128)(2,1)}, bf16[4,192,768]{2,1,0:T(8,128)(2,1)}, bf16[4,208,768]{2,1,0:T(8,128)(2,1)}, bf16[4,192,768]{2,1,0:T(8,128)(2,1)}, s32[8,128]{1,0:T(8,128)}) custom-call(s32[6]{0:T(128)} %stack.156.refs_0_, bf16[512,768]{1,0:T(8,128)(2,1)} %get-tuple-element.419.refs_1_, ...), custom_call_target="tpu_custom_call", output_to_operand_aliasing={{4}: (9, {})} | custom-call | tf_op jit(solution)/shard_map/attn_wgrad/pallas_call | solution.py:76
  351.9 11.6 %collective-permute-done.29.refs_2_ = bf16[304,768]{1,0:T(8,128)(2,1)S(1)} collective-permute-done((bf16[304,768]{1,0:T(8,128)(2,1)}, bf16[304,768]{1,0:T(8,128)(2,1)S(1)}, u32[]{:S(2)}, u32[]{:S(2)}) %collective-permute-start.29) | collective-permute-done | bytes 466976 | tf_op jit(solution)/shard_map/ppermute | solution.py:718
  364.4 3.4 collective-permute-start.30
  369.3 3.0 collective-permute-done.31.refs_1_
  373.7 2.4 fusion.27.refs_1_
  383.7 16.7 %collective-permute-done.34.refs_1_ = bf16[2,192,768]{2,1,0:T(8,128)(2,1)} collective-permute-done((bf16[2,192,768]{2,1,0:T(8,128)(2,1)}, bf16[2,192,768]{2,1,0:T(8,128)(2,1)}, u32[]{:S(2)}, u32[]{:S(2)}) %collective-permute-start.34) | collective-permute-done | bytes 589856 | tf_op jit(solution)/shard_map/ppermute | solution.py:718
  410.2 2.4 collective-permute-start.38
  412.9 5.3 %leave.3 = (f32[512,768]{1,0:T(8,128)}, f32[1,768]{1,0:T(1,128)}, f32[1,768]{1,0:T(1,128)}, s32[8,128]{1,0:T(8,128)}) custom-call(f32[512,768]{1,0:T(8,128)} %get-tuple-element.275.refs_1_.refs_0_, f32[512,768]{1,0:T(8,128)} %get-tuple-element.390.refs_1_, f32[512,768]{1,0:T(8,128)} %get-tuple-element.417.refs_2_, ...), custom_call_target="tpu_custom_call", output_to_operand_aliasing={{3}: (5, {})} | custom-call | tf_op jit(solution)/shard_map/leave/pallas_call | solution.py:76
  421.1 4.1 collective-permute-done.38.refs_1_
  425.1 12.7 %collective-permute-done.39.refs_2_ = bf16[192,768]{1,0:T(8,128)(2,1)} collective-permute-done((bf16[192,768]{1,0:T(8,128)(2,1)}, bf16[192,768]{1,0:T(8,128)(2,1)}, u32[]{:S(2)}, u32[]{:S(2)}) %collective-permute-start.39) | collective-permute-done | bytes 294944 | tf_op jit(solution)/shard_map/ppermute | solution.py:718
  440.1 2.3 collective-permute-start.41
  444.4 2.9 collective-permute-start.43
  450.6 6.5 %finish.2 = (f32[2,3,192,768]{3,2,1,0:T(8,128)}, f32[2,192,768]{2,1,0:T(8,128)}, f32[2,768,768]{2,1,0:T(8,128)}, f32[2,768,768]{2,1,0:T(8,128)}, f32[2,1024,256]{2,1,0:T(8,128)}, /*index=5*/s32[8,128]{1,0:T(8,128)}) custom-call(s32[6]{0:T(128)} %stack.156.refs_0_, bf16[8,352,768]{2,1,0:T(8,128)(2,1)} %get-tuple-element.490.refs_1_, ...), custom_call_target="tpu_custom_call", output_to_operand_aliasing={{5}: (2, {})} | custom-call | tf_op jit(solution)/shard_map/finish/pallas_call | solution.py:76
  458.4 4.9 collective-permute-done.46.refs_3_
  469.6 4.4 collective-permute-done.48.refs_1_
  474.5 5.8 %collective-permute-done.50.refs_3_ = bf16[176,768]{1,0:T(8,128)(2,1)S(1)} collective-permute-done((bf16[176,768]{1,0:T(8,128)(2,1)}, bf16[176,768]{1,0:T(8,128)(2,1)S(1)}, u32[]{:S(2)}, u32[]{:S(2)}) %collective-permute-start.50) | collective-permute-done | bytes 270368 | tf_op jit(solution)/shard_map/ppermute | solution.py:718
  485.6 6.8 %finish.3 = (f32[2,3,192,768]{3,2,1,0:T(8,128)}, f32[2,192,768]{2,1,0:T(8,128)}, f32[2,768,768]{2,1,0:T(8,128)}, f32[2,768,768]{2,1,0:T(8,128)}, f32[2,1024,256]...) custom-call(s32[6]{0:T(128)} %stack.156.refs_0_, ...), custom_call_target="tpu_custom_call", output_to_operand_aliasing={{0}: (17, {}), {1}: (18, {}), {2}: (19, {}), {3}: (20, {}),... | custom-call | tf_op jit(solution)/shard_map/finish/pallas_call | solution.py:76
  (403 shorter events, 121.9 us)
Async XLA Ops:
  7.2 173.4 %all-gather.5.cloned.1.call-start = ((), (), s32[]{:S(2)}) async-start(), calls=%async_computation.4 | async-start | bytes 14598144 | tf_op jit(solution)/shard_map/all_gather | solution.py:966
  10.3 16.9 %collective-permute-start.4 = (bf16[96,768]{1,0:T(8,128)(2,1)}, bf16[96,768]{1,0:T(8,128)(2,1)S(1)}, u32[]{:S(2)}, u32[]{:S(2)}) collective-permute-start(bf16[96,768]{1,0:T(8,128)(2,1)} %get-tuple-element.280), channel_id=1, source_target_pairs={{0,1},{1,0},{2,3},{3,2},{4,5},{5,4},{6,7},{7,6},{8,9},{9,8},{10,11... | collective-permute-start | bytes 442376 | tf_op jit(solution)/shard_map/ppermute | solution.py:718
  10.3 17.2 %collective-permute-start.5 = (bf16[96,768]{1,0:T(8,128)(2,1)}, bf16[96,768]{1,0:T(8,128)(2,1)S(1)}, u32[]{:S(2)}, u32[]{:S(2)}) collective-permute-start(bf16[96,768]{1,0:T(8,128)(2,1)} %get-tuple-element.280), channel_id=1, source_target_pairs={{0,2},{1,3},{2,0},{3,1},{4,6},{5,7},{6,4},{7,5},{8,10},{9,11},{10,... | collective-permute-start | bytes 442376 | tf_op jit(solution)/shard_map/ppermute | solution.py:718
  12.8 14.8 %collective-permute-start.6 = (bf16[96,768]{1,0:T(8,128)(2,1)}, bf16[96,768]{1,0:T(8,128)(2,1)S(1)}, u32[]{:S(2)}, u32[]{:S(2)}) collective-permute-start(bf16[96,768]{1,0:T(8,128)(2,1)} %get-tuple-element.280), channel_id=1, source_target_pairs={{0,3},{1,2},{2,1},{3,0},{4,7},{5,6},{6,5},{7,4},{8,11},{9,10},{10,... | collective-permute-start | bytes 442376 | tf_op jit(solution)/shard_map/ppermute | solution.py:718
  17.2 26.5 %collective-permute-start.1 = (bf16[192,768]{1,0:T(8,128)(2,1)}, bf16[192,768]{1,0:T(8,128)(2,1)S(1)}, u32[]{:S(2)}, u32[]{:S(2)}) collective-permute-start(bf16[192,768]{1,0:T(8,128)(2,1)} %get-tuple-element.279), channel_id=1, source_target_pairs={{0,1},{1,0},{2,3},{3,2},{4,5},{5,4},{6,7},{7,6},{8,9},{9,8},{10,11... | collective-permute-start | bytes 884744 | tf_op jit(solution)/shard_map/ppermute | solution.py:718
  18.3 25.8 %collective-permute-start.2 = (bf16[192,768]{1,0:T(8,128)(2,1)}, bf16[192,768]{1,0:T(8,128)(2,1)S(1)}, u32[]{:S(2)}, u32[]{:S(2)}) collective-permute-start(bf16[192,768]{1,0:T(8,128)(2,1)} %get-tuple-element.279), channel_id=1, source_target_pairs={{0,2},{1,3},{2,0},{3,1},{4,6},{5,7},{6,4},{7,5},{8,10},{9,11},{10,... | collective-permute-start | bytes 884744 | tf_op jit(solution)/shard_map/ppermute | solution.py:718
  27.3 23.7 %collective-permute-start.3 = (bf16[192,768]{1,0:T(8,128)(2,1)S(1)}, bf16[192,768]{1,0:T(8,128)(2,1)S(1)}, u32[]{:S(2)}, u32[]{:S(2)}) collective-permute-start(bf16[192,768]{1,0:T(8,128)(2,1)S(1)} %copy-done.24), channel_id=1, source_target_pairs={{0,3},{1,2},{2,1},{3,0},{4,7},{5,6},{6,5},{7,4},{8,11},{9,10},{10,... | collective-permute-start | bytes 884744 | tf_op jit(solution)/shard_map/ppermute | solution.py:718
  55.7 263.0 %reduce-scatter.3.cloned.1.call-start = ((), (), s32[]{:S(2)}) async-start(), calls=%async_computation.2 | async-start | bytes 10616832 | tf_op jit(solution)/shard_map/reduce_scatter | solution.py:832
  56.8 27.6 %collective-permute-start = (bf16[512,768]{1,0:T(8,128)(2,1)S(1)}, bf16[512,768]{1,0:T(8,128)(2,1)S(1)}, u32[]{:S(2)}, u32[]{:S(2)}) collective-permute-start(bf16[512,768]{1,0:T(8,128)(2,1)S(1)} %copy-done.7), channel_id=1, source_target_pairs={{0,1},{1,2},{2,3},{4,5},{5,6},{6,7},{8,9},{9,10},{10,11},{12,13},{... | collective-permute-start | bytes 2359304 | tf_op jit(solution)/shard_map/ppermute | solution.py:932
  60.1 25.2 %collective-permute-start.10 = (bf16[2,4,48,768]{3,2,1,0:T(8,128)(2,1)S(1)}, bf16[2,4,48,768]{3,2,1,0:T(8,128)(2,1)}, u32[]{:S(2)}, u32[]{:S(2)}) collective-permute-start(bf16[2,4,48,768]{3,2,1,0:T(8,128)(2,1)S(1)} %copy-done.9), channel_id=1, source_target_pairs={{0,8},{4,12},{8,0},{12,4},{16,24},{20,28},{24,16},{28,20},{1,9},{5... | collective-permute-start | bytes 1769480 | tf_op jit(solution)/shard_map/ppermute | solution.py:718
  61.4 23.9 %collective-permute-start.9 = (bf16[2,4,48,768]{3,2,1,0:T(8,128)(2,1)S(1)}, bf16[2,4,48,768]{3,2,1,0:T(8,128)(2,1)}, u32[]{:S(2)}, u32[]{:S(2)}) collective-permute-start(bf16[2,4,48,768]{3,2,1,0:T(8,128)(2,1)S(1)} %copy-done.11), channel_id=1, source_target_pairs={{0,16},{4,20},{8,24},{12,28},{16,0},{20,4},{24,8},{28,12},{1,17},{... | collective-permute-start | bytes 1769480 | tf_op jit(solution)/shard_map/ppermute | solution.py:718
  62.6 26.4 %collective-permute-start.11 = (bf16[4,96,768]{2,1,0:T(8,128)(2,1)}, bf16[4,96,768]{2,1,0:T(8,128)(2,1)S(1)}, u32[]{:S(2)}, u32[]{:S(2)}) collective-permute-start(bf16[4,96,768]{2,1,0:T(8,128)(2,1)} %get-tuple-element.305), channel_id=1, source_target_pairs={{0,8},{4,12},{8,0},{12,4},{16,24},{20,28},{24,16},{28,20},{1,9},{5... | collective-permute-start | bytes 1769480 | tf_op jit(solution)/shard_map/ppermute | solution.py:718
  62.9 27.0 %collective-permute-start.12 = (bf16[4,96,768]{2,1,0:T(8,128)(2,1)}, bf16[4,96,768]{2,1,0:T(8,128)(2,1)}, u32[]{:S(2)}, u32[]{:S(2)}) collective-permute-start(bf16[4,96,768]{2,1,0:T(8,128)(2,1)} %get-tuple-element.306), channel_id=1, source_target_pairs={{0,16},{4,20},{8,24},{12,28},{16,0},{20,4},{24,8},{28,12},{1,17},{... | collective-permute-start | bytes 1769480 | tf_op jit(solution)/shard_map/ppermute | solution.py:718
  97.8 7.2 %collective-permute-start.13 = (bf16[2,2,4,48,768]{4,3,2,1,0:T(8,128)(2,1)}, bf16[2,2,4,48,768]{4,3,2,1,0:T(8,128)(2,1)S(1)}, u32[]{:S(2)}, u32[]{:S(2)}) collective-permute-start(bf16[2,2,4,48,768]{4,3,2,1,0:T(8,128)(2,1)} %get-tuple-element.312), channel_id=1, source_target_pairs={{0,4},{4,0},{8,12},{12,8},{16,20},{20,16},{24,28},{28,24},{1,5},{5... | collective-permute-start | bytes 3538952 | tf_op jit(solution)/shard_map/ppermute | solution.py:718
  101.0 27.7 %collective-permute-start.15 = (bf16[2,4,96,768]{3,2,1,0:T(8,128)(2,1)}, bf16[2,4,96,768]{3,2,1,0:T(8,128)(2,1)}, u32[]{:S(2)}, u32[]{:S(2)}) collective-permute-start(bf16[2,4,96,768]{3,2,1,0:T(8,128)(2,1)} %get-tuple-element.320), channel_id=1, source_target_pairs={{0,16},{4,20},{8,24},{12,28},{16,0},{20,4},{24,8},{28,12},{1,17},{... | collective-permute-start | bytes 3538952 | tf_op jit(solution)/shard_map/ppermute | solution.py:718
  102.2 32.2 %collective-permute-start.16 = (bf16[2,4,96,768]{3,2,1,0:T(8,128)(2,1)S(1)}, bf16[2,4,96,768]{3,2,1,0:T(8,128)(2,1)}, u32[]{:S(2)}, u32[]{:S(2)}) collective-permute-start(bf16[2,4,96,768]{3,2,1,0:T(8,128)(2,1)S(1)} %copy-done.3), channel_id=1, source_target_pairs={{0,8},{4,12},{8,0},{12,4},{16,24},{20,28},{24,16},{28,20},{1,9},{5... | collective-permute-start | bytes 3538952 | tf_op jit(solution)/shard_map/ppermute | solution.py:718
  140.3 9.3 %collective-permute-start.17 = (bf16[2,2,4,96,768]{4,3,2,1,0:T(8,128)(2,1)}, bf16[2,2,4,96,768]{4,3,2,1,0:T(8,128)(2,1)S(1)}, u32[]{:S(2)}, u32[]{:S(2)}) collective-permute-start(bf16[2,2,4,96,768]{4,3,2,1,0:T(8,128)(2,1)} %get-tuple-element.326), channel_id=1, source_target_pairs={{0,4},{4,0},{8,12},{12,8},{16,20},{20,16},{24,28},{28,24},{1,5},{5... | collective-permute-start | bytes 7077896 | tf_op jit(solution)/shard_map/ppermute | solution.py:718
  141.9 8.0 %collective-permute-start.18 = (bf16[2,2,4,96,768]{4,3,2,1,0:T(8,128)(2,1)}, bf16[2,2,4,96,768]{4,3,2,1,0:T(8,128)(2,1)}, u32[]{:S(2)}, u32[]{:S(2)}) collective-permute-start(bf16[2,2,4,96,768]{4,3,2,1,0:T(8,128)(2,1)} %get-tuple-element.327), channel_id=1, source_target_pairs={{0,4},{4,0},{8,12},{12,8},{16,20},{20,16},{24,28},{28,24},{1,5},{5... | collective-permute-start | bytes 7077896 | tf_op jit(solution)/shard_map/ppermute | solution.py:718
  160.2 27.8 %collective-permute-start.19 = (bf16[512,768]{1,0:T(8,128)(2,1)}, bf16[512,768]{1,0:T(8,128)(2,1)S(1)}, u32[]{:S(2)}, u32[]{:S(2)}) collective-permute-start(bf16[512,768]{1,0:T(8,128)(2,1)} %get-tuple-element.337.refs_2_.refs_5_), channel_id=1, source_target_pairs={{0,1},{1,2},{2,3},{4,5},{5,6},{6,7},{8,9},{9,10},{10,11},{12,13},{... | collective-permute-start | bytes 2359304 | tf_op jit(solution)/shard_map/ppermute | solution.py:932
  227.9 177.4 %reduce-scatter.5.cloned.1.call-start = ((), (), s32[]{:S(2)}) async-start(), calls=%async_computation.3 | async-start | bytes 10616832 | tf_op jit(solution)/shard_map/reduce_scatter | solution.py:832
  244.2 20.8 %collective-permute-start.20 = (bf16[512,768]{1,0:T(8,128)(2,1)}, bf16[512,768]{1,0:T(8,128)(2,1)S(1)}, u32[]{:S(2)}, u32[]{:S(2)}) collective-permute-start(bf16[512,768]{1,0:T(8,128)(2,1)} %get-tuple-element.363), channel_id=1, source_target_pairs={{1,0},{2,1},{3,2},{5,4},{6,5},{7,6},{9,8},{10,9},{11,10},{13,12},{... | collective-permute-start | bytes 2359304 | tf_op jit(solution)/shard_map/ppermute | solution.py:935
  277.9 22.5 %collective-permute-start.23 = (bf16[2,208,768]{2,1,0:T(8,128)(2,1)}, bf16[2,208,768]{2,1,0:T(8,128)(2,1)S(1)}, u32[]{:S(2)}, u32[]{:S(2)}) collective-permute-start(bf16[2,208,768]{2,1,0:T(8,128)(2,1)} %get-tuple-element.399), channel_id=1, source_target_pairs={{0,16},{4,20},{8,24},{12,28},{16,0},{20,4},{24,8},{28,12},{1,17},{... | collective-permute-start | bytes 1916936 | tf_op jit(solution)/shard_map/ppermute | solution.py:718
  279.0 21.3 %collective-permute-start.24 = (bf16[2,192,768]{2,1,0:T(8,128)(2,1)}, bf16[2,192,768]{2,1,0:T(8,128)(2,1)S(1)}, u32[]{:S(2)}, u32[]{:S(2)}) collective-permute-start(bf16[2,192,768]{2,1,0:T(8,128)(2,1)} %get-tuple-element.400), channel_id=1, source_target_pairs={{0,8},{4,12},{8,0},{12,4},{16,24},{20,28},{24,16},{28,20},{1,9},{5... | collective-permute-start | bytes 1769480 | tf_op jit(solution)/shard_map/ppermute | solution.py:718
  301.4 148.9 %all-gather.7.cloned.1.call-start = ((), (), s32[]{:S(2)}) async-start(), calls=%async_computation.5 | async-start | bytes 4866048 | tf_op jit(solution)/shard_map/all_gather | solution.py:1046
  306.3 8.9 %collective-permute-start.25 = (bf16[208,768]{1,0:T(8,128)(2,1)}, bf16[208,768]{1,0:T(8,128)(2,1)S(1)}, u32[]{:S(2)}, u32[]{:S(2)}) collective-permute-start(bf16[208,768]{1,0:T(8,128)(2,1)} %get-tuple-element.407), channel_id=1, source_target_pairs={{0,8},{4,12},{8,0},{12,4},{16,24},{20,28},{24,16},{28,20},{1,9},{5... | collective-permute-start | bytes 958472 | tf_op jit(solution)/shard_map/ppermute | solution.py:718
  307.6 7.7 %collective-permute-start.26 = (bf16[192,768]{1,0:T(8,128)(2,1)}, bf16[192,768]{1,0:T(8,128)(2,1)}, u32[]{:S(2)}, u32[]{:S(2)}) collective-permute-start(bf16[192,768]{1,0:T(8,128)(2,1)} %get-tuple-element.408), channel_id=1, source_target_pairs={{0,16},{4,20},{8,24},{12,28},{16,0},{20,4},{24,8},{28,12},{1,17},{... | collective-permute-start | bytes 884744 | tf_op jit(solution)/shard_map/ppermute | solution.py:718
  322.4 29.5 %collective-permute-start.27 = (bf16[304,768]{1,0:T(8,128)(2,1)}, bf16[304,768]{1,0:T(8,128)(2,1)S(1)}, u32[]{:S(2)}, u32[]{:S(2)}) collective-permute-start(bf16[304,768]{1,0:T(8,128)(2,1)} %get-tuple-element.428), channel_id=1, source_target_pairs={{0,1},{1,0},{2,3},{3,2},{4,5},{5,4},{6,7},{7,6},{8,9},{9,8},{10,11... | collective-permute-start | bytes 1400840 | tf_op jit(solution)/shard_map/ppermute | solution.py:718
  322.5 29.4 %collective-permute-start.28 = (bf16[304,768]{1,0:T(8,128)(2,1)}, bf16[304,768]{1,0:T(8,128)(2,1)S(1)}, u32[]{:S(2)}, u32[]{:S(2)}) collective-permute-start(bf16[304,768]{1,0:T(8,128)(2,1)} %get-tuple-element.429), channel_id=1, source_target_pairs={{0,2},{1,3},{2,0},{3,1},{4,6},{5,7},{6,4},{7,5},{8,10},{9,11},{10,... | collective-permute-start | bytes 1400840 | tf_op jit(solution)/shard_map/ppermute | solution.py:718
  324.7 38.8 %collective-permute-start.29 = (bf16[304,768]{1,0:T(8,128)(2,1)}, bf16[304,768]{1,0:T(8,128)(2,1)S(1)}, u32[]{:S(2)}, u32[]{:S(2)}) collective-permute-start(bf16[304,768]{1,0:T(8,128)(2,1)} %get-tuple-element.430), channel_id=1, source_target_pairs={{0,3},{1,2},{2,1},{3,0},{4,7},{5,6},{6,5},{7,4},{8,11},{9,10},{10,... | collective-permute-start | bytes 1400840 | tf_op jit(solution)/shard_map/ppermute | solution.py:718
  364.4 7.9 %collective-permute-start.30 = (bf16[4,208,768]{2,1,0:T(8,128)(2,1)}, bf16[4,208,768]{2,1,0:T(8,128)(2,1)S(1)}, u32[]{:S(2)}, u32[]{:S(2)}) collective-permute-start(bf16[4,208,768]{2,1,0:T(8,128)(2,1)} %get-tuple-element.433), channel_id=1, source_target_pairs={{0,4},{4,0},{8,12},{12,8},{16,20},{20,16},{24,28},{28,24},{1,5},{5... | collective-permute-start | bytes 3833864 | tf_op jit(solution)/shard_map/ppermute | solution.py:718
  378.1 23.3 %collective-permute-start.33 = (bf16[2,208,768]{2,1,0:T(8,128)(2,1)}, bf16[2,208,768]{2,1,0:T(8,128)(2,1)}, u32[]{:S(2)}, u32[]{:S(2)}) collective-permute-start(bf16[2,208,768]{2,1,0:T(8,128)(2,1)} %get-tuple-element.442), channel_id=1, source_target_pairs={{0,16},{4,20},{8,24},{12,28},{16,0},{20,4},{24,8},{28,12},{1,17},{... | collective-permute-start | bytes 1916936 | tf_op jit(solution)/shard_map/ppermute | solution.py:718
  378.2 22.2 %collective-permute-start.34 = (bf16[2,192,768]{2,1,0:T(8,128)(2,1)}, bf16[2,192,768]{2,1,0:T(8,128)(2,1)}, u32[]{:S(2)}, u32[]{:S(2)}) collective-permute-start(bf16[2,192,768]{2,1,0:T(8,128)(2,1)} %get-tuple-element.443), channel_id=1, source_target_pairs={{0,8},{4,12},{8,0},{12,4},{16,24},{20,28},{24,16},{28,20},{1,9},{5... | collective-permute-start | bytes 1769480 | tf_op jit(solution)/shard_map/ppermute | solution.py:718
  380.0 25.3 %collective-permute-start.32 = (bf16[512,768]{1,0:T(8,128)(2,1)}, bf16[512,768]{1,0:T(8,128)(2,1)}, u32[]{:S(2)}, u32[]{:S(2)}) collective-permute-start(bf16[512,768]{1,0:T(8,128)(2,1)} %get-tuple-element.441), channel_id=1, source_target_pairs={{1,0},{2,1},{3,2},{5,4},{6,5},{7,6},{9,8},{10,9},{11,10},{13,12},{... | collective-permute-start | bytes 2359304 | tf_op jit(solution)/shard_map/ppermute | solution.py:935
  408.6 10.3 %collective-permute-start.35 = (bf16[208,768]{1,0:T(8,128)(2,1)S(1)}, bf16[208,768]{1,0:T(8,128)(2,1)S(1)}, u32[]{:S(2)}, u32[]{:S(2)}) collective-permute-start(bf16[208,768]{1,0:T(8,128)(2,1)S(1)} %copy-done.45), channel_id=1, source_target_pairs={{0,8},{4,12},{8,0},{12,4},{16,24},{20,28},{24,16},{28,20},{1,9},{5... | collective-permute-start | bytes 958472 | tf_op jit(solution)/shard_map/ppermute | solution.py:718
  409.8 9.1 %collective-permute-start.36 = (bf16[192,768]{1,0:T(8,128)(2,1)}, bf16[192,768]{1,0:T(8,128)(2,1)}, u32[]{:S(2)}, u32[]{:S(2)}) collective-permute-start(bf16[192,768]{1,0:T(8,128)(2,1)} %get-tuple-element.462), channel_id=1, source_target_pairs={{0,16},{4,20},{8,24},{12,28},{16,0},{20,4},{24,8},{28,12},{1,17},{... | collective-permute-start | bytes 884744 | tf_op jit(solution)/shard_map/ppermute | solution.py:718
  410.2 10.8 %collective-permute-start.37 = (bf16[192,768]{1,0:T(8,128)(2,1)}, bf16[192,768]{1,0:T(8,128)(2,1)S(1)}, u32[]{:S(2)}, u32[]{:S(2)}) collective-permute-start(bf16[192,768]{1,0:T(8,128)(2,1)} %get-tuple-element.474), channel_id=1, source_target_pairs={{0,1},{1,0},{2,3},{3,2},{4,5},{5,4},{6,7},{7,6},{8,9},{9,8},{10,11... | collective-permute-start | bytes 884744 | tf_op jit(solution)/shard_map/ppermute | solution.py:718
  410.2 14.9 %collective-permute-start.38 = (bf16[192,768]{1,0:T(8,128)(2,1)}, bf16[192,768]{1,0:T(8,128)(2,1)}, u32[]{:S(2)}, u32[]{:S(2)}) collective-permute-start(bf16[192,768]{1,0:T(8,128)(2,1)} %get-tuple-element.475), channel_id=1, source_target_pairs={{0,2},{1,3},{2,0},{3,1},{4,6},{5,7},{6,4},{7,5},{8,10},{9,11},{10,... | collective-permute-start | bytes 884744 | tf_op jit(solution)/shard_map/ppermute | solution.py:718
  412.6 25.3 %collective-permute-start.39 = (bf16[192,768]{1,0:T(8,128)(2,1)}, bf16[192,768]{1,0:T(8,128)(2,1)}, u32[]{:S(2)}, u32[]{:S(2)}) collective-permute-start(bf16[192,768]{1,0:T(8,128)(2,1)} %get-tuple-element.476), channel_id=1, source_target_pairs={{0,3},{1,2},{2,1},{3,0},{4,7},{5,6},{6,5},{7,4},{8,11},{9,10},{10,... | collective-permute-start | bytes 884744 | tf_op jit(solution)/shard_map/ppermute | solution.py:718
  440.1 8.6 %collective-permute-start.40 = (bf16[128,768]{1,0:T(8,128)(2,1)}, bf16[128,768]{1,0:T(8,128)(2,1)S(1)}, u32[]{:S(2)}, u32[]{:S(2)}) collective-permute-start(bf16[128,768]{1,0:T(8,128)(2,1)} %get-tuple-element.480), channel_id=1, source_target_pairs={{0,1},{1,0},{2,3},{3,2},{4,5},{5,4},{6,7},{7,6},{8,9},{9,8},{10,11... | collective-permute-start | bytes 589832 | tf_op jit(solution)/shard_map/ppermute | solution.py:718
  440.1 9.8 %collective-permute-start.41 = (bf16[128,768]{1,0:T(8,128)(2,1)}, bf16[128,768]{1,0:T(8,128)(2,1)S(1)}, u32[]{:S(2)}, u32[]{:S(2)}) collective-permute-start(bf16[128,768]{1,0:T(8,128)(2,1)} %get-tuple-element.481), channel_id=1, source_target_pairs={{0,2},{1,3},{2,0},{3,1},{4,6},{5,7},{6,4},{7,5},{8,10},{9,11},{10,... | collective-permute-start | bytes 589832 | tf_op jit(solution)/shard_map/ppermute | solution.py:718
  444.4 13.9 %collective-permute-start.43 = (bf16[192,768]{1,0:T(8,128)(2,1)}, bf16[192,768]{1,0:T(8,128)(2,1)S(1)}, u32[]{:S(2)}, u32[]{:S(2)}) collective-permute-start(bf16[192,768]{1,0:T(8,128)(2,1)} %get-tuple-element.496.refs_9_), channel_id=1, source_target_pairs={{0,4},{4,0},{8,12},{12,8},{16,20},{20,16},{24,28},{28,24},{1,5},{5... | collective-permute-start | bytes 884744 | tf_op jit(solution)/shard_map/ppermute | solution.py:718
  447.3 11.0 %collective-permute-start.44 = (bf16[192,768]{1,0:T(8,128)(2,1)}, bf16[192,768]{1,0:T(8,128)(2,1)S(1)}, u32[]{:S(2)}, u32[]{:S(2)}) collective-permute-start(bf16[192,768]{1,0:T(8,128)(2,1)} %get-tuple-element.496.refs_9_), channel_id=1, source_target_pairs={{0,8},{4,12},{8,0},{12,4},{16,24},{20,28},{24,16},{28,20},{1,9},{5... | collective-permute-start | bytes 884744 | tf_op jit(solution)/shard_map/ppermute | solution.py:718
  447.5 10.9 %collective-permute-start.45 = (bf16[192,768]{1,0:T(8,128)(2,1)}, bf16[192,768]{1,0:T(8,128)(2,1)S(1)}, u32[]{:S(2)}, u32[]{:S(2)}) collective-permute-start(bf16[192,768]{1,0:T(8,128)(2,1)} %get-tuple-element.496.refs_9_), channel_id=1, source_target_pairs={{0,16},{4,20},{8,24},{12,28},{16,0},{20,4},{24,8},{28,12},{1,17},{... | collective-permute-start | bytes 884744 | tf_op jit(solution)/shard_map/ppermute | solution.py:718
  448.7 14.6 %collective-permute-start.46 = (bf16[192,768]{1,0:T(8,128)(2,1)}, bf16[192,768]{1,0:T(8,128)(2,1)S(1)}, u32[]{:S(2)}, u32[]{:S(2)}) collective-permute-start(bf16[192,768]{1,0:T(8,128)(2,1)} %get-tuple-element.496.refs_9_), channel_id=1, source_target_pairs={{0,24},{4,28},{8,16},{12,20},{16,8},{20,12},{24,0},{28,4},{1,25},{... | collective-permute-start | bytes 884744 | tf_op jit(solution)/shard_map/ppermute | solution.py:718
  450.0 7.7 %collective-permute-start.42 = (bf16[128,768]{1,0:T(8,128)(2,1)S(1)}, bf16[128,768]{1,0:T(8,128)(2,1)S(1)}, u32[]{:S(2)}, u32[]{:S(2)}) collective-permute-start(bf16[128,768]{1,0:T(8,128)(2,1)S(1)} %copy-done.72), channel_id=1, source_target_pairs={{0,3},{1,2},{2,1},{3,0},{4,7},{5,6},{6,5},{7,4},{8,11},{9,10},{10,... | collective-permute-start | bytes 589832 | tf_op jit(solution)/shard_map/ppermute | solution.py:718
  466.3 7.8 %collective-permute-start.48 = (bf16[176,768]{1,0:T(8,128)(2,1)}, bf16[176,768]{1,0:T(8,128)(2,1)S(1)}, u32[]{:S(2)}, u32[]{:S(2)}) collective-permute-start(bf16[176,768]{1,0:T(8,128)(2,1)} %get-tuple-element.503.refs_1_), channel_id=1, source_target_pairs={{0,8},{4,12},{8,0},{12,4},{16,24},{20,28},{24,16},{28,20},{1,9},{5... | collective-permute-start | bytes 811016 | tf_op jit(solution)/shard_map/ppermute | solution.py:718
  467.0 7.5 %collective-permute-start.49 = (bf16[176,768]{1,0:T(8,128)(2,1)}, bf16[176,768]{1,0:T(8,128)(2,1)S(1)}, u32[]{:S(2)}, u32[]{:S(2)}) collective-permute-start(bf16[176,768]{1,0:T(8,128)(2,1)} %get-tuple-element.503.refs_1_), channel_id=1, source_target_pairs={{0,16},{4,20},{8,24},{12,28},{16,0},{20,4},{24,8},{28,12},{1,17},{... | collective-permute-start | bytes 811016 | tf_op jit(solution)/shard_map/ppermute | solution.py:718
  468.1 12.1 %collective-permute-start.50 = (bf16[176,768]{1,0:T(8,128)(2,1)}, bf16[176,768]{1,0:T(8,128)(2,1)S(1)}, u32[]{:S(2)}, u32[]{:S(2)}) collective-permute-start(bf16[176,768]{1,0:T(8,128)(2,1)} %get-tuple-element.503.refs_1_), channel_id=1, source_target_pairs={{0,24},{4,28},{8,16},{12,20},{16,8},{20,12},{24,0},{28,4},{1,25},{... | collective-permute-start | bytes 811016 | tf_op jit(solution)/shard_map/ppermute | solution.py:718
  (101 other events, 393.5 us)
Sparse Core Ops, SparseCore 0:
  55.8 124.7 all-gather.4
  228.0 81.3 reduce-scatter.2
  312.9 82.7 reduce-scatter.4
  407.8 36.7 all-gather.6

commit v9 on v8

--- a/solution.py
+++ b/solution.py
@@ -46,7 +46,10 @@
     return pl.BlockSpec(shape, lambda *_: (0,) * len(shape))
 
 
-def call(order, body, grid, in_specs, out_specs, out_shape, scratch=(), prefetch=0, name=None, aliases=None):
+def call(
+    order, body, grid, in_specs, out_specs, out_shape, scratch=(), prefetch=0, name=None, aliases=None,
+    limit=None, near_in=(), near_out=(),
+):
     first = prefetch + len(in_specs)
     second = first + 1 + len(out_specs)
     anywhere = pl.BlockSpec(memory_space=pl.ANY)
@@ -63,17 +66,27 @@
             out_specs=list(out_specs) + [anywhere],
             scratch_shapes=list(scratch),
         ),
-        out_shape=list(out_shape) + [shape_of(TOKEN, jnp.int32)],
+        out_shape=[
+            shape if limit is None or k in near_out else pltpu.HBM(shape.shape, shape.dtype)
+            for k, shape in enumerate(out_shape)
+        ]
+        + [shape_of(TOKEN, jnp.int32)],
         input_output_aliases={**(aliases or {}), first: len(out_specs)},
         compiler_params=pltpu.CompilerParams(
-            dimension_semantics=("arbitrary",) * len(grid), vmem_limit_bytes=VMEM_LIMIT
+            dimension_semantics=("arbitrary",) * len(grid), vmem_limit_bytes=limit or VMEM_LIMIT
         ),
         cost_estimate=pl.CostEstimate(flops=0, bytes_accessed=0, transcendentals=0),
         name=name,
     )
 
     def run(*operands):
-        *results, order.token = kernel(*operands, order.token)
+        placed = [
+            operand
+            if limit is None or k < prefetch or k - prefetch in near_in
+            else pltpu.with_memory_space_constraint(operand, pltpu.HBM)
+            for k, operand in enumerate(operands)
+        ]
+        *results, order.token = kernel(*placed, order.token)
         return results
 
     return run
@@ -130,25 +143,38 @@
     return (dot_nn(high, flip) + dot_nn(middle, flip)) + dot_nn(last, flip)
 
 
+THIRDS = 3
+
+
 def attn_specs(weights):
     if len(weights) == 4:
         return [whole(w.shape) for w in weights]
-    groups, _, mp, count, width = weights[0].shape
-    return [pl.BlockSpec((groups, 1, mp, count // 3, width), lambda i, place: (0, place[3] ^ i, 0, 0, 0))]
-
-
-def by_half(step, refs, place_ref, part):
-    if len(refs) == 1:
-        width = refs[0].shape[-1]
-        part(lambda m: refs[0][m, 0].reshape(-1, width))
-        return
-    for half in range(2):
-        wa, wb = refs[2 * half], refs[2 * half + 1]
-
-        def mat(m, wa=wa, wb=wb):
-            return jnp.concatenate([wa[place_ref[0] ^ m], wb[place_ref[0] ^ m]], axis=0)
-
-        pl.when(step == half)(functools.partial(part, mat))
+    groups, two, mp, count, width = weights[0].shape
+    return [pl.BlockSpec((groups, two, mp, count // 3, width), lambda i, place: (0, 0, 0, 0, 0))]
+
+
+def by_third(step, refs, place_ref, part):
+    def pieces(m):
+        if len(refs) == 4:
+            for ref in refs:
+                yield lambda here, ref=ref: ref[place_ref[0] ^ m, here], ref.shape[1]
+            return
+        for half in range(2):
+            for z in range(refs[0].shape[2]):
+                yield lambda here, half=half, z=z: refs[0][m, place_ref[3] ^ half, z, here], refs[0].shape[3]
+
+    def mat(m, third):
+        count = sum(length for _, length in pieces(m)) // THIRDS
+        first, last, at, out = third * count, (third + 1) * count, 0, []
+        for read, length in pieces(m):
+            low, high = max(first - at, 0), min(last - at, length)
+            if low < high:
+                out.append(read(slice(low, high)))
+            at += length
+        return jnp.concatenate(out, axis=0)
+
+    for third in range(THIRDS):
+        pl.when(step == third)(functools.partial(part, functools.partial(mat, third=third)))
 
 
 def attn_forward(order, layer, place, x, normed, halo, weights, pos_bias, seg_q, seg_k, gain, shift):
@@ -156,7 +182,7 @@
     seqs, block, _ = seg_q.shape
     keys = seg_k.shape[2]
     window = keys - block
-    half = width // 2
+    third = width // THIRDS
 
     def body(place_ref, x_ref, n_ref, h_ref, *rest):
         w_refs, rest = rest[: len(weights)], rest[len(weights) :]
@@ -204,20 +230,20 @@
             mixed_ref[...] = mixed
             x1_ref[...] += dot_nn(mixed, mat(3))
 
-        by_half(step, w_refs, place_ref, part)
-
-        @pl.when(step == 1)
+        by_third(step, w_refs, place_ref, part)
+
+        @pl.when(step == THIRDS - 1)
         def _():
             normal, _ = normalize(x1_ref[...])
             nb_ref[...] = (normal * g_ref[...] + s_ref[...]).astype(BF)
 
     def col(n):
-        return pl.BlockSpec((n, half), lambda i, *_: (0, i))
+        return pl.BlockSpec((n, third), lambda i, *_: (0, i))
 
     return call(
         order,
         body,
-        (2,),
+        (THIRDS,),
         [whole((rows, width))] * 3
         + attn_specs(weights)
         + [pl.BlockSpec((1, block, window), lambda i, place: (layer, place[1], 0))]
@@ -433,7 +459,7 @@
     rows, width = grad_low.shape
     seqs, block, keys = masked.shape
     window = keys - block
-    half = width // 2
+    third = width // THIRDS
 
     def body(place_ref, ga_ref, *rest):
         w_refs, rest = rest[: len(weights)], rest[len(weights) :]
@@ -475,9 +501,9 @@
                     wgrad[s, :, cols] += dot_nt(gnum[here], car_ref[there]) + dot_nt(gden[here], wsum_ref[there])
                     dn[there] += dot_nn(gk, wk) + dot_nn(gv, wv)
 
-        by_half(step, w_refs, place_ref, part)
-
-        @pl.when(step == 1)
+        by_third(step, w_refs, place_ref, part)
+
+        @pl.when(step == THIRDS - 1)
         def _():
             total = wgrad[0] * masked_ref[0]
             for s in range(1, seqs):
@@ -493,12 +519,12 @@
             own_ref[...] = dn[rows:]
 
     def col(n):
-        return pl.BlockSpec((n, half), lambda i, *_: (0, i))
+        return pl.BlockSpec((n, third), lambda i, *_: (0, i))
 
     return call(
         order,
         body,
-        (2,),
+        (THIRDS,),
         [whole((rows, width))]
         + attn_specs(weights)
         + [col(rows)] * 3 + [col(2 * rows)] * 3 + [whole((seqs, block, keys))],
@@ -518,6 +544,9 @@
         ],
         prefetch=1,
         name="attn_bwd",
+        limit=46 * 1024 * 1024,
+        near_in=(0,),
+        near_out=(0, 1, 2, 3, 4, 5),
     )(place, grad_low, *weights, sg, ratio, rden, v, wsum, carried, masked)
 
 
@@ -573,6 +602,8 @@
         [shape_of(shape, BF) for shape in shapes],
         prefetch=1,
         name="attn_wgrad",
+        limit=36 * 1024 * 1024,
+        near_in=(0, 1, 2, 6, 7),
     )(place, gq, gk, gv, mixed, normed, halo, grad_low, band)
 
 
@@ -1026,24 +1057,26 @@
         r_attn1.start()
         z_of_1 = mp_index if in_blocks else None
         attn1_sum, riders1 = r_attn1.wait_all()
-        z_1 = ReduceMp(links, attn1_sum + wide1.wait(), z_of_1, riders1)
+        z_ff1 = ReduceMp(links, wide1.wait(), z_of_1, None)
         gq, gk, gv, band0, dn_own0, back0 = attn_backward(order, place, grad3_low, w_attn0, *saved0)
         r_attn0 = Reduce(
             links, attn_weight_grads(order, place, gq, gk, gv, *rows0, grad3_low, band0, mp, False, in_blocks)
         )
-        sum1, riders1 = z_1.wait()
+        sum1_ff, _ = z_ff1.wait()
         r_attn0.start_cores()
+        z_attn1 = ReduceMp(links, attn1_sum, z_of_1, riders1)
         r_attn0.wait_cores()
+        sum1, riders1 = z_attn1.wait()
         r_attn0.start()
         (back0,) = order.pin(back0)
         back0 = backward_halo(back0)
+        (full1,) = order.pin(jnp.concatenate([sum1, sum1_ff] + riders1, axis=0))
+        full1 = lax.all_gather(full1, DP, axis=0, tiled=False)
         r_attn0.wait()
         (back0,) = order.pin(back0)
         ff0_sum = wide0.wait()
         r_attn0.start()
         z_ff0 = ReduceMp(links, ff0_sum, None, None)
-        (full1,) = order.pin(jnp.concatenate([sum1] + riders1, axis=0))
-        full1 = lax.all_gather(full1, DP, axis=0, tiled=False)
         grad4, gain_a0, shift_a0 = leave_attn(order, x, grad3, dn_own0, back0, gains[0, 0])
         norms = jnp.concatenate(
             [gain_a0, gain_b0, shift_a0, shift_b0, gain_a1, gain_b1, shift_a1, shift_b1], axis=0

time: 509 us -> 505 us (level)
  Pallas kernels: 171 us -> 160 us
  local copies, waits for them, and re-layouts: 38.9 us -> 48.2 us
    pallas_call x15, Pallas kernels: 171 us -> 160 us  [run(): *results, order.token = kernel(*placed, order.token)]
    unnamed x178 -> x240, local copies, waits for them, and re-layouts: 22.6 us -> 32.8 us
    ppermute x53 -> x56, starting transfers between devices: 48.4 us -> 52.3 us  [swap(): return lax.ppermute(value, axis, [(i, i ^ bit) for i in range(size)])]
    ppermute x53 -> x56, waiting for transfers between devices: 104 us -> 102 us  [swap(): return lax.ppermute(value, axis, [(i, i ^ bit) for i in range(size)])]
  transfers between devices with their start and end apart: 61 -> 64, of which waited for: 29 -> 32; matrix products, arithmetic and copies ran while one was open for 13% -> 13% of each run, Pallas kernels for 25% -> 23%
where the time goes in v9:
time: 505 us; the launch traced here: 499 us
  Pallas kernels  160 us (32%)
  waiting for transfers between devices  155 us (31%)
  starting transfers between devices  63.3 us (13%)
  other arithmetic  50.5 us (10%)
  local copies, waits for them, and re-layouts  48.2 us (10%)
  between operations  15.1 us (3%)
  matrix products  6.88 us (1%)
    pallas_call x15, Pallas kernels, run(): *results, order.token = kernel(*placed, order.token)  160 us
    ppermute x56, waiting for transfers between devices, swap(): return lax.ppermute(value, axis, [(i, i ^ bit) for i in range(size)])  102 us
    ppermute x56, starting transfers between devices, swap(): return lax.ppermute(value, axis, [(i, i ^ bit) for i in range(size)])  52.3 us
    unnamed x240, local copies, waits for them, and re-layouts  32.8 us
    ppermute x2, waiting for transfers between devices, forward_halo(): return lax.ppermute(value, 'mp', [(i, i + 1) for i in range(mp - 1)])  28.4 us
    all_gather x1, waiting for transfers between devices, shards(): later = lax.all_gather(later, ('g', 'c', 'mp'), axis=0, tiled=False)  17.2 us
    another operation x8, other arithmetic, wait(): self.values[k] = jnp.stack([self.values[k], coming[k]], axis=place)  16.4 us
    convert_element_type x8, other arithmetic, start(): sum((lax.index_in_dim(term, 1, place, keepdims=False).astype(F32) for ter...  16.2 us
  transfers between devices with their start and end apart: 64, of which 32 were waited for; matrix products, arithmetic and copies ran while one was open for 13% of the time, Pallas kernels for 23%

profile of v9, /device:TPU:9, one launch (start us, length us, event | category | flops | bytes accessed | tf_op | source)
XLA Modules:
  0.0 499.4 jit_solution(14036493350298730518)
XLA Ops:
  10.3 2.5 collective-permute-start.5
  24.6 2.7 enter.1
  35.9 3.4 collective-permute-done.7.refs_0_
  44.1 7.0 %collective-permute-done.3.refs_2_ = bf16[192,768]{1,0:T(8,128)(2,1)S(1)} collective-permute-done((bf16[192,768]{1,0:T(8,128)(2,1)S(1)}, bf16[192,768]{1,0:T(8,128)(2,1)S(1)}, u32[]{:S(2)}, u32[]{:S(2)}) %collective-permute-start.3) | collective-permute-done | bytes 294944 | tf_op jit(solution)/shard_map/ppermute | solution.py:749
  56.8 3.5 collective-permute-start
  63.3 21.1 %collective-permute-done.refs_0_ = bf16[512,768]{1,0:T(8,128)(2,1)S(1)} collective-permute-done((bf16[512,768]{1,0:T(8,128)(2,1)S(1)}, bf16[512,768]{1,0:T(8,128)(2,1)S(1)}, u32[]{:S(2)}, u32[]{:S(2)}) %collective-permute-start) | collective-permute-done | bytes 786464 | tf_op jit(solution)/shard_map/ppermute | solution.py:963
  85.3 3.9 collective-permute-done.11.refs_0_
  90.1 2.3 pad_maximum_fusion.5.refs_1_
  95.7 2.2 pad_maximum_fusion.2.refs_0_
  97.9 3.1 collective-permute-start.13
  106.5 13.9 %attn_fwd.2 = (bf16[512,768]{1,0:T(8,128)(2,1)}, bf16[512,768]{1,0:T(8,128)(2,1)}, bf16[512,768]{1,0:T(8,128)(2,1)}, bf16[1024,768]{1,0:T(8,128)(2,1)}, bf16[102...) custom-call(s32[6]{0:T(128)} %stack.156.refs_0_, ...), custom_call_target="tpu_custom_call", output_to_operand_aliasing={{10}: (13, {})} | custom-call | tf_op jit(solution)/shard_map/attn_fwd/pallas_call | solution.py:89
  120.4 8.5 %collective-permute-done.15.refs_0_ = bf16[2,4,96,768]{3,2,1,0:T(8,128)(2,1)} collective-permute-done((bf16[2,4,96,768]{3,2,1,0:T(8,128)(2,1)}, bf16[2,4,96,768]{3,2,1,0:T(8,128)(2,1)}, u32[]{:S(2)}, u32[]{:S(2)}) %collective-permute-start.15) | collective-permute-done | bytes 1179680 | tf_op jit(solution)/shard_map/ppermute | solution.py:749
  128.9 5.5 %collective-permute-done.16.refs_1_ = bf16[2,4,96,768]{3,2,1,0:T(8,128)(2,1)} collective-permute-done((bf16[2,4,96,768]{3,2,1,0:T(8,128)(2,1)S(1)}, bf16[2,4,96,768]{3,2,1,0:T(8,128)(2,1)}, u32[]{:S(2)}, u32[]{:S(2)}) %collective-permute-start.16) | collective-permute-done | bytes 1179680 | tf_op jit(solution)/shard_map/ppermute | solution.py:749
  134.4 3.0 pad_maximum_fusion.1.refs_1_
  137.4 2.9 pad_maximum_fusion.refs_0_
  141.9 7.7 %ff_fwd.2 = (bf16[512,1536]{1,0:T(8,128)(2,1)}, bf16[512,1536]{1,0:T(8,128)(2,1)}, f32[512,768]{1,0:T(8,128)}, s32[8,128]{1,0:T(8,128)}) custom-call(f32[512,768]{1,0:T(8,128)} %get-tuple-element.327.refs_0_.refs_1_, bf16[512,768]{1,0:T(8,128)(2,1)} %get-tuple-element.328.refs_1_.refs_2_, ...), custom_call_target="tpu_custom_call", output_to_operand_aliasing={{3}: (4, {})} | custom-call | tf_op jit(solution)/shard_map/ff_fwd/pallas_call | solution.py:89
  151.0 9.1 %ff_fwd.3 = (bf16[512,1536]{1,0:T(8,128)(2,1)}, bf16[512,1536]{1,0:T(8,128)(2,1)}, f32[512,768]{1,0:T(8,128)}, bf16[512,768]{1,0:T(8,128)(2,1)}, s32[8,128]{1,0:T(8,128)}) custom-call(f32[512,768]{1,0:T(8,128)} %get-tuple-element.338.refs_0_, bf16[512,768]{1,0:T(8,128)(2,1)} %get-tuple-element.328.refs_1_.refs_2_, ...), custom_call_target="tpu_custom_call", output_to_operand_aliasing={{4}: (6, {})} | custom-call | tf_op jit(solution)/shard_map/ff_fwd/pallas_call | solution.py:89
  160.2 3.3 collective-permute-start.19
  163.5 17.2 %all-gather.5.cloned.1.call-done = bf16[9216,768]{1,0:T(8,128)(2,1)} async-done(((bf16[288,768]{1,0:T(8,128)(2,1)}), bf16[9216,768]{1,0:T(8,128)(2,1)}) %all-gather.5.cloned.1.call-update) | async-done | bytes 14155792 | tf_op jit(solution)/shard_map/all_gather | solution.py:997
  180.7 7.3 %collective-permute-done.19.refs_0_ = bf16[512,768]{1,0:T(8,128)(2,1)S(1)} collective-permute-done((bf16[512,768]{1,0:T(8,128)(2,1)}, bf16[512,768]{1,0:T(8,128)(2,1)S(1)}, u32[]{:S(2)}, u32[]{:S(2)}) %collective-permute-start.19) | collective-permute-done | bytes 786464 | tf_op jit(solution)/shard_map/ppermute | solution.py:963
  188.9 13.6 %attn_fwd.3 = (bf16[512,768]{1,0:T(8,128)(2,1)}, bf16[512,768]{1,0:T(8,128)(2,1)}, bf16[512,768]{1,0:T(8,128)(2,1)}, bf16[1024,768]{1,0:T(8,128)(2,1)}, bf16[102...) custom-call(s32[6]{0:T(128)} %stack.156.refs_0_, ...), custom_call_target="tpu_custom_call", output_to_operand_aliasing={{10}: (10, {})} | custom-call | tf_op jit(solution)/shard_map/attn_fwd/pallas_call | solution.py:89
  202.5 24.2 %ff_bwd.2 = (bf16[4,2,2,384,768]{4,3,2,1,0:T(8,128)(2,1)}, f32[512,768]{1,0:T(8,128)}, bf16[512,768]{1,0:T(8,128)(2,1)}, f32[1,768]{1,0:T(1,128)}, f32[1,768]{1,...) custom-call(s32[6]{0:T(128)} %stack.156.refs_0_, ...), custom_call_target="tpu_custom_call", output_to_operand_aliasing={{6}: (7, {})} | custom-call | tf_op jit(solution)/shard_map/ff_bwd/pallas_call | solution.py:89
  227.9 12.8 %attn_bwd.2 = (bf16[512,768]{1,0:T(8,128)(2,1)S(1)}, bf16[1024,768]{1,0:T(8,128)(2,1)S(1)}, bf16[1024,768]{1,0:T(8,128)(2,1)S(1)}, f32[256,256]{1,0:T(8,128)S(1)...) custom-call(s32[6]{0:T(128)S(1)} %copy-done.15, ...), custom_call_target="tpu_custom_call", output_to_operand_aliasing={{6}: (10, {})} | custom-call | tf_op jit(solution)/shard_map/attn_bwd/pallas_call | solution.py:89
  248.5 8.7 %attn_wgrad.2 = (bf16[4,208,768]{2,1,0:T(8,128)(2,1)}, bf16[4,192,768]{2,1,0:T(8,128)(2,1)}, bf16[4,208,768]{2,1,0:T(8,128)(2,1)}, bf16[4,192,768]{2,1,0:T(8,128)(2,1)}, s32[8,128]{1,0:T(8,128)S(1)}) custom-call(s32[6]{0:T(128)S(1)} %copy-done.15, bf16[512,768]{1,0:T(8,128)(2,1)S(1)} %get-tuple-element.373.refs_1_, ...), custom_call_target="tpu_custom_call", output_to_operand_aliasing={{4}: (9, {})} | custom-call | tf_op jit(solution)/shard_map/attn_wgrad/pallas_call | solution.py:89
  257.9 7.2 %collective-permute-done.20.refs_0_ = bf16[512,768]{1,0:T(8,128)(2,1)} collective-permute-done((bf16[512,768]{1,0:T(8,128)(2,1)}, bf16[512,768]{1,0:T(8,128)(2,1)}, u32[]{:S(2)}, u32[]{:S(2)}) %collective-permute-start.20) | collective-permute-done | bytes 786464 | tf_op jit(solution)/shard_map/ppermute | solution.py:966
  266.7 4.9 leave.2
  273.1 2.3 fusion.26.refs_1_
  278.9 20.7 %ff_bwd.3 = (bf16[4,2,2,384,768]{4,3,2,1,0:T(8,128)(2,1)}, f32[512,768]{1,0:T(8,128)}, bf16[512,768]{1,0:T(8,128)(2,1)}, f32[1,768]{1,0:T(1,128)}, f32[1,768]{1,0:T(1,128)}, /*index=5*/s32[8,128]{1,0:T(8,128)}) custom-call(s32[6]{0:T(128)} %stack.156.refs_0_, f32[512,768]{1,0:T(8,128)} %get-tuple-element.327.refs_0_.refs_1_, ...), custom_call_target="tpu_custom_call", output_to_operand_aliasing={{5}: (13, {})} | custom-call | tf_op jit(solution)/shard_map/ff_bwd/pallas_call | solution.py:89
  307.0 7.0 %collective-permute-done.26.refs_1_ = bf16[192,768]{1,0:T(8,128)(2,1)S(1)} collective-permute-done((bf16[192,768]{1,0:T(8,128)(2,1)}, bf16[192,768]{1,0:T(8,128)(2,1)S(1)}, u32[]{:S(2)}, u32[]{:S(2)}) %collective-permute-start.26) | collective-permute-done | bytes 294944 | tf_op jit(solution)/shard_map/ppermute | solution.py:749
  317.3 2.6 collective-permute-start.28
  320.7 14.5 %attn_bwd.3 = (bf16[512,768]{1,0:T(8,128)(2,1)S(1)}, bf16[1024,768]{1,0:T(8,128)(2,1)S(1)}, bf16[1024,768]{1,0:T(8,128)(2,1)S(1)}, f32[256,256]{1,0:T(8,128)S(1)...) custom-call(s32[6]{0:T(128)S(1)} %copy-done.16, ...), custom_call_target="tpu_custom_call", output_to_operand_aliasing={{6}: (13, {})} | custom-call | tf_op jit(solution)/shard_map/attn_bwd/pallas_call | solution.py:89
  335.3 8.8 %attn_wgrad.3 = (bf16[4,208,768]{2,1,0:T(8,128)(2,1)}, bf16[4,192,768]{2,1,0:T(8,128)(2,1)}, bf16[4,208,768]{2,1,0:T(8,128)(2,1)}, bf16[4,192,768]{2,1,0:T(8,128)(2,1)}, s32[8,128]{1,0:T(8,128)S(1)}) custom-call(s32[6]{0:T(128)S(1)} %copy-done.16, bf16[512,768]{1,0:T(8,128)(2,1)S(1)} %get-tuple-element.426.refs_1_, ...), custom_call_target="tpu_custom_call", output_to_operand_aliasing={{4}: (9, {})} | custom-call | tf_op jit(solution)/shard_map/attn_wgrad/pallas_call | solution.py:89
  345.5 3.5 collective-permute-start.30
  357.9 4.6 collective-permute-done.33.refs_1_
  362.5 7.3 %collective-permute-done.34.refs_2_ = bf16[112,768]{1,0:T(8,128)(2,1)S(1)} collective-permute-done((bf16[112,768]{1,0:T(8,128)(2,1)}, bf16[112,768]{1,0:T(8,128)(2,1)S(1)}, u32[]{:S(2)}, u32[]{:S(2)}) %collective-permute-start.34) | collective-permute-done | bytes 172064 | tf_op jit(solution)/shard_map/ppermute | solution.py:749
  370.5 2.2 fusion.27.refs_1_
  382.7 15.8 %collective-permute-done.37.refs_1_ = bf16[2,192,768]{2,1,0:T(8,128)(2,1)S(1)} collective-permute-done((bf16[2,192,768]{2,1,0:T(8,128)(2,1)}, bf16[2,192,768]{2,1,0:T(8,128)(2,1)S(1)}, u32[]{:S(2)}, u32[]{:S(2)}) %collective-permute-start.37) | collective-permute-done | bytes 589856 | tf_op jit(solution)/shard_map/ppermute | solution.py:749
  409.0 2.5 collective-permute-start.41
  411.7 4.9 leave.3
  417.4 2.3 collective-permute-done.39.refs_1_
  423.5 12.5 %collective-permute-done.42.refs_2_ = bf16[192,768]{1,0:T(8,128)(2,1)} collective-permute-done((bf16[192,768]{1,0:T(8,128)(2,1)}, bf16[192,768]{1,0:T(8,128)(2,1)}, u32[]{:S(2)}, u32[]{:S(2)}) %collective-permute-start.42) | collective-permute-done | bytes 294944 | tf_op jit(solution)/shard_map/ppermute | solution.py:749
  438.2 2.7 collective-permute-start.44
  442.7 3.4 collective-permute-start.46
  449.5 6.5 %finish.2 = (f32[2,3,192,768]{3,2,1,0:T(8,128)}, f32[2,192,768]{2,1,0:T(8,128)}, f32[2,768,768]{2,1,0:T(8,128)}, f32[2,768,768]{2,1,0:T(8,128)}, f32[2,1024,256]{2,1,0:T(8,128)}, /*index=5*/s32[8,128]{1,0:T(8,128)}) custom-call(s32[6]{0:T(128)} %stack.156.refs_0_, bf16[8,352,768]{2,1,0:T(8,128)(2,1)} %get-tuple-element.508.refs_1_, ...), custom_call_target="tpu_custom_call", output_to_operand_aliasing={{5}: (2, {})} | custom-call | tf_op jit(solution)/shard_map/finish/pallas_call | solution.py:89
  456.0 3.2 collective-permute-done.45.refs_2_
  468.4 4.4 collective-permute-done.51.refs_1_
  473.4 5.6 %collective-permute-done.53.refs_3_ = bf16[176,768]{1,0:T(8,128)(2,1)S(1)} collective-permute-done((bf16[176,768]{1,0:T(8,128)(2,1)}, bf16[176,768]{1,0:T(8,128)(2,1)S(1)}, u32[]{:S(2)}, u32[]{:S(2)}) %collective-permute-start.53) | collective-permute-done | bytes 270368 | tf_op jit(solution)/shard_map/ppermute | solution.py:749
  484.4 6.8 %finish.3 = (f32[2,3,192,768]{3,2,1,0:T(8,128)}, f32[2,192,768]{2,1,0:T(8,128)}, f32[2,768,768]{2,1,0:T(8,128)}, f32[2,768,768]{2,1,0:T(8,128)}, f32[2,1024,256]...) custom-call(s32[6]{0:T(128)} %stack.156.refs_0_, ...), custom_call_target="tpu_custom_call", output_to_operand_aliasing={{0}: (17, {}), {1}: (18, {}), {2}: (19, {}), {3}: (20, {}),... | custom-call | tf_op jit(solution)/shard_map/finish/pallas_call | solution.py:89
  (472 shorter events, 138.7 us)
Async XLA Ops:
  7.2 173.5 %all-gather.5.cloned.1.call-start = ((), (), s32[]{:S(2)}) async-start(), calls=%async_computation.4 | async-start | bytes 14598144 | tf_op jit(solution)/shard_map/all_gather | solution.py:997
  10.3 17.0 %collective-permute-start.4 = (bf16[96,768]{1,0:T(8,128)(2,1)}, bf16[96,768]{1,0:T(8,128)(2,1)S(1)}, u32[]{:S(2)}, u32[]{:S(2)}) collective-permute-start(bf16[96,768]{1,0:T(8,128)(2,1)} %get-tuple-element.289), channel_id=1, source_target_pairs={{0,1},{1,0},{2,3},{3,2},{4,5},{5,4},{6,7},{7,6},{8,9},{9,8},{10,11... | collective-permute-start | bytes 442376 | tf_op jit(solution)/shard_map/ppermute | solution.py:749
  10.3 17.3 %collective-permute-start.5 = (bf16[96,768]{1,0:T(8,128)(2,1)}, bf16[96,768]{1,0:T(8,128)(2,1)S(1)}, u32[]{:S(2)}, u32[]{:S(2)}) collective-permute-start(bf16[96,768]{1,0:T(8,128)(2,1)} %get-tuple-element.289), channel_id=1, source_target_pairs={{0,2},{1,3},{2,0},{3,1},{4,6},{5,7},{6,4},{7,5},{8,10},{9,11},{10,... | collective-permute-start | bytes 442376 | tf_op jit(solution)/shard_map/ppermute | solution.py:749
  12.8 14.8 %collective-permute-start.6 = (bf16[96,768]{1,0:T(8,128)(2,1)}, bf16[96,768]{1,0:T(8,128)(2,1)S(1)}, u32[]{:S(2)}, u32[]{:S(2)}) collective-permute-start(bf16[96,768]{1,0:T(8,128)(2,1)} %get-tuple-element.289), channel_id=1, source_target_pairs={{0,3},{1,2},{2,1},{3,0},{4,7},{5,6},{6,5},{7,4},{8,11},{9,10},{10,... | collective-permute-start | bytes 442376 | tf_op jit(solution)/shard_map/ppermute | solution.py:749
  17.2 26.5 %collective-permute-start.1 = (bf16[192,768]{1,0:T(8,128)(2,1)}, bf16[192,768]{1,0:T(8,128)(2,1)S(1)}, u32[]{:S(2)}, u32[]{:S(2)}) collective-permute-start(bf16[192,768]{1,0:T(8,128)(2,1)} %get-tuple-element.288), channel_id=1, source_target_pairs={{0,1},{1,0},{2,3},{3,2},{4,5},{5,4},{6,7},{7,6},{8,9},{9,8},{10,11... | collective-permute-start | bytes 884744 | tf_op jit(solution)/shard_map/ppermute | solution.py:749
  18.3 25.8 %collective-permute-start.2 = (bf16[192,768]{1,0:T(8,128)(2,1)}, bf16[192,768]{1,0:T(8,128)(2,1)S(1)}, u32[]{:S(2)}, u32[]{:S(2)}) collective-permute-start(bf16[192,768]{1,0:T(8,128)(2,1)} %get-tuple-element.288), channel_id=1, source_target_pairs={{0,2},{1,3},{2,0},{3,1},{4,6},{5,7},{6,4},{7,5},{8,10},{9,11},{10,... | collective-permute-start | bytes 884744 | tf_op jit(solution)/shard_map/ppermute | solution.py:749
  27.3 23.7 %collective-permute-start.3 = (bf16[192,768]{1,0:T(8,128)(2,1)S(1)}, bf16[192,768]{1,0:T(8,128)(2,1)S(1)}, u32[]{:S(2)}, u32[]{:S(2)}) collective-permute-start(bf16[192,768]{1,0:T(8,128)(2,1)S(1)} %copy-done.37), channel_id=1, source_target_pairs={{0,3},{1,2},{2,1},{3,0},{4,7},{5,6},{6,5},{7,4},{8,11},{9,10},{10,... | collective-permute-start | bytes 884744 | tf_op jit(solution)/shard_map/ppermute | solution.py:749
  55.7 259.2 %reduce-scatter.3.cloned.1.call-start = ((), (), s32[]{:S(2)}) async-start(), calls=%async_computation.2 | async-start | bytes 10616832 | tf_op jit(solution)/shard_map/reduce_scatter | solution.py:863
  56.8 27.6 %collective-permute-start = (bf16[512,768]{1,0:T(8,128)(2,1)S(1)}, bf16[512,768]{1,0:T(8,128)(2,1)S(1)}, u32[]{:S(2)}, u32[]{:S(2)}) collective-permute-start(bf16[512,768]{1,0:T(8,128)(2,1)S(1)} %copy-done.24), channel_id=1, source_target_pairs={{0,1},{1,2},{2,3},{4,5},{5,6},{6,7},{8,9},{9,10},{10,11},{12,13},{... | collective-permute-start | bytes 2359304 | tf_op jit(solution)/shard_map/ppermute | solution.py:963
  60.3 25.0 %collective-permute-start.10 = (bf16[2,4,48,768]{3,2,1,0:T(8,128)(2,1)S(1)}, bf16[2,4,48,768]{3,2,1,0:T(8,128)(2,1)}, u32[]{:S(2)}, u32[]{:S(2)}) collective-permute-start(bf16[2,4,48,768]{3,2,1,0:T(8,128)(2,1)S(1)} %copy-done.26), channel_id=1, source_target_pairs={{0,8},{4,12},{8,0},{12,4},{16,24},{20,28},{24,16},{28,20},{1,9},{5... | collective-permute-start | bytes 1769480 | tf_op jit(solution)/shard_map/ppermute | solution.py:749
  61.6 23.7 %collective-permute-start.9 = (bf16[2,4,48,768]{3,2,1,0:T(8,128)(2,1)S(1)}, bf16[2,4,48,768]{3,2,1,0:T(8,128)(2,1)}, u32[]{:S(2)}, u32[]{:S(2)}) collective-permute-start(bf16[2,4,48,768]{3,2,1,0:T(8,128)(2,1)S(1)} %copy-done.28), channel_id=1, source_target_pairs={{0,16},{4,20},{8,24},{12,28},{16,0},{20,4},{24,8},{28,12},{1,17},{... | collective-permute-start | bytes 1769480 | tf_op jit(solution)/shard_map/ppermute | solution.py:749
  62.8 26.4 %collective-permute-start.11 = (bf16[4,96,768]{2,1,0:T(8,128)(2,1)}, bf16[4,96,768]{2,1,0:T(8,128)(2,1)S(1)}, u32[]{:S(2)}, u32[]{:S(2)}) collective-permute-start(bf16[4,96,768]{2,1,0:T(8,128)(2,1)} %get-tuple-element.314), channel_id=1, source_target_pairs={{0,8},{4,12},{8,0},{12,4},{16,24},{20,28},{24,16},{28,20},{1,9},{5... | collective-permute-start | bytes 1769480 | tf_op jit(solution)/shard_map/ppermute | solution.py:749
  63.1 27.0 %collective-permute-start.12 = (bf16[4,96,768]{2,1,0:T(8,128)(2,1)}, bf16[4,96,768]{2,1,0:T(8,128)(2,1)}, u32[]{:S(2)}, u32[]{:S(2)}) collective-permute-start(bf16[4,96,768]{2,1,0:T(8,128)(2,1)} %get-tuple-element.315), channel_id=1, source_target_pairs={{0,16},{4,20},{8,24},{12,28},{16,0},{20,4},{24,8},{28,12},{1,17},{... | collective-permute-start | bytes 1769480 | tf_op jit(solution)/shard_map/ppermute | solution.py:749
  101.1 27.8 %collective-permute-start.15 = (bf16[2,4,96,768]{3,2,1,0:T(8,128)(2,1)}, bf16[2,4,96,768]{3,2,1,0:T(8,128)(2,1)}, u32[]{:S(2)}, u32[]{:S(2)}) collective-permute-start(bf16[2,4,96,768]{3,2,1,0:T(8,128)(2,1)} %get-tuple-element.329), channel_id=1, source_target_pairs={{0,16},{4,20},{8,24},{12,28},{16,0},{20,4},{24,8},{28,12},{1,17},{... | collective-permute-start | bytes 3538952 | tf_op jit(solution)/shard_map/ppermute | solution.py:749
  102.3 32.0 %collective-permute-start.16 = (bf16[2,4,96,768]{3,2,1,0:T(8,128)(2,1)S(1)}, bf16[2,4,96,768]{3,2,1,0:T(8,128)(2,1)}, u32[]{:S(2)}, u32[]{:S(2)}) collective-permute-start(bf16[2,4,96,768]{3,2,1,0:T(8,128)(2,1)S(1)} %copy-done.20), channel_id=1, source_target_pairs={{0,8},{4,12},{8,0},{12,4},{16,24},{20,28},{24,16},{28,20},{1,9},{5... | collective-permute-start | bytes 3538952 | tf_op jit(solution)/shard_map/ppermute | solution.py:749
  140.3 9.3 %collective-permute-start.17 = (bf16[2,2,4,96,768]{4,3,2,1,0:T(8,128)(2,1)}, bf16[2,2,4,96,768]{4,3,2,1,0:T(8,128)(2,1)S(1)}, u32[]{:S(2)}, u32[]{:S(2)}) collective-permute-start(bf16[2,2,4,96,768]{4,3,2,1,0:T(8,128)(2,1)} %get-tuple-element.335), channel_id=1, source_target_pairs={{0,4},{4,0},{8,12},{12,8},{16,20},{20,16},{24,28},{28,24},{1,5},{5... | collective-permute-start | bytes 7077896 | tf_op jit(solution)/shard_map/ppermute | solution.py:749
  141.9 8.0 %collective-permute-start.18 = (bf16[2,2,4,96,768]{4,3,2,1,0:T(8,128)(2,1)}, bf16[2,2,4,96,768]{4,3,2,1,0:T(8,128)(2,1)}, u32[]{:S(2)}, u32[]{:S(2)}) collective-permute-start(bf16[2,2,4,96,768]{4,3,2,1,0:T(8,128)(2,1)} %get-tuple-element.336), channel_id=1, source_target_pairs={{0,4},{4,0},{8,12},{12,8},{16,20},{20,16},{24,28},{28,24},{1,5},{5... | collective-permute-start | bytes 7077896 | tf_op jit(solution)/shard_map/ppermute | solution.py:749
  160.2 27.8 %collective-permute-start.19 = (bf16[512,768]{1,0:T(8,128)(2,1)}, bf16[512,768]{1,0:T(8,128)(2,1)S(1)}, u32[]{:S(2)}, u32[]{:S(2)}) collective-permute-start(bf16[512,768]{1,0:T(8,128)(2,1)} %get-tuple-element.346.refs_2_.refs_5_), channel_id=1, source_target_pairs={{0,1},{1,2},{2,3},{4,5},{5,6},{6,7},{8,9},{9,10},{10,11},{12,13},{... | collective-permute-start | bytes 2359304 | tf_op jit(solution)/shard_map/ppermute | solution.py:963
  226.8 178.3 %reduce-scatter.5.cloned.1.call-start = ((), (), s32[]{:S(2)}) async-start(), calls=%async_computation.3 | async-start | bytes 10616832 | tf_op jit(solution)/shard_map/reduce_scatter | solution.py:863
  244.5 20.6 %collective-permute-start.20 = (bf16[512,768]{1,0:T(8,128)(2,1)}, bf16[512,768]{1,0:T(8,128)(2,1)}, u32[]{:S(2)}, u32[]{:S(2)}) collective-permute-start(bf16[512,768]{1,0:T(8,128)(2,1)} %get-tuple-element.372), channel_id=1, source_target_pairs={{1,0},{2,1},{3,2},{5,4},{6,5},{7,6},{9,8},{10,9},{11,10},{13,12},{... | collective-permute-start | bytes 2359304 | tf_op jit(solution)/shard_map/ppermute | solution.py:966
  277.5 22.2 %collective-permute-start.23 = (bf16[2,208,768]{2,1,0:T(8,128)(2,1)}, bf16[2,208,768]{2,1,0:T(8,128)(2,1)S(1)}, u32[]{:S(2)}, u32[]{:S(2)}) collective-permute-start(bf16[2,208,768]{2,1,0:T(8,128)(2,1)} %get-tuple-element.409), channel_id=1, source_target_pairs={{0,16},{4,20},{8,24},{12,28},{16,0},{20,4},{24,8},{28,12},{1,17},{... | collective-permute-start | bytes 1916936 | tf_op jit(solution)/shard_map/ppermute | solution.py:749
  278.7 21.0 %collective-permute-start.24 = (bf16[2,192,768]{2,1,0:T(8,128)(2,1)}, bf16[2,192,768]{2,1,0:T(8,128)(2,1)S(1)}, u32[]{:S(2)}, u32[]{:S(2)}) collective-permute-start(bf16[2,192,768]{2,1,0:T(8,128)(2,1)} %get-tuple-element.410), channel_id=1, source_target_pairs={{0,8},{4,12},{8,0},{12,4},{16,24},{20,28},{24,16},{28,20},{1,9},{5... | collective-permute-start | bytes 1769480 | tf_op jit(solution)/shard_map/ppermute | solution.py:749
  300.7 148.2 %all-gather.7.cloned.1.call-start = ((), (), s32[]{:S(2)}) async-start(), calls=%async_computation.5 | async-start | bytes 4866048 | tf_op jit(solution)/shard_map/all_gather | solution.py:1074
  305.4 8.6 %collective-permute-start.25 = (bf16[208,768]{1,0:T(8,128)(2,1)}, bf16[208,768]{1,0:T(8,128)(2,1)S(1)}, u32[]{:S(2)}, u32[]{:S(2)}) collective-permute-start(bf16[208,768]{1,0:T(8,128)(2,1)} %get-tuple-element.417), channel_id=1, source_target_pairs={{0,8},{4,12},{8,0},{12,4},{16,24},{20,28},{24,16},{28,20},{1,9},{5... | collective-permute-start | bytes 958472 | tf_op jit(solution)/shard_map/ppermute | solution.py:749
  317.3 27.4 %collective-permute-start.27 = (bf16[192,768]{1,0:T(8,128)(2,1)}, bf16[192,768]{1,0:T(8,128)(2,1)S(1)}, u32[]{:S(2)}, u32[]{:S(2)}) collective-permute-start(bf16[192,768]{1,0:T(8,128)(2,1)} %get-tuple-element.435), channel_id=1, source_target_pairs={{0,1},{1,0},{2,3},{3,2},{4,5},{5,4},{6,7},{7,6},{8,9},{9,8},{10,11... | collective-permute-start | bytes 884744 | tf_op jit(solution)/shard_map/ppermute | solution.py:749
  317.3 27.4 %collective-permute-start.28 = (bf16[192,768]{1,0:T(8,128)(2,1)}, bf16[192,768]{1,0:T(8,128)(2,1)S(1)}, u32[]{:S(2)}, u32[]{:S(2)}) collective-permute-start(bf16[192,768]{1,0:T(8,128)(2,1)} %get-tuple-element.436), channel_id=1, source_target_pairs={{0,2},{1,3},{2,0},{3,1},{4,6},{5,7},{6,4},{7,5},{8,10},{9,11},{10,... | collective-permute-start | bytes 884744 | tf_op jit(solution)/shard_map/ppermute | solution.py:749
  319.9 24.8 %collective-permute-start.29 = (bf16[192,768]{1,0:T(8,128)(2,1)}, bf16[192,768]{1,0:T(8,128)(2,1)}, u32[]{:S(2)}, u32[]{:S(2)}) collective-permute-start(bf16[192,768]{1,0:T(8,128)(2,1)} %get-tuple-element.437), channel_id=1, source_target_pairs={{0,3},{1,2},{2,1},{3,0},{4,7},{5,6},{6,5},{7,4},{8,11},{9,10},{10,... | collective-permute-start | bytes 884744 | tf_op jit(solution)/shard_map/ppermute | solution.py:749
  345.5 9.6 %collective-permute-start.30 = (bf16[4,208,768]{2,1,0:T(8,128)(2,1)}, bf16[4,208,768]{2,1,0:T(8,128)(2,1)S(1)}, u32[]{:S(2)}, u32[]{:S(2)}) collective-permute-start(bf16[4,208,768]{2,1,0:T(8,128)(2,1)} %get-tuple-element.440), channel_id=1, source_target_pairs={{0,4},{4,0},{8,12},{12,8},{16,20},{20,16},{24,28},{28,24},{1,5},{5... | collective-permute-start | bytes 3833864 | tf_op jit(solution)/shard_map/ppermute | solution.py:749
  352.8 9.6 %collective-permute-start.33 = (bf16[112,768]{1,0:T(8,128)(2,1)}, bf16[112,768]{1,0:T(8,128)(2,1)S(1)}, u32[]{:S(2)}, u32[]{:S(2)}) collective-permute-start(bf16[112,768]{1,0:T(8,128)(2,1)} %get-tuple-element.450), channel_id=1, source_target_pairs={{0,2},{1,3},{2,0},{3,1},{4,6},{5,7},{6,4},{7,5},{8,10},{9,11},{10,... | collective-permute-start | bytes 516104 | tf_op jit(solution)/shard_map/ppermute | solution.py:749
  354.9 14.9 %collective-permute-start.34 = (bf16[112,768]{1,0:T(8,128)(2,1)}, bf16[112,768]{1,0:T(8,128)(2,1)S(1)}, u32[]{:S(2)}, u32[]{:S(2)}) collective-permute-start(bf16[112,768]{1,0:T(8,128)(2,1)} %get-tuple-element.451), channel_id=1, source_target_pairs={{0,3},{1,2},{2,1},{3,0},{4,7},{5,6},{6,5},{7,4},{8,11},{9,10},{10,... | collective-permute-start | bytes 516104 | tf_op jit(solution)/shard_map/ppermute | solution.py:749
  379.8 19.7 %collective-permute-start.36 = (bf16[2,208,768]{2,1,0:T(8,128)(2,1)}, bf16[2,208,768]{2,1,0:T(8,128)(2,1)S(1)}, u32[]{:S(2)}, u32[]{:S(2)}) collective-permute-start(bf16[2,208,768]{2,1,0:T(8,128)(2,1)} %get-tuple-element.456), channel_id=1, source_target_pairs={{0,16},{4,20},{8,24},{12,28},{16,0},{20,4},{24,8},{28,12},{1,17},{... | collective-permute-start | bytes 1916936 | tf_op jit(solution)/shard_map/ppermute | solution.py:749
  380.6 17.8 %collective-permute-start.37 = (bf16[2,192,768]{2,1,0:T(8,128)(2,1)}, bf16[2,192,768]{2,1,0:T(8,128)(2,1)S(1)}, u32[]{:S(2)}, u32[]{:S(2)}) collective-permute-start(bf16[2,192,768]{2,1,0:T(8,128)(2,1)} %get-tuple-element.457), channel_id=1, source_target_pairs={{0,8},{4,12},{8,0},{12,4},{16,24},{20,28},{24,16},{28,20},{1,9},{5... | collective-permute-start | bytes 1769480 | tf_op jit(solution)/shard_map/ppermute | solution.py:749
  380.8 23.4 %collective-permute-start.35 = (bf16[512,768]{1,0:T(8,128)(2,1)S(1)}, bf16[512,768]{1,0:T(8,128)(2,1)S(1)}, u32[]{:S(2)}, u32[]{:S(2)}) collective-permute-start(bf16[512,768]{1,0:T(8,128)(2,1)S(1)} %copy-done.13), channel_id=1, source_target_pairs={{1,0},{2,1},{3,2},{5,4},{6,5},{7,6},{9,8},{10,9},{11,10},{13,12},{... | collective-permute-start | bytes 2359304 | tf_op jit(solution)/shard_map/ppermute | solution.py:966
  405.1 15.0 %collective-permute-start.38 = (bf16[208,768]{1,0:T(8,128)(2,1)}, bf16[208,768]{1,0:T(8,128)(2,1)S(1)}, u32[]{:S(2)}, u32[]{:S(2)}) collective-permute-start(bf16[208,768]{1,0:T(8,128)(2,1)} %get-tuple-element.479), channel_id=1, source_target_pairs={{0,8},{4,12},{8,0},{12,4},{16,24},{20,28},{24,16},{28,20},{1,9},{5... | collective-permute-start | bytes 958472 | tf_op jit(solution)/shard_map/ppermute | solution.py:749
  406.3 13.3 %collective-permute-start.39 = (bf16[192,768]{1,0:T(8,128)(2,1)}, bf16[192,768]{1,0:T(8,128)(2,1)S(1)}, u32[]{:S(2)}, u32[]{:S(2)}) collective-permute-start(bf16[192,768]{1,0:T(8,128)(2,1)} %get-tuple-element.480), channel_id=1, source_target_pairs={{0,16},{4,20},{8,24},{12,28},{16,0},{20,4},{24,8},{28,12},{1,17},{... | collective-permute-start | bytes 884744 | tf_op jit(solution)/shard_map/ppermute | solution.py:749
  409.0 13.1 %collective-permute-start.40 = (bf16[192,768]{1,0:T(8,128)(2,1)}, bf16[192,768]{1,0:T(8,128)(2,1)S(1)}, u32[]{:S(2)}, u32[]{:S(2)}) collective-permute-start(bf16[192,768]{1,0:T(8,128)(2,1)} %get-tuple-element.492), channel_id=1, source_target_pairs={{0,1},{1,0},{2,3},{3,2},{4,5},{5,4},{6,7},{7,6},{8,9},{9,8},{10,11... | collective-permute-start | bytes 884744 | tf_op jit(solution)/shard_map/ppermute | solution.py:749
  409.0 14.5 %collective-permute-start.41 = (bf16[192,768]{1,0:T(8,128)(2,1)}, bf16[192,768]{1,0:T(8,128)(2,1)S(1)}, u32[]{:S(2)}, u32[]{:S(2)}) collective-permute-start(bf16[192,768]{1,0:T(8,128)(2,1)} %get-tuple-element.493), channel_id=1, source_target_pairs={{0,2},{1,3},{2,0},{3,1},{4,6},{5,7},{6,4},{7,5},{8,10},{9,11},{10,... | collective-permute-start | bytes 884744 | tf_op jit(solution)/shard_map/ppermute | solution.py:749
  411.5 24.5 %collective-permute-start.42 = (bf16[192,768]{1,0:T(8,128)(2,1)}, bf16[192,768]{1,0:T(8,128)(2,1)}, u32[]{:S(2)}, u32[]{:S(2)}) collective-permute-start(bf16[192,768]{1,0:T(8,128)(2,1)} %get-tuple-element.494), channel_id=1, source_target_pairs={{0,3},{1,2},{2,1},{3,0},{4,7},{5,6},{6,5},{7,4},{8,11},{9,10},{10,... | collective-permute-start | bytes 884744 | tf_op jit(solution)/shard_map/ppermute | solution.py:749
  438.2 9.2 %collective-permute-start.43 = (bf16[128,768]{1,0:T(8,128)(2,1)}, bf16[128,768]{1,0:T(8,128)(2,1)S(1)}, u32[]{:S(2)}, u32[]{:S(2)}) collective-permute-start(bf16[128,768]{1,0:T(8,128)(2,1)} %get-tuple-element.498), channel_id=1, source_target_pairs={{0,1},{1,0},{2,3},{3,2},{4,5},{5,4},{6,7},{7,6},{8,9},{9,8},{10,11... | collective-permute-start | bytes 589832 | tf_op jit(solution)/shard_map/ppermute | solution.py:749
  438.2 10.6 %collective-permute-start.44 = (bf16[128,768]{1,0:T(8,128)(2,1)}, bf16[128,768]{1,0:T(8,128)(2,1)S(1)}, u32[]{:S(2)}, u32[]{:S(2)}) collective-permute-start(bf16[128,768]{1,0:T(8,128)(2,1)} %get-tuple-element.499), channel_id=1, source_target_pairs={{0,2},{1,3},{2,0},{3,1},{4,6},{5,7},{6,4},{7,5},{8,10},{9,11},{10,... | collective-permute-start | bytes 589832 | tf_op jit(solution)/shard_map/ppermute | solution.py:749
  442.7 17.1 %collective-permute-start.46 = (bf16[192,768]{1,0:T(8,128)(2,1)}, bf16[192,768]{1,0:T(8,128)(2,1)S(1)}, u32[]{:S(2)}, u32[]{:S(2)}) collective-permute-start(bf16[192,768]{1,0:T(8,128)(2,1)} %get-tuple-element.514.refs_9_), channel_id=1, source_target_pairs={{0,4},{4,0},{8,12},{12,8},{16,20},{20,16},{24,28},{28,24},{1,5},{5... | collective-permute-start | bytes 884744 | tf_op jit(solution)/shard_map/ppermute | solution.py:749
  446.1 13.7 %collective-permute-start.47 = (bf16[192,768]{1,0:T(8,128)(2,1)}, bf16[192,768]{1,0:T(8,128)(2,1)S(1)}, u32[]{:S(2)}, u32[]{:S(2)}) collective-permute-start(bf16[192,768]{1,0:T(8,128)(2,1)} %get-tuple-element.514.refs_9_), channel_id=1, source_target_pairs={{0,8},{4,12},{8,0},{12,4},{16,24},{20,28},{24,16},{28,20},{1,9},{5... | collective-permute-start | bytes 884744 | tf_op jit(solution)/shard_map/ppermute | solution.py:749
  446.9 13.0 %collective-permute-start.48 = (bf16[192,768]{1,0:T(8,128)(2,1)}, bf16[192,768]{1,0:T(8,128)(2,1)S(1)}, u32[]{:S(2)}, u32[]{:S(2)}) collective-permute-start(bf16[192,768]{1,0:T(8,128)(2,1)} %get-tuple-element.514.refs_9_), channel_id=1, source_target_pairs={{0,16},{4,20},{8,24},{12,28},{16,0},{20,4},{24,8},{28,12},{1,17},{... | collective-permute-start | bytes 884744 | tf_op jit(solution)/shard_map/ppermute | solution.py:749
  447.4 14.6 %collective-permute-start.49 = (bf16[192,768]{1,0:T(8,128)(2,1)}, bf16[192,768]{1,0:T(8,128)(2,1)S(1)}, u32[]{:S(2)}, u32[]{:S(2)}) collective-permute-start(bf16[192,768]{1,0:T(8,128)(2,1)} %get-tuple-element.514.refs_9_), channel_id=1, source_target_pairs={{0,24},{4,28},{8,16},{12,20},{16,8},{20,12},{24,0},{28,4},{1,25},{... | collective-permute-start | bytes 884744 | tf_op jit(solution)/shard_map/ppermute | solution.py:749
  448.8 10.3 %collective-permute-start.45 = (bf16[128,768]{1,0:T(8,128)(2,1)S(1)}, bf16[128,768]{1,0:T(8,128)(2,1)S(1)}, u32[]{:S(2)}, u32[]{:S(2)}) collective-permute-start(bf16[128,768]{1,0:T(8,128)(2,1)S(1)} %copy-done.97), channel_id=1, source_target_pairs={{0,3},{1,2},{2,1},{3,0},{4,7},{5,6},{6,5},{7,4},{8,11},{9,10},{10,... | collective-permute-start | bytes 589832 | tf_op jit(solution)/shard_map/ppermute | solution.py:749
  465.0 7.8 %collective-permute-start.51 = (bf16[176,768]{1,0:T(8,128)(2,1)}, bf16[176,768]{1,0:T(8,128)(2,1)S(1)}, u32[]{:S(2)}, u32[]{:S(2)}) collective-permute-start(bf16[176,768]{1,0:T(8,128)(2,1)} %get-tuple-element.521.refs_1_), channel_id=1, source_target_pairs={{0,8},{4,12},{8,0},{12,4},{16,24},{20,28},{24,16},{28,20},{1,9},{5... | collective-permute-start | bytes 811016 | tf_op jit(solution)/shard_map/ppermute | solution.py:749
  465.8 7.6 %collective-permute-start.52 = (bf16[176,768]{1,0:T(8,128)(2,1)}, bf16[176,768]{1,0:T(8,128)(2,1)S(1)}, u32[]{:S(2)}, u32[]{:S(2)}) collective-permute-start(bf16[176,768]{1,0:T(8,128)(2,1)} %get-tuple-element.521.refs_1_), channel_id=1, source_target_pairs={{0,16},{4,20},{8,24},{12,28},{16,0},{20,4},{24,8},{28,12},{1,17},{... | collective-permute-start | bytes 811016 | tf_op jit(solution)/shard_map/ppermute | solution.py:749
  466.9 12.1 %collective-permute-start.53 = (bf16[176,768]{1,0:T(8,128)(2,1)}, bf16[176,768]{1,0:T(8,128)(2,1)S(1)}, u32[]{:S(2)}, u32[]{:S(2)}) collective-permute-start(bf16[176,768]{1,0:T(8,128)(2,1)} %get-tuple-element.521.refs_1_), channel_id=1, source_target_pairs={{0,24},{4,28},{8,16},{12,20},{16,8},{20,12},{24,0},{28,4},{1,25},{... | collective-permute-start | bytes 811016 | tf_op jit(solution)/shard_map/ppermute | solution.py:749
  (133 other events, 461.6 us)
Sparse Core Ops, SparseCore 0:
  55.8 124.8 all-gather.4
  226.9 81.4 reduce-scatter.2
  311.9 78.8 reduce-scatter.4
  392.6 47.5 all-gather.6

commit v10 on v9

--- a/solution.py
+++ b/solution.py
@@ -222,7 +222,7 @@
                 num = dot_nn(mix[s, :, :window], carried[0][here]) + dot_nn(mix[s, :, window:], carried[1][here])
                 den = dot_nn(mix[s, :, :window], wsum[0][here]) + dot_nn(mix[s, :, window:], wsum[1][here])
                 rden = 1.0 / den
-                ratio = num * rden
+                ratio = num / den
                 rden_ref[here] = rden.astype(BF)
                 ratio_ref[here] = ratio.astype(BF)
                 mixed.append((sg[here] * ratio).astype(BF))

time: 505 us -> 505 us (level)
  no operation moved by 1% of the time
where the time goes in v10:
time: 505 us; the launch traced here: 499 us
  Pallas kernels  160 us (32%)
  waiting for transfers between devices  155 us (31%)
  starting transfers between devices  63.3 us (13%)
  other arithmetic  50.5 us (10%)
  local copies, waits for them, and re-layouts  48.2 us (10%)
  between operations  15.1 us (3%)
  matrix products  6.88 us (1%)
    pallas_call x15, Pallas kernels, run(): *results, order.token = kernel(*placed, order.token)  160 us
    ppermute x56, waiting for transfers between devices, swap(): return lax.ppermute(value, axis, [(i, i ^ bit) for i in range(size)])  102 us
    ppermute x56, starting transfers between devices, swap(): return lax.ppermute(value, axis, [(i, i ^ bit) for i in range(size)])  52.3 us
    unnamed x240, local copies, waits for them, and re-layouts  32.8 us
    ppermute x2, waiting for transfers between devices, forward_halo(): return lax.ppermute(value, 'mp', [(i, i + 1) for i in range(mp - 1)])  28.4 us
    all_gather x1, waiting for transfers between devices, shards(): later = lax.all_gather(later, ('g', 'c', 'mp'), axis=0, tiled=False)  17.2 us
    another operation x8, other arithmetic, wait(): self.values[k] = jnp.stack([self.values[k], coming[k]], axis=place)  16.4 us
    convert_element_type x8, other arithmetic, start(): sum((lax.index_in_dim(term, 1, place, keepdims=False).astype(F32) for ter...  16.2 us
  transfers between devices with their start and end apart: 64, of which 32 were waited for; matrix products, arithmetic and copies ran while one was open for 13% of the time, Pallas kernels for 23%

profile of v10, /device:TPU:9, one launch (start us, length us, event | category | flops | bytes accessed | tf_op | source)
XLA Modules:
  0.0 499.4 jit_solution(14036493350298730518)
XLA Ops:
  10.3 2.5 collective-permute-start.5
  24.6 2.7 enter.1
  35.9 3.4 collective-permute-done.7.refs_0_
  44.1 7.0 %collective-permute-done.3.refs_2_ = bf16[192,768]{1,0:T(8,128)(2,1)S(1)} collective-permute-done((bf16[192,768]{1,0:T(8,128)(2,1)S(1)}, bf16[192,768]{1,0:T(8,128)(2,1)S(1)}, u32[]{:S(2)}, u32[]{:S(2)}) %collective-permute-start.3) | collective-permute-done | bytes 294944 | tf_op jit(solution)/shard_map/ppermute | solution.py:749
  56.8 3.5 collective-permute-start
  63.3 21.1 %collective-permute-done.refs_0_ = bf16[512,768]{1,0:T(8,128)(2,1)S(1)} collective-permute-done((bf16[512,768]{1,0:T(8,128)(2,1)S(1)}, bf16[512,768]{1,0:T(8,128)(2,1)S(1)}, u32[]{:S(2)}, u32[]{:S(2)}) %collective-permute-start) | collective-permute-done | bytes 786464 | tf_op jit(solution)/shard_map/ppermute | solution.py:963
  85.3 3.9 collective-permute-done.11.refs_0_
  90.1 2.3 pad_maximum_fusion.5.refs_1_
  95.7 2.2 pad_maximum_fusion.2.refs_0_
  97.9 3.1 collective-permute-start.13
  106.5 13.9 %attn_fwd.2 = (bf16[512,768]{1,0:T(8,128)(2,1)}, bf16[512,768]{1,0:T(8,128)(2,1)}, bf16[512,768]{1,0:T(8,128)(2,1)}, bf16[1024,768]{1,0:T(8,128)(2,1)}, bf16[102...) custom-call(s32[6]{0:T(128)} %stack.156.refs_0_, ...), custom_call_target="tpu_custom_call", output_to_operand_aliasing={{10}: (13, {})} | custom-call | tf_op jit(solution)/shard_map/attn_fwd/pallas_call | solution.py:89
  120.4 8.5 %collective-permute-done.15.refs_0_ = bf16[2,4,96,768]{3,2,1,0:T(8,128)(2,1)} collective-permute-done((bf16[2,4,96,768]{3,2,1,0:T(8,128)(2,1)}, bf16[2,4,96,768]{3,2,1,0:T(8,128)(2,1)}, u32[]{:S(2)}, u32[]{:S(2)}) %collective-permute-start.15) | collective-permute-done | bytes 1179680 | tf_op jit(solution)/shard_map/ppermute | solution.py:749
  128.9 5.5 %collective-permute-done.16.refs_1_ = bf16[2,4,96,768]{3,2,1,0:T(8,128)(2,1)} collective-permute-done((bf16[2,4,96,768]{3,2,1,0:T(8,128)(2,1)S(1)}, bf16[2,4,96,768]{3,2,1,0:T(8,128)(2,1)}, u32[]{:S(2)}, u32[]{:S(2)}) %collective-permute-start.16) | collective-permute-done | bytes 1179680 | tf_op jit(solution)/shard_map/ppermute | solution.py:749
  134.4 3.0 pad_maximum_fusion.1.refs_1_
  137.4 2.9 pad_maximum_fusion.refs_0_
  141.9 7.7 %ff_fwd.2 = (bf16[512,1536]{1,0:T(8,128)(2,1)}, bf16[512,1536]{1,0:T(8,128)(2,1)}, f32[512,768]{1,0:T(8,128)}, s32[8,128]{1,0:T(8,128)}) custom-call(f32[512,768]{1,0:T(8,128)} %get-tuple-element.327.refs_0_.refs_1_, bf16[512,768]{1,0:T(8,128)(2,1)} %get-tuple-element.328.refs_1_.refs_2_, ...), custom_call_target="tpu_custom_call", output_to_operand_aliasing={{3}: (4, {})} | custom-call | tf_op jit(solution)/shard_map/ff_fwd/pallas_call | solution.py:89
  151.0 9.1 %ff_fwd.3 = (bf16[512,1536]{1,0:T(8,128)(2,1)}, bf16[512,1536]{1,0:T(8,128)(2,1)}, f32[512,768]{1,0:T(8,128)}, bf16[512,768]{1,0:T(8,128)(2,1)}, s32[8,128]{1,0:T(8,128)}) custom-call(f32[512,768]{1,0:T(8,128)} %get-tuple-element.338.refs_0_, bf16[512,768]{1,0:T(8,128)(2,1)} %get-tuple-element.328.refs_1_.refs_2_, ...), custom_call_target="tpu_custom_call", output_to_operand_aliasing={{4}: (6, {})} | custom-call | tf_op jit(solution)/shard_map/ff_fwd/pallas_call | solution.py:89
  160.2 3.3 collective-permute-start.19
  163.5 17.2 %all-gather.5.cloned.1.call-done = bf16[9216,768]{1,0:T(8,128)(2,1)} async-done(((bf16[288,768]{1,0:T(8,128)(2,1)}), bf16[9216,768]{1,0:T(8,128)(2,1)}) %all-gather.5.cloned.1.call-update) | async-done | bytes 14155792 | tf_op jit(solution)/shard_map/all_gather | solution.py:997
  180.7 7.3 %collective-permute-done.19.refs_0_ = bf16[512,768]{1,0:T(8,128)(2,1)S(1)} collective-permute-done((bf16[512,768]{1,0:T(8,128)(2,1)}, bf16[512,768]{1,0:T(8,128)(2,1)S(1)}, u32[]{:S(2)}, u32[]{:S(2)}) %collective-permute-start.19) | collective-permute-done | bytes 786464 | tf_op jit(solution)/shard_map/ppermute | solution.py:963
  188.9 13.6 %attn_fwd.3 = (bf16[512,768]{1,0:T(8,128)(2,1)}, bf16[512,768]{1,0:T(8,128)(2,1)}, bf16[512,768]{1,0:T(8,128)(2,1)}, bf16[1024,768]{1,0:T(8,128)(2,1)}, bf16[102...) custom-call(s32[6]{0:T(128)} %stack.156.refs_0_, ...), custom_call_target="tpu_custom_call", output_to_operand_aliasing={{10}: (10, {})} | custom-call | tf_op jit(solution)/shard_map/attn_fwd/pallas_call | solution.py:89
  202.5 24.2 %ff_bwd.2 = (bf16[4,2,2,384,768]{4,3,2,1,0:T(8,128)(2,1)}, f32[512,768]{1,0:T(8,128)}, bf16[512,768]{1,0:T(8,128)(2,1)}, f32[1,768]{1,0:T(1,128)}, f32[1,768]{1,...) custom-call(s32[6]{0:T(128)} %stack.156.refs_0_, ...), custom_call_target="tpu_custom_call", output_to_operand_aliasing={{6}: (7, {})} | custom-call | tf_op jit(solution)/shard_map/ff_bwd/pallas_call | solution.py:89
  227.9 12.8 %attn_bwd.2 = (bf16[512,768]{1,0:T(8,128)(2,1)S(1)}, bf16[1024,768]{1,0:T(8,128)(2,1)S(1)}, bf16[1024,768]{1,0:T(8,128)(2,1)S(1)}, f32[256,256]{1,0:T(8,128)S(1)...) custom-call(s32[6]{0:T(128)S(1)} %copy-done.15, ...), custom_call_target="tpu_custom_call", output_to_operand_aliasing={{6}: (10, {})} | custom-call | tf_op jit(solution)/shard_map/attn_bwd/pallas_call | solution.py:89
  248.5 8.7 %attn_wgrad.2 = (bf16[4,208,768]{2,1,0:T(8,128)(2,1)}, bf16[4,192,768]{2,1,0:T(8,128)(2,1)}, bf16[4,208,768]{2,1,0:T(8,128)(2,1)}, bf16[4,192,768]{2,1,0:T(8,128)(2,1)}, s32[8,128]{1,0:T(8,128)S(1)}) custom-call(s32[6]{0:T(128)S(1)} %copy-done.15, bf16[512,768]{1,0:T(8,128)(2,1)S(1)} %get-tuple-element.373.refs_1_, ...), custom_call_target="tpu_custom_call", output_to_operand_aliasing={{4}: (9, {})} | custom-call | tf_op jit(solution)/shard_map/attn_wgrad/pallas_call | solution.py:89
  257.9 7.2 %collective-permute-done.20.refs_0_ = bf16[512,768]{1,0:T(8,128)(2,1)} collective-permute-done((bf16[512,768]{1,0:T(8,128)(2,1)}, bf16[512,768]{1,0:T(8,128)(2,1)}, u32[]{:S(2)}, u32[]{:S(2)}) %collective-permute-start.20) | collective-permute-done | bytes 786464 | tf_op jit(solution)/shard_map/ppermute | solution.py:966
  266.7 4.9 leave.2
  273.1 2.3 fusion.26.refs_1_
  278.9 20.7 %ff_bwd.3 = (bf16[4,2,2,384,768]{4,3,2,1,0:T(8,128)(2,1)}, f32[512,768]{1,0:T(8,128)}, bf16[512,768]{1,0:T(8,128)(2,1)}, f32[1,768]{1,0:T(1,128)}, f32[1,768]{1,0:T(1,128)}, /*index=5*/s32[8,128]{1,0:T(8,128)}) custom-call(s32[6]{0:T(128)} %stack.156.refs_0_, f32[512,768]{1,0:T(8,128)} %get-tuple-element.327.refs_0_.refs_1_, ...), custom_call_target="tpu_custom_call", output_to_operand_aliasing={{5}: (13, {})} | custom-call | tf_op jit(solution)/shard_map/ff_bwd/pallas_call | solution.py:89
  307.0 7.0 %collective-permute-done.26.refs_1_ = bf16[192,768]{1,0:T(8,128)(2,1)S(1)} collective-permute-done((bf16[192,768]{1,0:T(8,128)(2,1)}, bf16[192,768]{1,0:T(8,128)(2,1)S(1)}, u32[]{:S(2)}, u32[]{:S(2)}) %collective-permute-start.26) | collective-permute-done | bytes 294944 | tf_op jit(solution)/shard_map/ppermute | solution.py:749
  317.3 2.6 collective-permute-start.28
  320.7 14.5 %attn_bwd.3 = (bf16[512,768]{1,0:T(8,128)(2,1)S(1)}, bf16[1024,768]{1,0:T(8,128)(2,1)S(1)}, bf16[1024,768]{1,0:T(8,128)(2,1)S(1)}, f32[256,256]{1,0:T(8,128)S(1)...) custom-call(s32[6]{0:T(128)S(1)} %copy-done.16, ...), custom_call_target="tpu_custom_call", output_to_operand_aliasing={{6}: (13, {})} | custom-call | tf_op jit(solution)/shard_map/attn_bwd/pallas_call | solution.py:89
  335.3 8.8 %attn_wgrad.3 = (bf16[4,208,768]{2,1,0:T(8,128)(2,1)}, bf16[4,192,768]{2,1,0:T(8,128)(2,1)}, bf16[4,208,768]{2,1,0:T(8,128)(2,1)}, bf16[4,192,768]{2,1,0:T(8,128)(2,1)}, s32[8,128]{1,0:T(8,128)S(1)}) custom-call(s32[6]{0:T(128)S(1)} %copy-done.16, bf16[512,768]{1,0:T(8,128)(2,1)S(1)} %get-tuple-element.426.refs_1_, ...), custom_call_target="tpu_custom_call", output_to_operand_aliasing={{4}: (9, {})} | custom-call | tf_op jit(solution)/shard_map/attn_wgrad/pallas_call | solution.py:89
  345.5 3.5 collective-permute-start.30
  357.9 4.6 collective-permute-done.33.refs_1_
  362.5 7.3 %collective-permute-done.34.refs_2_ = bf16[112,768]{1,0:T(8,128)(2,1)S(1)} collective-permute-done((bf16[112,768]{1,0:T(8,128)(2,1)}, bf16[112,768]{1,0:T(8,128)(2,1)S(1)}, u32[]{:S(2)}, u32[]{:S(2)}) %collective-permute-start.34) | collective-permute-done | bytes 172064 | tf_op jit(solution)/shard_map/ppermute | solution.py:749
  370.5 2.2 fusion.27.refs_1_
  382.7 15.8 %collective-permute-done.37.refs_1_ = bf16[2,192,768]{2,1,0:T(8,128)(2,1)S(1)} collective-permute-done((bf16[2,192,768]{2,1,0:T(8,128)(2,1)}, bf16[2,192,768]{2,1,0:T(8,128)(2,1)S(1)}, u32[]{:S(2)}, u32[]{:S(2)}) %collective-permute-start.37) | collective-permute-done | bytes 589856 | tf_op jit(solution)/shard_map/ppermute | solution.py:749
  409.0 2.5 collective-permute-start.41
  411.7 4.9 leave.3
  417.4 2.3 collective-permute-done.39.refs_1_
  423.5 12.5 %collective-permute-done.42.refs_2_ = bf16[192,768]{1,0:T(8,128)(2,1)} collective-permute-done((bf16[192,768]{1,0:T(8,128)(2,1)}, bf16[192,768]{1,0:T(8,128)(2,1)}, u32[]{:S(2)}, u32[]{:S(2)}) %collective-permute-start.42) | collective-permute-done | bytes 294944 | tf_op jit(solution)/shard_map/ppermute | solution.py:749
  438.2 2.7 collective-permute-start.44
  442.7 3.4 collective-permute-start.46
  449.5 6.5 %finish.2 = (f32[2,3,192,768]{3,2,1,0:T(8,128)}, f32[2,192,768]{2,1,0:T(8,128)}, f32[2,768,768]{2,1,0:T(8,128)}, f32[2,768,768]{2,1,0:T(8,128)}, f32[2,1024,256]{2,1,0:T(8,128)}, /*index=5*/s32[8,128]{1,0:T(8,128)}) custom-call(s32[6]{0:T(128)} %stack.156.refs_0_, bf16[8,352,768]{2,1,0:T(8,128)(2,1)} %get-tuple-element.508.refs_1_, ...), custom_call_target="tpu_custom_call", output_to_operand_aliasing={{5}: (2, {})} | custom-call | tf_op jit(solution)/shard_map/finish/pallas_call | solution.py:89
  456.0 3.2 collective-permute-done.45.refs_2_
  468.4 4.4 collective-permute-done.51.refs_1_
  473.4 5.6 %collective-permute-done.53.refs_3_ = bf16[176,768]{1,0:T(8,128)(2,1)S(1)} collective-permute-done((bf16[176,768]{1,0:T(8,128)(2,1)}, bf16[176,768]{1,0:T(8,128)(2,1)S(1)}, u32[]{:S(2)}, u32[]{:S(2)}) %collective-permute-start.53) | collective-permute-done | bytes 270368 | tf_op jit(solution)/shard_map/ppermute | solution.py:749
  484.4 6.8 %finish.3 = (f32[2,3,192,768]{3,2,1,0:T(8,128)}, f32[2,192,768]{2,1,0:T(8,128)}, f32[2,768,768]{2,1,0:T(8,128)}, f32[2,768,768]{2,1,0:T(8,128)}, f32[2,1024,256]...) custom-call(s32[6]{0:T(128)} %stack.156.refs_0_, ...), custom_call_target="tpu_custom_call", output_to_operand_aliasing={{0}: (17, {}), {1}: (18, {}), {2}: (19, {}), {3}: (20, {}),... | custom-call | tf_op jit(solution)/shard_map/finish/pallas_call | solution.py:89
  (472 shorter events, 138.7 us)
Async XLA Ops:
  7.2 173.5 %all-gather.5.cloned.1.call-start = ((), (), s32[]{:S(2)}) async-start(), calls=%async_computation.4 | async-start | bytes 14598144 | tf_op jit(solution)/shard_map/all_gather | solution.py:997
  10.3 17.0 %collective-permute-start.4 = (bf16[96,768]{1,0:T(8,128)(2,1)}, bf16[96,768]{1,0:T(8,128)(2,1)S(1)}, u32[]{:S(2)}, u32[]{:S(2)}) collective-permute-start(bf16[96,768]{1,0:T(8,128)(2,1)} %get-tuple-element.289), channel_id=1, source_target_pairs={{0,1},{1,0},{2,3},{3,2},{4,5},{5,4},{6,7},{7,6},{8,9},{9,8},{10,11... | collective-permute-start | bytes 442376 | tf_op jit(solution)/shard_map/ppermute | solution.py:749
  10.3 17.3 %collective-permute-start.5 = (bf16[96,768]{1,0:T(8,128)(2,1)}, bf16[96,768]{1,0:T(8,128)(2,1)S(1)}, u32[]{:S(2)}, u32[]{:S(2)}) collective-permute-start(bf16[96,768]{1,0:T(8,128)(2,1)} %get-tuple-element.289), channel_id=1, source_target_pairs={{0,2},{1,3},{2,0},{3,1},{4,6},{5,7},{6,4},{7,5},{8,10},{9,11},{10,... | collective-permute-start | bytes 442376 | tf_op jit(solution)/shard_map/ppermute | solution.py:749
  12.8 14.8 %collective-permute-start.6 = (bf16[96,768]{1,0:T(8,128)(2,1)}, bf16[96,768]{1,0:T(8,128)(2,1)S(1)}, u32[]{:S(2)}, u32[]{:S(2)}) collective-permute-start(bf16[96,768]{1,0:T(8,128)(2,1)} %get-tuple-element.289), channel_id=1, source_target_pairs={{0,3},{1,2},{2,1},{3,0},{4,7},{5,6},{6,5},{7,4},{8,11},{9,10},{10,... | collective-permute-start | bytes 442376 | tf_op jit(solution)/shard_map/ppermute | solution.py:749
  17.2 26.5 %collective-permute-start.1 = (bf16[192,768]{1,0:T(8,128)(2,1)}, bf16[192,768]{1,0:T(8,128)(2,1)S(1)}, u32[]{:S(2)}, u32[]{:S(2)}) collective-permute-start(bf16[192,768]{1,0:T(8,128)(2,1)} %get-tuple-element.288), channel_id=1, source_target_pairs={{0,1},{1,0},{2,3},{3,2},{4,5},{5,4},{6,7},{7,6},{8,9},{9,8},{10,11... | collective-permute-start | bytes 884744 | tf_op jit(solution)/shard_map/ppermute | solution.py:749
  18.3 25.8 %collective-permute-start.2 = (bf16[192,768]{1,0:T(8,128)(2,1)}, bf16[192,768]{1,0:T(8,128)(2,1)S(1)}, u32[]{:S(2)}, u32[]{:S(2)}) collective-permute-start(bf16[192,768]{1,0:T(8,128)(2,1)} %get-tuple-element.288), channel_id=1, source_target_pairs={{0,2},{1,3},{2,0},{3,1},{4,6},{5,7},{6,4},{7,5},{8,10},{9,11},{10,... | collective-permute-start | bytes 884744 | tf_op jit(solution)/shard_map/ppermute | solution.py:749
  27.3 23.7 %collective-permute-start.3 = (bf16[192,768]{1,0:T(8,128)(2,1)S(1)}, bf16[192,768]{1,0:T(8,128)(2,1)S(1)}, u32[]{:S(2)}, u32[]{:S(2)}) collective-permute-start(bf16[192,768]{1,0:T(8,128)(2,1)S(1)} %copy-done.37), channel_id=1, source_target_pairs={{0,3},{1,2},{2,1},{3,0},{4,7},{5,6},{6,5},{7,4},{8,11},{9,10},{10,... | collective-permute-start | bytes 884744 | tf_op jit(solution)/shard_map/ppermute | solution.py:749
  55.7 259.2 %reduce-scatter.3.cloned.1.call-start = ((), (), s32[]{:S(2)}) async-start(), calls=%async_computation.2 | async-start | bytes 10616832 | tf_op jit(solution)/shard_map/reduce_scatter | solution.py:863
  56.8 27.6 %collective-permute-start = (bf16[512,768]{1,0:T(8,128)(2,1)S(1)}, bf16[512,768]{1,0:T(8,128)(2,1)S(1)}, u32[]{:S(2)}, u32[]{:S(2)}) collective-permute-start(bf16[512,768]{1,0:T(8,128)(2,1)S(1)} %copy-done.24), channel_id=1, source_target_pairs={{0,1},{1,2},{2,3},{4,5},{5,6},{6,7},{8,9},{9,10},{10,11},{12,13},{... | collective-permute-start | bytes 2359304 | tf_op jit(solution)/shard_map/ppermute | solution.py:963
  60.3 25.0 %collective-permute-start.10 = (bf16[2,4,48,768]{3,2,1,0:T(8,128)(2,1)S(1)}, bf16[2,4,48,768]{3,2,1,0:T(8,128)(2,1)}, u32[]{:S(2)}, u32[]{:S(2)}) collective-permute-start(bf16[2,4,48,768]{3,2,1,0:T(8,128)(2,1)S(1)} %copy-done.26), channel_id=1, source_target_pairs={{0,8},{4,12},{8,0},{12,4},{16,24},{20,28},{24,16},{28,20},{1,9},{5... | collective-permute-start | bytes 1769480 | tf_op jit(solution)/shard_map/ppermute | solution.py:749
  61.6 23.7 %collective-permute-start.9 = (bf16[2,4,48,768]{3,2,1,0:T(8,128)(2,1)S(1)}, bf16[2,4,48,768]{3,2,1,0:T(8,128)(2,1)}, u32[]{:S(2)}, u32[]{:S(2)}) collective-permute-start(bf16[2,4,48,768]{3,2,1,0:T(8,128)(2,1)S(1)} %copy-done.28), channel_id=1, source_target_pairs={{0,16},{4,20},{8,24},{12,28},{16,0},{20,4},{24,8},{28,12},{1,17},{... | collective-permute-start | bytes 1769480 | tf_op jit(solution)/shard_map/ppermute | solution.py:749
  62.8 26.4 %collective-permute-start.11 = (bf16[4,96,768]{2,1,0:T(8,128)(2,1)}, bf16[4,96,768]{2,1,0:T(8,128)(2,1)S(1)}, u32[]{:S(2)}, u32[]{:S(2)}) collective-permute-start(bf16[4,96,768]{2,1,0:T(8,128)(2,1)} %get-tuple-element.314), channel_id=1, source_target_pairs={{0,8},{4,12},{8,0},{12,4},{16,24},{20,28},{24,16},{28,20},{1,9},{5... | collective-permute-start | bytes 1769480 | tf_op jit(solution)/shard_map/ppermute | solution.py:749
  63.1 27.0 %collective-permute-start.12 = (bf16[4,96,768]{2,1,0:T(8,128)(2,1)}, bf16[4,96,768]{2,1,0:T(8,128)(2,1)}, u32[]{:S(2)}, u32[]{:S(2)}) collective-permute-start(bf16[4,96,768]{2,1,0:T(8,128)(2,1)} %get-tuple-element.315), channel_id=1, source_target_pairs={{0,16},{4,20},{8,24},{12,28},{16,0},{20,4},{24,8},{28,12},{1,17},{... | collective-permute-start | bytes 1769480 | tf_op jit(solution)/shard_map/ppermute | solution.py:749
  101.1 27.8 %collective-permute-start.15 = (bf16[2,4,96,768]{3,2,1,0:T(8,128)(2,1)}, bf16[2,4,96,768]{3,2,1,0:T(8,128)(2,1)}, u32[]{:S(2)}, u32[]{:S(2)}) collective-permute-start(bf16[2,4,96,768]{3,2,1,0:T(8,128)(2,1)} %get-tuple-element.329), channel_id=1, source_target_pairs={{0,16},{4,20},{8,24},{12,28},{16,0},{20,4},{24,8},{28,12},{1,17},{... | collective-permute-start | bytes 3538952 | tf_op jit(solution)/shard_map/ppermute | solution.py:749
  102.3 32.0 %collective-permute-start.16 = (bf16[2,4,96,768]{3,2,1,0:T(8,128)(2,1)S(1)}, bf16[2,4,96,768]{3,2,1,0:T(8,128)(2,1)}, u32[]{:S(2)}, u32[]{:S(2)}) collective-permute-start(bf16[2,4,96,768]{3,2,1,0:T(8,128)(2,1)S(1)} %copy-done.20), channel_id=1, source_target_pairs={{0,8},{4,12},{8,0},{12,4},{16,24},{20,28},{24,16},{28,20},{1,9},{5... | collective-permute-start | bytes 3538952 | tf_op jit(solution)/shard_map/ppermute | solution.py:749
  140.3 9.3 %collective-permute-start.17 = (bf16[2,2,4,96,768]{4,3,2,1,0:T(8,128)(2,1)}, bf16[2,2,4,96,768]{4,3,2,1,0:T(8,128)(2,1)S(1)}, u32[]{:S(2)}, u32[]{:S(2)}) collective-permute-start(bf16[2,2,4,96,768]{4,3,2,1,0:T(8,128)(2,1)} %get-tuple-element.335), channel_id=1, source_target_pairs={{0,4},{4,0},{8,12},{12,8},{16,20},{20,16},{24,28},{28,24},{1,5},{5... | collective-permute-start | bytes 7077896 | tf_op jit(solution)/shard_map/ppermute | solution.py:749
  141.9 8.0 %collective-permute-start.18 = (bf16[2,2,4,96,768]{4,3,2,1,0:T(8,128)(2,1)}, bf16[2,2,4,96,768]{4,3,2,1,0:T(8,128)(2,1)}, u32[]{:S(2)}, u32[]{:S(2)}) collective-permute-start(bf16[2,2,4,96,768]{4,3,2,1,0:T(8,128)(2,1)} %get-tuple-element.336), channel_id=1, source_target_pairs={{0,4},{4,0},{8,12},{12,8},{16,20},{20,16},{24,28},{28,24},{1,5},{5... | collective-permute-start | bytes 7077896 | tf_op jit(solution)/shard_map/ppermute | solution.py:749
  160.2 27.8 %collective-permute-start.19 = (bf16[512,768]{1,0:T(8,128)(2,1)}, bf16[512,768]{1,0:T(8,128)(2,1)S(1)}, u32[]{:S(2)}, u32[]{:S(2)}) collective-permute-start(bf16[512,768]{1,0:T(8,128)(2,1)} %get-tuple-element.346.refs_2_.refs_5_), channel_id=1, source_target_pairs={{0,1},{1,2},{2,3},{4,5},{5,6},{6,7},{8,9},{9,10},{10,11},{12,13},{... | collective-permute-start | bytes 2359304 | tf_op jit(solution)/shard_map/ppermute | solution.py:963
  226.8 178.3 %reduce-scatter.5.cloned.1.call-start = ((), (), s32[]{:S(2)}) async-start(), calls=%async_computation.3 | async-start | bytes 10616832 | tf_op jit(solution)/shard_map/reduce_scatter | solution.py:863
  244.5 20.6 %collective-permute-start.20 = (bf16[512,768]{1,0:T(8,128)(2,1)}, bf16[512,768]{1,0:T(8,128)(2,1)}, u32[]{:S(2)}, u32[]{:S(2)}) collective-permute-start(bf16[512,768]{1,0:T(8,128)(2,1)} %get-tuple-element.372), channel_id=1, source_target_pairs={{1,0},{2,1},{3,2},{5,4},{6,5},{7,6},{9,8},{10,9},{11,10},{13,12},{... | collective-permute-start | bytes 2359304 | tf_op jit(solution)/shard_map/ppermute | solution.py:966
  277.5 22.2 %collective-permute-start.23 = (bf16[2,208,768]{2,1,0:T(8,128)(2,1)}, bf16[2,208,768]{2,1,0:T(8,128)(2,1)S(1)}, u32[]{:S(2)}, u32[]{:S(2)}) collective-permute-start(bf16[2,208,768]{2,1,0:T(8,128)(2,1)} %get-tuple-element.409), channel_id=1, source_target_pairs={{0,16},{4,20},{8,24},{12,28},{16,0},{20,4},{24,8},{28,12},{1,17},{... | collective-permute-start | bytes 1916936 | tf_op jit(solution)/shard_map/ppermute | solution.py:749
  278.7 21.0 %collective-permute-start.24 = (bf16[2,192,768]{2,1,0:T(8,128)(2,1)}, bf16[2,192,768]{2,1,0:T(8,128)(2,1)S(1)}, u32[]{:S(2)}, u32[]{:S(2)}) collective-permute-start(bf16[2,192,768]{2,1,0:T(8,128)(2,1)} %get-tuple-element.410), channel_id=1, source_target_pairs={{0,8},{4,12},{8,0},{12,4},{16,24},{20,28},{24,16},{28,20},{1,9},{5... | collective-permute-start | bytes 1769480 | tf_op jit(solution)/shard_map/ppermute | solution.py:749
  300.7 148.2 %all-gather.7.cloned.1.call-start = ((), (), s32[]{:S(2)}) async-start(), calls=%async_computation.5 | async-start | bytes 4866048 | tf_op jit(solution)/shard_map/all_gather | solution.py:1074
  305.4 8.6 %collective-permute-start.25 = (bf16[208,768]{1,0:T(8,128)(2,1)}, bf16[208,768]{1,0:T(8,128)(2,1)S(1)}, u32[]{:S(2)}, u32[]{:S(2)}) collective-permute-start(bf16[208,768]{1,0:T(8,128)(2,1)} %get-tuple-element.417), channel_id=1, source_target_pairs={{0,8},{4,12},{8,0},{12,4},{16,24},{20,28},{24,16},{28,20},{1,9},{5... | collective-permute-start | bytes 958472 | tf_op jit(solution)/shard_map/ppermute | solution.py:749
  317.3 27.4 %collective-permute-start.27 = (bf16[192,768]{1,0:T(8,128)(2,1)}, bf16[192,768]{1,0:T(8,128)(2,1)S(1)}, u32[]{:S(2)}, u32[]{:S(2)}) collective-permute-start(bf16[192,768]{1,0:T(8,128)(2,1)} %get-tuple-element.435), channel_id=1, source_target_pairs={{0,1},{1,0},{2,3},{3,2},{4,5},{5,4},{6,7},{7,6},{8,9},{9,8},{10,11... | collective-permute-start | bytes 884744 | tf_op jit(solution)/shard_map/ppermute | solution.py:749
  317.3 27.4 %collective-permute-start.28 = (bf16[192,768]{1,0:T(8,128)(2,1)}, bf16[192,768]{1,0:T(8,128)(2,1)S(1)}, u32[]{:S(2)}, u32[]{:S(2)}) collective-permute-start(bf16[192,768]{1,0:T(8,128)(2,1)} %get-tuple-element.436), channel_id=1, source_target_pairs={{0,2},{1,3},{2,0},{3,1},{4,6},{5,7},{6,4},{7,5},{8,10},{9,11},{10,... | collective-permute-start | bytes 884744 | tf_op jit(solution)/shard_map/ppermute | solution.py:749
  319.9 24.8 %collective-permute-start.29 = (bf16[192,768]{1,0:T(8,128)(2,1)}, bf16[192,768]{1,0:T(8,128)(2,1)}, u32[]{:S(2)}, u32[]{:S(2)}) collective-permute-start(bf16[192,768]{1,0:T(8,128)(2,1)} %get-tuple-element.437), channel_id=1, source_target_pairs={{0,3},{1,2},{2,1},{3,0},{4,7},{5,6},{6,5},{7,4},{8,11},{9,10},{10,... | collective-permute-start | bytes 884744 | tf_op jit(solution)/shard_map/ppermute | solution.py:749
  345.5 9.6 %collective-permute-start.30 = (bf16[4,208,768]{2,1,0:T(8,128)(2,1)}, bf16[4,208,768]{2,1,0:T(8,128)(2,1)S(1)}, u32[]{:S(2)}, u32[]{:S(2)}) collective-permute-start(bf16[4,208,768]{2,1,0:T(8,128)(2,1)} %get-tuple-element.440), channel_id=1, source_target_pairs={{0,4},{4,0},{8,12},{12,8},{16,20},{20,16},{24,28},{28,24},{1,5},{5... | collective-permute-start | bytes 3833864 | tf_op jit(solution)/shard_map/ppermute | solution.py:749
  352.8 9.6 %collective-permute-start.33 = (bf16[112,768]{1,0:T(8,128)(2,1)}, bf16[112,768]{1,0:T(8,128)(2,1)S(1)}, u32[]{:S(2)}, u32[]{:S(2)}) collective-permute-start(bf16[112,768]{1,0:T(8,128)(2,1)} %get-tuple-element.450), channel_id=1, source_target_pairs={{0,2},{1,3},{2,0},{3,1},{4,6},{5,7},{6,4},{7,5},{8,10},{9,11},{10,... | collective-permute-start | bytes 516104 | tf_op jit(solution)/shard_map/ppermute | solution.py:749
  354.9 14.9 %collective-permute-start.34 = (bf16[112,768]{1,0:T(8,128)(2,1)}, bf16[112,768]{1,0:T(8,128)(2,1)S(1)}, u32[]{:S(2)}, u32[]{:S(2)}) collective-permute-start(bf16[112,768]{1,0:T(8,128)(2,1)} %get-tuple-element.451), channel_id=1, source_target_pairs={{0,3},{1,2},{2,1},{3,0},{4,7},{5,6},{6,5},{7,4},{8,11},{9,10},{10,... | collective-permute-start | bytes 516104 | tf_op jit(solution)/shard_map/ppermute | solution.py:749
  379.8 19.7 %collective-permute-start.36 = (bf16[2,208,768]{2,1,0:T(8,128)(2,1)}, bf16[2,208,768]{2,1,0:T(8,128)(2,1)S(1)}, u32[]{:S(2)}, u32[]{:S(2)}) collective-permute-start(bf16[2,208,768]{2,1,0:T(8,128)(2,1)} %get-tuple-element.456), channel_id=1, source_target_pairs={{0,16},{4,20},{8,24},{12,28},{16,0},{20,4},{24,8},{28,12},{1,17},{... | collective-permute-start | bytes 1916936 | tf_op jit(solution)/shard_map/ppermute | solution.py:749
  380.6 17.8 %collective-permute-start.37 = (bf16[2,192,768]{2,1,0:T(8,128)(2,1)}, bf16[2,192,768]{2,1,0:T(8,128)(2,1)S(1)}, u32[]{:S(2)}, u32[]{:S(2)}) collective-permute-start(bf16[2,192,768]{2,1,0:T(8,128)(2,1)} %get-tuple-element.457), channel_id=1, source_target_pairs={{0,8},{4,12},{8,0},{12,4},{16,24},{20,28},{24,16},{28,20},{1,9},{5... | collective-permute-start | bytes 1769480 | tf_op jit(solution)/shard_map/ppermute | solution.py:749
  380.8 23.4 %collective-permute-start.35 = (bf16[512,768]{1,0:T(8,128)(2,1)S(1)}, bf16[512,768]{1,0:T(8,128)(2,1)S(1)}, u32[]{:S(2)}, u32[]{:S(2)}) collective-permute-start(bf16[512,768]{1,0:T(8,128)(2,1)S(1)} %copy-done.13), channel_id=1, source_target_pairs={{1,0},{2,1},{3,2},{5,4},{6,5},{7,6},{9,8},{10,9},{11,10},{13,12},{... | collective-permute-start | bytes 2359304 | tf_op jit(solution)/shard_map/ppermute | solution.py:966
  405.1 15.0 %collective-permute-start.38 = (bf16[208,768]{1,0:T(8,128)(2,1)}, bf16[208,768]{1,0:T(8,128)(2,1)S(1)}, u32[]{:S(2)}, u32[]{:S(2)}) collective-permute-start(bf16[208,768]{1,0:T(8,128)(2,1)} %get-tuple-element.479), channel_id=1, source_target_pairs={{0,8},{4,12},{8,0},{12,4},{16,24},{20,28},{24,16},{28,20},{1,9},{5... | collective-permute-start | bytes 958472 | tf_op jit(solution)/shard_map/ppermute | solution.py:749
  406.3 13.3 %collective-permute-start.39 = (bf16[192,768]{1,0:T(8,128)(2,1)}, bf16[192,768]{1,0:T(8,128)(2,1)S(1)}, u32[]{:S(2)}, u32[]{:S(2)}) collective-permute-start(bf16[192,768]{1,0:T(8,128)(2,1)} %get-tuple-element.480), channel_id=1, source_target_pairs={{0,16},{4,20},{8,24},{12,28},{16,0},{20,4},{24,8},{28,12},{1,17},{... | collective-permute-start | bytes 884744 | tf_op jit(solution)/shard_map/ppermute | solution.py:749
  409.0 13.1 %collective-permute-start.40 = (bf16[192,768]{1,0:T(8,128)(2,1)}, bf16[192,768]{1,0:T(8,128)(2,1)S(1)}, u32[]{:S(2)}, u32[]{:S(2)}) collective-permute-start(bf16[192,768]{1,0:T(8,128)(2,1)} %get-tuple-element.492), channel_id=1, source_target_pairs={{0,1},{1,0},{2,3},{3,2},{4,5},{5,4},{6,7},{7,6},{8,9},{9,8},{10,11... | collective-permute-start | bytes 884744 | tf_op jit(solution)/shard_map/ppermute | solution.py:749
  409.0 14.5 %collective-permute-start.41 = (bf16[192,768]{1,0:T(8,128)(2,1)}, bf16[192,768]{1,0:T(8,128)(2,1)S(1)}, u32[]{:S(2)}, u32[]{:S(2)}) collective-permute-start(bf16[192,768]{1,0:T(8,128)(2,1)} %get-tuple-element.493), channel_id=1, source_target_pairs={{0,2},{1,3},{2,0},{3,1},{4,6},{5,7},{6,4},{7,5},{8,10},{9,11},{10,... | collective-permute-start | bytes 884744 | tf_op jit(solution)/shard_map/ppermute | solution.py:749
  411.5 24.5 %collective-permute-start.42 = (bf16[192,768]{1,0:T(8,128)(2,1)}, bf16[192,768]{1,0:T(8,128)(2,1)}, u32[]{:S(2)}, u32[]{:S(2)}) collective-permute-start(bf16[192,768]{1,0:T(8,128)(2,1)} %get-tuple-element.494), channel_id=1, source_target_pairs={{0,3},{1,2},{2,1},{3,0},{4,7},{5,6},{6,5},{7,4},{8,11},{9,10},{10,... | collective-permute-start | bytes 884744 | tf_op jit(solution)/shard_map/ppermute | solution.py:749
  438.2 9.2 %collective-permute-start.43 = (bf16[128,768]{1,0:T(8,128)(2,1)}, bf16[128,768]{1,0:T(8,128)(2,1)S(1)}, u32[]{:S(2)}, u32[]{:S(2)}) collective-permute-start(bf16[128,768]{1,0:T(8,128)(2,1)} %get-tuple-element.498), channel_id=1, source_target_pairs={{0,1},{1,0},{2,3},{3,2},{4,5},{5,4},{6,7},{7,6},{8,9},{9,8},{10,11... | collective-permute-start | bytes 589832 | tf_op jit(solution)/shard_map/ppermute | solution.py:749
  438.2 10.6 %collective-permute-start.44 = (bf16[128,768]{1,0:T(8,128)(2,1)}, bf16[128,768]{1,0:T(8,128)(2,1)S(1)}, u32[]{:S(2)}, u32[]{:S(2)}) collective-permute-start(bf16[128,768]{1,0:T(8,128)(2,1)} %get-tuple-element.499), channel_id=1, source_target_pairs={{0,2},{1,3},{2,0},{3,1},{4,6},{5,7},{6,4},{7,5},{8,10},{9,11},{10,... | collective-permute-start | bytes 589832 | tf_op jit(solution)/shard_map/ppermute | solution.py:749
  442.7 17.1 %collective-permute-start.46 = (bf16[192,768]{1,0:T(8,128)(2,1)}, bf16[192,768]{1,0:T(8,128)(2,1)S(1)}, u32[]{:S(2)}, u32[]{:S(2)}) collective-permute-start(bf16[192,768]{1,0:T(8,128)(2,1)} %get-tuple-element.514.refs_9_), channel_id=1, source_target_pairs={{0,4},{4,0},{8,12},{12,8},{16,20},{20,16},{24,28},{28,24},{1,5},{5... | collective-permute-start | bytes 884744 | tf_op jit(solution)/shard_map/ppermute | solution.py:749
  446.1 13.7 %collective-permute-start.47 = (bf16[192,768]{1,0:T(8,128)(2,1)}, bf16[192,768]{1,0:T(8,128)(2,1)S(1)}, u32[]{:S(2)}, u32[]{:S(2)}) collective-permute-start(bf16[192,768]{1,0:T(8,128)(2,1)} %get-tuple-element.514.refs_9_), channel_id=1, source_target_pairs={{0,8},{4,12},{8,0},{12,4},{16,24},{20,28},{24,16},{28,20},{1,9},{5... | collective-permute-start | bytes 884744 | tf_op jit(solution)/shard_map/ppermute | solution.py:749
  446.9 13.0 %collective-permute-start.48 = (bf16[192,768]{1,0:T(8,128)(2,1)}, bf16[192,768]{1,0:T(8,128)(2,1)S(1)}, u32[]{:S(2)}, u32[]{:S(2)}) collective-permute-start(bf16[192,768]{1,0:T(8,128)(2,1)} %get-tuple-element.514.refs_9_), channel_id=1, source_target_pairs={{0,16},{4,20},{8,24},{12,28},{16,0},{20,4},{24,8},{28,12},{1,17},{... | collective-permute-start | bytes 884744 | tf_op jit(solution)/shard_map/ppermute | solution.py:749
  447.4 14.6 %collective-permute-start.49 = (bf16[192,768]{1,0:T(8,128)(2,1)}, bf16[192,768]{1,0:T(8,128)(2,1)S(1)}, u32[]{:S(2)}, u32[]{:S(2)}) collective-permute-start(bf16[192,768]{1,0:T(8,128)(2,1)} %get-tuple-element.514.refs_9_), channel_id=1, source_target_pairs={{0,24},{4,28},{8,16},{12,20},{16,8},{20,12},{24,0},{28,4},{1,25},{... | collective-permute-start | bytes 884744 | tf_op jit(solution)/shard_map/ppermute | solution.py:749
  448.8 10.3 %collective-permute-start.45 = (bf16[128,768]{1,0:T(8,128)(2,1)S(1)}, bf16[128,768]{1,0:T(8,128)(2,1)S(1)}, u32[]{:S(2)}, u32[]{:S(2)}) collective-permute-start(bf16[128,768]{1,0:T(8,128)(2,1)S(1)} %copy-done.97), channel_id=1, source_target_pairs={{0,3},{1,2},{2,1},{3,0},{4,7},{5,6},{6,5},{7,4},{8,11},{9,10},{10,... | collective-permute-start | bytes 589832 | tf_op jit(solution)/shard_map/ppermute | solution.py:749
  465.0 7.8 %collective-permute-start.51 = (bf16[176,768]{1,0:T(8,128)(2,1)}, bf16[176,768]{1,0:T(8,128)(2,1)S(1)}, u32[]{:S(2)}, u32[]{:S(2)}) collective-permute-start(bf16[176,768]{1,0:T(8,128)(2,1)} %get-tuple-element.521.refs_1_), channel_id=1, source_target_pairs={{0,8},{4,12},{8,0},{12,4},{16,24},{20,28},{24,16},{28,20},{1,9},{5... | collective-permute-start | bytes 811016 | tf_op jit(solution)/shard_map/ppermute | solution.py:749
  465.8 7.6 %collective-permute-start.52 = (bf16[176,768]{1,0:T(8,128)(2,1)}, bf16[176,768]{1,0:T(8,128)(2,1)S(1)}, u32[]{:S(2)}, u32[]{:S(2)}) collective-permute-start(bf16[176,768]{1,0:T(8,128)(2,1)} %get-tuple-element.521.refs_1_), channel_id=1, source_target_pairs={{0,16},{4,20},{8,24},{12,28},{16,0},{20,4},{24,8},{28,12},{1,17},{... | collective-permute-start | bytes 811016 | tf_op jit(solution)/shard_map/ppermute | solution.py:749
  466.9 12.1 %collective-permute-start.53 = (bf16[176,768]{1,0:T(8,128)(2,1)}, bf16[176,768]{1,0:T(8,128)(2,1)S(1)}, u32[]{:S(2)}, u32[]{:S(2)}) collective-permute-start(bf16[176,768]{1,0:T(8,128)(2,1)} %get-tuple-element.521.refs_1_), channel_id=1, source_target_pairs={{0,24},{4,28},{8,16},{12,20},{16,8},{20,12},{24,0},{28,4},{1,25},{... | collective-permute-start | bytes 811016 | tf_op jit(solution)/shard_map/ppermute | solution.py:749
  (133 other events, 461.6 us)
Sparse Core Ops, SparseCore 0:
  55.8 124.8 all-gather.4
  226.9 81.4 reduce-scatter.2
  311.9 78.8 reduce-scatter.4
  392.6 47.5 all-gather.6

commit v11 on v10

--- a/solution.py
+++ b/solution.py
@@ -1056,12 +1056,12 @@
         wide0 = ReduceWide(links, wide0)
         r_attn1.start()
         z_of_1 = mp_index if in_blocks else None
-        attn1_sum, riders1 = r_attn1.wait_all()
         z_ff1 = ReduceMp(links, wide1.wait(), z_of_1, None)
         gq, gk, gv, band0, dn_own0, back0 = attn_backward(order, place, grad3_low, w_attn0, *saved0)
         r_attn0 = Reduce(
             links, attn_weight_grads(order, place, gq, gk, gv, *rows0, grad3_low, band0, mp, False, in_blocks)
         )
+        attn1_sum, riders1 = r_attn1.wait_all()
         sum1_ff, _ = z_ff1.wait()
         r_attn0.start_cores()
         z_attn1 = ReduceMp(links, attn1_sum, z_of_1, riders1)

time: 505 us -> 506 us (level)
    unnamed x240 -> x234, local copies, waits for them, and re-layouts: 32.8 us -> 32 us
  transfers between devices with their start and end apart: 64 -> 64, of which waited for: 32 -> 31; matrix products, arithmetic and copies ran while one was open for 13% -> 13% of each run, Pallas kernels for 23% -> 23%
where the time goes in v11:
time: 506 us; the launch traced here: 499 us
  Pallas kernels  159 us (31%)
  waiting for transfers between devices  158 us (31%)
  starting transfers between devices  62 us (12%)
  other arithmetic  50.5 us (10%)
  local copies, waits for them, and re-layouts  47.4 us (9%)
  between operations  15.2 us (3%)
  matrix products  6.88 us (1%)
    pallas_call x15, Pallas kernels, run(): *results, order.token = kernel(*placed, order.token)  159 us
    ppermute x56, waiting for transfers between devices, swap(): return lax.ppermute(value, axis, [(i, i ^ bit) for i in range(size)])  104 us
    ppermute x56, starting transfers between devices, swap(): return lax.ppermute(value, axis, [(i, i ^ bit) for i in range(size)])  51 us
    unnamed x234, local copies, waits for them, and re-layouts  32 us
    ppermute x2, waiting for transfers between devices, forward_halo(): return lax.ppermute(value, 'mp', [(i, i + 1) for i in range(mp - 1)])  28.4 us
    all_gather x1, waiting for transfers between devices, shards(): later = lax.all_gather(later, ('g', 'c', 'mp'), axis=0, tiled=False)  17.2 us
    another operation x8, other arithmetic, wait(): self.values[k] = jnp.stack([self.values[k], coming[k]], axis=place)  16.4 us
    convert_element_type x8, other arithmetic, start(): sum((lax.index_in_dim(term, 1, place, keepdims=False).astype(F32) for ter...  16.2 us
  transfers between devices with their start and end apart: 64, of which 31 were waited for; matrix products, arithmetic and copies ran while one was open for 13% of the time, Pallas kernels for 23%

profile of v11, /device:TPU:9, one launch (start us, length us, event | category | flops | bytes accessed | tf_op | source)
XLA Modules:
  0.0 499.4 jit_solution(3595020831352761337)
XLA Ops:
  10.3 2.5 collective-permute-start.5
  24.6 2.7 enter.1
  35.9 3.3 collective-permute-done.7.refs_0_
  44.1 7.0 %collective-permute-done.3.refs_2_ = bf16[192,768]{1,0:T(8,128)(2,1)S(1)} collective-permute-done((bf16[192,768]{1,0:T(8,128)(2,1)S(1)}, bf16[192,768]{1,0:T(8,128)(2,1)S(1)}, u32[]{:S(2)}, u32[]{:S(2)}) %collective-permute-start.3) | collective-permute-done | bytes 294944 | tf_op jit(solution)/shard_map/ppermute | solution.py:749
  56.8 3.5 collective-permute-start
  63.3 21.1 %collective-permute-done.refs_0_ = bf16[512,768]{1,0:T(8,128)(2,1)S(1)} collective-permute-done((bf16[512,768]{1,0:T(8,128)(2,1)S(1)}, bf16[512,768]{1,0:T(8,128)(2,1)S(1)}, u32[]{:S(2)}, u32[]{:S(2)}) %collective-permute-start) | collective-permute-done | bytes 786464 | tf_op jit(solution)/shard_map/ppermute | solution.py:963
  85.3 3.9 collective-permute-done.11.refs_0_
  90.1 2.3 pad_maximum_fusion.5.refs_1_
  93.5 2.2 pad_maximum_fusion.3.refs_1_
  95.7 2.2 pad_maximum_fusion.2.refs_0_
  97.9 3.1 collective-permute-start.13
  106.6 13.9 %attn_fwd.2 = (bf16[512,768]{1,0:T(8,128)(2,1)}, bf16[512,768]{1,0:T(8,128)(2,1)}, bf16[512,768]{1,0:T(8,128)(2,1)}, bf16[1024,768]{1,0:T(8,128)(2,1)}, bf16[102...) custom-call(s32[6]{0:T(128)} %stack.156.refs_0_, ...), custom_call_target="tpu_custom_call", output_to_operand_aliasing={{10}: (13, {})} | custom-call | tf_op jit(solution)/shard_map/attn_fwd/pallas_call | solution.py:89
  120.4 8.4 %collective-permute-done.15.refs_0_ = bf16[2,4,96,768]{3,2,1,0:T(8,128)(2,1)} collective-permute-done((bf16[2,4,96,768]{3,2,1,0:T(8,128)(2,1)}, bf16[2,4,96,768]{3,2,1,0:T(8,128)(2,1)}, u32[]{:S(2)}, u32[]{:S(2)}) %collective-permute-start.15) | collective-permute-done | bytes 1179680 | tf_op jit(solution)/shard_map/ppermute | solution.py:749
  128.9 5.5 %collective-permute-done.16.refs_1_ = bf16[2,4,96,768]{3,2,1,0:T(8,128)(2,1)} collective-permute-done((bf16[2,4,96,768]{3,2,1,0:T(8,128)(2,1)S(1)}, bf16[2,4,96,768]{3,2,1,0:T(8,128)(2,1)}, u32[]{:S(2)}, u32[]{:S(2)}) %collective-permute-start.16) | collective-permute-done | bytes 1179680 | tf_op jit(solution)/shard_map/ppermute | solution.py:749
  134.4 3.0 pad_maximum_fusion.1.refs_1_
  137.4 2.9 pad_maximum_fusion.refs_0_
  141.9 7.7 %ff_fwd.2 = (bf16[512,1536]{1,0:T(8,128)(2,1)}, bf16[512,1536]{1,0:T(8,128)(2,1)}, f32[512,768]{1,0:T(8,128)}, s32[8,128]{1,0:T(8,128)}) custom-call(f32[512,768]{1,0:T(8,128)} %get-tuple-element.327.refs_0_.refs_1_, bf16[512,768]{1,0:T(8,128)(2,1)} %get-tuple-element.328.refs_1_.refs_2_, ...), custom_call_target="tpu_custom_call", output_to_operand_aliasing={{3}: (4, {})} | custom-call | tf_op jit(solution)/shard_map/ff_fwd/pallas_call | solution.py:89
  151.0 9.1 %ff_fwd.3 = (bf16[512,1536]{1,0:T(8,128)(2,1)}, bf16[512,1536]{1,0:T(8,128)(2,1)}, f32[512,768]{1,0:T(8,128)}, bf16[512,768]{1,0:T(8,128)(2,1)}, s32[8,128]{1,0:T(8,128)}) custom-call(f32[512,768]{1,0:T(8,128)} %get-tuple-element.338.refs_0_, bf16[512,768]{1,0:T(8,128)(2,1)} %get-tuple-element.328.refs_1_.refs_2_, ...), custom_call_target="tpu_custom_call", output_to_operand_aliasing={{4}: (6, {})} | custom-call | tf_op jit(solution)/shard_map/ff_fwd/pallas_call | solution.py:89
  160.2 3.3 collective-permute-start.19
  163.5 17.2 %all-gather.5.cloned.1.call-done = bf16[9216,768]{1,0:T(8,128)(2,1)} async-done(((bf16[288,768]{1,0:T(8,128)(2,1)}), bf16[9216,768]{1,0:T(8,128)(2,1)}) %all-gather.5.cloned.1.call-update) | async-done | bytes 14155792 | tf_op jit(solution)/shard_map/all_gather | solution.py:997
  180.7 7.3 %collective-permute-done.19.refs_0_ = bf16[512,768]{1,0:T(8,128)(2,1)S(1)} collective-permute-done((bf16[512,768]{1,0:T(8,128)(2,1)}, bf16[512,768]{1,0:T(8,128)(2,1)S(1)}, u32[]{:S(2)}, u32[]{:S(2)}) %collective-permute-start.19) | collective-permute-done | bytes 786464 | tf_op jit(solution)/shard_map/ppermute | solution.py:963
  188.9 13.6 %attn_fwd.3 = (bf16[512,768]{1,0:T(8,128)(2,1)}, bf16[512,768]{1,0:T(8,128)(2,1)}, bf16[512,768]{1,0:T(8,128)(2,1)}, bf16[1024,768]{1,0:T(8,128)(2,1)}, bf16[102...) custom-call(s32[6]{0:T(128)} %stack.156.refs_0_, ...), custom_call_target="tpu_custom_call", output_to_operand_aliasing={{10}: (10, {})} | custom-call | tf_op jit(solution)/shard_map/attn_fwd/pallas_call | solution.py:89
  202.5 24.2 %ff_bwd.2 = (bf16[4,2,2,384,768]{4,3,2,1,0:T(8,128)(2,1)}, f32[512,768]{1,0:T(8,128)}, bf16[512,768]{1,0:T(8,128)(2,1)}, f32[1,768]{1,0:T(1,128)}, f32[1,768]{1,...) custom-call(s32[6]{0:T(128)} %stack.156.refs_0_, ...), custom_call_target="tpu_custom_call", output_to_operand_aliasing={{6}: (7, {})} | custom-call | tf_op jit(solution)/shard_map/ff_bwd/pallas_call | solution.py:89
  227.9 12.8 %attn_bwd.2 = (bf16[512,768]{1,0:T(8,128)(2,1)S(1)}, bf16[1024,768]{1,0:T(8,128)(2,1)S(1)}, bf16[1024,768]{1,0:T(8,128)(2,1)S(1)}, f32[256,256]{1,0:T(8,128)S(1)...) custom-call(s32[6]{0:T(128)S(1)} %copy-done.15, ...), custom_call_target="tpu_custom_call", output_to_operand_aliasing={{6}: (10, {})} | custom-call | tf_op jit(solution)/shard_map/attn_bwd/pallas_call | solution.py:89
  248.5 8.7 %attn_wgrad.2 = (bf16[4,208,768]{2,1,0:T(8,128)(2,1)}, bf16[4,192,768]{2,1,0:T(8,128)(2,1)}, bf16[4,208,768]{2,1,0:T(8,128)(2,1)}, bf16[4,192,768]{2,1,0:T(8,128)(2,1)}, s32[8,128]{1,0:T(8,128)S(1)}) custom-call(s32[6]{0:T(128)S(1)} %copy-done.15, bf16[512,768]{1,0:T(8,128)(2,1)S(1)} %get-tuple-element.373.refs_1_, ...), custom_call_target="tpu_custom_call", output_to_operand_aliasing={{4}: (9, {})} | custom-call | tf_op jit(solution)/shard_map/attn_wgrad/pallas_call | solution.py:89
  257.8 7.2 %collective-permute-done.20.refs_0_ = bf16[512,768]{1,0:T(8,128)(2,1)} collective-permute-done((bf16[512,768]{1,0:T(8,128)(2,1)}, bf16[512,768]{1,0:T(8,128)(2,1)}, u32[]{:S(2)}, u32[]{:S(2)}) %collective-permute-start.20) | collective-permute-done | bytes 786464 | tf_op jit(solution)/shard_map/ppermute | solution.py:966
  266.7 4.9 leave.2
  273.1 2.3 fusion.26.refs_1_
  278.9 20.7 %ff_bwd.3 = (bf16[4,2,2,384,768]{4,3,2,1,0:T(8,128)(2,1)}, f32[512,768]{1,0:T(8,128)}, bf16[512,768]{1,0:T(8,128)(2,1)}, f32[1,768]{1,0:T(1,128)}, f32[1,768]{1,0:T(1,128)}, /*index=5*/s32[8,128]{1,0:T(8,128)}) custom-call(s32[6]{0:T(128)} %stack.156.refs_0_, f32[512,768]{1,0:T(8,128)} %get-tuple-element.327.refs_0_.refs_1_, ...), custom_call_target="tpu_custom_call", output_to_operand_aliasing={{5}: (13, {})} | custom-call | tf_op jit(solution)/shard_map/ff_bwd/pallas_call | solution.py:89
  311.1 2.3 collective-permute-start.26
  314.2 13.4 %attn_bwd.3 = (bf16[512,768]{1,0:T(8,128)(2,1)S(1)}, bf16[1024,768]{1,0:T(8,128)(2,1)S(1)}, bf16[1024,768]{1,0:T(8,128)(2,1)S(1)}, f32[256,256]{1,0:T(8,128)S(1)...) custom-call(s32[6]{0:T(128)S(1)} %copy-done.16, ...), custom_call_target="tpu_custom_call", output_to_operand_aliasing={{6}: (13, {})} | custom-call | tf_op jit(solution)/shard_map/attn_bwd/pallas_call | solution.py:89
  327.7 9.1 %attn_wgrad.3 = (bf16[4,208,768]{2,1,0:T(8,128)(2,1)}, bf16[4,192,768]{2,1,0:T(8,128)(2,1)}, bf16[4,208,768]{2,1,0:T(8,128)(2,1)}, bf16[4,192,768]{2,1,0:T(8,128)(2,1)}, s32[8,128]{1,0:T(8,128)S(1)}) custom-call(s32[6]{0:T(128)S(1)} %copy-done.16, bf16[512,768]{1,0:T(8,128)(2,1)S(1)} %get-tuple-element.423.refs_1_, ...), custom_call_target="tpu_custom_call", output_to_operand_aliasing={{4}: (9, {})} | custom-call | tf_op jit(solution)/shard_map/attn_wgrad/pallas_call | solution.py:89
  349.8 5.2 %collective-permute-done.33.refs_1_ = bf16[112,768]{1,0:T(8,128)(2,1)S(1)} collective-permute-done((bf16[112,768]{1,0:T(8,128)(2,1)}, bf16[112,768]{1,0:T(8,128)(2,1)S(1)}, u32[]{:S(2)}, u32[]{:S(2)}) %collective-permute-start.33) | collective-permute-done | bytes 172064 | tf_op jit(solution)/shard_map/ppermute | solution.py:749
  355.1 7.5 %collective-permute-done.34.refs_2_ = bf16[112,768]{1,0:T(8,128)(2,1)S(1)} collective-permute-done((bf16[112,768]{1,0:T(8,128)(2,1)}, bf16[112,768]{1,0:T(8,128)(2,1)S(1)}, u32[]{:S(2)}, u32[]{:S(2)}) %collective-permute-start.34) | collective-permute-done | bytes 172064 | tf_op jit(solution)/shard_map/ppermute | solution.py:749
  363.2 2.2 fusion.27.refs_1_
  375.8 22.7 %collective-permute-done.37.refs_1_ = bf16[2,192,768]{2,1,0:T(8,128)(2,1)S(1)} collective-permute-done((bf16[2,192,768]{2,1,0:T(8,128)(2,1)}, bf16[2,192,768]{2,1,0:T(8,128)(2,1)S(1)}, u32[]{:S(2)}, u32[]{:S(2)}) %collective-permute-start.37) | collective-permute-done | bytes 589856 | tf_op jit(solution)/shard_map/ppermute | solution.py:749
  409.2 2.4 collective-permute-start.41
  411.9 4.9 leave.3
  419.8 3.8 collective-permute-done.41.refs_1_
  423.6 12.7 %collective-permute-done.42.refs_2_ = bf16[192,768]{1,0:T(8,128)(2,1)} collective-permute-done((bf16[192,768]{1,0:T(8,128)(2,1)}, bf16[192,768]{1,0:T(8,128)(2,1)}, u32[]{:S(2)}, u32[]{:S(2)}) %collective-permute-start.42) | collective-permute-done | bytes 294944 | tf_op jit(solution)/shard_map/ppermute | solution.py:749
  438.6 2.4 collective-permute-start.44
  442.8 3.3 collective-permute-start.46
  449.5 6.5 %finish.2 = (f32[2,3,192,768]{3,2,1,0:T(8,128)}, f32[2,192,768]{2,1,0:T(8,128)}, f32[2,768,768]{2,1,0:T(8,128)}, f32[2,768,768]{2,1,0:T(8,128)}, f32[2,1024,256]{2,1,0:T(8,128)}, /*index=5*/s32[8,128]{1,0:T(8,128)}) custom-call(s32[6]{0:T(128)} %stack.156.refs_0_, bf16[8,352,768]{2,1,0:T(8,128)(2,1)} %get-tuple-element.508.refs_1_, ...), custom_call_target="tpu_custom_call", output_to_operand_aliasing={{5}: (2, {})} | custom-call | tf_op jit(solution)/shard_map/finish/pallas_call | solution.py:89
  456.0 3.1 collective-permute-done.45.refs_2_
  459.8 2.4 collective-permute-done.49.refs_3_
  468.6 4.4 collective-permute-done.51.refs_1_
  473.4 5.7 %collective-permute-done.53.refs_3_ = bf16[176,768]{1,0:T(8,128)(2,1)S(1)} collective-permute-done((bf16[176,768]{1,0:T(8,128)(2,1)}, bf16[176,768]{1,0:T(8,128)(2,1)S(1)}, u32[]{:S(2)}, u32[]{:S(2)}) %collective-permute-start.53) | collective-permute-done | bytes 270368 | tf_op jit(solution)/shard_map/ppermute | solution.py:749
  484.5 6.8 %finish.3 = (f32[2,3,192,768]{3,2,1,0:T(8,128)}, f32[2,192,768]{2,1,0:T(8,128)}, f32[2,768,768]{2,1,0:T(8,128)}, f32[2,768,768]{2,1,0:T(8,128)}, f32[2,1024,256]...) custom-call(s32[6]{0:T(128)} %stack.156.refs_0_, ...), custom_call_target="tpu_custom_call", output_to_operand_aliasing={{0}: (17, {}), {1}: (18, {}), {2}: (19, {}), {3}: (20, {}),... | custom-call | tf_op jit(solution)/shard_map/finish/pallas_call | solution.py:89
  (466 shorter events, 136.8 us)
Async XLA Ops:
  7.2 173.5 %all-gather.5.cloned.1.call-start = ((), (), s32[]{:S(2)}) async-start(), calls=%async_computation.4 | async-start | bytes 14598144 | tf_op jit(solution)/shard_map/all_gather | solution.py:997
  10.3 17.0 %collective-permute-start.4 = (bf16[96,768]{1,0:T(8,128)(2,1)}, bf16[96,768]{1,0:T(8,128)(2,1)S(1)}, u32[]{:S(2)}, u32[]{:S(2)}) collective-permute-start(bf16[96,768]{1,0:T(8,128)(2,1)} %get-tuple-element.289), channel_id=1, source_target_pairs={{0,1},{1,0},{2,3},{3,2},{4,5},{5,4},{6,7},{7,6},{8,9},{9,8},{10,11... | collective-permute-start | bytes 442376 | tf_op jit(solution)/shard_map/ppermute | solution.py:749
  10.3 17.3 %collective-permute-start.5 = (bf16[96,768]{1,0:T(8,128)(2,1)}, bf16[96,768]{1,0:T(8,128)(2,1)S(1)}, u32[]{:S(2)}, u32[]{:S(2)}) collective-permute-start(bf16[96,768]{1,0:T(8,128)(2,1)} %get-tuple-element.289), channel_id=1, source_target_pairs={{0,2},{1,3},{2,0},{3,1},{4,6},{5,7},{6,4},{7,5},{8,10},{9,11},{10,... | collective-permute-start | bytes 442376 | tf_op jit(solution)/shard_map/ppermute | solution.py:749
  12.8 14.8 %collective-permute-start.6 = (bf16[96,768]{1,0:T(8,128)(2,1)}, bf16[96,768]{1,0:T(8,128)(2,1)S(1)}, u32[]{:S(2)}, u32[]{:S(2)}) collective-permute-start(bf16[96,768]{1,0:T(8,128)(2,1)} %get-tuple-element.289), channel_id=1, source_target_pairs={{0,3},{1,2},{2,1},{3,0},{4,7},{5,6},{6,5},{7,4},{8,11},{9,10},{10,... | collective-permute-start | bytes 442376 | tf_op jit(solution)/shard_map/ppermute | solution.py:749
  17.2 26.5 %collective-permute-start.1 = (bf16[192,768]{1,0:T(8,128)(2,1)}, bf16[192,768]{1,0:T(8,128)(2,1)S(1)}, u32[]{:S(2)}, u32[]{:S(2)}) collective-permute-start(bf16[192,768]{1,0:T(8,128)(2,1)} %get-tuple-element.288), channel_id=1, source_target_pairs={{0,1},{1,0},{2,3},{3,2},{4,5},{5,4},{6,7},{7,6},{8,9},{9,8},{10,11... | collective-permute-start | bytes 884744 | tf_op jit(solution)/shard_map/ppermute | solution.py:749
  18.3 25.8 %collective-permute-start.2 = (bf16[192,768]{1,0:T(8,128)(2,1)}, bf16[192,768]{1,0:T(8,128)(2,1)S(1)}, u32[]{:S(2)}, u32[]{:S(2)}) collective-permute-start(bf16[192,768]{1,0:T(8,128)(2,1)} %get-tuple-element.288), channel_id=1, source_target_pairs={{0,2},{1,3},{2,0},{3,1},{4,6},{5,7},{6,4},{7,5},{8,10},{9,11},{10,... | collective-permute-start | bytes 884744 | tf_op jit(solution)/shard_map/ppermute | solution.py:749
  27.3 23.7 %collective-permute-start.3 = (bf16[192,768]{1,0:T(8,128)(2,1)S(1)}, bf16[192,768]{1,0:T(8,128)(2,1)S(1)}, u32[]{:S(2)}, u32[]{:S(2)}) collective-permute-start(bf16[192,768]{1,0:T(8,128)(2,1)S(1)} %copy-done.37), channel_id=1, source_target_pairs={{0,3},{1,2},{2,1},{3,0},{4,7},{5,6},{6,5},{7,4},{8,11},{9,10},{10,... | collective-permute-start | bytes 884744 | tf_op jit(solution)/shard_map/ppermute | solution.py:749
  55.7 252.8 %reduce-scatter.3.cloned.1.call-start = ((), (), s32[]{:S(2)}) async-start(), calls=%async_computation.2 | async-start | bytes 10616832 | tf_op jit(solution)/shard_map/reduce_scatter | solution.py:863
  56.8 27.6 %collective-permute-start = (bf16[512,768]{1,0:T(8,128)(2,1)S(1)}, bf16[512,768]{1,0:T(8,128)(2,1)S(1)}, u32[]{:S(2)}, u32[]{:S(2)}) collective-permute-start(bf16[512,768]{1,0:T(8,128)(2,1)S(1)} %copy-done.24), channel_id=1, source_target_pairs={{0,1},{1,2},{2,3},{4,5},{5,6},{6,7},{8,9},{9,10},{10,11},{12,13},{... | collective-permute-start | bytes 2359304 | tf_op jit(solution)/shard_map/ppermute | solution.py:963
  60.3 25.0 %collective-permute-start.10 = (bf16[2,4,48,768]{3,2,1,0:T(8,128)(2,1)S(1)}, bf16[2,4,48,768]{3,2,1,0:T(8,128)(2,1)}, u32[]{:S(2)}, u32[]{:S(2)}) collective-permute-start(bf16[2,4,48,768]{3,2,1,0:T(8,128)(2,1)S(1)} %copy-done.26), channel_id=1, source_target_pairs={{0,8},{4,12},{8,0},{12,4},{16,24},{20,28},{24,16},{28,20},{1,9},{5... | collective-permute-start | bytes 1769480 | tf_op jit(solution)/shard_map/ppermute | solution.py:749
  61.6 23.7 %collective-permute-start.9 = (bf16[2,4,48,768]{3,2,1,0:T(8,128)(2,1)S(1)}, bf16[2,4,48,768]{3,2,1,0:T(8,128)(2,1)}, u32[]{:S(2)}, u32[]{:S(2)}) collective-permute-start(bf16[2,4,48,768]{3,2,1,0:T(8,128)(2,1)S(1)} %copy-done.28), channel_id=1, source_target_pairs={{0,16},{4,20},{8,24},{12,28},{16,0},{20,4},{24,8},{28,12},{1,17},{... | collective-permute-start | bytes 1769480 | tf_op jit(solution)/shard_map/ppermute | solution.py:749
  62.8 26.4 %collective-permute-start.11 = (bf16[4,96,768]{2,1,0:T(8,128)(2,1)}, bf16[4,96,768]{2,1,0:T(8,128)(2,1)S(1)}, u32[]{:S(2)}, u32[]{:S(2)}) collective-permute-start(bf16[4,96,768]{2,1,0:T(8,128)(2,1)} %get-tuple-element.314), channel_id=1, source_target_pairs={{0,8},{4,12},{8,0},{12,4},{16,24},{20,28},{24,16},{28,20},{1,9},{5... | collective-permute-start | bytes 1769480 | tf_op jit(solution)/shard_map/ppermute | solution.py:749
  63.1 27.0 %collective-permute-start.12 = (bf16[4,96,768]{2,1,0:T(8,128)(2,1)}, bf16[4,96,768]{2,1,0:T(8,128)(2,1)}, u32[]{:S(2)}, u32[]{:S(2)}) collective-permute-start(bf16[4,96,768]{2,1,0:T(8,128)(2,1)} %get-tuple-element.315), channel_id=1, source_target_pairs={{0,16},{4,20},{8,24},{12,28},{16,0},{20,4},{24,8},{28,12},{1,17},{... | collective-permute-start | bytes 1769480 | tf_op jit(solution)/shard_map/ppermute | solution.py:749
  101.1 27.8 %collective-permute-start.15 = (bf16[2,4,96,768]{3,2,1,0:T(8,128)(2,1)}, bf16[2,4,96,768]{3,2,1,0:T(8,128)(2,1)}, u32[]{:S(2)}, u32[]{:S(2)}) collective-permute-start(bf16[2,4,96,768]{3,2,1,0:T(8,128)(2,1)} %get-tuple-element.329), channel_id=1, source_target_pairs={{0,16},{4,20},{8,24},{12,28},{16,0},{20,4},{24,8},{28,12},{1,17},{... | collective-permute-start | bytes 3538952 | tf_op jit(solution)/shard_map/ppermute | solution.py:749
  102.3 32.1 %collective-permute-start.16 = (bf16[2,4,96,768]{3,2,1,0:T(8,128)(2,1)S(1)}, bf16[2,4,96,768]{3,2,1,0:T(8,128)(2,1)}, u32[]{:S(2)}, u32[]{:S(2)}) collective-permute-start(bf16[2,4,96,768]{3,2,1,0:T(8,128)(2,1)S(1)} %copy-done.20), channel_id=1, source_target_pairs={{0,8},{4,12},{8,0},{12,4},{16,24},{20,28},{24,16},{28,20},{1,9},{5... | collective-permute-start | bytes 3538952 | tf_op jit(solution)/shard_map/ppermute | solution.py:749
  140.3 9.3 %collective-permute-start.17 = (bf16[2,2,4,96,768]{4,3,2,1,0:T(8,128)(2,1)}, bf16[2,2,4,96,768]{4,3,2,1,0:T(8,128)(2,1)S(1)}, u32[]{:S(2)}, u32[]{:S(2)}) collective-permute-start(bf16[2,2,4,96,768]{4,3,2,1,0:T(8,128)(2,1)} %get-tuple-element.335), channel_id=1, source_target_pairs={{0,4},{4,0},{8,12},{12,8},{16,20},{20,16},{24,28},{28,24},{1,5},{5... | collective-permute-start | bytes 7077896 | tf_op jit(solution)/shard_map/ppermute | solution.py:749
  141.9 8.0 %collective-permute-start.18 = (bf16[2,2,4,96,768]{4,3,2,1,0:T(8,128)(2,1)}, bf16[2,2,4,96,768]{4,3,2,1,0:T(8,128)(2,1)}, u32[]{:S(2)}, u32[]{:S(2)}) collective-permute-start(bf16[2,2,4,96,768]{4,3,2,1,0:T(8,128)(2,1)} %get-tuple-element.336), channel_id=1, source_target_pairs={{0,4},{4,0},{8,12},{12,8},{16,20},{20,16},{24,28},{28,24},{1,5},{5... | collective-permute-start | bytes 7077896 | tf_op jit(solution)/shard_map/ppermute | solution.py:749
  160.2 27.8 %collective-permute-start.19 = (bf16[512,768]{1,0:T(8,128)(2,1)}, bf16[512,768]{1,0:T(8,128)(2,1)S(1)}, u32[]{:S(2)}, u32[]{:S(2)}) collective-permute-start(bf16[512,768]{1,0:T(8,128)(2,1)} %get-tuple-element.346.refs_2_.refs_5_), channel_id=1, source_target_pairs={{0,1},{1,2},{2,3},{4,5},{5,6},{6,7},{8,9},{9,10},{10,11},{12,13},{... | collective-permute-start | bytes 2359304 | tf_op jit(solution)/shard_map/ppermute | solution.py:963
  226.8 178.5 %reduce-scatter.5.cloned.1.call-start = ((), (), s32[]{:S(2)}) async-start(), calls=%async_computation.3 | async-start | bytes 10616832 | tf_op jit(solution)/shard_map/reduce_scatter | solution.py:863
  244.5 20.6 %collective-permute-start.20 = (bf16[512,768]{1,0:T(8,128)(2,1)}, bf16[512,768]{1,0:T(8,128)(2,1)}, u32[]{:S(2)}, u32[]{:S(2)}) collective-permute-start(bf16[512,768]{1,0:T(8,128)(2,1)} %get-tuple-element.372), channel_id=1, source_target_pairs={{1,0},{2,1},{3,2},{5,4},{6,5},{7,6},{9,8},{10,9},{11,10},{13,12},{... | collective-permute-start | bytes 2359304 | tf_op jit(solution)/shard_map/ppermute | solution.py:966
  277.5 22.2 %collective-permute-start.23 = (bf16[2,208,768]{2,1,0:T(8,128)(2,1)}, bf16[2,208,768]{2,1,0:T(8,128)(2,1)S(1)}, u32[]{:S(2)}, u32[]{:S(2)}) collective-permute-start(bf16[2,208,768]{2,1,0:T(8,128)(2,1)} %get-tuple-element.409), channel_id=1, source_target_pairs={{0,16},{4,20},{8,24},{12,28},{16,0},{20,4},{24,8},{28,12},{1,17},{... | collective-permute-start | bytes 1916936 | tf_op jit(solution)/shard_map/ppermute | solution.py:749
  278.7 21.0 %collective-permute-start.24 = (bf16[2,192,768]{2,1,0:T(8,128)(2,1)}, bf16[2,192,768]{2,1,0:T(8,128)(2,1)S(1)}, u32[]{:S(2)}, u32[]{:S(2)}) collective-permute-start(bf16[2,192,768]{2,1,0:T(8,128)(2,1)} %get-tuple-element.410), channel_id=1, source_target_pairs={{0,8},{4,12},{8,0},{12,4},{16,24},{20,28},{24,16},{28,20},{1,9},{5... | collective-permute-start | bytes 1769480 | tf_op jit(solution)/shard_map/ppermute | solution.py:749
  300.7 148.4 %all-gather.7.cloned.1.call-start = ((), (), s32[]{:S(2)}) async-start(), calls=%async_computation.5 | async-start | bytes 4866048 | tf_op jit(solution)/shard_map/all_gather | solution.py:1074
  305.5 31.9 %collective-permute-start.28 = (bf16[208,768]{1,0:T(8,128)(2,1)}, bf16[208,768]{1,0:T(8,128)(2,1)S(1)}, u32[]{:S(2)}, u32[]{:S(2)}) collective-permute-start(bf16[208,768]{1,0:T(8,128)(2,1)} %get-tuple-element.435), channel_id=1, source_target_pairs={{0,8},{4,12},{8,0},{12,4},{16,24},{20,28},{24,16},{28,20},{1,9},{5... | collective-permute-start | bytes 958472 | tf_op jit(solution)/shard_map/ppermute | solution.py:749
  306.7 30.7 %collective-permute-start.29 = (bf16[192,768]{1,0:T(8,128)(2,1)}, bf16[192,768]{1,0:T(8,128)(2,1)}, u32[]{:S(2)}, u32[]{:S(2)}) collective-permute-start(bf16[192,768]{1,0:T(8,128)(2,1)} %get-tuple-element.436), channel_id=1, source_target_pairs={{0,16},{4,20},{8,24},{12,28},{16,0},{20,4},{24,8},{28,12},{1,17},{... | collective-permute-start | bytes 884744 | tf_op jit(solution)/shard_map/ppermute | solution.py:749
  310.9 27.2 %collective-permute-start.25 = (bf16[192,768]{1,0:T(8,128)(2,1)}, bf16[192,768]{1,0:T(8,128)(2,1)S(1)}, u32[]{:S(2)}, u32[]{:S(2)}) collective-permute-start(bf16[192,768]{1,0:T(8,128)(2,1)} %get-tuple-element.432), channel_id=1, source_target_pairs={{0,1},{1,0},{2,3},{3,2},{4,5},{5,4},{6,7},{7,6},{8,9},{9,8},{10,11... | collective-permute-start | bytes 884744 | tf_op jit(solution)/shard_map/ppermute | solution.py:749
  311.1 27.0 %collective-permute-start.26 = (bf16[192,768]{1,0:T(8,128)(2,1)}, bf16[192,768]{1,0:T(8,128)(2,1)}, u32[]{:S(2)}, u32[]{:S(2)}) collective-permute-start(bf16[192,768]{1,0:T(8,128)(2,1)} %get-tuple-element.433), channel_id=1, source_target_pairs={{0,2},{1,3},{2,0},{3,1},{4,6},{5,7},{6,4},{7,5},{8,10},{9,11},{10,... | collective-permute-start | bytes 884744 | tf_op jit(solution)/shard_map/ppermute | solution.py:749
  313.4 25.9 %collective-permute-start.27 = (bf16[192,768]{1,0:T(8,128)(2,1)}, bf16[192,768]{1,0:T(8,128)(2,1)}, u32[]{:S(2)}, u32[]{:S(2)}) collective-permute-start(bf16[192,768]{1,0:T(8,128)(2,1)} %get-tuple-element.434), channel_id=1, source_target_pairs={{0,3},{1,2},{2,1},{3,0},{4,7},{5,6},{6,5},{7,4},{8,11},{9,10},{10,... | collective-permute-start | bytes 884744 | tf_op jit(solution)/shard_map/ppermute | solution.py:749
  339.3 8.3 %collective-permute-start.30 = (bf16[4,208,768]{2,1,0:T(8,128)(2,1)}, bf16[4,208,768]{2,1,0:T(8,128)(2,1)S(1)}, u32[]{:S(2)}, u32[]{:S(2)}) collective-permute-start(bf16[4,208,768]{2,1,0:T(8,128)(2,1)} %get-tuple-element.440), channel_id=1, source_target_pairs={{0,4},{4,0},{8,12},{12,8},{16,20},{20,16},{24,28},{28,24},{1,5},{5... | collective-permute-start | bytes 3833864 | tf_op jit(solution)/shard_map/ppermute | solution.py:749
  345.4 9.7 %collective-permute-start.33 = (bf16[112,768]{1,0:T(8,128)(2,1)}, bf16[112,768]{1,0:T(8,128)(2,1)S(1)}, u32[]{:S(2)}, u32[]{:S(2)}) collective-permute-start(bf16[112,768]{1,0:T(8,128)(2,1)} %get-tuple-element.450), channel_id=1, source_target_pairs={{0,2},{1,3},{2,0},{3,1},{4,6},{5,7},{6,4},{7,5},{8,10},{9,11},{10,... | collective-permute-start | bytes 516104 | tf_op jit(solution)/shard_map/ppermute | solution.py:749
  347.3 15.3 %collective-permute-start.34 = (bf16[112,768]{1,0:T(8,128)(2,1)}, bf16[112,768]{1,0:T(8,128)(2,1)S(1)}, u32[]{:S(2)}, u32[]{:S(2)}) collective-permute-start(bf16[112,768]{1,0:T(8,128)(2,1)} %get-tuple-element.451), channel_id=1, source_target_pairs={{0,3},{1,2},{2,1},{3,0},{4,7},{5,6},{6,5},{7,4},{8,11},{9,10},{10,... | collective-permute-start | bytes 516104 | tf_op jit(solution)/shard_map/ppermute | solution.py:749
  372.5 27.2 %collective-permute-start.36 = (bf16[2,208,768]{2,1,0:T(8,128)(2,1)}, bf16[2,208,768]{2,1,0:T(8,128)(2,1)S(1)}, u32[]{:S(2)}, u32[]{:S(2)}) collective-permute-start(bf16[2,208,768]{2,1,0:T(8,128)(2,1)} %get-tuple-element.456), channel_id=1, source_target_pairs={{0,16},{4,20},{8,24},{12,28},{16,0},{20,4},{24,8},{28,12},{1,17},{... | collective-permute-start | bytes 1916936 | tf_op jit(solution)/shard_map/ppermute | solution.py:749
  372.9 25.6 %collective-permute-start.37 = (bf16[2,192,768]{2,1,0:T(8,128)(2,1)}, bf16[2,192,768]{2,1,0:T(8,128)(2,1)S(1)}, u32[]{:S(2)}, u32[]{:S(2)}) collective-permute-start(bf16[2,192,768]{2,1,0:T(8,128)(2,1)} %get-tuple-element.457), channel_id=1, source_target_pairs={{0,8},{4,12},{8,0},{12,4},{16,24},{20,28},{24,16},{28,20},{1,9},{5... | collective-permute-start | bytes 1769480 | tf_op jit(solution)/shard_map/ppermute | solution.py:749
  373.9 30.5 %collective-permute-start.35 = (bf16[512,768]{1,0:T(8,128)(2,1)S(1)}, bf16[512,768]{1,0:T(8,128)(2,1)S(1)}, u32[]{:S(2)}, u32[]{:S(2)}) collective-permute-start(bf16[512,768]{1,0:T(8,128)(2,1)S(1)} %copy-done.13), channel_id=1, source_target_pairs={{1,0},{2,1},{3,2},{5,4},{6,5},{7,6},{9,8},{10,9},{11,10},{13,12},{... | collective-permute-start | bytes 2359304 | tf_op jit(solution)/shard_map/ppermute | solution.py:966
  405.3 12.4 %collective-permute-start.38 = (bf16[208,768]{1,0:T(8,128)(2,1)}, bf16[208,768]{1,0:T(8,128)(2,1)S(1)}, u32[]{:S(2)}, u32[]{:S(2)}) collective-permute-start(bf16[208,768]{1,0:T(8,128)(2,1)} %get-tuple-element.479), channel_id=1, source_target_pairs={{0,8},{4,12},{8,0},{12,4},{16,24},{20,28},{24,16},{28,20},{1,9},{5... | collective-permute-start | bytes 958472 | tf_op jit(solution)/shard_map/ppermute | solution.py:749
  406.5 11.2 %collective-permute-start.39 = (bf16[192,768]{1,0:T(8,128)(2,1)}, bf16[192,768]{1,0:T(8,128)(2,1)S(1)}, u32[]{:S(2)}, u32[]{:S(2)}) collective-permute-start(bf16[192,768]{1,0:T(8,128)(2,1)} %get-tuple-element.480), channel_id=1, source_target_pairs={{0,16},{4,20},{8,24},{12,28},{16,0},{20,4},{24,8},{28,12},{1,17},{... | collective-permute-start | bytes 884744 | tf_op jit(solution)/shard_map/ppermute | solution.py:749
  409.2 10.6 %collective-permute-start.40 = (bf16[192,768]{1,0:T(8,128)(2,1)}, bf16[192,768]{1,0:T(8,128)(2,1)S(1)}, u32[]{:S(2)}, u32[]{:S(2)}) collective-permute-start(bf16[192,768]{1,0:T(8,128)(2,1)} %get-tuple-element.492), channel_id=1, source_target_pairs={{0,1},{1,0},{2,3},{3,2},{4,5},{5,4},{6,7},{7,6},{8,9},{9,8},{10,11... | collective-permute-start | bytes 884744 | tf_op jit(solution)/shard_map/ppermute | solution.py:749
  409.2 14.4 %collective-permute-start.41 = (bf16[192,768]{1,0:T(8,128)(2,1)}, bf16[192,768]{1,0:T(8,128)(2,1)S(1)}, u32[]{:S(2)}, u32[]{:S(2)}) collective-permute-start(bf16[192,768]{1,0:T(8,128)(2,1)} %get-tuple-element.493), channel_id=1, source_target_pairs={{0,2},{1,3},{2,0},{3,1},{4,6},{5,7},{6,4},{7,5},{8,10},{9,11},{10,... | collective-permute-start | bytes 884744 | tf_op jit(solution)/shard_map/ppermute | solution.py:749
  411.6 24.7 %collective-permute-start.42 = (bf16[192,768]{1,0:T(8,128)(2,1)}, bf16[192,768]{1,0:T(8,128)(2,1)}, u32[]{:S(2)}, u32[]{:S(2)}) collective-permute-start(bf16[192,768]{1,0:T(8,128)(2,1)} %get-tuple-element.494), channel_id=1, source_target_pairs={{0,3},{1,2},{2,1},{3,0},{4,7},{5,6},{6,5},{7,4},{8,11},{9,10},{10,... | collective-permute-start | bytes 884744 | tf_op jit(solution)/shard_map/ppermute | solution.py:749
  438.6 8.9 %collective-permute-start.43 = (bf16[128,768]{1,0:T(8,128)(2,1)}, bf16[128,768]{1,0:T(8,128)(2,1)S(1)}, u32[]{:S(2)}, u32[]{:S(2)}) collective-permute-start(bf16[128,768]{1,0:T(8,128)(2,1)} %get-tuple-element.498), channel_id=1, source_target_pairs={{0,1},{1,0},{2,3},{3,2},{4,5},{5,4},{6,7},{7,6},{8,9},{9,8},{10,11... | collective-permute-start | bytes 589832 | tf_op jit(solution)/shard_map/ppermute | solution.py:749
  438.6 10.2 %collective-permute-start.44 = (bf16[128,768]{1,0:T(8,128)(2,1)}, bf16[128,768]{1,0:T(8,128)(2,1)S(1)}, u32[]{:S(2)}, u32[]{:S(2)}) collective-permute-start(bf16[128,768]{1,0:T(8,128)(2,1)} %get-tuple-element.499), channel_id=1, source_target_pairs={{0,2},{1,3},{2,0},{3,1},{4,6},{5,7},{6,4},{7,5},{8,10},{9,11},{10,... | collective-permute-start | bytes 589832 | tf_op jit(solution)/shard_map/ppermute | solution.py:749
  442.8 17.0 %collective-permute-start.46 = (bf16[192,768]{1,0:T(8,128)(2,1)}, bf16[192,768]{1,0:T(8,128)(2,1)S(1)}, u32[]{:S(2)}, u32[]{:S(2)}) collective-permute-start(bf16[192,768]{1,0:T(8,128)(2,1)} %get-tuple-element.514.refs_9_), channel_id=1, source_target_pairs={{0,4},{4,0},{8,12},{12,8},{16,20},{20,16},{24,28},{28,24},{1,5},{5... | collective-permute-start | bytes 884744 | tf_op jit(solution)/shard_map/ppermute | solution.py:749
  446.1 13.6 %collective-permute-start.47 = (bf16[192,768]{1,0:T(8,128)(2,1)}, bf16[192,768]{1,0:T(8,128)(2,1)S(1)}, u32[]{:S(2)}, u32[]{:S(2)}) collective-permute-start(bf16[192,768]{1,0:T(8,128)(2,1)} %get-tuple-element.514.refs_9_), channel_id=1, source_target_pairs={{0,8},{4,12},{8,0},{12,4},{16,24},{20,28},{24,16},{28,20},{1,9},{5... | collective-permute-start | bytes 884744 | tf_op jit(solution)/shard_map/ppermute | solution.py:749
  447.0 12.8 %collective-permute-start.48 = (bf16[192,768]{1,0:T(8,128)(2,1)}, bf16[192,768]{1,0:T(8,128)(2,1)S(1)}, u32[]{:S(2)}, u32[]{:S(2)}) collective-permute-start(bf16[192,768]{1,0:T(8,128)(2,1)} %get-tuple-element.514.refs_9_), channel_id=1, source_target_pairs={{0,16},{4,20},{8,24},{12,28},{16,0},{20,4},{24,8},{28,12},{1,17},{... | collective-permute-start | bytes 884744 | tf_op jit(solution)/shard_map/ppermute | solution.py:749
  447.5 14.7 %collective-permute-start.49 = (bf16[192,768]{1,0:T(8,128)(2,1)}, bf16[192,768]{1,0:T(8,128)(2,1)S(1)}, u32[]{:S(2)}, u32[]{:S(2)}) collective-permute-start(bf16[192,768]{1,0:T(8,128)(2,1)} %get-tuple-element.514.refs_9_), channel_id=1, source_target_pairs={{0,24},{4,28},{8,16},{12,20},{16,8},{20,12},{24,0},{28,4},{1,25},{... | collective-permute-start | bytes 884744 | tf_op jit(solution)/shard_map/ppermute | solution.py:749
  448.8 10.2 %collective-permute-start.45 = (bf16[128,768]{1,0:T(8,128)(2,1)S(1)}, bf16[128,768]{1,0:T(8,128)(2,1)S(1)}, u32[]{:S(2)}, u32[]{:S(2)}) collective-permute-start(bf16[128,768]{1,0:T(8,128)(2,1)S(1)} %copy-done.94), channel_id=1, source_target_pairs={{0,3},{1,2},{2,1},{3,0},{4,7},{5,6},{6,5},{7,4},{8,11},{9,10},{10,... | collective-permute-start | bytes 589832 | tf_op jit(solution)/shard_map/ppermute | solution.py:749
  465.2 7.8 %collective-permute-start.51 = (bf16[176,768]{1,0:T(8,128)(2,1)}, bf16[176,768]{1,0:T(8,128)(2,1)S(1)}, u32[]{:S(2)}, u32[]{:S(2)}) collective-permute-start(bf16[176,768]{1,0:T(8,128)(2,1)} %get-tuple-element.521.refs_1_), channel_id=1, source_target_pairs={{0,8},{4,12},{8,0},{12,4},{16,24},{20,28},{24,16},{28,20},{1,9},{5... | collective-permute-start | bytes 811016 | tf_op jit(solution)/shard_map/ppermute | solution.py:749
  467.0 12.0 %collective-permute-start.53 = (bf16[176,768]{1,0:T(8,128)(2,1)}, bf16[176,768]{1,0:T(8,128)(2,1)S(1)}, u32[]{:S(2)}, u32[]{:S(2)}) collective-permute-start(bf16[176,768]{1,0:T(8,128)(2,1)} %get-tuple-element.521.refs_1_), channel_id=1, source_target_pairs={{0,24},{4,28},{8,16},{12,20},{16,8},{20,12},{24,0},{28,4},{1,25},{... | collective-permute-start | bytes 811016 | tf_op jit(solution)/shard_map/ppermute | solution.py:749
  (130 other events, 463.9 us)
Sparse Core Ops, SparseCore 0:
  55.8 124.8 all-gather.4
  226.9 81.4 reduce-scatter.2
  311.9 86.4 reduce-scatter.4
  400.2 40.9 all-gather.6
